TPU v7x, 32 devices: a whole 2x2x4 slice. The times are simulated.
32 devices in a mesh: shots: 2 (over x), gx: 16 (over z, y, core).
Axes of the slice: x: 2, y: 2, z: 4, core: 2. Of those that a mesh axis runs over, the one named last changes fastest.
Arguments:
- forward_field: bfloat16 [512, 2, 8, 4096], P(('shots', 'gx')), parts along dimension 0, may hold values from -3 to 3
- adjoint_field: bfloat16 [512, 2, 8, 4096], P(('shots', 'gx')), parts along dimension 0, may hold values from -3 to 3
Outputs:
- filtered_image: float32 [33, 512, 4096], P(None, ('shots', 'gx')), parts along dimension 1
There are 2 independent parts, one for each index of `shots`. A program takes and returns all parts, laid end to end along the dimension named above; each array names one. Nothing has to cross between parts.
All inputs are finite; a program needn't handle non-finite values.
Results may differ from a plain program's by a relative error of at most 0.0003.
Values may be sent and summed in bfloat16 or wider, within the bound.
No kernel may reach another device: no remote copies, remote signals or barrier semaphores. Data moves between devices by JAX's collectives and lax.ppermute only.
A program may use at most 128 MiB of HBM per device.

v0:
```python
import jax
import jax.numpy as jnp
from jax import lax
from jax.sharding import PartitionSpec as P

Z = 64
HALF = 16
LAGS = 33


def padded_2(value, sides, width):
    for axis, dim in sides:
        peers, length = (lax.axis_size(axis), value.shape[dim])
        up = [(i, (i + 1) % peers) for i in range(peers - 1)]
        down = [(j, i) for i, j in up]
        last = lax.slice_in_dim(value, length - width, length, axis=dim)
        first = lax.slice_in_dim(value, 0, width, axis=dim)
        before = lax.ppermute(last, axis, up)
        after = lax.ppermute(first, axis, down)
        value = jnp.concatenate([before, value, after], axis=dim)
    return value


def correlate(forward_wide, adjoint_wide, cells_kept):

    def per_offset(offset_index):
        source_part = lax.dynamic_slice_in_dim(
            forward_wide, 2 * HALF - offset_index, cells_kept, 0
        ).astype(jnp.float32)
        receiver_part = lax.dynamic_slice_in_dim(adjoint_wide, offset_index, cells_kept, 0).astype(
            jnp.float32
        )
        return jnp.sum(source_part * receiver_part, axis=(1, 2))

    return lax.map(per_offset, jnp.arange(LAGS, dtype=jnp.int32))


def laplace(padded):
    middle = padded[:, 1:-1]
    shaped = middle.reshape(middle.shape[0], middle.shape[1], middle.shape[2] // Z, Z)
    deeper = jnp.pad(shaped, ((0, 0), (0, 0), (0, 0), (1, 1)))
    along_depth = (deeper[..., 2:] + deeper[..., :-2]).reshape(middle.shape)
    return 0.25 * (padded[:, 2:] + padded[:, :-2] + along_depth - 4.0 * middle)


def on_device(forward_field, adjoint_field):
    cells_local = forward_field.shape[0]
    stacked = jnp.stack([forward_field, adjoint_field], 0)
    widened = padded_2(stacked, (("gx", 1),), HALF)
    offset_image = correlate(widened[0], widened[1], cells_local)
    rimmed = padded_2(offset_image, (("gx", 1),), 1)
    return laplace(rimmed)


def solution(mesh):
    placed = (P(("shots", "gx"), None, None, None), P(("shots", "gx"), None, None, None))
    return jax.shard_map(
        on_device,
        mesh=mesh,
        in_specs=placed,
        out_specs=P(None, ("shots", "gx"), None),
        check_vma=False,
    )
```

profile of v0, /device:TPU:17, one launch (start us, length us, event | category | flops | bytes accessed | tf_op | source)
XLA Modules:
  0.0 455.8 jit_solution(4907795537857488979)
XLA Ops:
  0.0 4.8 %pad_maximum_fusion.3 = bf16[2,16,2,8,4096]{4,3,2,1,0:T(8,128)(2,1)} fusion(bf16[1,16,2,8,4096]{4,3,2,1,0:T(8,128)(2,1)} %bitcast.15, bf16[1,16,2,8,4096]{4,3,2,1,0:T(8,128)(2,1)} %bitcast.17), kind=kLoop, calls=%fused_computation.12 | loop fusion | flops 2097152 | bytes 8388608 | tf_op jit(solution)/shard_map/stack | solution.py:48
  4.8 2.6 collective-permute-start.1
  7.4 3.0 collective-permute-start
  10.4 89.5 %collective-permute-done.1 = bf16[2,16,2,8,4096]{4,3,2,1,0:T(8,128)(2,1)} collective-permute-done((bf16[2,16,2,8,4096]{4,3,2,1,0:T(8,128)(2,1)}, bf16[2,16,2,8,4096]{4,3,2,1,0:T(8,128)(2,1)}, u32[]{:S(2)}, u32[]{:S(2)}) %collective-permute-start.1) | collective-permute-done | bytes 4194336 | tf_op jit(solution)/shard_map/ppermute | solution.py:19
  100.1 6.3 %pad_maximum_fusion = bf16[2,48,2,8,4096]{4,3,2,1,0:T(8,128)(2,1)S(1)} fusion(bf16[2,16,2,8,4096]{4,3,2,1,0:T(8,128)(2,1)} %collective-permute-done.1, bf16[1,16,2,8,4096]{4,3,2,1,0:T(8,128)(2,1)S(1)} %bitcast.16, bf16[1,16,2,8,4096]{4,3,2,1,0:T(8,128)(2,1)} %bitcast.18, bf16[2,16,2,8,4096]{4,3,2,1,0:T(8,128)(2,1)} %collective-permute-done), kind=kLoop, calls=%fused_computation.3 | loop fusion | flops 18874368 | bytes 25165824 | tf_op jit(solution)/shard_map/concatenate | solution.py:20
  106.3 5.1 %slice_bitcast_fusion = (bf16[48,2,8,4096]{3,2,1,0:T(8,128)(2,1)}, bf16[48,2,8,4096]{3,2,1,0:T(8,128)(2,1)}) fusion(bf16[2,48,2,8,4096]{4,3,2,1,0:T(8,128)(2,1)S(1)} %pad_maximum_fusion), kind=kLoop, calls=%fused_computation.10 | loop fusion | bytes 25165824 | tf_op jit(solution)/shard_map/squeeze | solution.py:50
  111.5 259.1 %while.12 = (s32[]{:T(128)}, f32[33,16,4096]{2,1,0:T(8,128)}, s32[33]{0:T(128)S(1)}, bf16[48,2,8,4096]{3,2,1,0:T(8,128)(2,1)}, bf16[48,2,8,4096]{3,2,1,0:T(8,128...) while((s32[]{:T(128)}, f32[33,16,4096]{2,1,0:T(8,128)}, s32[33]{0:T(128)S(1)}, ...), condition=%wide.region_2.3_spmd, body=%wide.region_0.2_spmd.sunk | while | flops 4128777 | bytes 4980949 | solution.py:35
  115.2 3.3 multiply_reduce_fusion.2
  118.6 0.7 bitcast_dynamic-update-slice_fusion.2
  123.1 3.3 multiply_reduce_fusion.2
  131.0 3.3 multiply_reduce_fusion.2
  138.8 3.3 multiply_reduce_fusion.2
  146.6 3.3 multiply_reduce_fusion.2
  154.5 3.3 multiply_reduce_fusion.2
  162.3 3.3 multiply_reduce_fusion.2
  165.7 0.7 bitcast_dynamic-update-slice_fusion.2
  170.2 3.3 multiply_reduce_fusion.2
  173.5 0.8 bitcast_dynamic-update-slice_fusion.2
  178.1 3.3 multiply_reduce_fusion.2
  181.4 0.7 bitcast_dynamic-update-slice_fusion.2
  185.9 3.3 multiply_reduce_fusion.2
  189.3 0.7 bitcast_dynamic-update-slice_fusion.2
  193.8 3.3 multiply_reduce_fusion.2
  201.6 3.3 multiply_reduce_fusion.2
  205.0 0.7 bitcast_dynamic-update-slice_fusion.2
  209.5 3.3 multiply_reduce_fusion.2
  217.3 3.3 multiply_reduce_fusion.2
  225.2 3.3 multiply_reduce_fusion.2
  228.5 0.7 bitcast_dynamic-update-slice_fusion.2
  233.0 3.3 multiply_reduce_fusion.2
  240.9 3.3 multiply_reduce_fusion.2
  248.7 3.3 multiply_reduce_fusion.2
  252.1 0.7 bitcast_dynamic-update-slice_fusion.2
  256.6 3.3 multiply_reduce_fusion.2
  264.5 3.3 multiply_reduce_fusion.2
  272.3 3.3 multiply_reduce_fusion.2
  280.1 3.3 multiply_reduce_fusion.2
  283.5 0.7 bitcast_dynamic-update-slice_fusion.2
  288.0 3.3 multiply_reduce_fusion.2
  295.9 3.3 multiply_reduce_fusion.2
  299.2 0.7 bitcast_dynamic-update-slice_fusion.2
  303.7 3.3 multiply_reduce_fusion.2
  311.6 3.3 multiply_reduce_fusion.2
  314.9 0.7 bitcast_dynamic-update-slice_fusion.2
  319.4 3.3 multiply_reduce_fusion.2
  322.8 0.7 bitcast_dynamic-update-slice_fusion.2
  327.3 3.3 multiply_reduce_fusion.2
  330.6 0.7 bitcast_dynamic-update-slice_fusion.2
  335.1 3.3 multiply_reduce_fusion.2
  343.0 3.3 multiply_reduce_fusion.2
  350.8 3.3 multiply_reduce_fusion.2
  354.2 0.7 bitcast_dynamic-update-slice_fusion.2
  358.7 3.3 multiply_reduce_fusion.2
  366.5 3.3 multiply_reduce_fusion.2
  370.6 14.7 %reshape.6 = f32[33,16,64,64]{3,2,1,0:T(8,128)} reshape(f32[33,16,4096]{2,1,0:T(8,128)} %get-tuple-element.70) | data formatting | bytes 17301504 | tf_op jit(solution)/shard_map/reshape | solution.py:40
  385.3 12.8 %copy.3 = f32[33,16,4096]{2,0,1:T(8,128)} copy(f32[33,16,4096]{2,1,0:T(8,128)} %get-tuple-element.70) | data formatting | bytes 17301504 | tf_op jit(solution)/shard_map/while | solution.py:35
  398.1 2.5 fusion.4
  400.5 4.4 collective-permute-start.3
  404.9 2.1 collective-permute-start.2
  407.0 11.2 %slice_add_fusion = f32[33,16,64,64]{3,2,1,0:T(8,128)} fusion(f32[33,16,64,64]{3,2,1,0:T(8,128)S(1)} %copy-done), kind=kLoop, calls=%fused_computation.2 | loop fusion | flops 2162688 | bytes 17301504 | tf_op jit(solution)/shard_map/add | solution.py:42
  418.2 15.2 %reshape.7 = f32[33,16,4096]{2,1,0:T(8,128)} reshape(f32[33,16,64,64]{3,2,1,0:T(8,128)} %slice_add_fusion) | data formatting | bytes 17301504 | tf_op jit(solution)/shard_map/reshape | solution.py:42
  433.5 1.6 copy.6
  435.2 1.6 copy.4
  436.8 19.0 %fusion.3 = f32[33,16,4096]{2,1,0:T(8,128)} fusion(f32[33,16,4096]{2,1,0:T(8,128)} %reshape.7, f32[33,16,4096]{2,1,0:T(8,128)} %get-tuple-element.70, f32[33,1,4096]{2,1,0:T(1,128)S(1)} %copy.6, f32[33,1,4096]{2,1,0:T(1,128)S(1)} %copy.4), kind=kLoop, calls=%fused_computation.8 | loop fusion | flops 15138816 | bytes 27033600 | tf_op jit(solution)/shard_map/mul | solution.py:43
  (61 shorter events, 33.8 us)
Async XLA Ops:
  0.0 100.1 %copy-start.1 = (bf16[16,2,8,4096]{3,2,1,0:T(8,128)(2,1)S(1)}, bf16[16,2,8,4096]{3,2,1,0:T(8,128)(2,1)}, u32[]{:S(2)}) copy-start(bf16[16,2,8,4096]{3,2,1,0:T(8,128)(2,1)} %param.5) | copy-start | bytes 6291460
  4.8 95.1 %collective-permute-start.1 = (bf16[2,16,2,8,4096]{4,3,2,1,0:T(8,128)(2,1)}, bf16[2,16,2,8,4096]{4,3,2,1,0:T(8,128)(2,1)}, u32[]{:S(2)}, u32[]{:S(2)}) collective-permute-start(bf16[2,16,2,8,4096]{4,3,2,1,0:T(8,128)(2,1)} %pad_maximum_fusion.3), channel_id=1, source_target_pairs={{1,0},{2,1},{3,2},{4,3},{5,4},{6,5},{7,6},{8,7},{9,8},{10,9},{11,1... | collective-permute-start | bytes 12582920 | tf_op jit(solution)/shard_map/ppermute | solution.py:19
  7.4 92.7 %collective-permute-start = (bf16[2,16,2,8,4096]{4,3,2,1,0:T(8,128)(2,1)}, bf16[2,16,2,8,4096]{4,3,2,1,0:T(8,128)(2,1)}, u32[]{:S(2)}, u32[]{:S(2)}) collective-permute-start(bf16[2,16,2,8,4096]{4,3,2,1,0:T(8,128)(2,1)} %pad_maximum_fusion.3), channel_id=1, source_target_pairs={{0,1},{1,2},{2,3},{3,4},{4,5},{5,6},{6,7},{7,8},{8,9},{9,10},{10,1... | collective-permute-start | bytes 12582920 | tf_op jit(solution)/shard_map/ppermute | solution.py:18
  385.3 21.8 %copy-start = (f32[33,16,64,64]{3,2,1,0:T(8,128)S(1)}, f32[33,16,64,64]{3,2,1,0:T(8,128)}, u32[]{:S(2)}) copy-start(f32[33,16,64,64]{3,2,1,0:T(8,128)} %reshape.6) | copy-start | bytes 25952260
  400.5 33.0 %collective-permute-start.3 = (f32[33,1,4096]{2,0,1:T(8,128)}, f32[33,1,4096]{2,0,1:T(8,128)}, u32[]{:S(2)}, u32[]{:S(2)}) collective-permute-start(f32[33,1,4096]{2,0,1:T(8,128)} %get-tuple-element.84), channel_id=1, source_target_pairs={{0,1},{1,2},{2,3},{3,4},{4,5},{5,6},{6,7},{7,8},{8,9},{9,10},{10,1... | collective-permute-start | bytes 1622024 | tf_op jit(solution)/shard_map/ppermute | solution.py:18
  404.9 30.2 %collective-permute-start.2 = (f32[33,1,4096]{2,0,1:T(8,128)}, f32[33,1,4096]{2,0,1:T(8,128)}, u32[]{:S(2)}, u32[]{:S(2)}) collective-permute-start(f32[33,1,4096]{2,0,1:T(8,128)} %get-tuple-element.83), channel_id=1, source_target_pairs={{1,0},{2,1},{3,2},{4,3},{5,4},{6,5},{7,6},{8,7},{9,8},{10,9},{11,1... | collective-permute-start | bytes 1622024 | tf_op jit(solution)/shard_map/ppermute | solution.py:19
where the time goes:
time: 459 us; the launch traced here: 456 us
  other arithmetic  151 us (33%)
  loops' own time  105 us (23%)
  local copies, waits for them, and re-layouts  97.5 us (21%)
  waiting for transfers between devices  89.7 us (20%)
  starting transfers between devices  12.1 us (3%)
    reduce_sum x33, other arithmetic, per_offset(): return jnp.sum(source_part * receiver_part, axis=(1, 2))  110 us
    another operation x1, loops' own time, correlate(): return lax.map(per_offset, jnp.arange(LAGS, dtype=jnp.int32))  105 us
    ppermute x2, waiting for transfers between devices, padded_2(): after = lax.ppermute(first, axis, down)  89.5 us
    dynamic_update_slice x33, local copies, waits for them, and re-layouts, correlate(): return lax.map(per_offset, jnp.arange(LAGS, dtype=jnp.int32))  24 us
    dynamic_slice x33, local copies, waits for them, and re-layouts, correlate(): return lax.map(per_offset, jnp.arange(LAGS, dtype=jnp.int32))  19.9 us
    mul x1, other arithmetic, laplace(): return 0.25 * (padded[:, 2:] + padded[:, :-2] + along_depth - 4.0 * middle)  19 us
    reshape x1, local copies, waits for them, and re-layouts, laplace(): along_depth = (deeper[..., 2:] + deeper[..., :-2]).reshape(middle.shape)  15.2 us
    reshape x1, local copies, waits for them, and re-layouts, laplace(): middle.reshape(middle.shape[0], middle.shape[1], middle.shape[2] // Z, Z)  14.7 us
  transfers between devices with their start and end apart: 4, of which 2 were waited for; matrix products, arithmetic and copies ran while one was open for 6% of the time, Pallas kernels for 0%

commit v1 on v0

v1 whole, which is shorter than its diff:
```python
import functools

import jax
import jax.numpy as jnp
from jax import lax
from jax.experimental import pallas as pl
from jax.experimental.pallas import tpu as pltpu
from jax.sharding import PartitionSpec as P

Z = 64
HALF = 16
LAGS = 33
BLOCK = 3
OFF = 17
WIDE = 50
LANES = 128
CELLS = 512

CHUNKS = ((16, 1), (5, 4, 3, 2), (11, 10, 9, 8, 7, 6), (14, 13, 12), (15,))
BLOCKS = ((5, 4, 6), (2, 3, 7, 8), (1, 9), (0, 10))


def left_rows(chunk):
    return [-i for i in chunk]


def right_rows(chunk, cells):
    return [cells - 1 + i for i in reversed(chunk)]


def take(field, rows):
    spans, out = [], []
    for r in rows:
        if spans and spans[-1][1] == r:
            spans[-1][1] = r + 1
        else:
            spans.append([r, r + 1])
    for a, b in spans:
        out.append(lax.slice_in_dim(field, a, b, axis=0))
    return out


def correlate_rows(s, r):
    t = s * r
    return jnp.sum(t[:, 0] + t[:, 1], axis=1)


def edge_kernel(a_ref, b_ref, lo_ref, hi_ref):
    def row(ref, k):
        return ref[k : k + 1].astype(jnp.float32)

    lo_ref[0:1] = correlate_rows(row(b_ref, 0), row(a_ref, 2))
    lo_ref[1:2] = correlate_rows(row(a_ref, 0), row(b_ref, 2))
    hi_ref[0:1] = correlate_rows(row(b_ref, 1), row(a_ref, 3))
    hi_ref[1:2] = correlate_rows(row(a_ref, 1), row(b_ref, 3))


def lag_block(blk, nblk, blocks):
    out = jnp.int32(blocks[0])
    for k in range(1, nblk):
        out = jnp.where(blk == k, blocks[k], out)
    return out


def lag_kernel(cells, blocks, places, rim, *refs):
    n_in = len(places)
    ins = refs[:n_in]
    pos = n_in
    if rim:
        lo_ref, hi_ref = refs[pos : pos + 2]
        pos += 2
    if refs[pos].shape[0] == LAGS:
        pos += 1
    out_ref, wide, padded = refs[pos : pos + 3]
    blk = pl.program_id(1)

    @pl.when(blk == 0)
    def _():
        if rim:
            wide[:, 0:1] = jnp.zeros_like(wide[:, 0:1])
            wide[:, WIDE - 1 : WIDE] = jnp.zeros_like(wide[:, 0:1])
        for ref, place in zip(ins, places):
            for src, field, dst, n in place:
                wide[field, dst : dst + n] = ref[src : src + n].astype(jnp.float32)

    base = lag_block(blk, len(blocks), blocks) * BLOCK
    lane = lax.broadcasted_iota(jnp.int32, (cells, LANES), 1) % Z
    first = lane == 0
    last = lane == Z - 1

    def tile(j, _):
        cols = pl.ds(pl.multiple_of(j * LANES, LANES), LANES)

        for t in range(BLOCK):
            h = base + t - HALF
            s = wide[0, pl.ds(OFF - 1 - h, cells + 2), :, :, cols]
            r = wide[1, pl.ds(OFF - 1 + h, cells + 2), :, :, cols]
            u = correlate_rows(s, r)
            padded[7 : 9 + cells] = u
            if rim:
                for at, outer in ((0, h == -HALF), (1, h == HALF)):
                    lo = jnp.where(outer, lo_ref[at : at + 1, cols], 0.0)
                    hi = jnp.where(outer, hi_ref[at : at + 1, cols], 0.0)
                    padded[7:8] = padded[7:8] + lo
                    padded[8 + cells : 9 + cells] = padded[8 + cells : 9 + cells] + hi
            mid = padded[8 : 8 + cells]
            down = jnp.where(first, 0.0, pltpu.roll(mid, 1, 1))
            up = jnp.where(last, 0.0, pltpu.roll(mid, LANES - 1, 1))
            around = padded[7 : 7 + cells] + padded[9 : 9 + cells] + (down + up)
            out_ref[t, :, cols] = 0.25 * (around - 4.0 * mid)
        return 0

    lax.fori_loop(0, CELLS // LANES, tile, 0)


def on_device(forward_field, adjoint_field):
    cells, parts, freqs, width = forward_field.shape
    peers = lax.axis_size("gx")
    up = [(i, (i + 1) % peers) for i in range(peers - 1)]
    down = [(j, i) for i, j in up]
    field_bytes = parts * freqs * width * 2

    from_left, from_right = [], []
    for chunk in CHUNKS:
        to_right = [cells + r for r in left_rows(chunk)]
        to_left = [r - cells for r in right_rows(chunk, cells)]
        sent_up = jnp.concatenate(
            take(forward_field, to_right) + take(adjoint_field, to_right), axis=0
        )
        sent_down = jnp.concatenate(
            take(forward_field, to_left) + take(adjoint_field, to_left), axis=0
        )
        from_left.append(lax.ppermute(sent_up, "gx", up))
        from_right.append(lax.ppermute(sent_down, "gx", down))

    steps = width // CELLS
    rows4 = pl.BlockSpec((4, parts, freqs, CELLS), lambda c: (0, 0, 0, c))
    rim_spec = pl.BlockSpec((2, CELLS), lambda c: (0, c))
    lo, hi = pl.pallas_call(
        edge_kernel,
        grid=(steps,),
        in_specs=[rows4, rows4],
        out_specs=[rim_spec, rim_spec],
        out_shape=[jax.ShapeDtypeStruct((2, width), jnp.float32)] * 2,
        cost_estimate=pl.CostEstimate(
            flops=8 * parts * freqs * width, bytes_accessed=12 * field_bytes, transcendentals=0
        ),
        name="rim",
    )(from_left[0], from_right[0])
    rim_hi = lax.ppermute(lo, "gx", down)
    rim_lo = lax.ppermute(hi, "gx", up)

    image = None
    for stage, blocks in enumerate(BLOCKS):
        reach = max(max(abs(3 * b - HALF), abs(3 * b + 2 - HALF)) for b in blocks)
        rim = reach == HALF
        operands = [forward_field, adjoint_field]
        places = [[(0, 0, OFF, cells)], [(0, 1, OFF, cells)]]
        for g in range(stage + 2):
            n = len(CHUNKS[g])
            for got, rows in (
                (from_left[g], left_rows(CHUNKS[g])),
                (from_right[g], right_rows(CHUNKS[g], cells)),
            ):
                place = []
                for field in (0, 1):
                    k = 0
                    while k < n:
                        m = 1
                        while k + m < n and rows[k + m] == rows[k] + m:
                            m += 1
                        place.append((field * n + k, field, OFF + rows[k], m))
                        k += m
                operands.append(got)
                places.append(place)
        specs = [
            pl.BlockSpec((o.shape[0], parts, freqs, CELLS), lambda c, b: (0, 0, 0, c))
            for o in operands
        ]
        if rim:
            operands += [rim_lo, rim_hi]
            specs += [pl.BlockSpec((2, CELLS), lambda c, b: (0, c))] * 2
        aliases = {}
        if image is not None:
            aliases = {len(operands): 0}
            operands.append(image)
            specs.append(pl.BlockSpec(memory_space=pl.ANY))
        nblk = len(blocks)
        image = pl.pallas_call(
            functools.partial(lag_kernel, cells, blocks, places, rim),
            grid=(steps, nblk),
            in_specs=specs,
            out_specs=pl.BlockSpec(
                (BLOCK, cells, CELLS),
                lambda c, b, nblk=nblk, blocks=blocks: (lag_block(b, nblk, blocks), 0, c),
            ),
            out_shape=jax.ShapeDtypeStruct((LAGS, cells, width), jnp.float32),
            scratch_shapes=[
                pltpu.VMEM((2, WIDE, parts, freqs, CELLS), jnp.float32),
                pltpu.VMEM((32, LANES), jnp.float32),
            ],
            input_output_aliases=aliases,
            compiler_params=pltpu.CompilerParams(vmem_limit_bytes=40 * 2**20),
            cost_estimate=pl.CostEstimate(
                flops=2 * 3 * nblk * (cells + 2) * parts * freqs * width,
                bytes_accessed=3 * nblk * cells * width * 4
                + sum(o.shape[0] for o in operands[: len(places)]) * field_bytes,
                transcendentals=0,
            ),
            name="lags_%d" % stage,
        )(*operands)
    return image


def solution(mesh):
    placed = (P(("shots", "gx"), None, None, None), P(("shots", "gx"), None, None, None))
    return jax.shard_map(
        on_device,
        mesh=mesh,
        in_specs=placed,
        out_specs=P(None, ("shots", "gx"), None),
        check_vma=False,
    )
```

time: 459 us -> 210 us (0.46)
  other arithmetic: 151 us -> 4.08 us
  loops' own time: 105 us -> 0 us
  Pallas kernels: 0 us -> 96.9 us
  local copies, waits for them, and re-layouts: 97.5 us -> 9.78 us
  waiting for transfers between devices: 89.7 us -> 62.8 us
  starting transfers between devices: 12.1 us -> 34 us
    reduce_sum x33 -> x0, other arithmetic: 110 us -> none  [per_offset(): return jnp.sum(source_part * receiver_part, axis=(1, 2))]
    another operation x1 -> x0, loops' own time: 105 us -> none  [correlate(): return lax.map(per_offset, jnp.arange(LAGS, dtype=jnp.int32))]
    pallas_call x0 -> x5, Pallas kernels: none -> 96.9 us  [the longest x4 92 us: on_device(): pl.pallas_call(functools.partial(lag_kernel, cells, blocks, places, rim),...]
    reshape x2 -> x0, local copies, waits for them, and re-layouts: 29.9 us -> none  [the longest x1 15.2 us: laplace(): along_depth = (deeper[..., 2:] + deeper[..., :-2]).reshape(middle.shape)]
    ppermute x4 -> x12, waiting for transfers between devices: 89.7 us -> 62.8 us  [the longest x5 62.6 us: on_device(): from_left.append(lax.ppermute(sent_up, 'gx', up))]
    dynamic_update_slice x33 -> x0, local copies, waits for them, and re-layouts: 24 us -> none  [correlate(): return lax.map(per_offset, jnp.arange(LAGS, dtype=jnp.int32))]
    ppermute x4 -> x12, starting transfers between devices: 12.1 us -> 34 us  [the longest x5 18 us: on_device(): from_left.append(lax.ppermute(sent_up, 'gx', up))]
    dynamic_slice x33 -> x0, local copies, waits for them, and re-layouts: 19.9 us -> none  [correlate(): return lax.map(per_offset, jnp.arange(LAGS, dtype=jnp.int32))]
  transfers between devices with their start and end apart: 4 -> 12, of which waited for: 2 -> 4; matrix products, arithmetic and copies ran while one was open for 6% -> 2% of each run, Pallas kernels for 0% -> 37%
where the time goes in v1:
time: 210 us; the launch traced here: 208 us
  Pallas kernels  96.9 us (46%)
  waiting for transfers between devices  62.8 us (30%)
  starting transfers between devices  34 us (16%)
  local copies, waits for them, and re-layouts  9.78 us (5%)
  other arithmetic  4.08 us (2%)
    pallas_call x4, Pallas kernels, on_device(): pl.pallas_call(functools.partial(lag_kernel, cells, blocks, places, rim),...  92 us
    ppermute x5, waiting for transfers between devices, on_device(): from_left.append(lax.ppermute(sent_up, 'gx', up))  62.6 us
    ppermute x5, starting transfers between devices, on_device(): from_left.append(lax.ppermute(sent_up, 'gx', up))  18 us
    ppermute x5, starting transfers between devices, on_device(): from_right.append(lax.ppermute(sent_down, 'gx', down))  10.5 us
    unnamed x26, local copies, waits for them, and re-layouts  8.12 us
    pallas_call x1, Pallas kernels, on_device(): pl.pallas_call(edge_kernel, grid=(steps,), in_specs=[rows4, rows4], out_s...  4.89 us
  transfers between devices with their start and end apart: 12, of which 4 were waited for; matrix products, arithmetic and copies ran while one was open for 2% of the time, Pallas kernels for 37%

profile of v1, /device:TPU:17, one launch (start us, length us, event | category | flops | bytes accessed | tf_op | source)
XLA Modules:
  0.0 208.0 jit_solution(4518402535720593014)
XLA Ops:
  0.0 1.4 fusion
  1.4 0.0 slice-start
  1.4 0.0 slice-start.1
  1.4 0.1 pad_maximum_fusion.5
  1.5 2.7 %collective-permute-start.1 = (bf16[4,2,8,4096]{3,2,1,0:T(8,128)(2,1)S(1)}, bf16[4,2,8,4096]{3,2,1,0:T(8,128)(2,1)S(1)}, u32[]{:S(2)}, u32[]{:S(2)}) collective-permute-start(bf16[4,2,8,4096]{3,2,1,0:T(8,128)(2,1)S(1)} %pad_maximum_fusion.5), channel_id=1, source_target_pairs={{1,0},{2,1},{3,2},{4,3},{5,4},{6,5},{7,6},{8,7},{9,8},{10,9},{11,1... | collective-permute-start | bytes 1572872 | tf_op jit(solution)/shard_map/ppermute | solution.py:134
  4.2 3.0 %collective-permute-start = (bf16[4,2,8,4096]{3,2,1,0:T(8,128)(2,1)S(1)}, bf16[4,2,8,4096]{3,2,1,0:T(8,128)(2,1)S(1)}, u32[]{:S(2)}, u32[]{:S(2)}) collective-permute-start(bf16[4,2,8,4096]{3,2,1,0:T(8,128)(2,1)S(1)} %pad_maximum_fusion.5), channel_id=1, source_target_pairs={{0,1},{1,2},{2,3},{3,4},{4,5},{5,6},{6,7},{7,8},{8,9},{9,10},{10,1... | collective-permute-start | bytes 1572872 | tf_op jit(solution)/shard_map/ppermute | solution.py:133
  7.2 0.0 copy-start
  7.2 0.0 copy-start.1
  7.3 0.0 slice-done
  7.3 0.0 slice-done.1
  7.3 1.3 pad_maximum_fusion
  8.6 2.0 collective-permute-start.5
  10.6 3.6 %collective-permute-start.4 = (bf16[12,2,8,4096]{3,2,1,0:T(8,128)(2,1)}, bf16[12,2,8,4096]{3,2,1,0:T(8,128)(2,1)}, u32[]{:S(2)}, u32[]{:S(2)}) collective-permute-start(bf16[12,2,8,4096]{3,2,1,0:T(8,128)(2,1)} %pad_maximum_fusion), channel_id=1, source_target_pairs={{0,1},{1,2},{2,3},{3,4},{4,5},{5,6},{6,7},{7,8},{8,9},{9,10},{10,1... | collective-permute-start | bytes 4718600 | tf_op jit(solution)/shard_map/ppermute | solution.py:133
  14.3 0.0 copy-done
  14.3 0.0 copy-done.1
  14.3 0.1 fusion.2
  14.4 0.1 pad_maximum_fusion.3
  14.5 2.6 %collective-permute-start.6 = (bf16[6,2,8,4096]{3,2,1,0:T(8,128)(2,1)S(1)}, bf16[6,2,8,4096]{3,2,1,0:T(8,128)(2,1)S(1)}, u32[]{:S(2)}, u32[]{:S(2)}) collective-permute-start(bf16[6,2,8,4096]{3,2,1,0:T(8,128)(2,1)S(1)} %pad_maximum_fusion.3), channel_id=1, source_target_pairs={{0,1},{1,2},{2,3},{3,4},{4,5},{5,6},{6,7},{7,8},{8,9},{9,10},{10,1... | collective-permute-start | bytes 2359304 | tf_op jit(solution)/shard_map/ppermute | solution.py:133
  17.1 0.2 fusion.4
  17.3 0.1 pad_maximum_fusion.2
  17.4 0.1 pad_maximum_fusion.1
  17.5 0.3 collective-permute-done.1.b_ref.refs_3_
  17.8 0.0 copy-start.7
  17.8 4.3 %collective-permute-start.2 = (bf16[8,2,8,4096]{3,2,1,0:T(8,128)(2,1)S(1)}, bf16[8,2,8,4096]{3,2,1,0:T(8,128)(2,1)S(1)}, u32[]{:S(2)}, u32[]{:S(2)}) collective-permute-start(bf16[8,2,8,4096]{3,2,1,0:T(8,128)(2,1)S(1)} %pad_maximum_fusion.1), channel_id=1, source_target_pairs={{0,1},{1,2},{2,3},{3,4},{4,5},{5,6},{6,7},{7,8},{8,9},{9,10},{10,1... | collective-permute-start | bytes 3145736 | tf_op jit(solution)/shard_map/ppermute | solution.py:133
  22.1 23.9 %collective-permute-done.a_ref.refs_2_ = bf16[4,2,8,4096]{3,2,1,0:T(8,128)(2,1)S(1)} collective-permute-done((bf16[4,2,8,4096]{3,2,1,0:T(8,128)(2,1)S(1)}, bf16[4,2,8,4096]{3,2,1,0:T(8,128)(2,1)S(1)}, u32[]{:S(2)}, u32[]{:S(2)}) %collective-permute-start) | collective-permute-done | bytes 524320 | tf_op jit(solution)/shard_map/ppermute | solution.py:133
  46.0 0.0 copy-start.10
  46.0 1.9 collective-permute-start.3
  47.9 1.0 pad_maximum_fusion.4
  48.9 30.8 %collective-permute-done.6.refs_8_ = bf16[6,2,8,4096]{3,2,1,0:T(8,128)(2,1)S(1)} collective-permute-done((bf16[6,2,8,4096]{3,2,1,0:T(8,128)(2,1)S(1)}, bf16[6,2,8,4096]{3,2,1,0:T(8,128)(2,1)S(1)}, u32[]{:S(2)}, u32[]{:S(2)}) %collective-permute-start.6) | collective-permute-done | bytes 786464 | tf_op jit(solution)/shard_map/ppermute | solution.py:133
  79.7 1.9 collective-permute-start.7
  81.7 0.7 pad_maximum_fusion.7
  82.4 0.7 pad_maximum_fusion.6
  83.1 7.8 %collective-permute-done.2.refs_4_ = bf16[8,2,8,4096]{3,2,1,0:T(8,128)(2,1)S(1)} collective-permute-done((bf16[8,2,8,4096]{3,2,1,0:T(8,128)(2,1)S(1)}, bf16[8,2,8,4096]{3,2,1,0:T(8,128)(2,1)S(1)}, u32[]{:S(2)}, u32[]{:S(2)}) %collective-permute-start.2) | collective-permute-done | bytes 1048608 | tf_op jit(solution)/shard_map/ppermute | solution.py:133
  91.0 0.0 copy-start.3
  91.0 1.0 copy-done.3
  91.9 4.4 %collective-permute-start.8 = (bf16[2,2,8,4096]{3,2,1,0:T(8,128)(2,1)}, bf16[2,2,8,4096]{3,2,1,0:T(8,128)(2,1)}, u32[]{:S(2)}, u32[]{:S(2)}) collective-permute-start(bf16[2,2,8,4096]{3,2,1,0:T(8,128)(2,1)} %pad_maximum_fusion.6), channel_id=1, source_target_pairs={{0,1},{1,2},{2,3},{3,4},{4,5},{5,6},{6,7},{7,8},{8,9},{9,10},{10,1... | collective-permute-start | bytes 786440 | tf_op jit(solution)/shard_map/ppermute | solution.py:133
  96.3 0.0 collective-permute-done.3.refs_5_
  96.3 0.0 copy-done.10
  96.4 0.0 copy-start.5
  96.4 1.0 copy-done.5
  97.4 1.9 collective-permute-start.9
  99.3 0.0 copy-done.7
  99.3 4.9 %rim.1 = (f32[2,4096]{1,0:T(2,128)}, f32[2,4096]{1,0:T(2,128)}) custom-call(bf16[4,2,8,4096]{3,2,1,0:T(8,128)(2,1)} %copy-done.10, bf16[4,2,8,4096]{3,2,1,0:T(8,128)(2,1)} %copy-done.7), custom_call_target="tpu_custom_call" | custom-call | flops 524288 | bytes 1572864 | tf_op jit(solution)/shard_map/rim/pallas_call | solution.py:139
  104.2 0.0 collective-permute-done.5.refs_7_
  104.2 3.6 %collective-permute-start.10 = (f32[2,4096]{1,0:T(2,128)}, f32[2,4096]{1,0:T(2,128)S(1)}, u32[]{:S(2)}, u32[]{:S(2)}) collective-permute-start(f32[2,4096]{1,0:T(2,128)} %get-tuple-element.7), channel_id=1, source_target_pairs={{0,1},{1,2},{2,3},{3,4},{4,5},{5,6},{6,7},{7,8},{8,9},{9,10},{10,1... | collective-permute-start | bytes 98312 | tf_op jit(solution)/shard_map/ppermute | solution.py:151
  107.8 0.0 collective-permute-done.4.refs_6_
  107.8 1.9 collective-permute-start.11
  109.8 0.0 copy-start.2
  109.8 1.6 copy-done.2
  111.4 1.2 copy-done.4
  112.6 1.2 copy-done.6
  113.8 1.0 copy-done.8
  114.9 1.0 copy-done.11
  115.9 21.9 %lags_0.1.refs_8_ = f32[33,16,4096]{2,1,0:T(8,128)} custom-call(bf16[16,2,8,4096]{3,2,1,0:T(8,128)(2,1)S(1)} %copy-done, bf16[16,2,8,4096]{3,2,1,0:T(8,128)(2,1)S(1)} %copy-done.2, bf16[4,2,8,4096]{3,2,1,0:T(8,128)(2,1)S(1)} %copy-done.11, bf16[4,2,8,4096]{3,2,1,0:T(8,128)(2,1)S(1)} %copy-done.8, bf16[8,2,8,4096]{3,2,1,0:T(8,128)(2,1)S(1)} %copy-done.4, ...), custom_call_target="tpu_custom_call" | custom-call | flops 21233664 | bytes 9699328 | tf_op jit(solution)/shard_map/lags_0/pallas_call | solution.py:189
  137.8 0.0 copy-done.9
  137.8 0.0 copy-done.12
  137.8 31.5 %lags_1.1.refs_10_ = f32[33,16,4096]{2,1,0:T(8,128)} custom-call(bf16[16,2,8,4096]{3,2,1,0:T(8,128)(2,1)S(1)} %copy-done, bf16[16,2,8,4096]{3,2,1,0:T(8,128)(2,1)S(1)} %copy-done.2, bf16[4,2,8,4096]{3,2,1,0:T(8,128)(2,1)S(1)} %copy-done.12, bf16[4,2,8,4096]{3,2,1,0:T(8,128)(2,1)S(1)} %copy-done.9, ...), custom_call_target="tpu_custom_call", output_to_operand_aliasing={{}: (8, {})} | custom-call | flops 28311552 | bytes 13631488 | tf_op jit(solution)/shard_map/lags_1/pallas_call | solution.py:189
  169.3 0.0 collective-permute-done.7.refs_9_
  169.3 18.8 %lags_2.1.refs_14_ = f32[33,16,4096]{2,1,0:T(8,128)} custom-call(bf16[16,2,8,4096]{3,2,1,0:T(8,128)(2,1)S(1)} %copy-done, bf16[16,2,8,4096]{3,2,1,0:T(8,128)(2,1)S(1)} %copy-done.2, bf16[4,2,8,4096]{3,2,1,0:T(8,128)(2,1)S(1)} %copy-done.12, bf16[4,2,8,4096]{3,2,1,0:T(8,128)(2,1)S(1)} %copy-done.9, ...), custom_call_target="tpu_custom_call", output_to_operand_aliasing={{}: (10, {})} | custom-call | flops 14155776 | bytes 13631488 | tf_op jit(solution)/shard_map/lags_2/pallas_call | solution.py:189
  188.1 0.0 collective-permute-done.8.refs_10_
  188.1 0.0 collective-permute-done.9.refs_11_
  188.1 0.0 collective-permute-done.10.refs_12_
  188.1 0.0 collective-permute-done.11.refs_13_
  188.1 19.8 %lags_3.1 = f32[33,16,4096]{2,1,0:T(8,128)} custom-call(bf16[16,2,8,4096]{3,2,1,0:T(8,128)(2,1)S(1)} %copy-done, bf16[16,2,8,4096]{3,2,1,0:T(8,128)(2,1)S(1)} %copy-done.2, bf16[4,2,8,4096]{3,2,1,0:T(8,128)(2,1)S(1)} %copy-done.12, bf16[4,2,8,4096]{3,2,1,0:T(8,128)(2,1)S(1)} %copy-done.9, ...), custom_call_target="tpu_custom_call", output_to_operand_aliasing={{}: (14, {})} | custom-call | flops 14155776 | bytes 14155776 | tf_op jit(solution)/shard_map/lags_3/pallas_call | solution.py:189
  (6 shorter events, 0.0 us)
Async XLA Ops:
  1.4 5.9 %slice-start = ((bf16[16,2,8,4096]{3,2,1,0:T(8,128)(2,1)}), bf16[6,2,8,4096]{3,2,1,0:T(8,128)(2,1)S(1)}, s32[]{:S(2)}) async-start(bf16[16,2,8,4096]{3,2,1,0:T(8,128)(2,1)} %refs_0_.7), calls=%async_computation | async-start | bytes 1572864 | tf_op jit(solution)/shard_map/slice | solution.py:39
  1.4 5.9 %slice-start.1 = ((bf16[16,2,8,4096]{3,2,1,0:T(8,128)(2,1)}), bf16[6,2,8,4096]{3,2,1,0:T(8,128)(2,1)S(1)}, s32[]{:S(2)}) async-start(bf16[16,2,8,4096]{3,2,1,0:T(8,128)(2,1)} %refs_1_.7), calls=%async_computation.1 | async-start | bytes 1572864 | tf_op jit(solution)/shard_map/slice | solution.py:39
  1.5 16.3 %collective-permute-start.1 = (bf16[4,2,8,4096]{3,2,1,0:T(8,128)(2,1)S(1)}, bf16[4,2,8,4096]{3,2,1,0:T(8,128)(2,1)S(1)}, u32[]{:S(2)}, u32[]{:S(2)}) collective-permute-start(bf16[4,2,8,4096]{3,2,1,0:T(8,128)(2,1)S(1)} %pad_maximum_fusion.5), channel_id=1, source_target_pairs={{1,0},{2,1},{3,2},{4,3},{5,4},{6,5},{7,6},{8,7},{9,8},{10,9},{11,1... | collective-permute-start | bytes 1572872 | tf_op jit(solution)/shard_map/ppermute | solution.py:134
  4.2 41.8 %collective-permute-start = (bf16[4,2,8,4096]{3,2,1,0:T(8,128)(2,1)S(1)}, bf16[4,2,8,4096]{3,2,1,0:T(8,128)(2,1)S(1)}, u32[]{:S(2)}, u32[]{:S(2)}) collective-permute-start(bf16[4,2,8,4096]{3,2,1,0:T(8,128)(2,1)S(1)} %pad_maximum_fusion.5), channel_id=1, source_target_pairs={{0,1},{1,2},{2,3},{3,4},{4,5},{5,6},{6,7},{7,8},{8,9},{9,10},{10,1... | collective-permute-start | bytes 1572872 | tf_op jit(solution)/shard_map/ppermute | solution.py:133
  7.2 7.0 %copy-start = (bf16[16,2,8,4096]{3,2,1,0:T(8,128)(2,1)S(1)}, bf16[16,2,8,4096]{3,2,1,0:T(8,128)(2,1)}, u32[]{:S(2)}) copy-start(bf16[16,2,8,4096]{3,2,1,0:T(8,128)(2,1)} %refs_0_.7) | copy-start | bytes 6291460
  7.2 7.0 %copy-start.1 = (bf16[16,2,8,4096]{3,2,1,0:T(8,128)(2,1)S(1)}, bf16[16,2,8,4096]{3,2,1,0:T(8,128)(2,1)}, u32[]{:S(2)}) copy-start(bf16[16,2,8,4096]{3,2,1,0:T(8,128)(2,1)} %refs_1_.7) | copy-start | bytes 6291460
  8.6 95.6 %collective-permute-start.5 = (bf16[12,2,8,4096]{3,2,1,0:T(8,128)(2,1)}, bf16[12,2,8,4096]{3,2,1,0:T(8,128)(2,1)}, u32[]{:S(2)}, u32[]{:S(2)}) collective-permute-start(bf16[12,2,8,4096]{3,2,1,0:T(8,128)(2,1)} %pad_maximum_fusion), channel_id=1, source_target_pairs={{1,0},{2,1},{3,2},{4,3},{5,4},{6,5},{7,6},{8,7},{9,8},{10,9},{11,1... | collective-permute-start | bytes 4718600 | tf_op jit(solution)/shard_map/ppermute | solution.py:134
  10.6 97.2 %collective-permute-start.4 = (bf16[12,2,8,4096]{3,2,1,0:T(8,128)(2,1)}, bf16[12,2,8,4096]{3,2,1,0:T(8,128)(2,1)}, u32[]{:S(2)}, u32[]{:S(2)}) collective-permute-start(bf16[12,2,8,4096]{3,2,1,0:T(8,128)(2,1)} %pad_maximum_fusion), channel_id=1, source_target_pairs={{0,1},{1,2},{2,3},{3,4},{4,5},{5,6},{6,7},{7,8},{8,9},{9,10},{10,1... | collective-permute-start | bytes 4718600 | tf_op jit(solution)/shard_map/ppermute | solution.py:133
  14.5 65.2 %collective-permute-start.6 = (bf16[6,2,8,4096]{3,2,1,0:T(8,128)(2,1)S(1)}, bf16[6,2,8,4096]{3,2,1,0:T(8,128)(2,1)S(1)}, u32[]{:S(2)}, u32[]{:S(2)}) collective-permute-start(bf16[6,2,8,4096]{3,2,1,0:T(8,128)(2,1)S(1)} %pad_maximum_fusion.3), channel_id=1, source_target_pairs={{0,1},{1,2},{2,3},{3,4},{4,5},{5,6},{6,7},{7,8},{8,9},{9,10},{10,1... | collective-permute-start | bytes 2359304 | tf_op jit(solution)/shard_map/ppermute | solution.py:133
  17.8 81.5 %copy-start.7 = (bf16[4,2,8,4096]{3,2,1,0:T(8,128)(2,1)}, bf16[4,2,8,4096]{3,2,1,0:T(8,128)(2,1)S(1)}, u32[]{:S(2)}) copy-start(bf16[4,2,8,4096]{3,2,1,0:T(8,128)(2,1)S(1)} %collective-permute-done.1.b_ref.refs_3_) | copy-start | bytes 1572868
  17.8 73.2 %collective-permute-start.2 = (bf16[8,2,8,4096]{3,2,1,0:T(8,128)(2,1)S(1)}, bf16[8,2,8,4096]{3,2,1,0:T(8,128)(2,1)S(1)}, u32[]{:S(2)}, u32[]{:S(2)}) collective-permute-start(bf16[8,2,8,4096]{3,2,1,0:T(8,128)(2,1)S(1)} %pad_maximum_fusion.1), channel_id=1, source_target_pairs={{0,1},{1,2},{2,3},{3,4},{4,5},{5,6},{6,7},{7,8},{8,9},{9,10},{10,1... | collective-permute-start | bytes 3145736 | tf_op jit(solution)/shard_map/ppermute | solution.py:133
  46.0 50.3 %copy-start.10 = (bf16[4,2,8,4096]{3,2,1,0:T(8,128)(2,1)}, bf16[4,2,8,4096]{3,2,1,0:T(8,128)(2,1)S(1)}, u32[]{:S(2)}) copy-start(bf16[4,2,8,4096]{3,2,1,0:T(8,128)(2,1)S(1)} %collective-permute-done.a_ref.refs_2_) | copy-start | bytes 1572868
  46.0 50.3 %collective-permute-start.3 = (bf16[8,2,8,4096]{3,2,1,0:T(8,128)(2,1)S(1)}, bf16[8,2,8,4096]{3,2,1,0:T(8,128)(2,1)S(1)}, u32[]{:S(2)}, u32[]{:S(2)}) collective-permute-start(bf16[8,2,8,4096]{3,2,1,0:T(8,128)(2,1)S(1)} %pad_maximum_fusion.2), channel_id=1, source_target_pairs={{1,0},{2,1},{3,2},{4,3},{5,4},{6,5},{7,6},{8,7},{9,8},{10,9},{11,1... | collective-permute-start | bytes 3145736 | tf_op jit(solution)/shard_map/ppermute | solution.py:134
  79.7 89.5 %collective-permute-start.7 = (bf16[6,2,8,4096]{3,2,1,0:T(8,128)(2,1)}, bf16[6,2,8,4096]{3,2,1,0:T(8,128)(2,1)}, u32[]{:S(2)}, u32[]{:S(2)}) collective-permute-start(bf16[6,2,8,4096]{3,2,1,0:T(8,128)(2,1)} %pad_maximum_fusion.4), channel_id=1, source_target_pairs={{1,0},{2,1},{3,2},{4,3},{5,4},{6,5},{7,6},{8,7},{9,8},{10,9},{11,1... | collective-permute-start | bytes 2359304 | tf_op jit(solution)/shard_map/ppermute | solution.py:134
  91.0 1.0 copy-start.3
  91.9 96.2 %collective-permute-start.8 = (bf16[2,2,8,4096]{3,2,1,0:T(8,128)(2,1)}, bf16[2,2,8,4096]{3,2,1,0:T(8,128)(2,1)}, u32[]{:S(2)}, u32[]{:S(2)}) collective-permute-start(bf16[2,2,8,4096]{3,2,1,0:T(8,128)(2,1)} %pad_maximum_fusion.6), channel_id=1, source_target_pairs={{0,1},{1,2},{2,3},{3,4},{4,5},{5,6},{6,7},{7,8},{8,9},{9,10},{10,1... | collective-permute-start | bytes 786440 | tf_op jit(solution)/shard_map/ppermute | solution.py:133
  96.4 1.0 copy-start.5
  97.4 90.8 %collective-permute-start.9 = (bf16[2,2,8,4096]{3,2,1,0:T(8,128)(2,1)}, bf16[2,2,8,4096]{3,2,1,0:T(8,128)(2,1)}, u32[]{:S(2)}, u32[]{:S(2)}) collective-permute-start(bf16[2,2,8,4096]{3,2,1,0:T(8,128)(2,1)} %pad_maximum_fusion.7), channel_id=1, source_target_pairs={{1,0},{2,1},{3,2},{4,3},{5,4},{6,5},{7,6},{8,7},{9,8},{10,9},{11,1... | collective-permute-start | bytes 786440 | tf_op jit(solution)/shard_map/ppermute | solution.py:134
  104.2 83.9 %collective-permute-start.10 = (f32[2,4096]{1,0:T(2,128)}, f32[2,4096]{1,0:T(2,128)S(1)}, u32[]{:S(2)}, u32[]{:S(2)}) collective-permute-start(f32[2,4096]{1,0:T(2,128)} %get-tuple-element.7), channel_id=1, source_target_pairs={{0,1},{1,2},{2,3},{3,4},{4,5},{5,6},{6,7},{7,8},{8,9},{9,10},{10,1... | collective-permute-start | bytes 98312 | tf_op jit(solution)/shard_map/ppermute | solution.py:151
  107.8 80.3 %collective-permute-start.11 = (f32[2,4096]{1,0:T(2,128)}, f32[2,4096]{1,0:T(2,128)S(1)}, u32[]{:S(2)}, u32[]{:S(2)}) collective-permute-start(f32[2,4096]{1,0:T(2,128)} %get-tuple-element.8), channel_id=1, source_target_pairs={{1,0},{2,1},{3,2},{4,3},{5,4},{6,5},{7,6},{8,7},{9,8},{10,9},{11,1... | collective-permute-start | bytes 98312 | tf_op jit(solution)/shard_map/ppermute | solution.py:150
  109.8 1.6 copy-start.2
  111.4 1.2 copy-start.4
  112.6 1.2 copy-start.6
  113.8 1.0 copy-start.8
  114.9 1.0 copy-start.11
  115.9 21.9 %copy-start.9 = (bf16[4,2,8,4096]{3,2,1,0:T(8,128)(2,1)S(1)}, bf16[4,2,8,4096]{3,2,1,0:T(8,128)(2,1)}, u32[]{:S(2)}) copy-start(bf16[4,2,8,4096]{3,2,1,0:T(8,128)(2,1)} %copy-done.7) | copy-start | bytes 1572868
  115.9 21.9 %copy-start.12 = (bf16[4,2,8,4096]{3,2,1,0:T(8,128)(2,1)S(1)}, bf16[4,2,8,4096]{3,2,1,0:T(8,128)(2,1)}, u32[]{:S(2)}) copy-start(bf16[4,2,8,4096]{3,2,1,0:T(8,128)(2,1)} %copy-done.10) | copy-start | bytes 1572868

commit v2 on v0

v2 whole, which is shorter than its diff:
```python
import functools

import jax
import jax.numpy as jnp
from jax import lax
from jax.experimental import pallas as pl
from jax.experimental.pallas import tpu as pltpu
from jax.sharding import PartitionSpec as P

Z = 64
HALF = 16
LAGS = 33
BLOCK = 3
LANES = 128
SUB = 16
SPAN = 6
RATE = 200

CHUNKS = ((16, 1), (5, 4, 3, 2), (11, 10, 9, 8, 7, 6), (14, 13, 12), (15,))
BLOCKS = ((5, 4, 6), (2, 3, 7, 8), (1, 9), (0, 10))

VMEM = pl.BlockSpec(memory_space=pltpu.VMEM)
ANY = pl.BlockSpec(memory_space=pl.ANY)


def left_rows(chunk):
    return [-i for i in chunk]


def right_rows(chunk, cells):
    return [cells - 1 + i for i in reversed(chunk)]


def take(field, rows):
    spans = []
    for r in rows:
        if spans and spans[-1][1] == r:
            spans[-1][1] = r + 1
        else:
            spans.append([r, r + 1])
    return [lax.slice_in_dim(field, a, b, axis=0) for a, b in spans]


def pack_kernel(s_ref, r_ref, so_ref, ro_ref, flip):
    rows, parts, freqs, width = s_ref.shape
    for row in range(rows):
        for field, (src, dst) in enumerate(((s_ref, so_ref), (r_ref, ro_ref))):
            for p in range(parts):
                for g in range(width // (SUB * LANES)):
                    slot = flip.at[(field * parts + p) * 2 + g % 2]
                    for t in range(SUB):
                        c = (g * SUB + t) * LANES
                        slot[pl.ds(t, freqs, SUB), :] = src[row, p, :, c : c + LANES].astype(
                            jnp.float32
                        )
                    for f in range(freqs):
                        dst[row, p * freqs + f, g * SUB : (g + 1) * SUB] = slot[
                            f * SUB : (f + 1) * SUB
                        ].astype(jnp.bfloat16)


def pack(forward_field, adjoint_field):
    cells, parts, freqs, width = forward_field.shape
    rows = 2
    spec = pl.BlockSpec((rows, parts, freqs, width), lambda i: (i, 0, 0, 0))
    tiles = width // LANES
    out = pl.BlockSpec((rows, parts * freqs, tiles, LANES), lambda i: (i, 0, 0, 0))
    shape = jax.ShapeDtypeStruct((cells, parts * freqs, tiles, LANES), jnp.bfloat16)
    return pl.pallas_call(
        pack_kernel,
        grid=(cells // rows,),
        in_specs=[spec, spec],
        out_specs=[out, out],
        out_shape=[shape, shape],
        scratch_shapes=[pltpu.VMEM((4 * parts, SUB * freqs, LANES), jnp.float32)],
        cost_estimate=pl.CostEstimate(
            flops=0, bytes_accessed=8 * cells * parts * freqs * width, transcendentals=0
        ),
        name="pack",
    )(forward_field, adjoint_field)


def rim_kernel(a_ref, b_ref, lo_ref, hi_ref):
    def dot(s, r):
        total = s[0].astype(jnp.float32) * r[0].astype(jnp.float32)
        for k in range(1, s.shape[0]):
            total += s[k].astype(jnp.float32) * r[k].astype(jnp.float32)
        return total

    def tile(g, _):
        at = pl.ds(pl.multiple_of(g * SUB, SUB), SUB)
        lo_ref[0, at] = dot(b_ref.at[0, :, at], a_ref.at[2, :, at])
        lo_ref[1, at] = dot(a_ref.at[0, :, at], b_ref.at[2, :, at])
        hi_ref[0, at] = dot(b_ref.at[1, :, at], a_ref.at[3, :, at])
        hi_ref[1, at] = dot(a_ref.at[1, :, at], b_ref.at[3, :, at])
        return 0

    lax.fori_loop(0, a_ref.shape[2] // SUB, tile, 0)


def lag_kernel(cells, blocks, where, rim, aliased, *refs):
    refs = list(refs)
    ins = [refs.pop(0) for _ in range(1 + max(w[0] for w in where.values()))]
    rims = [refs.pop(0) for _ in range(2)] if rim else None
    if aliased:
        refs.pop(0)
    out_ref, sums, flip, ready, sems = refs
    terms, tiles = ins[0].shape[1], ins[0].shape[2]
    lane = lax.broadcasted_iota(jnp.int32, (SUB, LANES), 1) % Z
    first = lane == 0
    last = lane == Z - 1

    def copies(n, g):
        cols = pl.ds(pl.multiple_of(g * (SUB * LANES), SUB * LANES), SUB * LANES)
        return pltpu.make_async_copy(
            ready.at[n, g],
            out_ref.at[pl.ds(blocks[n] * BLOCK, BLOCK), :, cols],
            sems.at[n, g],
        )

    def tile(g, _):
        at = pl.ds(pl.multiple_of(g * SUB, SUB), SUB)

        for n, blk in enumerate(blocks):
            lags = [blk * BLOCK + t - HALF for t in range(BLOCK)]
            for x0 in range(-1, cells + 1, SPAN):
                pairs = [
                    (t, x)
                    for t in range(BLOCK)
                    for x in range(x0, x0 + SPAN)
                    if (0, x - lags[t]) in where and (1, x + lags[t]) in where
                ]
                pairs.sort(key=lambda p: (p[1] - lags[p[0]], p[1]))

                def step(k, accs):
                    got = {}

                    def row(field, a):
                        if (field, a) not in got:
                            n_in, src = where[field, a]
                            got[field, a] = ins[n_in][src, k, at].astype(jnp.float32)
                        return got[field, a]

                    return tuple(
                        acc + row(0, x - lags[t]) * row(1, x + lags[t])
                        for acc, (t, x) in zip(accs, pairs)
                    )

                zero = jnp.zeros((SUB, LANES), jnp.float32)
                accs = lax.fori_loop(0, terms, step, (zero,) * len(pairs))
                for acc, (t, x) in zip(accs, pairs):
                    sums[t, x + 1] = acc
            for t in range(BLOCK):
                if abs(lags[t]) == HALF:
                    sums[t, 0] = rims[0][int(lags[t] > 0), at]
                    sums[t, cells + 1] = rims[1][int(lags[t] > 0), at]
                for x in range(cells):
                    mid = sums[t, x + 1]
                    down = jnp.where(first, 0.0, pltpu.roll(mid, 1, 1))
                    up = jnp.where(last, 0.0, pltpu.roll(mid, LANES - 1, 1))
                    around = (sums[t, x] + sums[t, x + 2]) + (down + up)
                    flip[t, pl.ds(x, SUB, cells), :] = 0.25 * (around - 4.0 * mid)
                for c in range(SUB):
                    ready[n, g, t, :, c * LANES : (c + 1) * LANES] = flip[
                        t, c * cells : (c + 1) * cells
                    ]
            copies(n, g).start()
        return 0

    groups = tiles // SUB
    lax.fori_loop(0, groups, tile, 0)
    for n in range(len(blocks)):
        for g in range(groups):
            copies(n, g).wait()


def on_device(forward_field, adjoint_field):
    cells, parts, freqs, width = forward_field.shape
    terms, tiles = parts * freqs, width // LANES
    peers = lax.axis_size("gx")
    up = [(i, (i + 1) % peers) for i in range(peers - 1)]
    down = [(j, i) for i, j in up]
    field_bytes = terms * width * 2

    source, receiver = pack(forward_field, adjoint_field)

    from_left, from_right = [], []
    for g, chunk in enumerate(CHUNKS):
        to_right = [cells + r for r in left_rows(chunk)]
        to_left = [r - cells for r in right_rows(chunk, cells)]
        sent_up = jnp.concatenate(take(source, to_right) + take(receiver, to_right), axis=0)
        sent_down = jnp.concatenate(take(source, to_left) + take(receiver, to_left), axis=0)
        if g >= 2:
            sent_up, sent_down, from_left[g - 2], from_right[g - 2] = lax.optimization_barrier(
                (sent_up, sent_down, from_left[g - 2], from_right[g - 2])
            )
        from_left.append(lax.ppermute(sent_up, "gx", up))
        from_right.append(lax.ppermute(sent_down, "gx", down))

    lo, hi = pl.pallas_call(
        rim_kernel,
        in_specs=[VMEM, VMEM],
        out_specs=[VMEM, VMEM],
        out_shape=[jax.ShapeDtypeStruct((2, tiles, LANES), jnp.float32)] * 2,
        cost_estimate=pl.CostEstimate(
            flops=8 * terms * width, bytes_accessed=12 * field_bytes, transcendentals=0
        ),
        name="rim",
    )(from_left[0], from_right[0])
    rim_hi = lax.ppermute(lo, "gx", down)
    rim_lo = lax.ppermute(hi, "gx", up)

    image = None
    for stage, blocks in enumerate(BLOCKS):
        rim = 0 in blocks
        operands = [source, receiver]
        where = {(field, a): (field, a) for field in (0, 1) for a in range(cells)}
        for g in range(stage + 2):
            n = len(CHUNKS[g])
            for got, rows in (
                (from_left[g], left_rows(CHUNKS[g])),
                (from_right[g], right_rows(CHUNKS[g], cells)),
            ):
                for field in (0, 1):
                    for k, a in enumerate(rows):
                        where[field, a] = (len(operands), field * n + k)
                operands.append(got)
        n_fields = len(operands)
        if rim:
            operands += [rim_lo, rim_hi]
        specs = [VMEM] * len(operands)
        aliases = {}
        if image is not None:
            aliases = {len(operands): 0}
            operands.append(image)
            specs.append(ANY)
        nblk = len(blocks)
        groups = tiles // SUB
        image = pl.pallas_call(
            functools.partial(lag_kernel, cells, blocks, where, rim, image is not None),
            in_specs=specs,
            out_specs=ANY,
            out_shape=jax.ShapeDtypeStruct((LAGS, cells, width), jnp.float32),
            scratch_shapes=[
                pltpu.VMEM((BLOCK, cells + 2, SUB, LANES), jnp.float32),
                pltpu.VMEM((BLOCK, SUB * cells, LANES), jnp.float32),
                pltpu.VMEM((nblk, groups, BLOCK, cells, SUB * LANES), jnp.float32),
                pltpu.SemaphoreType.DMA((nblk, groups)),
            ],
            input_output_aliases=aliases,
            compiler_params=pltpu.CompilerParams(vmem_limit_bytes=36 * 2**20),
            cost_estimate=pl.CostEstimate(
                flops=RATE * 2 * 3 * nblk * (cells + 2) * terms * width,
                bytes_accessed=3 * nblk * cells * width * 4
                + sum(o.shape[0] for o in operands[:n_fields]) * field_bytes,
                transcendentals=0,
            ),
            name="lags_%d" % stage,
        )(*operands)
    return image


def solution(mesh):
    placed = (P(("shots", "gx"), None, None, None), P(("shots", "gx"), None, None, None))
    return jax.shard_map(
        on_device,
        mesh=mesh,
        in_specs=placed,
        out_specs=P(None, ("shots", "gx"), None),
        check_vma=False,
    )
```

time: 459 us -> 151 us (0.33)
  other arithmetic: 151 us -> 6.28 us
  loops' own time: 105 us -> 0 us
  local copies, waits for them, and re-layouts: 97.5 us -> 7.22 us
  Pallas kernels: 0 us -> 53.3 us
  waiting for transfers between devices: 89.7 us -> 53.1 us
  starting transfers between devices: 12.1 us -> 30.4 us
    reduce_sum x33 -> x0, other arithmetic: 110 us -> none  [per_offset(): return jnp.sum(source_part * receiver_part, axis=(1, 2))]
    another operation x1 -> x0, loops' own time: 105 us -> none  [correlate(): return lax.map(per_offset, jnp.arange(LAGS, dtype=jnp.int32))]
    pallas_call x0 -> x6, Pallas kernels: none -> 53.3 us  [the longest x4 44.1 us: on_device(): pl.pallas_call(functools.partial(lag_kernel, cells, blocks, where, rim, i...]
    ppermute x4 -> x12, waiting for transfers between devices: 89.7 us -> 53.1 us  [the longest x5 51.7 us: on_device(): from_right.append(lax.ppermute(sent_down, 'gx', down))]
    reshape x2 -> x0, local copies, waits for them, and re-layouts: 29.9 us -> none  [the longest x1 15.2 us: laplace(): along_depth = (deeper[..., 2:] + deeper[..., :-2]).reshape(middle.shape)]
    dynamic_update_slice x33 -> x0, local copies, waits for them, and re-layouts: 24 us -> none  [correlate(): return lax.map(per_offset, jnp.arange(LAGS, dtype=jnp.int32))]
    dynamic_slice x33 -> x0, local copies, waits for them, and re-layouts: 19.9 us -> none  [correlate(): return lax.map(per_offset, jnp.arange(LAGS, dtype=jnp.int32))]
    mul x1 -> x0, other arithmetic: 19 us -> none  [laplace(): return 0.25 * (padded[:, 2:] + padded[:, :-2] + along_depth - 4.0 * middle)]
  transfers between devices with their start and end apart: 4 -> 12, of which waited for: 2 -> 3; matrix products, arithmetic and copies ran while one was open for 6% -> 5% of each run, Pallas kernels for 0% -> 25%
where the time goes in v2:
time: 151 us
  Pallas kernels  53.3 us (35%)
  waiting for transfers between devices  53.1 us (35%)
  starting transfers between devices  30.4 us (20%)
  local copies, waits for them, and re-layouts  7.22 us (5%)
  other arithmetic  6.28 us (4%)
    ppermute x5, waiting for transfers between devices, on_device(): from_right.append(lax.ppermute(sent_down, 'gx', down))  51.7 us
    pallas_call x4, Pallas kernels, on_device(): pl.pallas_call(functools.partial(lag_kernel, cells, blocks, where, rim, i...  44.1 us
    ppermute x5, starting transfers between devices, on_device(): from_left.append(lax.ppermute(sent_up, 'gx', up))  13.7 us
    ppermute x5, starting transfers between devices, on_device(): from_right.append(lax.ppermute(sent_down, 'gx', down))  11.2 us
    pallas_call x1, Pallas kernels, pack(): pl.pallas_call(pack_kernel, grid=(cells // rows,), in_specs=[spec, spec],...  7.32 us
    concatenate x5, other arithmetic, on_device(): jnp.concatenate(take(source, to_right) + take(receiver, to_right), axis=0)  4.15 us
    unnamed x22, local copies, waits for them, and re-layouts  3.7 us
    ppermute x1, starting transfers between devices, on_device(): rim_lo = lax.ppermute(hi, 'gx', up)  3.63 us
  transfers between devices with their start and end apart: 12, of which 3 were waited for; matrix products, arithmetic and copies ran while one was open for 5% of the time, Pallas kernels for 25%

profile of v2, /device:TPU:17, one launch (start us, length us, event | category | flops | bytes accessed | tf_op | source)
XLA Modules:
  0.0 150.6 jit_solution(11163459835856847751)
XLA Ops:
  0.0 7.3 %pack.1 = (bf16[16,16,32,128]{3,2,1,0:T(8,128)(2,1)}, bf16[16,16,32,128]{3,2,1,0:T(8,128)(2,1)}) custom-call(bf16[16,2,8,4096]{3,2,1,0:T(8,128)(2,1)} %s_ref.1, bf16[16,2,8,4096]{3,2,1,0:T(8,128)(2,1)} %r_ref.1), custom_call_target="tpu_custom_call" | custom-call | bytes 8388608 | tf_op jit(solution)/shard_map/pack/pallas_call | solution.py:69
  7.3 0.0 copy-start
  7.3 1.5 %fusion = (bf16[1,16,32,128]{3,2,1,0:T(8,128)(2,1)S(1)}, bf16[1,16,32,128]{3,2,1,0:T(8,128)(2,1)S(1)}, bf16[1,16,32,128]{3,2,1,0:T(8,128)(2,1)S(1)}, bf16[1,16,3...) fusion(bf16[16,16,32,128]{3,2,1,0:T(8,128)(2,1)} %get-tuple-ele, ...), kind=kLoop, calls=%fused_computation.8 | loop fusion | bytes 2097152 | tf_op jit(solution)/shard_map/slice | solution.py:41
  8.8 0.1 pad_maximum_fusion.5
  8.9 2.6 %collective-permute-start.1 = (bf16[4,16,32,128]{3,2,1,0:T(8,128)(2,1)S(1)}, bf16[4,16,32,128]{3,2,1,0:T(8,128)(2,1)S(1)}, u32[]{:S(2)}, u32[]{:S(2)}) collective-permute-start(bf16[4,16,32,128]{3,2,1,0:T(8,128)(2,1)S(1)} %pad_maximum_fusion.5), channel_id=1, source_target_pairs={{1,0},{2,1},{3,2},{4,3},{5,4},{6,5},{7,6},{8,7},{9,8},{10,9},{11,1... | collective-permute-start | bytes 1572872 | tf_op jit(solution)/shard_map/ppermute | solution.py:198
  11.5 3.0 %collective-permute-start = (bf16[4,16,32,128]{3,2,1,0:T(8,128)(2,1)S(1)}, bf16[4,16,32,128]{3,2,1,0:T(8,128)(2,1)S(1)}, u32[]{:S(2)}, u32[]{:S(2)}) collective-permute-start(bf16[4,16,32,128]{3,2,1,0:T(8,128)(2,1)S(1)} %pad_maximum_fusion.5), channel_id=1, source_target_pairs={{0,1},{1,2},{2,3},{3,4},{4,5},{5,6},{6,7},{7,8},{8,9},{9,10},{10,1... | collective-permute-start | bytes 1572872 | tf_op jit(solution)/shard_map/ppermute | solution.py:197
  14.6 0.0 copy-done
  14.6 1.6 %fusion.2 = (bf16[4,16,32,128]{3,2,1,0:T(8,128)(2,1)S(1)}, bf16[4,16,32,128]{3,2,1,0:T(8,128)(2,1)S(1)}, bf16[4,16,32,128]{3,2,1,0:T(8,128)(2,1)S(1)}, bf16[4,16,32,128]{3,2,1,0:T(8,128)(2,1)S(1)}) fusion(bf16[16,16,32,128]{3,2,1,0:T(8,128)(2,1)S(1)} %copy-done, bf16[16,16,32,128]{3,2,1,0:T(8,128)(2,1)} %get-tuple-element.22.refs_1_), kind=kLoop, calls=%fused_computation.10 | loop fusion | bytes 4194304 | tf_op jit(solution)/shard_map/slice | solution.py:41
  16.1 0.0 copy-start.1
  16.2 1.1 pad_maximum_fusion.1
  17.2 2.4 %collective-permute-start.2 = (bf16[8,16,32,128]{3,2,1,0:T(8,128)(2,1)}, bf16[8,16,32,128]{3,2,1,0:T(8,128)(2,1)S(1)}, u32[]{:S(2)}, u32[]{:S(2)}) collective-permute-start(bf16[8,16,32,128]{3,2,1,0:T(8,128)(2,1)} %pad_maximum_fusion.1), channel_id=1, source_target_pairs={{0,1},{1,2},{2,3},{3,4},{4,5},{5,6},{6,7},{7,8},{8,9},{9,10},{10,1... | collective-permute-start | bytes 3145736 | tf_op jit(solution)/shard_map/ppermute | solution.py:197
  19.6 0.1 slice.60
  19.7 0.0 copy-done.1
  19.7 0.1 slice.61
  19.8 1.3 pad_maximum_fusion
  21.1 32.1 %collective-permute-done.1.b_ref.refs_3_ = bf16[4,16,32,128]{3,2,1,0:T(8,128)(2,1)S(1)} collective-permute-done((bf16[4,16,32,128]{3,2,1,0:T(8,128)(2,1)S(1)}, bf16[4,16,32,128]{3,2,1,0:T(8,128)(2,1)S(1)}, u32[]{:S(2)}, u32[]{:S(2)}) %collective-permute-start.1) | collective-permute-done | bytes 524320 | tf_op jit(solution)/shard_map/ppermute | solution.py:198
  53.2 0.0 copy-start.3
  53.2 0.0 collective-permute-done.a_ref.refs_2_
  53.2 0.0 copy-start.6
  53.2 1.9 %collective-permute-start.4 = (bf16[12,16,32,128]{3,2,1,0:T(8,128)(2,1)}, bf16[12,16,32,128]{3,2,1,0:T(8,128)(2,1)}, u32[]{:S(2)}, u32[]{:S(2)}) collective-permute-start(bf16[12,16,32,128]{3,2,1,0:T(8,128)(2,1)} %pad_maximum_fusion), channel_id=1, source_target_pairs={{0,1},{1,2},{2,3},{3,4},{4,5},{5,6},{6,7},{7,8},{8,9},{9,10},{10,1... | collective-permute-start | bytes 4718600 | tf_op jit(solution)/shard_map/ppermute | solution.py:197
  55.1 2.4 %collective-permute-start.5 = (bf16[12,16,32,128]{3,2,1,0:T(8,128)(2,1)}, bf16[12,16,32,128]{3,2,1,0:T(8,128)(2,1)}, u32[]{:S(2)}, u32[]{:S(2)}) collective-permute-start(bf16[12,16,32,128]{3,2,1,0:T(8,128)(2,1)} %pad_maximum_fusion), channel_id=1, source_target_pairs={{1,0},{2,1},{3,2},{4,3},{5,4},{6,5},{7,6},{8,7},{9,8},{10,9},{11,1... | collective-permute-start | bytes 4718600 | tf_op jit(solution)/shard_map/ppermute | solution.py:198
  57.5 1.1 pad_maximum_fusion.2
  58.7 1.9 %collective-permute-start.3 = (bf16[8,16,32,128]{3,2,1,0:T(8,128)(2,1)}, bf16[8,16,32,128]{3,2,1,0:T(8,128)(2,1)}, u32[]{:S(2)}, u32[]{:S(2)}) collective-permute-start(bf16[8,16,32,128]{3,2,1,0:T(8,128)(2,1)} %pad_maximum_fusion.2), channel_id=1, source_target_pairs={{1,0},{2,1},{3,2},{4,3},{5,4},{6,5},{7,6},{8,7},{9,8},{10,9},{11,1... | collective-permute-start | bytes 3145736 | tf_op jit(solution)/shard_map/ppermute | solution.py:198
  60.6 0.7 pad_maximum_fusion.6
  61.4 0.3 fusion.4
  61.7 0.0 copy-done.3
  61.7 0.0 copy-done.6
  61.7 1.0 pad_maximum_fusion.4
  62.7 1.0 pad_maximum_fusion.3
  63.6 1.9 %rim.1 = (f32[2,32,128]{2,1,0:T(8,128)}, f32[2,32,128]{2,1,0:T(8,128)}) custom-call(bf16[4,16,32,128]{3,2,1,0:T(8,128)(2,1)} %copy-done.6, bf16[4,16,32,128]{3,2,1,0:T(8,128)(2,1)} %copy-done.3), custom_call_target="tpu_custom_call" | custom-call | flops 524288 | bytes 1572864 | tf_op jit(solution)/shard_map/rim/pallas_call | solution.py:200
  65.5 3.6 %collective-permute-start.10 = (f32[2,32,128]{2,1,0:T(8,128)}, f32[2,32,128]{2,1,0:T(8,128)S(1)}, u32[]{:S(2)}, u32[]{:S(2)}) collective-permute-start(f32[2,32,128]{2,1,0:T(8,128)} %get-tuple-element.35), channel_id=1, source_target_pairs={{0,1},{1,2},{2,3},{3,4},{4,5},{5,6},{6,7},{7,8},{8,9},{9,10},{10,1... | collective-permute-start | bytes 98312 | tf_op jit(solution)/shard_map/ppermute | solution.py:211
  69.2 0.0 collective-permute-done.2.refs_4_
  69.2 19.6 %collective-permute-done.3.refs_5_ = bf16[8,16,32,128]{3,2,1,0:T(8,128)(2,1)} collective-permute-done((bf16[8,16,32,128]{3,2,1,0:T(8,128)(2,1)}, bf16[8,16,32,128]{3,2,1,0:T(8,128)(2,1)}, u32[]{:S(2)}, u32[]{:S(2)}) %collective-permute-start.3) | collective-permute-done | bytes 1048608 | tf_op jit(solution)/shard_map/ppermute | solution.py:198
  88.8 1.9 %collective-permute-start.6 = (bf16[6,16,32,128]{3,2,1,0:T(8,128)(2,1)}, bf16[6,16,32,128]{3,2,1,0:T(8,128)(2,1)S(1)}, u32[]{:S(2)}, u32[]{:S(2)}) collective-permute-start(bf16[6,16,32,128]{3,2,1,0:T(8,128)(2,1)} %pad_maximum_fusion.3), channel_id=1, source_target_pairs={{0,1},{1,2},{2,3},{3,4},{4,5},{5,6},{6,7},{7,8},{8,9},{9,10},{10,1... | collective-permute-start | bytes 2359304 | tf_op jit(solution)/shard_map/ppermute | solution.py:197
  90.7 2.4 %collective-permute-start.7 = (bf16[6,16,32,128]{3,2,1,0:T(8,128)(2,1)}, bf16[6,16,32,128]{3,2,1,0:T(8,128)(2,1)S(1)}, u32[]{:S(2)}, u32[]{:S(2)}) collective-permute-start(bf16[6,16,32,128]{3,2,1,0:T(8,128)(2,1)} %pad_maximum_fusion.4), channel_id=1, source_target_pairs={{1,0},{2,1},{3,2},{4,3},{5,4},{6,5},{7,6},{8,7},{9,8},{10,9},{11,1... | collective-permute-start | bytes 2359304 | tf_op jit(solution)/shard_map/ppermute | solution.py:198
  93.1 0.0 copy-start.2
  93.1 1.6 %copy-done.2 = bf16[16,16,32,128]{3,2,1,0:T(8,128)(2,1)S(1)} copy-done((bf16[16,16,32,128]{3,2,1,0:T(8,128)(2,1)S(1)}, bf16[16,16,32,128]{3,2,1,0:T(8,128)(2,1)}, u32[]{:S(2)}) %copy-start.2) | copy-done | bytes 2097176
  94.7 0.0 copy-start.4
  94.7 1.0 copy-done.4
  95.7 0.0 copy-start.7
  95.7 1.0 copy-done.7
  96.8 0.0 copy-start.10
  96.8 0.0 copy-start.9
  96.8 0.0 copy-start.5
  96.8 0.0 copy-start.8
  96.8 11.1 %lags_0.1.refs_8_ = f32[33,16,4096]{2,1,0:T(8,128)} custom-call(bf16[16,16,32,128]{3,2,1,0:T(8,128)(2,1)S(1)} %copy-done, bf16[16,16,32,128]{3,2,1,0:T(8,128)(2,1)S(1)} %copy-done.2, bf16[4,16,32,128]{3,2,1,0:T(8,128)(2,1)S(1)} %copy-done.7, bf16[4,16,32,128]{3,2,1,0:T(8,128)(2,1)S(1)} %copy-done.4, ...), custom_call_target="tpu_custom_call" | custom-call | flops 4246732800 | bytes 9699328 | tf_op jit(solution)/shard_map/lags_0/pallas_call | solution.py:239
  107.9 1.4 collective-permute-done.4.refs_6_
  109.3 0.0 copy-done.10
  109.3 1.9 %collective-permute-start.11 = (f32[2,32,128]{2,1,0:T(8,128)S(1)}, f32[2,32,128]{2,1,0:T(8,128)S(1)}, u32[]{:S(2)}, u32[]{:S(2)}) collective-permute-start(f32[2,32,128]{2,1,0:T(8,128)S(1)} %copy-done.10), channel_id=1, source_target_pairs={{1,0},{2,1},{3,2},{4,3},{5,4},{6,5},{7,6},{8,7},{9,8},{10,9},{11,1... | collective-permute-start | bytes 98312 | tf_op jit(solution)/shard_map/ppermute | solution.py:210
  111.2 0.0 collective-permute-done.5.refs_7_
  111.2 0.0 copy-done.9
  111.2 4.4 %collective-permute-start.8 = (bf16[2,16,32,128]{3,2,1,0:T(8,128)(2,1)S(1)}, bf16[2,16,32,128]{3,2,1,0:T(8,128)(2,1)S(1)}, u32[]{:S(2)}, u32[]{:S(2)}) collective-permute-start(bf16[2,16,32,128]{3,2,1,0:T(8,128)(2,1)S(1)} %copy-done.9), channel_id=1, source_target_pairs={{0,1},{1,2},{2,3},{3,4},{4,5},{5,6},{6,7},{7,8},{8,9},{9,10},{10,1... | collective-permute-start | bytes 786440 | tf_op jit(solution)/shard_map/ppermute | solution.py:197
  115.6 0.0 copy-done.5
  115.6 0.0 copy-done.8
  115.7 15.0 %lags_1.1.refs_10_ = f32[33,16,4096]{2,1,0:T(8,128)} custom-call(bf16[16,16,32,128]{3,2,1,0:T(8,128)(2,1)S(1)} %copy-done, bf16[16,16,32,128]{3,2,1,0:T(8,128)(2,1)S(1)} %copy-done.2, bf16[4,16,32,128]{3,2,1,0:T(8,128)(2,1)S(1)} %copy-done.8, bf16[4,16,32,128]{3,2,1,0:T(8,128)(2,1)S(1)} %copy-done.5, ...), custom_call_target="tpu_custom_call", output_to_operand_aliasing={{}: (8, {})} | custom-call | flops 5662310400 | bytes 13631488 | tf_op jit(solution)/shard_map/lags_1/pallas_call | solution.py:239
  130.7 0.0 collective-permute-done.6.refs_8_
  130.7 1.9 %collective-permute-start.9 = (bf16[2,16,32,128]{3,2,1,0:T(8,128)(2,1)S(1)}, bf16[2,16,32,128]{3,2,1,0:T(8,128)(2,1)S(1)}, u32[]{:S(2)}, u32[]{:S(2)}) collective-permute-start(bf16[2,16,32,128]{3,2,1,0:T(8,128)(2,1)S(1)} %pad_maximum_fusion.7), channel_id=1, source_target_pairs={{1,0},{2,1},{3,2},{4,3},{5,4},{6,5},{7,6},{8,7},{9,8},{10,9},{11,1... | collective-permute-start | bytes 786440 | tf_op jit(solution)/shard_map/ppermute | solution.py:198
  132.6 0.0 collective-permute-done.7.refs_9_
  132.6 9.0 %lags_2.1.refs_14_ = f32[33,16,4096]{2,1,0:T(8,128)} custom-call(bf16[16,16,32,128]{3,2,1,0:T(8,128)(2,1)S(1)} %copy-done, bf16[16,16,32,128]{3,2,1,0:T(8,128)(2,1)S(1)} %copy-done.2, bf16[4,16,32,128]{3,2,1,0:T(8,128)(2,1)S(1)} %copy-done.8, bf16[4,16,32,128]{3,2,1,0:T(8,128)(2,1)S(1)} %copy-done.5, ...), custom_call_target="tpu_custom_call", output_to_operand_aliasing={{}: (10, {})} | custom-call | flops 2831155200 | bytes 13631488 | tf_op jit(solution)/shard_map/lags_2/pallas_call | solution.py:239
  141.6 0.0 collective-permute-done.10.refs_12_
  141.6 0.0 collective-permute-done.11.refs_13_
  141.7 0.0 collective-permute-done.8.refs_10_
  141.7 0.0 collective-permute-done.9.refs_11_
  141.7 8.9 %lags_3.1 = f32[33,16,4096]{2,1,0:T(8,128)} custom-call(bf16[16,16,32,128]{3,2,1,0:T(8,128)(2,1)S(1)} %copy-done, bf16[16,16,32,128]{3,2,1,0:T(8,128)(2,1)S(1)} %copy-done.2, bf16[4,16,32,128]{3,2,1,0:T(8,128)(2,1)S(1)} %copy-done.8, bf16[4,16,32,128]{3,2,1,0:T(8,128)(2,1)S(1)} %copy-done.5, ...), custom_call_target="tpu_custom_call", output_to_operand_aliasing={{}: (14, {})} | custom-call | flops 2831155200 | bytes 14155776 | tf_op jit(solution)/shard_map/lags_3/pallas_call | solution.py:239
  (1 shorter events, 0.0 us)
Async XLA Ops:
  7.3 7.3 %copy-start = (bf16[16,16,32,128]{3,2,1,0:T(8,128)(2,1)S(1)}, bf16[16,16,32,128]{3,2,1,0:T(8,128)(2,1)}, u32[]{:S(2)}) copy-start(bf16[16,16,32,128]{3,2,1,0:T(8,128)(2,1)} %get-tuple-element.21.refs_0_) | copy-start | bytes 6291460
  8.9 44.3 %collective-permute-start.1 = (bf16[4,16,32,128]{3,2,1,0:T(8,128)(2,1)S(1)}, bf16[4,16,32,128]{3,2,1,0:T(8,128)(2,1)S(1)}, u32[]{:S(2)}, u32[]{:S(2)}) collective-permute-start(bf16[4,16,32,128]{3,2,1,0:T(8,128)(2,1)S(1)} %pad_maximum_fusion.5), channel_id=1, source_target_pairs={{1,0},{2,1},{3,2},{4,3},{5,4},{6,5},{7,6},{8,7},{9,8},{10,9},{11,1... | collective-permute-start | bytes 1572872 | tf_op jit(solution)/shard_map/ppermute | solution.py:198
  11.5 41.7 %collective-permute-start = (bf16[4,16,32,128]{3,2,1,0:T(8,128)(2,1)S(1)}, bf16[4,16,32,128]{3,2,1,0:T(8,128)(2,1)S(1)}, u32[]{:S(2)}, u32[]{:S(2)}) collective-permute-start(bf16[4,16,32,128]{3,2,1,0:T(8,128)(2,1)S(1)} %pad_maximum_fusion.5), channel_id=1, source_target_pairs={{0,1},{1,2},{2,3},{3,4},{4,5},{5,6},{6,7},{7,8},{8,9},{9,10},{10,1... | collective-permute-start | bytes 1572872 | tf_op jit(solution)/shard_map/ppermute | solution.py:197
  16.1 3.6 %copy-start.1 = (bf16[16,16,32,128]{3,2,1,0:T(8,128)(2,1)S(1)}, bf16[16,16,32,128]{3,2,1,0:T(8,128)(2,1)}, u32[]{:S(2)}) copy-start(bf16[16,16,32,128]{3,2,1,0:T(8,128)(2,1)} %get-tuple-element.22.refs_1_) | copy-start | bytes 6291460
  17.2 52.0 %collective-permute-start.2 = (bf16[8,16,32,128]{3,2,1,0:T(8,128)(2,1)}, bf16[8,16,32,128]{3,2,1,0:T(8,128)(2,1)S(1)}, u32[]{:S(2)}, u32[]{:S(2)}) collective-permute-start(bf16[8,16,32,128]{3,2,1,0:T(8,128)(2,1)} %pad_maximum_fusion.1), channel_id=1, source_target_pairs={{0,1},{1,2},{2,3},{3,4},{4,5},{5,6},{6,7},{7,8},{8,9},{9,10},{10,1... | collective-permute-start | bytes 3145736 | tf_op jit(solution)/shard_map/ppermute | solution.py:197
  53.2 8.5 %copy-start.3 = (bf16[4,16,32,128]{3,2,1,0:T(8,128)(2,1)}, bf16[4,16,32,128]{3,2,1,0:T(8,128)(2,1)S(1)}, u32[]{:S(2)}) copy-start(bf16[4,16,32,128]{3,2,1,0:T(8,128)(2,1)S(1)} %collective-permute-done.1.b_ref.refs_3_) | copy-start | bytes 1572868
  53.2 8.5 %copy-start.6 = (bf16[4,16,32,128]{3,2,1,0:T(8,128)(2,1)}, bf16[4,16,32,128]{3,2,1,0:T(8,128)(2,1)S(1)}, u32[]{:S(2)}) copy-start(bf16[4,16,32,128]{3,2,1,0:T(8,128)(2,1)S(1)} %collective-permute-done.a_ref.refs_2_) | copy-start | bytes 1572868
  53.2 56.1 %collective-permute-start.4 = (bf16[12,16,32,128]{3,2,1,0:T(8,128)(2,1)}, bf16[12,16,32,128]{3,2,1,0:T(8,128)(2,1)}, u32[]{:S(2)}, u32[]{:S(2)}) collective-permute-start(bf16[12,16,32,128]{3,2,1,0:T(8,128)(2,1)} %pad_maximum_fusion), channel_id=1, source_target_pairs={{0,1},{1,2},{2,3},{3,4},{4,5},{5,6},{6,7},{7,8},{8,9},{9,10},{10,1... | collective-permute-start | bytes 4718600 | tf_op jit(solution)/shard_map/ppermute | solution.py:197
  55.1 56.1 %collective-permute-start.5 = (bf16[12,16,32,128]{3,2,1,0:T(8,128)(2,1)}, bf16[12,16,32,128]{3,2,1,0:T(8,128)(2,1)}, u32[]{:S(2)}, u32[]{:S(2)}) collective-permute-start(bf16[12,16,32,128]{3,2,1,0:T(8,128)(2,1)} %pad_maximum_fusion), channel_id=1, source_target_pairs={{1,0},{2,1},{3,2},{4,3},{5,4},{6,5},{7,6},{8,7},{9,8},{10,9},{11,1... | collective-permute-start | bytes 4718600 | tf_op jit(solution)/shard_map/ppermute | solution.py:198
  58.7 30.1 %collective-permute-start.3 = (bf16[8,16,32,128]{3,2,1,0:T(8,128)(2,1)}, bf16[8,16,32,128]{3,2,1,0:T(8,128)(2,1)}, u32[]{:S(2)}, u32[]{:S(2)}) collective-permute-start(bf16[8,16,32,128]{3,2,1,0:T(8,128)(2,1)} %pad_maximum_fusion.2), channel_id=1, source_target_pairs={{1,0},{2,1},{3,2},{4,3},{5,4},{6,5},{7,6},{8,7},{9,8},{10,9},{11,1... | collective-permute-start | bytes 3145736 | tf_op jit(solution)/shard_map/ppermute | solution.py:198
  65.5 76.1 %collective-permute-start.10 = (f32[2,32,128]{2,1,0:T(8,128)}, f32[2,32,128]{2,1,0:T(8,128)S(1)}, u32[]{:S(2)}, u32[]{:S(2)}) collective-permute-start(f32[2,32,128]{2,1,0:T(8,128)} %get-tuple-element.35), channel_id=1, source_target_pairs={{0,1},{1,2},{2,3},{3,4},{4,5},{5,6},{6,7},{7,8},{8,9},{9,10},{10,1... | collective-permute-start | bytes 98312 | tf_op jit(solution)/shard_map/ppermute | solution.py:211
  88.8 41.9 %collective-permute-start.6 = (bf16[6,16,32,128]{3,2,1,0:T(8,128)(2,1)}, bf16[6,16,32,128]{3,2,1,0:T(8,128)(2,1)S(1)}, u32[]{:S(2)}, u32[]{:S(2)}) collective-permute-start(bf16[6,16,32,128]{3,2,1,0:T(8,128)(2,1)} %pad_maximum_fusion.3), channel_id=1, source_target_pairs={{0,1},{1,2},{2,3},{3,4},{4,5},{5,6},{6,7},{7,8},{8,9},{9,10},{10,1... | collective-permute-start | bytes 2359304 | tf_op jit(solution)/shard_map/ppermute | solution.py:197
  90.7 41.9 %collective-permute-start.7 = (bf16[6,16,32,128]{3,2,1,0:T(8,128)(2,1)}, bf16[6,16,32,128]{3,2,1,0:T(8,128)(2,1)S(1)}, u32[]{:S(2)}, u32[]{:S(2)}) collective-permute-start(bf16[6,16,32,128]{3,2,1,0:T(8,128)(2,1)} %pad_maximum_fusion.4), channel_id=1, source_target_pairs={{1,0},{2,1},{3,2},{4,3},{5,4},{6,5},{7,6},{8,7},{9,8},{10,9},{11,1... | collective-permute-start | bytes 2359304 | tf_op jit(solution)/shard_map/ppermute | solution.py:198
  93.1 1.6 %copy-start.2 = (bf16[16,16,32,128]{3,2,1,0:T(8,128)(2,1)S(1)}, bf16[16,16,32,128]{3,2,1,0:T(8,128)(2,1)}, u32[]{:S(2)}) copy-start(bf16[16,16,32,128]{3,2,1,0:T(8,128)(2,1)} %get-tuple-element.22.refs_1_) | copy-start | bytes 6291460
  94.7 1.0 copy-start.4
  95.7 1.0 copy-start.7
  96.8 12.5 %copy-start.10 = (f32[2,32,128]{2,1,0:T(8,128)S(1)}, f32[2,32,128]{2,1,0:T(8,128)}, u32[]{:S(2)}) copy-start(f32[2,32,128]{2,1,0:T(8,128)} %get-tuple-element.36) | copy-start | bytes 98308
  96.8 14.5 %copy-start.9 = (bf16[2,16,32,128]{3,2,1,0:T(8,128)(2,1)S(1)}, bf16[2,16,32,128]{3,2,1,0:T(8,128)(2,1)}, u32[]{:S(2)}) copy-start(bf16[2,16,32,128]{3,2,1,0:T(8,128)(2,1)} %pad_maximum_fusion.6) | copy-start | bytes 786436
  96.8 18.9 %copy-start.5 = (bf16[4,16,32,128]{3,2,1,0:T(8,128)(2,1)S(1)}, bf16[4,16,32,128]{3,2,1,0:T(8,128)(2,1)}, u32[]{:S(2)}) copy-start(bf16[4,16,32,128]{3,2,1,0:T(8,128)(2,1)} %copy-done.3) | copy-start | bytes 1572868
  96.8 18.9 %copy-start.8 = (bf16[4,16,32,128]{3,2,1,0:T(8,128)(2,1)S(1)}, bf16[4,16,32,128]{3,2,1,0:T(8,128)(2,1)}, u32[]{:S(2)}) copy-start(bf16[4,16,32,128]{3,2,1,0:T(8,128)(2,1)} %copy-done.6) | copy-start | bytes 1572868
  109.3 32.3 %collective-permute-start.11 = (f32[2,32,128]{2,1,0:T(8,128)S(1)}, f32[2,32,128]{2,1,0:T(8,128)S(1)}, u32[]{:S(2)}, u32[]{:S(2)}) collective-permute-start(f32[2,32,128]{2,1,0:T(8,128)S(1)} %copy-done.10), channel_id=1, source_target_pairs={{1,0},{2,1},{3,2},{4,3},{5,4},{6,5},{7,6},{8,7},{9,8},{10,9},{11,1... | collective-permute-start | bytes 98312 | tf_op jit(solution)/shard_map/ppermute | solution.py:210
  111.2 30.4 %collective-permute-start.8 = (bf16[2,16,32,128]{3,2,1,0:T(8,128)(2,1)S(1)}, bf16[2,16,32,128]{3,2,1,0:T(8,128)(2,1)S(1)}, u32[]{:S(2)}, u32[]{:S(2)}) collective-permute-start(bf16[2,16,32,128]{3,2,1,0:T(8,128)(2,1)S(1)} %copy-done.9), channel_id=1, source_target_pairs={{0,1},{1,2},{2,3},{3,4},{4,5},{5,6},{6,7},{7,8},{8,9},{9,10},{10,1... | collective-permute-start | bytes 786440 | tf_op jit(solution)/shard_map/ppermute | solution.py:197
  130.7 11.0 %collective-permute-start.9 = (bf16[2,16,32,128]{3,2,1,0:T(8,128)(2,1)S(1)}, bf16[2,16,32,128]{3,2,1,0:T(8,128)(2,1)S(1)}, u32[]{:S(2)}, u32[]{:S(2)}) collective-permute-start(bf16[2,16,32,128]{3,2,1,0:T(8,128)(2,1)S(1)} %pad_maximum_fusion.7), channel_id=1, source_target_pairs={{1,0},{2,1},{3,2},{4,3},{5,4},{6,5},{7,6},{8,7},{9,8},{10,9},{11,1... | collective-permute-start | bytes 786440 | tf_op jit(solution)/shard_map/ppermute | solution.py:198

commit v3 on v2

--- a/solution.py
+++ b/solution.py
@@ -13,11 +13,12 @@
 BLOCK = 3
 LANES = 128
 SUB = 16
-SPAN = 6
+SPAN = 3
 RATE = 200
 
-CHUNKS = ((16, 1), (5, 4, 3, 2), (11, 10, 9, 8, 7, 6), (14, 13, 12), (15,))
-BLOCKS = ((5, 4, 6), (2, 3, 7, 8), (1, 9), (0, 10))
+CHUNKS = ((16, 2, 1), (5, 4, 3), (8, 7, 6), (14, 13, 12, 11, 10, 9), (15,))
+BUNDLES = ((0, 1), (2,))
+BLOCKS = ((1, (5, 4, 6)), (2, (3, 7)), (3, (2, 8, 1, 9)), (4, (0, 10)))
 
 VMEM = pl.BlockSpec(memory_space=pltpu.VMEM)
 ANY = pl.BlockSpec(memory_space=pl.ANY)
@@ -80,22 +81,27 @@
     )(forward_field, adjoint_field)
 
 
-def rim_kernel(a_ref, b_ref, lo_ref, hi_ref):
-    def dot(s, r):
-        total = s[0].astype(jnp.float32) * r[0].astype(jnp.float32)
-        for k in range(1, s.shape[0]):
-            total += s[k].astype(jnp.float32) * r[k].astype(jnp.float32)
-        return total
+def rim_kernel(cells, where, *refs):
+    ins, (lo_ref, hi_ref) = refs[:-2], refs[-2:]
 
     def tile(g, _):
         at = pl.ds(pl.multiple_of(g * SUB, SUB), SUB)
-        lo_ref[0, at] = dot(b_ref.at[0, :, at], a_ref.at[2, :, at])
-        lo_ref[1, at] = dot(a_ref.at[0, :, at], b_ref.at[2, :, at])
-        hi_ref[0, at] = dot(b_ref.at[1, :, at], a_ref.at[3, :, at])
-        hi_ref[1, at] = dot(a_ref.at[1, :, at], b_ref.at[3, :, at])
+
+        def dot(a, b):
+            (s_in, s), (r_in, r) = where[0, a], where[1, b]
+            total = jnp.zeros((SUB, LANES), jnp.float32)
+            for k in range(ins[0].shape[1]):
+                total += ins[s_in][s, k, at].astype(jnp.float32) * ins[r_in][r, k, at].astype(
+                    jnp.float32
+                )
+            return total
+
+        for ref, x in ((lo_ref, 0), (hi_ref, cells - 1)):
+            ref[0, at] = dot(x + HALF, x - HALF)
+            ref[1, at] = dot(x - HALF, x + HALF)
         return 0
 
-    lax.fori_loop(0, a_ref.shape[2] // SUB, tile, 0)
+    lax.fori_loop(0, ins[0].shape[2] // SUB, tile, 0)
 
 
 def lag_kernel(cells, blocks, where, rim, aliased, *refs):
@@ -147,7 +153,7 @@
                     )
 
                 zero = jnp.zeros((SUB, LANES), jnp.float32)
-                accs = lax.fori_loop(0, terms, step, (zero,) * len(pairs))
+                accs = lax.fori_loop(0, terms, step, (zero,) * len(pairs), unroll=terms)
                 for acc, (t, x) in zip(accs, pairs):
                     sums[t, x + 1] = acc
             for t in range(BLOCK):
@@ -174,57 +180,122 @@
             copies(n, g).wait()
 
 
+def neighbours(peers):
+    up = [(i, i + 1) for i in range(peers - 1)]
+    return up, [(j, i) for i, j in up]
+
+
+def routes(peers, chunk):
+    up, down = neighbours(peers)
+    if peers != 16 or chunk > 2:
+        return up, down, (), ()
+    steps = peers // 4
+    far_up = range(0, steps - 1 - chunk)
+    far_down = range(chunk, steps - 1)
+    up = [p for p in up if p not in [(4 * z + 3, 4 * z + 4) for z in far_up]]
+    up += [(4 * z + 3, 4 * z) for z in far_up]
+    down = [p for p in down if p not in [(4 * z + 4, 4 * z + 3) for z in far_down]]
+    down += [(4 * z + 4, 4 * z + 7) for z in far_down]
+    swap_up = sorted({4 * z for z in far_up} | {4 * z + 4 for z in far_up})
+    swap_down = sorted({4 * z + 7 for z in far_down} | {4 * z + 3 for z in far_down})
+    return up, down, swap_up, swap_down
+
+
+def is_one_of(me, devices):
+    found = jnp.bool_(False)
+    for d in devices:
+        found |= me == d
+    return found
+
+
 def on_device(forward_field, adjoint_field):
     cells, parts, freqs, width = forward_field.shape
     terms, tiles = parts * freqs, width // LANES
     peers = lax.axis_size("gx")
-    up = [(i, (i + 1) % peers) for i in range(peers - 1)]
-    down = [(j, i) for i, j in up]
+    me = lax.axis_index("gx")
+    plain_up, plain_down = neighbours(peers)
     field_bytes = terms * width * 2
 
-    source, receiver = pack(forward_field, adjoint_field)
-
-    from_left, from_right = [], []
-    for g, chunk in enumerate(CHUNKS):
+    def outgoing(source, receiver, chunk):
         to_right = [cells + r for r in left_rows(chunk)]
         to_left = [r - cells for r in right_rows(chunk, cells)]
-        sent_up = jnp.concatenate(take(source, to_right) + take(receiver, to_right), axis=0)
-        sent_down = jnp.concatenate(take(source, to_left) + take(receiver, to_left), axis=0)
+        return (
+            jnp.concatenate(take(source, to_right) + take(receiver, to_right), axis=0),
+            jnp.concatenate(take(source, to_left) + take(receiver, to_left), axis=0),
+        )
+
+    def send(pair, g):
+        up, down, _, _ = routes(peers, g)
+        return lax.ppermute(pair[0], "gx", up), lax.ppermute(pair[1], "gx", down)
+
+    def after(values, earlier):
+        out = lax.optimization_barrier((*values, *earlier))
+        return out[:2], out[2:]
+
+    arrived = [send(outgoing(forward_field, adjoint_field, CHUNKS[0]), 0)]
+    source, receiver = pack(forward_field, adjoint_field)
+    for g in range(1, len(CHUNKS)):
+        sent = outgoing(source, receiver, CHUNKS[g])
         if g >= 2:
-            sent_up, sent_down, from_left[g - 2], from_right[g - 2] = lax.optimization_barrier(
-                (sent_up, sent_down, from_left[g - 2], from_right[g - 2])
-            )
-        from_left.append(lax.ppermute(sent_up, "gx", up))
-        from_right.append(lax.ppermute(sent_down, "gx", down))
-
+            sent, arrived[g - 2] = after(sent, arrived[g - 2])
+        arrived.append(send(sent, g))
+    arrived[0] = pack(*arrived[0])
+
+    pieces = []
+    for bundle in BUNDLES:
+        got = [jnp.concatenate([arrived[g][side] for g in bundle], axis=0) for side in (0, 1)]
+        if peers == 16:
+            hop_up = [(4 * z, 4 * z + 4) for z in range(peers // 4 - 1)]
+            hop_down = [(4 * z + 7, 4 * z + 3) for z in range(peers // 4 - 1)]
+            hops = [lax.ppermute(got[0], "gx", hop_up), lax.ppermute(got[1], "gx", hop_down)]
+            for side in (0, 1):
+                swapped = jnp.concatenate(
+                    [
+                        jnp.broadcast_to(
+                            is_one_of(me, routes(peers, g)[2 + side]), (2 * len(CHUNKS[g]),)
+                        )
+                        for g in bundle
+                    ]
+                )
+                got[side] = jnp.where(swapped[:, None, None, None], hops[side], got[side])
+        pieces.append((bundle, got))
+    for g in range(3, len(CHUNKS)):
+        pieces.append(((g,), list(arrived[g])))
+
+    def layout(count, own):
+        operands = [source, receiver] if own else []
+        where = {(f, a): (f, a) for f in (0, 1) for a in range(cells)} if own else {}
+        for bundle, got in pieces[:count]:
+            for side in (0, 1):
+                base = 0
+                for g in bundle:
+                    n = len(CHUNKS[g])
+                    rows = right_rows(CHUNKS[g], cells) if side else left_rows(CHUNKS[g])
+                    for field in (0, 1):
+                        for k, a in enumerate(rows):
+                            where[field, a] = (len(operands), base + field * n + k)
+                    base += 2 * n
+                operands.append(got[side])
+        return operands, where
+
+    operands, where = layout(1, False)
     lo, hi = pl.pallas_call(
-        rim_kernel,
-        in_specs=[VMEM, VMEM],
+        functools.partial(rim_kernel, cells, where),
+        in_specs=[VMEM] * len(operands),
         out_specs=[VMEM, VMEM],
         out_shape=[jax.ShapeDtypeStruct((2, tiles, LANES), jnp.float32)] * 2,
         cost_estimate=pl.CostEstimate(
-            flops=8 * terms * width, bytes_accessed=12 * field_bytes, transcendentals=0
+            flops=RATE * 8 * terms * width, bytes_accessed=12 * field_bytes, transcendentals=0
         ),
         name="rim",
-    )(from_left[0], from_right[0])
-    rim_hi = lax.ppermute(lo, "gx", down)
-    rim_lo = lax.ppermute(hi, "gx", up)
+    )(*operands)
+    rim_hi = lax.ppermute(lo, "gx", plain_down)
+    rim_lo = lax.ppermute(hi, "gx", plain_up)
 
     image = None
-    for stage, blocks in enumerate(BLOCKS):
+    for stage, (count, blocks) in enumerate(BLOCKS):
         rim = 0 in blocks
-        operands = [source, receiver]
-        where = {(field, a): (field, a) for field in (0, 1) for a in range(cells)}
-        for g in range(stage + 2):
-            n = len(CHUNKS[g])
-            for got, rows in (
-                (from_left[g], left_rows(CHUNKS[g])),
-                (from_right[g], right_rows(CHUNKS[g], cells)),
-            ):
-                for field in (0, 1):
-                    for k, a in enumerate(rows):
-                        where[field, a] = (len(operands), field * n + k)
-                operands.append(got)
+        operands, where = layout(count, True)
         n_fields = len(operands)
         if rim:
             operands += [rim_lo, rim_hi]

time: 151 us -> 135 us (0.89); the launches traced: 151 us -> 133 us
  waiting for transfers between devices: 53.1 us -> 20.1 us
  Pallas kernels: 53.3 us -> 36.8 us
  starting transfers between devices: 30.4 us -> 42 us
  other arithmetic: 6.28 us -> 17.2 us
  local copies, waits for them, and re-layouts: 7.22 us -> 16.3 us
    ppermute x12 -> x16, waiting for transfers between devices: 53.1 us -> 20.1 us  [the longest x10 20.1 us: send(): return (lax.ppermute(pair[0], 'gx', up), lax.ppermute(pair[1], 'gx', down))]
    pallas_call x4, Pallas kernels: 44.1 us -> 23.2 us  [on_device(): pl.pallas_call(functools.partial(lag_kernel, cells, blocks, where, rim, i...]
    ppermute x12 -> x16, starting transfers between devices: 30.4 us -> 42 us  [the longest x10 29.3 us: send(): return (lax.ppermute(pair[0], 'gx', up), lax.ppermute(pair[1], 'gx', down))]
    select_n x0 -> x4, other arithmetic: none -> 8.02 us  [on_device(): got[side] = jnp.where(swapped[:, None, None, None], hops[side], got[side])]
    concatenate x0 -> x4, local copies, waits for them, and re-layouts: none -> 4.24 us  [the longest x2 4.22 us: on_device(): jnp.concatenate([arrived[g][side] for g in bundle], axis=0)]
    pallas_call x1 -> x2, Pallas kernels: 7.32 us -> 11 us  [pack(): pl.pallas_call(pack_kernel, grid=(cells // rows,), in_specs=[spec, spec],...]
    slice x5, local copies, waits for them, and re-layouts: 3.53 us -> 6.54 us  [take(): return [lax.slice_in_dim(field, a, b, axis=0) for a, b in spans]]
    concatenate x8 -> x10, other arithmetic: 6.28 us -> 9.23 us  [the longest x5 4.97 us: outgoing(): jnp.concatenate(take(source, to_right) + take(receiver, to_right), axis=0)]
  transfers between devices with their start and end apart: 12 -> 16, of which waited for: 3 -> 3; matrix products, arithmetic and copies ran while one was open for 5% -> 19% of each run, Pallas kernels for 25% -> 24%
where the time goes in v3:
time: 135 us; the launch traced here: 133 us
  starting transfers between devices  42 us (31%)
  Pallas kernels  36.8 us (27%)
  waiting for transfers between devices  20.1 us (15%)
  other arithmetic  17.2 us (13%)
  local copies, waits for them, and re-layouts  16.3 us (12%)
    ppermute x10, starting transfers between devices, send(): return (lax.ppermute(pair[0], 'gx', up), lax.ppermute(pair[1], 'gx', down))  29.3 us
    pallas_call x4, Pallas kernels, on_device(): pl.pallas_call(functools.partial(lag_kernel, cells, blocks, where, rim, i...  23.2 us
    ppermute x10, waiting for transfers between devices, send(): return (lax.ppermute(pair[0], 'gx', up), lax.ppermute(pair[1], 'gx', down))  20.1 us
    pallas_call x2, Pallas kernels, pack(): pl.pallas_call(pack_kernel, grid=(cells // rows,), in_specs=[spec, spec],...  11 us
    select_n x4, other arithmetic, on_device(): got[side] = jnp.where(swapped[:, None, None, None], hops[side], got[side])  8.02 us
    slice x5, local copies, waits for them, and re-layouts, take(): return [lax.slice_in_dim(field, a, b, axis=0) for a, b in spans]  6.54 us
    unnamed x22, local copies, waits for them, and re-layouts  5.46 us
    concatenate x5, other arithmetic, outgoing(): jnp.concatenate(take(source, to_right) + take(receiver, to_right), axis=0)  4.97 us
  transfers between devices with their start and end apart: 16, of which 3 were waited for; matrix products, arithmetic and copies ran while one was open for 19% of the time, Pallas kernels for 24%

profile of v3, /device:TPU:17, one launch (start us, length us, event | category | flops | bytes accessed | tf_op | source)
XLA Modules:
  0.0 132.9 jit_solution(18370298406999115957)
XLA Ops:
  0.0 1.1 fusion.7
  1.1 1.3 fusion.6
  2.4 1.0 pad_maximum_fusion.4
  3.4 3.7 %collective-permute-start = (bf16[6,2,8,4096]{3,2,1,0:T(8,128)(2,1)}, bf16[6,2,8,4096]{3,2,1,0:T(8,128)(2,1)S(1)}, u32[]{:S(2)}, u32[]{:S(2)}) collective-permute-start(bf16[6,2,8,4096]{3,2,1,0:T(8,128)(2,1)} %pad_maximum_fusion.4), channel_id=1, source_target_pairs={{0,1},{1,2},{2,3},{4,5},{5,6},{6,7},{8,9},{9,10},{10,11},{12,13},{... | collective-permute-start | bytes 2359304 | tf_op jit(solution)/shard_map/ppermute | solution.py:229
  7.1 1.0 pad_maximum_fusion.5
  8.1 1.9 %collective-permute-start.1 = (bf16[6,2,8,4096]{3,2,1,0:T(8,128)(2,1)}, bf16[6,2,8,4096]{3,2,1,0:T(8,128)(2,1)}, u32[]{:S(2)}, u32[]{:S(2)}) collective-permute-start(bf16[6,2,8,4096]{3,2,1,0:T(8,128)(2,1)} %pad_maximum_fusion.5), channel_id=1, source_target_pairs={{1,0},{2,1},{3,2},{5,4},{6,5},{7,6},{9,8},{10,9},{11,10},{13,12},{... | collective-permute-start | bytes 2359304 | tf_op jit(solution)/shard_map/ppermute | solution.py:229
  10.0 7.3 %pack.2 = (bf16[16,16,32,128]{3,2,1,0:T(8,128)(2,1)}, bf16[16,16,32,128]{3,2,1,0:T(8,128)(2,1)}) custom-call(bf16[16,2,8,4096]{3,2,1,0:T(8,128)(2,1)} %s_ref.1, bf16[16,2,8,4096]{3,2,1,0:T(8,128)(2,1)} %r_ref.1), custom_call_target="tpu_custom_call" | custom-call | bytes 8388608 | tf_op jit(solution)/shard_map/pack/pallas_call | solution.py:70
  17.4 2.4 %fusion.2 = (bf16[3,16,32,128]{3,2,1,0:T(8,128)(2,1)S(1)}, bf16[3,16,32,128]{3,2,1,0:T(8,128)(2,1)S(1)}, bf16[3,16,32,128]{3,2,1,0:T(8,128)(2,1)S(1)}, bf16[3,16...) fusion(bf16[16,16,32,128]{3,2,1,0:T(8,128)(2,1)} %get-tuple-ele, ...), kind=kLoop, calls=%fused_computation.20 | loop fusion | bytes 6291456 | tf_op jit(solution)/shard_map/slice | solution.py:42
  19.8 1.0 pad_maximum_fusion.6
  20.8 3.6 %collective-permute-start.2 = (bf16[6,16,32,128]{3,2,1,0:T(8,128)(2,1)}, bf16[6,16,32,128]{3,2,1,0:T(8,128)(2,1)}, u32[]{:S(2)}, u32[]{:S(2)}) collective-permute-start(bf16[6,16,32,128]{3,2,1,0:T(8,128)(2,1)} %pad_maximum_fusion.6), channel_id=1, source_target_pairs={{0,1},{1,2},{2,3},{4,5},{5,6},{6,7},{8,9},{9,10},{10,11},{11,12},{... | collective-permute-start | bytes 2359304 | tf_op jit(solution)/shard_map/ppermute | solution.py:229
  24.4 1.0 pad_maximum_fusion.7
  25.4 1.9 %collective-permute-start.3 = (bf16[6,16,32,128]{3,2,1,0:T(8,128)(2,1)}, bf16[6,16,32,128]{3,2,1,0:T(8,128)(2,1)}, u32[]{:S(2)}, u32[]{:S(2)}) collective-permute-start(bf16[6,16,32,128]{3,2,1,0:T(8,128)(2,1)} %pad_maximum_fusion.7), channel_id=1, source_target_pairs={{1,0},{2,1},{3,2},{4,3},{5,4},{6,5},{7,6},{9,8},{10,9},{11,10},{13... | collective-permute-start | bytes 2359304 | tf_op jit(solution)/shard_map/ppermute | solution.py:229
  27.3 0.0 copy-start
  27.4 1.0 pad_maximum_fusion.3
  28.3 1.0 pad_maximum_fusion.2
  29.3 0.7 fusion.4
  30.0 1.3 pad_maximum_fusion.1
  31.3 1.3 pad_maximum_fusion
  32.6 0.0 collective-permute-done.s_ref
  32.6 0.0 collective-permute-done.1.r_ref
  32.6 0.9 copy-done.6
  33.5 3.6 %pack.3 = (bf16[6,16,32,128]{3,2,1,0:T(8,128)(2,1)}, bf16[6,16,32,128]{3,2,1,0:T(8,128)(2,1)}) custom-call(bf16[6,2,8,4096]{3,2,1,0:T(8,128)(2,1)} %copy-done.6, bf16[6,2,8,4096]{3,2,1,0:T(8,128)(2,1)} %collective-permute-done.1.r_ref), custom_call_target="tpu_custom_call" | custom-call | bytes 3145728 | tf_op jit(solution)/shard_map/pack/pallas_call | solution.py:70
  37.1 2.2 %constant_dynamic-update-slice_fusion.3 = bf16[12,16,32,128]{3,2,1,0:T(8,128)(2,1)} fusion(bf16[6,16,32,128]{3,2,1,0:T(8,128)(2,1)} %get-tuple-element.29), kind=kLoop, calls=%fused_computation.17 | loop fusion | bytes 1572864
  39.3 0.0 collective-permute-done.2
  39.3 0.0 collective-permute-done.3
  39.3 2.1 %constant_dynamic-update-slice_fusion.2 = bf16[12,16,32,128]{3,2,1,0:T(8,128)(2,1)} fusion(bf16[12,16,32,128]{3,2,1,0:T(8,128)(2,1)} %constant_dynamic-update-slice_fusion.3, bf16[6,16,32,128]{3,2,1,0:T(8,128)(2,1)} %collective-permute-done.3), kind=kLoop, calls=%fused_computation.16 | loop fusion | bytes 1572864 | tf_op jit(solution)/shard_map/concatenate | solution.py:246
  41.4 1.8 %collective-permute-start.5 = (bf16[12,16,32,128]{3,2,1,0:T(8,128)(2,1)}, bf16[12,16,32,128]{3,2,1,0:T(8,128)(2,1)}, u32[]{:S(2)}, u32[]{:S(2)}) collective-permute-start(bf16[12,16,32,128]{3,2,1,0:T(8,128)(2,1)} %constant_dynamic-update-slice_fusion.2), channel_id=1, source_target_pairs={{7,3},{11,7},{15,11},{23,19},{27,23},{31,27}} | collective-permute-start | bytes 4718600 | tf_op jit(solution)/shard_map/ppermute | solution.py:250
  43.3 1.0 constant_dynamic-update-slice_fusion.1
  44.2 2.1 %constant_dynamic-update-slice_fusion = bf16[12,16,32,128]{3,2,1,0:T(8,128)(2,1)} fusion(bf16[12,16,32,128]{3,2,1,0:T(8,128)(2,1)} %constant_dynamic-update-slice_fusion.1, bf16[6,16,32,128]{3,2,1,0:T(8,128)(2,1)} %collective-permute-done.2), kind=kLoop, calls=%fused_computation.14 | loop fusion | bytes 1572864 | tf_op jit(solution)/shard_map/concatenate | solution.py:246
  46.3 1.8 %collective-permute-start.4 = (bf16[12,16,32,128]{3,2,1,0:T(8,128)(2,1)}, bf16[12,16,32,128]{3,2,1,0:T(8,128)(2,1)}, u32[]{:S(2)}, u32[]{:S(2)}) collective-permute-start(bf16[12,16,32,128]{3,2,1,0:T(8,128)(2,1)} %constant_dynamic-update-slice_fusion), channel_id=1, source_target_pairs={{0,4},{4,8},{8,12},{16,20},{20,24},{24,28}} | collective-permute-start | bytes 4718600 | tf_op jit(solution)/shard_map/ppermute | solution.py:250
  48.1 3.8 %collective-permute-start.6 = (bf16[6,16,32,128]{3,2,1,0:T(8,128)(2,1)}, bf16[6,16,32,128]{3,2,1,0:T(8,128)(2,1)}, u32[]{:S(2)}, u32[]{:S(2)}) collective-permute-start(bf16[6,16,32,128]{3,2,1,0:T(8,128)(2,1)} %pad_maximum_fusion.2), channel_id=1, source_target_pairs={{0,1},{1,2},{2,3},{4,5},{5,6},{6,7},{7,8},{8,9},{9,10},{10,11},{11... | collective-permute-start | bytes 2359304 | tf_op jit(solution)/shard_map/ppermute | solution.py:229
  51.9 4.9 %collective-permute-start.7 = (bf16[6,16,32,128]{3,2,1,0:T(8,128)(2,1)S(1)}, bf16[6,16,32,128]{3,2,1,0:T(8,128)(2,1)S(1)}, u32[]{:S(2)}, u32[]{:S(2)}) collective-permute-start(bf16[6,16,32,128]{3,2,1,0:T(8,128)(2,1)S(1)} %copy-done.5), channel_id=1, source_target_pairs={{1,0},{2,1},{3,2},{4,3},{5,4},{6,5},{7,6},{8,7},{9,8},{10,9},{11,1... | collective-permute-start | bytes 2359304 | tf_op jit(solution)/shard_map/ppermute | solution.py:229
  56.8 1.0 fusion
  57.9 0.7 pad_maximum_fusion.8
  58.6 2.5 %collective-permute-done.6 = bf16[6,16,32,128]{3,2,1,0:T(8,128)(2,1)} collective-permute-done((bf16[6,16,32,128]{3,2,1,0:T(8,128)(2,1)}, bf16[6,16,32,128]{3,2,1,0:T(8,128)(2,1)}, u32[]{:S(2)}, u32[]{:S(2)}) %collective-permute-start.6) | collective-permute-done | bytes 786464 | tf_op jit(solution)/shard_map/ppermute | solution.py:229
  61.1 14.4 %collective-permute-done.7 = bf16[6,16,32,128]{3,2,1,0:T(8,128)(2,1)S(1)} collective-permute-done((bf16[6,16,32,128]{3,2,1,0:T(8,128)(2,1)S(1)}, bf16[6,16,32,128]{3,2,1,0:T(8,128)(2,1)S(1)}, u32[]{:S(2)}, u32[]{:S(2)}) %collective-permute-start.7) | collective-permute-done | bytes 786464 | tf_op jit(solution)/shard_map/ppermute | solution.py:229
  75.5 1.6 %collective-permute-start.8 = (bf16[6,16,32,128]{3,2,1,0:T(8,128)(2,1)}, bf16[6,16,32,128]{3,2,1,0:T(8,128)(2,1)}, u32[]{:S(2)}, u32[]{:S(2)}) collective-permute-start(bf16[6,16,32,128]{3,2,1,0:T(8,128)(2,1)} %collective-permute-done.6), channel_id=1, source_target_pairs={{0,4},{4,8},{8,12},{16,20},{20,24},{24,28}} | collective-permute-start | bytes 2359304 | tf_op jit(solution)/shard_map/ppermute | solution.py:250
  77.1 1.9 %collective-permute-start.10 = (bf16[12,16,32,128]{3,2,1,0:T(8,128)(2,1)}, bf16[12,16,32,128]{3,2,1,0:T(8,128)(2,1)}, u32[]{:S(2)}, u32[]{:S(2)}) collective-permute-start(bf16[12,16,32,128]{3,2,1,0:T(8,128)(2,1)} %pad_maximum_fusion), channel_id=1, source_target_pairs={{0,1},{1,2},{2,3},{3,4},{4,5},{5,6},{6,7},{7,8},{8,9},{9,10},{10,1... | collective-permute-start | bytes 4718600 | tf_op jit(solution)/shard_map/ppermute | solution.py:229
  79.1 2.4 %collective-permute-start.11 = (bf16[12,16,32,128]{3,2,1,0:T(8,128)(2,1)}, bf16[12,16,32,128]{3,2,1,0:T(8,128)(2,1)}, u32[]{:S(2)}, u32[]{:S(2)}) collective-permute-start(bf16[12,16,32,128]{3,2,1,0:T(8,128)(2,1)} %pad_maximum_fusion.1), channel_id=1, source_target_pairs={{1,0},{2,1},{3,2},{4,3},{5,4},{6,5},{7,6},{8,7},{9,8},{10,9},{11,1... | collective-permute-start | bytes 4718600 | tf_op jit(solution)/shard_map/ppermute | solution.py:229
  81.5 0.0 collective-permute-done.5
  81.5 1.6 %collective-permute-start.9 = (bf16[6,16,32,128]{3,2,1,0:T(8,128)(2,1)S(1)}, bf16[6,16,32,128]{3,2,1,0:T(8,128)(2,1)}, u32[]{:S(2)}, u32[]{:S(2)}) collective-permute-start(bf16[6,16,32,128]{3,2,1,0:T(8,128)(2,1)S(1)} %collective-permute-done.7), channel_id=1, source_target_pairs={{7,3},{11,7},{15,11},{23,19},{27,23},{31,27}} | collective-permute-start | bytes 2359304 | tf_op jit(solution)/shard_map/ppermute | solution.py:250
  83.0 3.3 %broadcast_select_fusion.refs_1_.refs_3_ = bf16[12,16,32,128]{3,2,1,0:T(8,128)(2,1)} fusion(bf16[12,16,32,128]{3,2,1,0:T(8,128)(2,1)} %collective-permute-done.5, bf16[12,16,32,128]{3,2,1,0:T(8,128)(2,1)} %constant_dynamic-update-slice_fusion.2, pred[12]{0:T(512)(128)(4,1)S(1)} %concatenate.52), kind=kLoop, calls=%fused_computation.2 | loop fusion | flops 786432 | bytes 4718604 | tf_op jit(solution)/shard_map/jit(_where)/select_n | solution.py:260
  86.4 0.0 collective-permute-done.4
  86.4 3.1 %collective-permute-start.12 = (bf16[2,16,32,128]{3,2,1,0:T(8,128)(2,1)}, bf16[2,16,32,128]{3,2,1,0:T(8,128)(2,1)S(1)}, u32[]{:S(2)}, u32[]{:S(2)}) collective-permute-start(bf16[2,16,32,128]{3,2,1,0:T(8,128)(2,1)} %pad_maximum_fusion.8), channel_id=1, source_target_pairs={{0,1},{1,2},{2,3},{3,4},{4,5},{5,6},{6,7},{7,8},{8,9},{9,10},{10,1... | collective-permute-start | bytes 786440 | tf_op jit(solution)/shard_map/ppermute | solution.py:229
  89.5 3.3 %broadcast_select_fusion.1.refs_0_.refs_2_ = bf16[12,16,32,128]{3,2,1,0:T(8,128)(2,1)} fusion(bf16[12,16,32,128]{3,2,1,0:T(8,128)(2,1)} %collective-permute-done.4, bf16[12,16,32,128]{3,2,1,0:T(8,128)(2,1)} %constant_dynamic-update-slice_fusion, pred[12]{0:T(512)(128)(4,1)S(1)} %concatenate.42), kind=kLoop, calls=%fused_computation.3 | loop fusion | flops 786432 | bytes 4718604 | tf_op jit(solution)/shard_map/jit(_where)/select_n | solution.py:260
  92.8 2.6 %rim.1 = (f32[2,32,128]{2,1,0:T(8,128)}, f32[2,32,128]{2,1,0:T(8,128)}) custom-call(bf16[12,16,32,128]{3,2,1,0:T(8,128)(2,1)} %broadcast_select_fusion.1.refs_0_.refs_2_, bf16[12,16,32,128]{3,2,1,0:T(8,128)(2,1)} %broadcast_select_fusion.refs_1_.refs_3_), custom_call_target="tpu_custom_call" | custom-call | flops 104857600 | bytes 1572864 | tf_op jit(solution)/shard_map/rim/pallas_call | solution.py:282
  95.4 0.0 collective-permute-done.8
  95.4 2.0 %collective-permute-start.13 = (bf16[2,16,32,128]{3,2,1,0:T(8,128)(2,1)S(1)}, bf16[2,16,32,128]{3,2,1,0:T(8,128)(2,1)S(1)}, u32[]{:S(2)}, u32[]{:S(2)}) collective-permute-start(bf16[2,16,32,128]{3,2,1,0:T(8,128)(2,1)S(1)} %pad_maximum_fusion.9), channel_id=1, source_target_pairs={{1,0},{2,1},{3,2},{4,3},{5,4},{6,5},{7,6},{8,7},{9,8},{10,9},{11,1... | collective-permute-start | bytes 786440 | tf_op jit(solution)/shard_map/ppermute | solution.py:229
  97.4 1.3 %broadcast_select_fusion.3.refs_4_ = bf16[6,16,32,128]{3,2,1,0:T(8,128)(2,1)S(1)} fusion(bf16[6,16,32,128]{3,2,1,0:T(8,128)(2,1)} %collective-permute-done.8, bf16[6,16,32,128]{3,2,1,0:T(8,128)(2,1)} %collective-permute-done.6, pred[]{:T(512)S(6)} %or.34), kind=kLoop, calls=%fused_computation.11 | loop fusion | flops 393216 | bytes 2359297 | tf_op jit(solution)/shard_map/jit(_where)/select_n | solution.py:260
  98.8 0.0 collective-permute-done.9
  98.8 3.8 %collective-permute-start.14 = (f32[2,32,128]{2,1,0:T(8,128)S(1)}, f32[2,32,128]{2,1,0:T(8,128)S(1)}, u32[]{:S(2)}, u32[]{:S(2)}) collective-permute-start(f32[2,32,128]{2,1,0:T(8,128)S(1)} %copy-done.9), channel_id=1, source_target_pairs={{0,1},{1,2},{2,3},{3,4},{4,5},{5,6},{6,7},{7,8},{8,9},{9,10},{10,1... | collective-permute-start | bytes 98312 | tf_op jit(solution)/shard_map/ppermute | solution.py:293
  102.6 0.1 broadcast_select_fusion.2.refs_5_
  102.7 0.0 copy-start.4
  102.7 1.4 %copy-done.4 = bf16[12,16,32,128]{3,2,1,0:T(8,128)(2,1)S(1)} copy-done((bf16[12,16,32,128]{3,2,1,0:T(8,128)(2,1)S(1)}, bf16[12,16,32,128]{3,2,1,0:T(8,128)(2,1)}, u32[]{:S(2)}) %copy-start.4) | copy-done | bytes 1572888
  104.1 5.3 %lags_0.1.refs_6_ = f32[33,16,4096]{2,1,0:T(8,128)} custom-call(bf16[16,16,32,128]{3,2,1,0:T(8,128)(2,1)S(1)} %copy-done, bf16[16,16,32,128]{3,2,1,0:T(8,128)(2,1)S(1)} %copy-done.2, bf16[12,16,32,128]{3,2,1,0:T(8,128)(2,1)S(1)} %copy-done.4, bf16[12,16,32,128]{3,2,1,0:T(8,128)(2,1)S(1)} %copy-done.3), custom_call_target="tpu_custom_call" | custom-call | flops 4246732800 | bytes 9699328 | tf_op jit(solution)/shard_map/lags_0/pallas_call | solution.py:310
  109.4 3.8 %lags_1.1.refs_8_ = f32[33,16,4096]{2,1,0:T(8,128)} custom-call(bf16[16,16,32,128]{3,2,1,0:T(8,128)(2,1)S(1)} %copy-done, bf16[16,16,32,128]{3,2,1,0:T(8,128)(2,1)S(1)} %copy-done.2, bf16[12,16,32,128]{3,2,1,0:T(8,128)(2,1)S(1)} %copy-done.4, bf16[12,16,32,128]{3,2,1,0:T(8,128)(2,1)S(1)} %copy-done.3, ...), custom_call_target="tpu_custom_call", output_to_operand_aliasing={{}: (6, {})} | custom-call | flops 2831155200 | bytes 10485760 | tf_op jit(solution)/shard_map/lags_1/pallas_call | solution.py:310
  113.2 3.2 %collective-permute-done.10.refs_6_ = bf16[12,16,32,128]{3,2,1,0:T(8,128)(2,1)} collective-permute-done((bf16[12,16,32,128]{3,2,1,0:T(8,128)(2,1)}, bf16[12,16,32,128]{3,2,1,0:T(8,128)(2,1)}, u32[]{:S(2)}, u32[]{:S(2)}) %collective-permute-start.10) | collective-permute-done | bytes 1572896 | tf_op jit(solution)/shard_map/ppermute | solution.py:229
  116.4 2.1 %collective-permute-start.15 = (f32[2,32,128]{2,1,0:T(8,128)S(1)}, f32[2,32,128]{2,1,0:T(8,128)S(1)}, u32[]{:S(2)}, u32[]{:S(2)}) collective-permute-start(f32[2,32,128]{2,1,0:T(8,128)S(1)} %copy-done.8), channel_id=1, source_target_pairs={{1,0},{2,1},{3,2},{4,3},{5,4},{6,5},{7,6},{8,7},{9,8},{10,9},{11,1... | collective-permute-start | bytes 98312 | tf_op jit(solution)/shard_map/ppermute | solution.py:292
  118.5 0.0 collective-permute-done.11.refs_7_
  118.5 8.6 %lags_2.1.refs_12_ = f32[33,16,4096]{2,1,0:T(8,128)} custom-call(bf16[16,16,32,128]{3,2,1,0:T(8,128)(2,1)S(1)} %copy-done, bf16[16,16,32,128]{3,2,1,0:T(8,128)(2,1)S(1)} %copy-done.2, bf16[12,16,32,128]{3,2,1,0:T(8,128)(2,1)S(1)} %copy-done.4, bf16[12,16,32,128]{3,2,1,0:T(8,128)(2,1)S(1)} %copy-done.3, ...), custom_call_target="tpu_custom_call", output_to_operand_aliasing={{}: (8, {})} | custom-call | flops 5662310400 | bytes 15204352 | tf_op jit(solution)/shard_map/lags_2/pallas_call | solution.py:310
  127.1 0.0 collective-permute-done.12.refs_8_
  127.1 0.0 collective-permute-done.13.refs_9_
  127.2 0.0 collective-permute-done.14.refs_10_
  127.2 5.6 %lags_3.1 = f32[33,16,4096]{2,1,0:T(8,128)} custom-call(bf16[16,16,32,128]{3,2,1,0:T(8,128)(2,1)S(1)} %copy-done, bf16[16,16,32,128]{3,2,1,0:T(8,128)(2,1)S(1)} %copy-done.2, bf16[12,16,32,128]{3,2,1,0:T(8,128)(2,1)S(1)} %copy-done.4, bf16[12,16,32,128]{3,2,1,0:T(8,128)(2,1)S(1)} %copy-done.3, ...), custom_call_target="tpu_custom_call", output_to_operand_aliasing={{}: (12, {})} | custom-call | flops 2831155200 | bytes 14155776 | tf_op jit(solution)/shard_map/lags_3/pallas_call | solution.py:310
  (22 shorter events, 0.1 us)
Async XLA Ops:
  3.4 29.2 %collective-permute-start = (bf16[6,2,8,4096]{3,2,1,0:T(8,128)(2,1)}, bf16[6,2,8,4096]{3,2,1,0:T(8,128)(2,1)S(1)}, u32[]{:S(2)}, u32[]{:S(2)}) collective-permute-start(bf16[6,2,8,4096]{3,2,1,0:T(8,128)(2,1)} %pad_maximum_fusion.4), channel_id=1, source_target_pairs={{0,1},{1,2},{2,3},{4,5},{5,6},{6,7},{8,9},{9,10},{10,11},{12,13},{... | collective-permute-start | bytes 2359304 | tf_op jit(solution)/shard_map/ppermute | solution.py:229
  8.1 24.5 %collective-permute-start.1 = (bf16[6,2,8,4096]{3,2,1,0:T(8,128)(2,1)}, bf16[6,2,8,4096]{3,2,1,0:T(8,128)(2,1)}, u32[]{:S(2)}, u32[]{:S(2)}) collective-permute-start(bf16[6,2,8,4096]{3,2,1,0:T(8,128)(2,1)} %pad_maximum_fusion.5), channel_id=1, source_target_pairs={{1,0},{2,1},{3,2},{5,4},{6,5},{7,6},{9,8},{10,9},{11,10},{13,12},{... | collective-permute-start | bytes 2359304 | tf_op jit(solution)/shard_map/ppermute | solution.py:229
  20.8 18.5 %collective-permute-start.2 = (bf16[6,16,32,128]{3,2,1,0:T(8,128)(2,1)}, bf16[6,16,32,128]{3,2,1,0:T(8,128)(2,1)}, u32[]{:S(2)}, u32[]{:S(2)}) collective-permute-start(bf16[6,16,32,128]{3,2,1,0:T(8,128)(2,1)} %pad_maximum_fusion.6), channel_id=1, source_target_pairs={{0,1},{1,2},{2,3},{4,5},{5,6},{6,7},{8,9},{9,10},{10,11},{11,12},{... | collective-permute-start | bytes 2359304 | tf_op jit(solution)/shard_map/ppermute | solution.py:229
  24.4 4.9 %copy-start.1 = (bf16[16,16,32,128]{3,2,1,0:T(8,128)(2,1)S(1)}, bf16[16,16,32,128]{3,2,1,0:T(8,128)(2,1)}, u32[]{:S(2)}) copy-start(bf16[16,16,32,128]{3,2,1,0:T(8,128)(2,1)} %get-tuple-element.24.refs_1_) | copy-start | bytes 6291460
  25.4 13.9 %collective-permute-start.3 = (bf16[6,16,32,128]{3,2,1,0:T(8,128)(2,1)}, bf16[6,16,32,128]{3,2,1,0:T(8,128)(2,1)}, u32[]{:S(2)}, u32[]{:S(2)}) collective-permute-start(bf16[6,16,32,128]{3,2,1,0:T(8,128)(2,1)} %pad_maximum_fusion.7), channel_id=1, source_target_pairs={{1,0},{2,1},{3,2},{4,3},{5,4},{6,5},{7,6},{9,8},{10,9},{11,10},{13... | collective-permute-start | bytes 2359304 | tf_op jit(solution)/shard_map/ppermute | solution.py:229
  27.3 1.9 %copy-start = (bf16[16,16,32,128]{3,2,1,0:T(8,128)(2,1)S(1)}, bf16[16,16,32,128]{3,2,1,0:T(8,128)(2,1)}, u32[]{:S(2)}) copy-start(bf16[16,16,32,128]{3,2,1,0:T(8,128)(2,1)} %get-tuple-element.23.refs_0_) | copy-start | bytes 6291460
  32.6 0.9 copy-start.6
  37.1 6.2 %copy-start.7 = (bf16[6,16,32,128]{3,2,1,0:T(8,128)(2,1)S(1)}, bf16[6,16,32,128]{3,2,1,0:T(8,128)(2,1)}, u32[]{:S(2)}) copy-start(bf16[6,16,32,128]{3,2,1,0:T(8,128)(2,1)} %get-tuple-element.27) | copy-start | bytes 2359300
  41.4 40.1 %collective-permute-start.5 = (bf16[12,16,32,128]{3,2,1,0:T(8,128)(2,1)}, bf16[12,16,32,128]{3,2,1,0:T(8,128)(2,1)}, u32[]{:S(2)}, u32[]{:S(2)}) collective-permute-start(bf16[12,16,32,128]{3,2,1,0:T(8,128)(2,1)} %constant_dynamic-update-slice_fusion.2), channel_id=1, source_target_pairs={{7,3},{11,7},{15,11},{23,19},{27,23},{31,27}} | collective-permute-start | bytes 4718600 | tf_op jit(solution)/shard_map/ppermute | solution.py:250
  43.3 8.6 %copy-start.5 = (bf16[6,16,32,128]{3,2,1,0:T(8,128)(2,1)S(1)}, bf16[6,16,32,128]{3,2,1,0:T(8,128)(2,1)}, u32[]{:S(2)}) copy-start(bf16[6,16,32,128]{3,2,1,0:T(8,128)(2,1)} %pad_maximum_fusion.3) | copy-start | bytes 2359300
  46.3 40.0 %collective-permute-start.4 = (bf16[12,16,32,128]{3,2,1,0:T(8,128)(2,1)}, bf16[12,16,32,128]{3,2,1,0:T(8,128)(2,1)}, u32[]{:S(2)}, u32[]{:S(2)}) collective-permute-start(bf16[12,16,32,128]{3,2,1,0:T(8,128)(2,1)} %constant_dynamic-update-slice_fusion), channel_id=1, source_target_pairs={{0,4},{4,8},{8,12},{16,20},{20,24},{24,28}} | collective-permute-start | bytes 4718600 | tf_op jit(solution)/shard_map/ppermute | solution.py:250
  48.1 13.0 %collective-permute-start.6 = (bf16[6,16,32,128]{3,2,1,0:T(8,128)(2,1)}, bf16[6,16,32,128]{3,2,1,0:T(8,128)(2,1)}, u32[]{:S(2)}, u32[]{:S(2)}) collective-permute-start(bf16[6,16,32,128]{3,2,1,0:T(8,128)(2,1)} %pad_maximum_fusion.2), channel_id=1, source_target_pairs={{0,1},{1,2},{2,3},{4,5},{5,6},{6,7},{7,8},{8,9},{9,10},{10,11},{11... | collective-permute-start | bytes 2359304 | tf_op jit(solution)/shard_map/ppermute | solution.py:229
  51.9 23.6 %collective-permute-start.7 = (bf16[6,16,32,128]{3,2,1,0:T(8,128)(2,1)S(1)}, bf16[6,16,32,128]{3,2,1,0:T(8,128)(2,1)S(1)}, u32[]{:S(2)}, u32[]{:S(2)}) collective-permute-start(bf16[6,16,32,128]{3,2,1,0:T(8,128)(2,1)S(1)} %copy-done.5), channel_id=1, source_target_pairs={{1,0},{2,1},{3,2},{4,3},{5,4},{6,5},{7,6},{8,7},{9,8},{10,9},{11,1... | collective-permute-start | bytes 2359304 | tf_op jit(solution)/shard_map/ppermute | solution.py:229
  75.5 19.8 %collective-permute-start.8 = (bf16[6,16,32,128]{3,2,1,0:T(8,128)(2,1)}, bf16[6,16,32,128]{3,2,1,0:T(8,128)(2,1)}, u32[]{:S(2)}, u32[]{:S(2)}) collective-permute-start(bf16[6,16,32,128]{3,2,1,0:T(8,128)(2,1)} %collective-permute-done.6), channel_id=1, source_target_pairs={{0,4},{4,8},{8,12},{16,20},{20,24},{24,28}} | collective-permute-start | bytes 2359304 | tf_op jit(solution)/shard_map/ppermute | solution.py:250
  77.1 39.2 %collective-permute-start.10 = (bf16[12,16,32,128]{3,2,1,0:T(8,128)(2,1)}, bf16[12,16,32,128]{3,2,1,0:T(8,128)(2,1)}, u32[]{:S(2)}, u32[]{:S(2)}) collective-permute-start(bf16[12,16,32,128]{3,2,1,0:T(8,128)(2,1)} %pad_maximum_fusion), channel_id=1, source_target_pairs={{0,1},{1,2},{2,3},{3,4},{4,5},{5,6},{6,7},{7,8},{8,9},{9,10},{10,1... | collective-permute-start | bytes 4718600 | tf_op jit(solution)/shard_map/ppermute | solution.py:229
  79.1 39.4 %collective-permute-start.11 = (bf16[12,16,32,128]{3,2,1,0:T(8,128)(2,1)}, bf16[12,16,32,128]{3,2,1,0:T(8,128)(2,1)}, u32[]{:S(2)}, u32[]{:S(2)}) collective-permute-start(bf16[12,16,32,128]{3,2,1,0:T(8,128)(2,1)} %pad_maximum_fusion.1), channel_id=1, source_target_pairs={{1,0},{2,1},{3,2},{4,3},{5,4},{6,5},{7,6},{8,7},{9,8},{10,9},{11,1... | collective-permute-start | bytes 4718600 | tf_op jit(solution)/shard_map/ppermute | solution.py:229
  81.5 17.3 %collective-permute-start.9 = (bf16[6,16,32,128]{3,2,1,0:T(8,128)(2,1)S(1)}, bf16[6,16,32,128]{3,2,1,0:T(8,128)(2,1)}, u32[]{:S(2)}, u32[]{:S(2)}) collective-permute-start(bf16[6,16,32,128]{3,2,1,0:T(8,128)(2,1)S(1)} %collective-permute-done.7), channel_id=1, source_target_pairs={{7,3},{11,7},{15,11},{23,19},{27,23},{31,27}} | collective-permute-start | bytes 2359304 | tf_op jit(solution)/shard_map/ppermute | solution.py:250
  86.4 40.8 %collective-permute-start.12 = (bf16[2,16,32,128]{3,2,1,0:T(8,128)(2,1)}, bf16[2,16,32,128]{3,2,1,0:T(8,128)(2,1)S(1)}, u32[]{:S(2)}, u32[]{:S(2)}) collective-permute-start(bf16[2,16,32,128]{3,2,1,0:T(8,128)(2,1)} %pad_maximum_fusion.8), channel_id=1, source_target_pairs={{0,1},{1,2},{2,3},{3,4},{4,5},{5,6},{6,7},{7,8},{8,9},{9,10},{10,1... | collective-permute-start | bytes 786440 | tf_op jit(solution)/shard_map/ppermute | solution.py:229
  95.4 3.4 %copy-start.9 = (f32[2,32,128]{2,1,0:T(8,128)S(1)}, f32[2,32,128]{2,1,0:T(8,128)}, u32[]{:S(2)}) copy-start(f32[2,32,128]{2,1,0:T(8,128)} %get-tuple-element.39) | copy-start | bytes 98308
  95.4 31.8 %collective-permute-start.13 = (bf16[2,16,32,128]{3,2,1,0:T(8,128)(2,1)S(1)}, bf16[2,16,32,128]{3,2,1,0:T(8,128)(2,1)S(1)}, u32[]{:S(2)}, u32[]{:S(2)}) collective-permute-start(bf16[2,16,32,128]{3,2,1,0:T(8,128)(2,1)S(1)} %pad_maximum_fusion.9), channel_id=1, source_target_pairs={{1,0},{2,1},{3,2},{4,3},{5,4},{6,5},{7,6},{8,7},{9,8},{10,9},{11,1... | collective-permute-start | bytes 786440 | tf_op jit(solution)/shard_map/ppermute | solution.py:229
  97.4 5.3 %copy-start.3 = (bf16[12,16,32,128]{3,2,1,0:T(8,128)(2,1)S(1)}, bf16[12,16,32,128]{3,2,1,0:T(8,128)(2,1)}, u32[]{:S(2)}) copy-start(bf16[12,16,32,128]{3,2,1,0:T(8,128)(2,1)} %broadcast_select_fusion.refs_1_.refs_3_) | copy-start | bytes 4718596
  98.8 3.9 %copy-start.2 = (bf16[16,16,32,128]{3,2,1,0:T(8,128)(2,1)S(1)}, bf16[16,16,32,128]{3,2,1,0:T(8,128)(2,1)}, u32[]{:S(2)}) copy-start(bf16[16,16,32,128]{3,2,1,0:T(8,128)(2,1)} %get-tuple-element.24.refs_1_) | copy-start | bytes 6291460
  98.8 28.4 %collective-permute-start.14 = (f32[2,32,128]{2,1,0:T(8,128)S(1)}, f32[2,32,128]{2,1,0:T(8,128)S(1)}, u32[]{:S(2)}, u32[]{:S(2)}) collective-permute-start(f32[2,32,128]{2,1,0:T(8,128)S(1)} %copy-done.9), channel_id=1, source_target_pairs={{0,1},{1,2},{2,3},{3,4},{4,5},{5,6},{6,7},{7,8},{8,9},{9,10},{10,1... | collective-permute-start | bytes 98312 | tf_op jit(solution)/shard_map/ppermute | solution.py:293
  102.7 1.4 %copy-start.4 = (bf16[12,16,32,128]{3,2,1,0:T(8,128)(2,1)S(1)}, bf16[12,16,32,128]{3,2,1,0:T(8,128)(2,1)}, u32[]{:S(2)}) copy-start(bf16[12,16,32,128]{3,2,1,0:T(8,128)(2,1)} %broadcast_select_fusion.1.refs_0_.refs_2_) | copy-start | bytes 4718596
  109.4 7.0 %copy-start.8 = (f32[2,32,128]{2,1,0:T(8,128)S(1)}, f32[2,32,128]{2,1,0:T(8,128)}, u32[]{:S(2)}) copy-start(f32[2,32,128]{2,1,0:T(8,128)} %get-tuple-element.40) | copy-start | bytes 98308
  116.4 10.8 %collective-permute-start.15 = (f32[2,32,128]{2,1,0:T(8,128)S(1)}, f32[2,32,128]{2,1,0:T(8,128)S(1)}, u32[]{:S(2)}, u32[]{:S(2)}) collective-permute-start(f32[2,32,128]{2,1,0:T(8,128)S(1)} %copy-done.8), channel_id=1, source_target_pairs={{1,0},{2,1},{3,2},{4,3},{5,4},{6,5},{7,6},{8,7},{9,8},{10,9},{11,1... | collective-permute-start | bytes 98312 | tf_op jit(solution)/shard_map/ppermute | solution.py:292

commit v4 on v0

v4 whole, which is shorter than its diff:
```python
import functools

import jax
import jax.numpy as jnp
from jax import lax
from jax.experimental import pallas as pl
from jax.experimental.pallas import tpu as pltpu
from jax.sharding import PartitionSpec as P

Z = 64
HALF = 16
LAGS = 33
BLOCK = 3
LANES = 128
SUB = 16
SPAN = 3
RATE = 50

CHUNKS = ((16, 2, 1), (5, 4, 3), (8, 7, 6), (15, 14, 13, 12, 11, 10, 9))
BUNDLES = ((0, 1), (2,))
NEAR = ((1, (5, 4, 6)), (2, (3, 7)))
FAR = (2, 8, 1, 9, 0, 10)

VMEM = pl.BlockSpec(memory_space=pltpu.VMEM)
ANY = pl.BlockSpec(memory_space=pl.ANY)


SMEM = pl.BlockSpec(memory_space=pltpu.SMEM)


def pack_kernel(core_ref, s_ref, r_ref, out_ref, flip):
    _, parts, freqs, width = s_ref.shape
    for field, src in enumerate((s_ref, r_ref)):
        for p in range(parts):
            for g in range(width // (SUB * LANES)):
                slot = flip.at[(field * parts + p) * 2 + g % 2]
                for t in range(SUB):
                    c = (g * SUB + t) * LANES
                    slot[pl.ds(t, freqs, SUB), :] = src[0, p, :, c : c + LANES].astype(jnp.float32)
                for f in range(freqs):
                    out_ref[0, field, p * freqs + f, g * SUB : (g + 1) * SUB] = slot[
                        f * SUB : (f + 1) * SUB
                    ].astype(jnp.bfloat16)


def pack(core, forward_field, adjoint_field):
    cells, parts, freqs, width = forward_field.shape
    spec = pl.BlockSpec(
        (1, parts, freqs, width),
        lambda i, core: (jnp.where(core[0] == 1, i, cells - 1 - i), 0, 0, 0),
    )
    tiles = width // LANES
    return pl.pallas_call(
        pack_kernel,
        grid_spec=pltpu.PrefetchScalarGridSpec(
            num_scalar_prefetch=1,
            grid=(cells,),
            in_specs=[spec, spec],
            out_specs=pl.BlockSpec(
                (1, 2, parts * freqs, tiles, LANES), lambda i, core: (i, 0, 0, 0, 0)
            ),
            scratch_shapes=[pltpu.VMEM((4 * parts, SUB * freqs, LANES), jnp.float32)],
        ),
        out_shape=jax.ShapeDtypeStruct((cells, 2, parts * freqs, tiles, LANES), jnp.bfloat16),
        cost_estimate=pl.CostEstimate(
            flops=0, bytes_accessed=8 * cells * parts * freqs * width, transcendentals=0
        ),
        name="pack",
    )(core, forward_field, adjoint_field)


def rim_kernel(cells, where, *refs):
    ins, (lo_ref, hi_ref) = refs[:-2], refs[-2:]

    def tile(g, _):
        at = pl.ds(pl.multiple_of(g * SUB, SUB), SUB)

        def dot(a, b):
            (s_in, s), (r_in, r) = where[a], where[b]
            total = jnp.zeros((SUB, LANES), jnp.float32)
            for k in range(ins[0].shape[2]):
                total += ins[s_in][s, 0, k, at].astype(jnp.float32) * ins[r_in][
                    r, 1, k, at
                ].astype(jnp.float32)
            return total

        for ref, x in ((lo_ref, 0), (hi_ref, cells - 1)):
            ref[0, at] = dot(x - HALF, x + HALF)
            ref[1, at] = dot(x + HALF, x - HALF)
        return 0

    lax.fori_loop(0, ins[0].shape[3] // SUB, tile, 0)


def sum_pairs(ins, where, lags, pairs, k_count, at, init):
    pairs = sorted(pairs, key=lambda p: (p[1] // SPAN, p[1] - lags[p[0]], p[1]))

    def step(k, accs):
        got = {}

        def row(field, a):
            if (field, a) not in got:
                n_in, src = where[a]
                got[field, a] = ins[n_in][src, field, k, at].astype(jnp.float32)
            return got[field, a]

        return tuple(
            acc + row(0, x - lags[t]) * row(1, x + lags[t]) for acc, (t, x) in zip(accs, pairs)
        )

    accs = lax.fori_loop(0, k_count, step, tuple(init(*p) for p in pairs), unroll=k_count)
    return zip(pairs, accs)


def blocks_of(cells, lags, keep):
    spans = []
    for x0 in range(-1, cells + 1, SPAN):
        pairs = [
            (t, x)
            for t in range(BLOCK)
            for x in range(x0, x0 + SPAN)
            if (abs(lags[t]) < HALF or 0 <= x < cells) and keep(x - lags[t], x + lags[t])
        ]
        if spans and len(spans[-1]) + len(pairs) <= BLOCK * SPAN:
            spans[-1] += pairs
        elif pairs:
            spans.append(pairs)
    return spans


def part_kernel(cells, blocks, where, *refs):
    ins, out_ref = refs[:-1], refs[-1]
    terms, tiles = ins[0].shape[2], ins[0].shape[3]
    zero = jnp.zeros((SUB, LANES), jnp.float32)

    def tile(g, _):
        at = pl.ds(pl.multiple_of(g * SUB, SUB), SUB)
        for n, blk in enumerate(blocks):
            lags = [blk * BLOCK + t - HALF for t in range(BLOCK)]
            for pairs in blocks_of(cells, lags, lambda a, b: a in where and b in where):
                for (t, x), acc in sum_pairs(
                    ins, where, lags, pairs, terms, at, lambda t, x: zero
                ):
                    out_ref[n, t, x + 1, at] = acc
        return 0

    lax.fori_loop(0, tiles // SUB, tile, 0)


def lag_kernel(cells, blocks, where, early, aliased, *refs):
    refs = list(refs)
    core = refs.pop(0)[0]
    ins = [refs.pop(0) for _ in range(1 + max(w[0] for w in where.values()))]
    if early is not None:
        partial = refs.pop(0)
        rims = [refs.pop(0) for _ in range(2)]
    if aliased:
        refs.pop(0)
    out_ref, sums, flip, ready, sems = refs
    terms, tiles = ins[0].shape[2], ins[0].shape[3]
    lane = lax.broadcasted_iota(jnp.int32, (SUB, LANES), 1) % Z
    first = lane == 0
    last = lane == Z - 1
    zero = jnp.zeros((SUB, LANES), jnp.float32)
    straight = core == 1

    def copies(n, g):
        cols = pl.ds(pl.multiple_of(g * (SUB * LANES), SUB * LANES), SUB * LANES)
        low = jnp.where(straight, blocks[n] * BLOCK, LAGS - (blocks[n] + 1) * BLOCK)
        return pltpu.make_async_copy(
            ready.at[n, g], out_ref.at[pl.ds(low, BLOCK), :, cols], sems.at[n, g]
        )

    def keep(a, b):
        return early is None or a not in early or b not in early

    def tile(g, _):
        at = pl.ds(pl.multiple_of(g * SUB, SUB), SUB)
        for n, blk in enumerate(blocks):
            lags = [blk * BLOCK + t - HALF for t in range(BLOCK)]
            new = set()

            def init(t, x):
                return zero

            for pairs in blocks_of(cells, lags, keep):
                new |= set(pairs)
                for (t, x), acc in sum_pairs(ins, where, lags, pairs, terms, at, init):
                    sums[t, x + 1] = acc

            def value(t, x):
                if abs(lags[t]) == HALF and not 0 <= x < cells:
                    return rims[int(x > 0)][int(lags[t] > 0), at]
                if (t, x) in new:
                    return sums[t, x + 1]
                return partial[n, t, x + 1, at]

            for t in range(BLOCK):
                for x in range(cells):
                    mid = value(t, x)
                    down = jnp.where(first, 0.0, pltpu.roll(mid, 1, 1))
                    up = jnp.where(last, 0.0, pltpu.roll(mid, LANES - 1, 1))
                    around = (value(t, x - 1) + value(t, x + 1)) + (down + up)
                    to = jnp.where(straight, x, cells - 1 - x)
                    flip[t, pl.ds(to, SUB, cells), :] = 0.25 * (around - 4.0 * mid)
                lag = jnp.where(straight, t, BLOCK - 1 - t)
                for c in range(SUB):
                    ready[n, g, lag, :, c * LANES : (c + 1) * LANES] = flip[
                        t, c * cells : (c + 1) * cells
                    ]
            copies(n, g).start()
        return 0

    groups = tiles // SUB
    lax.fori_loop(0, groups, tile, 0)
    for n in range(len(blocks)):
        for g in range(groups):
            copies(n, g).wait()


def exchange(peers):
    up = [(i, i + 1) for i in range(1, peers - 1, 2)]
    return up, [(j, i) for i, j in up]


def routes(peers, chunk):
    up, down = exchange(peers)
    if peers != 16 or chunk > 2:
        return up + down, ()
    steps = peers // 4
    far_up = range(0, steps - 1 - chunk)
    far_down = range(chunk, steps - 1)
    up = [p for p in up if p not in [(4 * z + 3, 4 * z + 4) for z in far_up]]
    up += [(4 * z + 3, 4 * z) for z in far_up]
    down = [p for p in down if p not in [(4 * z + 4, 4 * z + 3) for z in far_down]]
    down += [(4 * z + 4, 4 * z + 7) for z in far_down]
    swap = {4 * z for z in far_up} | {4 * z + 4 for z in far_up}
    swap |= {4 * z + 7 for z in far_down} | {4 * z + 3 for z in far_down}
    return up + down, sorted(swap)


def is_one_of(me, devices):
    found = jnp.bool_(False)
    for d in devices:
        found |= me == d
    return found


def on_device(forward_field, adjoint_field):
    cells, parts, freqs, width = forward_field.shape
    terms, tiles = parts * freqs, width // LANES
    peers = lax.axis_size("gx")
    me = lax.axis_index("gx")
    core = (me % 2).astype(jnp.int32).reshape(1)
    cores = [(i, i + 1) for i in range(0, peers, 2)] + [(i + 1, i) for i in range(0, peers, 2)]
    links = sum(exchange(peers), [])
    row_bytes = 2 * terms * width * 2

    own = pack(core, forward_field, adjoint_field)
    arrived = []
    for g, chunk in enumerate(CHUNKS):
        spans = []
        for i in chunk:
            r = cells - i
            if spans and spans[-1][1] == r:
                spans[-1][1] = r + 1
            else:
                spans.append([r, r + 1])
        sent = jnp.concatenate([lax.slice_in_dim(own, a, b, axis=0) for a, b in spans], axis=0)
        arrived.append(lax.ppermute(sent, "gx", routes(peers, g)[0]))
    beside = lax.ppermute(own, "gx", cores)

    pieces = []
    for bundle in BUNDLES:
        got = jnp.concatenate([arrived[g] for g in bundle], axis=0) if len(bundle) > 1 else arrived[bundle[0]]
        if peers == 16:
            steps = peers // 4
            hop = [(4 * z, 4 * z + 4) for z in range(steps - 1)]
            hop += [(4 * z + 7, 4 * z + 3) for z in range(steps - 1)]
            relayed = lax.ppermute(got, "gx", hop)
            swapped = jnp.concatenate(
                [
                    jnp.broadcast_to(is_one_of(me, routes(peers, g)[1]), (len(CHUNKS[g]),))
                    for g in bundle
                ]
            )
            got = jnp.where(swapped[:, None, None, None, None], relayed, got)
        pieces.append((bundle, got))
    for g in range(1 + BUNDLES[-1][-1], len(CHUNKS)):
        pieces.append(((g,), arrived[g]))

    def layout(count):
        operands = [own, beside]
        where = {a: (0, a) for a in range(cells)}
        where.update({-1 - a: (1, a) for a in range(cells)})
        for bundle, got in pieces[:count]:
            order = [i for g in bundle for i in CHUNKS[g]]
            where.update({cells - 1 + i: (len(operands), k) for k, i in enumerate(order)})
            operands.append(got)
        return operands, where

    operands, where = layout(1)
    lo, hi = pl.pallas_call(
        functools.partial(rim_kernel, cells, where),
        in_specs=[VMEM] * len(operands),
        out_specs=[VMEM, VMEM],
        out_shape=[jax.ShapeDtypeStruct((2, tiles, LANES), jnp.float32)] * 2,
        cost_estimate=pl.CostEstimate(
            flops=RATE * 8 * terms * width, bytes_accessed=6 * row_bytes, transcendentals=0
        ),
        name="rim",
    )(*operands)
    rim_lo = lax.ppermute(lo, "gx", cores)
    rim_hi = lax.ppermute(hi, "gx", links)

    def cost(operands, nblk, share):
        return pl.CostEstimate(
            flops=int(share * RATE * 2 * 3 * nblk * (cells + 2) * terms * width),
            bytes_accessed=3 * nblk * cells * width * 4
            + sum(o.shape[0] for o in operands) * row_bytes,
            transcendentals=0,
        )

    groups = tiles // SUB

    def lags(name, image, blocks, operands, where, early, extra):
        specs = [SMEM] + [VMEM] * (len(operands) + len(extra))
        operands = [core] + operands + extra
        aliases = {}
        if image is not None:
            aliases = {len(operands): 0}
            operands.append(image)
            specs.append(ANY)
        nblk = len(blocks)
        return pl.pallas_call(
            functools.partial(lag_kernel, cells, blocks, where, early, image is not None),
            in_specs=specs,
            out_specs=ANY,
            out_shape=jax.ShapeDtypeStruct((LAGS, cells, width), jnp.float32),
            scratch_shapes=[
                pltpu.VMEM((BLOCK, cells + 2, SUB, LANES), jnp.float32),
                pltpu.VMEM((BLOCK, SUB * cells, LANES), jnp.float32),
                pltpu.VMEM((nblk, groups, BLOCK, cells, SUB * LANES), jnp.float32),
                pltpu.SemaphoreType.DMA((nblk, groups)),
            ],
            input_output_aliases=aliases,
            compiler_params=pltpu.CompilerParams(vmem_limit_bytes=36 * 2**20),
            cost_estimate=cost(operands[1 : 1 + max(w[0] for w in where.values())], nblk, 1.0 if early is None else 0.5),
            name=name,
        )(*operands)

    image = None
    for stage, (count, blocks) in enumerate(NEAR):
        operands, where = layout(count)
        image = lags("lags_%d" % stage, image, blocks, operands, where, None, [])
    operands, early = layout(len(pieces) - 1)
    partial = pl.pallas_call(
        functools.partial(part_kernel, cells, FAR, early),
        in_specs=[VMEM] * len(operands),
        out_specs=VMEM,
        out_shape=jax.ShapeDtypeStruct((len(FAR), BLOCK, cells + 2, tiles, LANES), jnp.float32),
        compiler_params=pltpu.CompilerParams(vmem_limit_bytes=36 * 2**20),
        cost_estimate=cost(operands, len(FAR), 0.7),
        name="partial",
    )(*operands)
    operands, where = layout(len(pieces))
    return lags("lags_far", image, FAR, operands, where, set(early), [partial, rim_lo, rim_hi])


def solution(mesh):
    placed = (P(("shots", "gx"), None, None, None), P(("shots", "gx"), None, None, None))
    return jax.shard_map(
        on_device,
        mesh=mesh,
        in_specs=placed,
        out_specs=P(None, ("shots", "gx"), None),
        check_vma=False,
    )
```

time: 459 us -> 131 us (0.29)
  other arithmetic: 151 us -> 2.94 us
  loops' own time: 105 us -> 0 us
  local copies, waits for them, and re-layouts: 97.5 us -> 14.1 us
  waiting for transfers between devices: 89.7 us -> 28.2 us
  Pallas kernels: 0 us -> 43.8 us
  starting transfers between devices: 12.1 us -> 41 us
    reduce_sum x33 -> x0, other arithmetic: 110 us -> none  [per_offset(): return jnp.sum(source_part * receiver_part, axis=(1, 2))]
    another operation x1 -> x0, loops' own time: 105 us -> none  [correlate(): return lax.map(per_offset, jnp.arange(LAGS, dtype=jnp.int32))]
    ppermute x4 -> x9, waiting for transfers between devices: 89.7 us -> 28.2 us  [the longest x4 28.2 us: on_device(): arrived.append(lax.ppermute(sent, 'gx', routes(peers, g)[0]))]
    pallas_call x0 -> x6, Pallas kernels: none -> 43.8 us  [the longest x3 21.4 us: lags(): pl.pallas_call(functools.partial(lag_kernel, cells, blocks, where, early,...]
    reshape x2 -> x0, local copies, waits for them, and re-layouts: 29.9 us -> none  [the longest x1 15.2 us: laplace(): along_depth = (deeper[..., 2:] + deeper[..., :-2]).reshape(middle.shape)]
    ppermute x4 -> x9, starting transfers between devices: 12.1 us -> 41 us  [the longest x1 20.9 us: on_device(): rim_lo = lax.ppermute(lo, 'gx', cores)]
    dynamic_update_slice x33 -> x0, local copies, waits for them, and re-layouts: 24 us -> none  [correlate(): return lax.map(per_offset, jnp.arange(LAGS, dtype=jnp.int32))]
    dynamic_slice x33 -> x0, local copies, waits for them, and re-layouts: 19.9 us -> none  [correlate(): return lax.map(per_offset, jnp.arange(LAGS, dtype=jnp.int32))]
  transfers between devices with their start and end apart: 4 -> 9, of which waited for: 2 -> 3; matrix products, arithmetic and copies ran while one was open for 6% -> 8% of each run, Pallas kernels for 0% -> 19%
where the time goes in v4:
time: 131 us; the launch traced here: 130 us
  Pallas kernels  43.8 us (33%)
  starting transfers between devices  41 us (31%)
  waiting for transfers between devices  28.2 us (22%)
  local copies, waits for them, and re-layouts  14.1 us (11%)
  other arithmetic  2.94 us (2%)
    ppermute x4, waiting for transfers between devices, on_device(): arrived.append(lax.ppermute(sent, 'gx', routes(peers, g)[0]))  28.2 us
    pallas_call x3, Pallas kernels, lags(): pl.pallas_call(functools.partial(lag_kernel, cells, blocks, where, early,...  21.4 us
    ppermute x1, starting transfers between devices, on_device(): rim_lo = lax.ppermute(lo, 'gx', cores)  20.9 us
    ppermute x4, starting transfers between devices, on_device(): arrived.append(lax.ppermute(sent, 'gx', routes(peers, g)[0]))  11.7 us
    pallas_call x1, Pallas kernels, pack(): pl.pallas_call(pack_kernel, grid_spec=pltpu.PrefetchScalarGridSpec(num_sc...  11.4 us
    unnamed x11, local copies, waits for them, and re-layouts  7.08 us
    slice x4, local copies, waits for them, and re-layouts, on_device(): lax.slice_in_dim(own, a, b, axis=0)  6.88 us
    pallas_call x1, Pallas kernels, on_device(): pl.pallas_call(functools.partial(part_kernel, cells, FAR, early), in_spec...  6.26 us
  transfers between devices with their start and end apart: 9, of which 3 were waited for; matrix products, arithmetic and copies ran while one was open for 8% of the time, Pallas kernels for 19%

profile of v4, /device:TPU:17, one launch (start us, length us, event | category | flops | bytes accessed | tf_op | source)
XLA Modules:
  0.0 130.2 jit_solution(11262160890914435830)
XLA Ops:
  0.0 11.4 %pack.1.refs_0_.refs_1_ = bf16[16,2,16,32,128]{4,3,2,1,0:T(8,128)(2,1)} custom-call(s32[1]{0:T(128)} %bitcast.core_ref.refs_0_, bf16[16,2,8,4096]{3,2,1,0:T(8,128)(2,1)} %s_ref.1, bf16[16,2,8,4096]{3,2,1,0:T(8,128)(2,1)} %r_ref.1), custom_call_target="tpu_custom_call" | custom-call | bytes 8388608 | tf_op jit(solution)/shard_map/pack/pallas_call | solution.py:53
  11.4 0.7 collective-permute-start
  12.1 1.0 slice.20
  13.0 1.1 slice.21
  14.1 0.1 pad_maximum_fusion
  14.2 3.0 %collective-permute-start.1 = (bf16[3,2,16,32,128]{4,3,2,1,0:T(8,128)(2,1)S(1)}, bf16[3,2,16,32,128]{4,3,2,1,0:T(8,128)(2,1)S(1)}, u32[]{:S(2)}, u32[]{:S(2)}) collective-permute-start(bf16[3,2,16,32,128]{4,3,2,1,0:T(8,128)(2,1)S(1)} %pad_maximum_fusion), channel_id=1, source_target_pairs={{1,2},{5,6},{9,10},{13,14},{3,0},{7,4},{11,8},{2,1},{6,5},{10,9},{... | collective-permute-start | bytes 2359304 | tf_op jit(solution)/shard_map/ppermute | solution.py:270
  17.2 1.6 %fusion = (bf16[3,2,16,32,128]{4,3,2,1,0:T(8,128)(2,1)S(1)}, bf16[3,2,16,32,128]{4,3,2,1,0:T(8,128)(2,1)S(1)}) fusion(bf16[16,2,16,32,128]{4,3,2,1,0:T(8,128)(2,1)} %pack.1.refs_0_.refs_1_), kind=kLoop, calls=%fused_computation.5 | loop fusion | bytes 3145728 | tf_op jit(solution)/shard_map/slice | solution.py:269
  18.9 2.5 %collective-permute-start.2 = (bf16[3,2,16,32,128]{4,3,2,1,0:T(8,128)(2,1)S(1)}, bf16[3,2,16,32,128]{4,3,2,1,0:T(8,128)(2,1)S(1)}, u32[]{:S(2)}, u32[]{:S(2)}) collective-permute-start(bf16[3,2,16,32,128]{4,3,2,1,0:T(8,128)(2,1)S(1)} %get-tuple-element.10), channel_id=1, source_target_pairs={{1,2},{5,6},{9,10},{11,12},{13,14},{3,0},{7,4},{2,1},{4,3},{6,5},{... | collective-permute-start | bytes 2359304 | tf_op jit(solution)/shard_map/ppermute | solution.py:270
  21.4 3.0 %collective-permute-start.4 = (bf16[3,2,16,32,128]{4,3,2,1,0:T(8,128)(2,1)S(1)}, bf16[3,2,16,32,128]{4,3,2,1,0:T(8,128)(2,1)S(1)}, u32[]{:S(2)}, u32[]{:S(2)}) collective-permute-start(bf16[3,2,16,32,128]{4,3,2,1,0:T(8,128)(2,1)S(1)} %get-tuple-element.9), channel_id=1, source_target_pairs={{1,2},{5,6},{7,8},{9,10},{11,12},{13,14},{3,0},{2,1},{4,3},{6,5},{... | collective-permute-start | bytes 2359304 | tf_op jit(solution)/shard_map/ppermute | solution.py:270
  24.5 19.2 %collective-permute-done.1 = bf16[3,2,16,32,128]{4,3,2,1,0:T(8,128)(2,1)S(1)} collective-permute-done((bf16[3,2,16,32,128]{4,3,2,1,0:T(8,128)(2,1)S(1)}, bf16[3,2,16,32,128]{4,3,2,1,0:T(8,128)(2,1)S(1)}, u32[]{:S(2)}, u32[]{:S(2)}) %collective-permute-start.1) | collective-permute-done | bytes 786464 | tf_op jit(solution)/shard_map/ppermute | solution.py:270
  43.7 0.1 constant_dynamic-update-slice_fusion.1
  43.8 8.3 %collective-permute-done.2 = bf16[3,2,16,32,128]{4,3,2,1,0:T(8,128)(2,1)S(1)} collective-permute-done((bf16[3,2,16,32,128]{4,3,2,1,0:T(8,128)(2,1)S(1)}, bf16[3,2,16,32,128]{4,3,2,1,0:T(8,128)(2,1)S(1)}, u32[]{:S(2)}, u32[]{:S(2)}) %collective-permute-start.2) | collective-permute-done | bytes 786464 | tf_op jit(solution)/shard_map/ppermute | solution.py:270
  52.1 0.1 constant_dynamic-update-slice_fusion
  52.2 1.8 %collective-permute-start.3 = (bf16[6,2,16,32,128]{4,3,2,1,0:T(8,128)(2,1)S(1)}, bf16[6,2,16,32,128]{4,3,2,1,0:T(8,128)(2,1)}, u32[]{:S(2)}, u32[]{:S(2)}) collective-permute-start(bf16[6,2,16,32,128]{4,3,2,1,0:T(8,128)(2,1)S(1)} %constant_dynamic-update-slice_fusion), channel_id=1, source_target_pairs={{0,4},{4,8},{8,12},{7,3},{11,7},{15,11},{16,20},{20,24},{24,28},{2... | collective-permute-start | bytes 4718600 | tf_op jit(solution)/shard_map/ppermute | solution.py:280
  54.0 3.2 %slice.24 = bf16[7,2,16,32,128]{4,3,2,1,0:T(8,128)(2,1)} slice(bf16[16,2,16,32,128]{4,3,2,1,0:T(8,128)(2,1)} %pack.1.refs_0_.refs_1_), slice={[1:8], [0:2], [0:16], [0:32], [0:128]} | slice | bytes 3670016 | tf_op jit(solution)/shard_map/slice | solution.py:269
  57.2 3.1 %collective-permute-start.6 = (bf16[7,2,16,32,128]{4,3,2,1,0:T(8,128)(2,1)}, bf16[7,2,16,32,128]{4,3,2,1,0:T(8,128)(2,1)}, u32[]{:S(2)}, u32[]{:S(2)}) collective-permute-start(bf16[7,2,16,32,128]{4,3,2,1,0:T(8,128)(2,1)} %slice.24), channel_id=1, source_target_pairs={{1,2},{3,4},{5,6},{7,8},{9,10},{11,12},{13,14},{2,1},{4,3},{6,5},{... | collective-permute-start | bytes 5505032 | tf_op jit(solution)/shard_map/ppermute | solution.py:270
  60.3 0.6 collective-permute-done.4
  60.9 1.6 %collective-permute-start.5 = (bf16[3,2,16,32,128]{4,3,2,1,0:T(8,128)(2,1)S(1)}, bf16[3,2,16,32,128]{4,3,2,1,0:T(8,128)(2,1)}, u32[]{:S(2)}, u32[]{:S(2)}) collective-permute-start(bf16[3,2,16,32,128]{4,3,2,1,0:T(8,128)(2,1)S(1)} %collective-permute-done.4), channel_id=1, source_target_pairs={{0,4},{4,8},{8,12},{7,3},{11,7},{15,11},{16,20},{20,24},{24,28},{2... | collective-permute-start | bytes 2359304 | tf_op jit(solution)/shard_map/ppermute | solution.py:280
  62.5 0.0 collective-permute-done.5
  62.5 0.1 broadcast_select_fusion.1.refs_3_.refs_4_
  62.6 0.0 collective-permute-done.3
  62.6 2.8 %broadcast_select_fusion.refs_2_.refs_3_ = bf16[6,2,16,32,128]{4,3,2,1,0:T(8,128)(2,1)} fusion(bf16[6,2,16,32,128]{4,3,2,1,0:T(8,128)(2,1)} %collective-permute-done.3, bf16[6,2,16,32,128]{4,3,2,1,0:T(8,128)(2,1)S(1)} %constant_dynamic-update-slice_fusion, pred[6]{0:T(512)(128)(4,1)S(1)} %concatenate.9), kind=kLoop, calls=%fused_computation | loop fusion | flops 786432 | bytes 4718598 | tf_op jit(solution)/shard_map/jit(_where)/select_n | solution.py:287
  65.4 0.0 copy-start.2
  65.4 0.0 collective-permute-done.refs_1_.refs_2_
  65.4 4.7 %rim.1 = (f32[2,32,128]{2,1,0:T(8,128)}, f32[2,32,128]{2,1,0:T(8,128)}) custom-call(bf16[16,2,16,32,128]{4,3,2,1,0:T(8,128)(2,1)} %pack.1.refs_0_.refs_1_, bf16[16,2,16,32,128]{4,3,2,1,0:T(8,128)(2,1)} %collective-permute-done.refs_1_.refs_2_, bf16[6,2,16,32,128]{4,3,2,1,0:T(8,128)(2,1)} %broadcast_select_fusion.refs_2_.refs_3_), custom_call_target="tpu_custom_call" | custom-call | flops 26214400 | bytes 1572864 | tf_op jit(solution)/shard_map/rim/pallas_call | solution.py:303
  70.1 20.9 %collective-permute-start.7 = (f32[2,32,128]{2,1,0:T(8,128)}, f32[2,32,128]{2,1,0:T(8,128)S(1)}, u32[]{:S(2)}, u32[]{:S(2)}) collective-permute-start(f32[2,32,128]{2,1,0:T(8,128)} %get-tuple-element.7), channel_id=1, source_target_pairs={{0,1},{2,3},{4,5},{6,7},{8,9},{10,11},{12,13},{14,15},{1,0},{3,2},... | collective-permute-start | bytes 98312 | tf_op jit(solution)/shard_map/ppermute | solution.py:313
  91.0 4.4 %collective-permute-start.8 = (f32[2,32,128]{2,1,0:T(8,128)}, f32[2,32,128]{2,1,0:T(8,128)S(1)}, u32[]{:S(2)}, u32[]{:S(2)}) collective-permute-start(f32[2,32,128]{2,1,0:T(8,128)} %get-tuple-element.8), channel_id=1, source_target_pairs={{1,2},{3,4},{5,6},{7,8},{9,10},{11,12},{13,14},{2,1},{4,3},{6,5},{... | collective-permute-start | bytes 98312 | tf_op jit(solution)/shard_map/ppermute | solution.py:314
  95.4 0.0 copy-done.2
  95.4 0.0 copy-start
  95.4 2.2 %copy-done = bf16[16,2,16,32,128]{4,3,2,1,0:T(8,128)(2,1)S(1)} copy-done((bf16[16,2,16,32,128]{4,3,2,1,0:T(8,128)(2,1)S(1)}, bf16[16,2,16,32,128]{4,3,2,1,0:T(8,128)(2,1)}, u32[]{:S(2)}) %copy-start) | copy-done | bytes 4194328
  97.6 0.0 copy-start.1
  97.6 7.6 %lags_0.1.refs_5_ = f32[33,16,4096]{2,1,0:T(8,128)} custom-call(s32[1]{0:T(128)} %bitcast.core_ref.refs_0_, bf16[16,2,16,32,128]{4,3,2,1,0:T(8,128)(2,1)S(1)} %copy-done, bf16[16,2,16,32,128]{4,3,2,1,0:T(8,128)(2,1)} %collective-permute-done.refs_1_.refs_2_, bf16[6,2,16,32,128]{4,3,2,1,0:T(8,128)(2,1)S(1)} %copy-done.2), custom_call_target="tpu_custom_call" | custom-call | flops 1061683200 | bytes 10747904 | tf_op jit(solution)/shard_map/lags_0/pallas_call | solution.py:335
  105.2 0.0 copy-done.1
  105.2 6.3 %partial.1.refs_6_ = f32[6,3,18,32,128]{4,3,2,1,0:T(8,128)S(1)} custom-call(bf16[16,2,16,32,128]{4,3,2,1,0:T(8,128)(2,1)S(1)} %copy-done.1, bf16[16,2,16,32,128]{4,3,2,1,0:T(8,128)(2,1)} %collective-permute-done.refs_1_.refs_2_, bf16[6,2,16,32,128]{4,3,2,1,0:T(8,128)(2,1)S(1)} %copy-done.2, ...), custom_call_target="tpu_custom_call" | custom-call | flops 1486356480 | bytes 15466496 | tf_op jit(solution)/shard_map/partial/pallas_call | solution.py:357
  111.5 0.0 copy-start.3
  111.5 2.3 %copy-done.3 = f32[6,3,18,32,128]{4,3,2,1,0:T(8,128)} copy-done((f32[6,3,18,32,128]{4,3,2,1,0:T(8,128)}, f32[6,3,18,32,128]{4,3,2,1,0:T(8,128)S(1)}, u32[]{:S(2)}) %copy-start.3) | copy-done | bytes 5308440
  113.8 6.0 %lags_1.1.refs_9_ = f32[33,16,4096]{2,1,0:T(8,128)} custom-call(s32[1]{0:T(128)} %bitcast.core_ref.refs_0_, bf16[16,2,16,32,128]{4,3,2,1,0:T(8,128)(2,1)S(1)} %copy-done.1, bf16[16,2,16,32,128]{4,3,2,1,0:T(8,128)(2,1)} %collective-permute-done.refs_1_.refs_2_, bf16[6,2,16,32,128]{4,3,2,1,0:T(8,128)(2,1)S(1)} %copy-done.2, ...), custom_call_target="tpu_custom_call", output_to_operand_aliasing={{}: (5, {})} | custom-call | flops 707788800 | bytes 11534336 | tf_op jit(solution)/shard_map/lags_1/pallas_call | solution.py:335
  119.8 0.0 collective-permute-done.6.refs_5_
  119.8 0.0 collective-permute-done.7.refs_7_
  119.8 0.0 collective-permute-done.8.refs_8_
  119.9 0.0 copy-start.4
  119.9 2.5 %copy-done.4 = f32[6,3,18,32,128]{4,3,2,1,0:T(8,128)S(1)} copy-done((f32[6,3,18,32,128]{4,3,2,1,0:T(8,128)S(1)}, f32[6,3,18,32,128]{4,3,2,1,0:T(8,128)}, u32[]{:S(2)}) %copy-start.4) | copy-done | bytes 5308440
  122.4 7.8 %lags_far.1 = f32[33,16,4096]{2,1,0:T(8,128)} custom-call(s32[1]{0:T(128)} %bitcast.core_ref.refs_0_, bf16[16,2,16,32,128]{4,3,2,1,0:T(8,128)(2,1)S(1)} %copy-done.1, bf16[16,2,16,32,128]{4,3,2,1,0:T(8,128)(2,1)} %collective-permute-done.refs_1_.refs_2_, bf16[6,2,16,32,128]{4,3,2,1,0:T(8,128)(2,1)S(1)} %copy-done.2, ...), custom_call_target="tpu_custom_call", output_to_operand_aliasing={{}: (9, {})} | custom-call | flops 1061683200 | bytes 15466496 | tf_op jit(solution)/shard_map/lags_far/pallas_call | solution.py:335
  (2 shorter events, 0.0 us)
Async XLA Ops:
  11.4 54.0 %collective-permute-start = (bf16[16,2,16,32,128]{4,3,2,1,0:T(8,128)(2,1)}, bf16[16,2,16,32,128]{4,3,2,1,0:T(8,128)(2,1)}, u32[]{:S(2)}, u32[]{:S(2)}) collective-permute-start(bf16[16,2,16,32,128]{4,3,2,1,0:T(8,128)(2,1)} %pack.1.refs_0_.refs_1_), channel_id=1, source_target_pairs={{0,1},{2,3},{4,5},{6,7},{8,9},{10,11},{12,13},{14,15},{1,0},{3,2},... | collective-permute-start | bytes 12582920 | tf_op jit(solution)/shard_map/ppermute | solution.py:271
  14.2 29.5 %collective-permute-start.1 = (bf16[3,2,16,32,128]{4,3,2,1,0:T(8,128)(2,1)S(1)}, bf16[3,2,16,32,128]{4,3,2,1,0:T(8,128)(2,1)S(1)}, u32[]{:S(2)}, u32[]{:S(2)}) collective-permute-start(bf16[3,2,16,32,128]{4,3,2,1,0:T(8,128)(2,1)S(1)} %pad_maximum_fusion), channel_id=1, source_target_pairs={{1,2},{5,6},{9,10},{13,14},{3,0},{7,4},{11,8},{2,1},{6,5},{10,9},{... | collective-permute-start | bytes 2359304 | tf_op jit(solution)/shard_map/ppermute | solution.py:270
  18.9 33.2 %collective-permute-start.2 = (bf16[3,2,16,32,128]{4,3,2,1,0:T(8,128)(2,1)S(1)}, bf16[3,2,16,32,128]{4,3,2,1,0:T(8,128)(2,1)S(1)}, u32[]{:S(2)}, u32[]{:S(2)}) collective-permute-start(bf16[3,2,16,32,128]{4,3,2,1,0:T(8,128)(2,1)S(1)} %get-tuple-element.10), channel_id=1, source_target_pairs={{1,2},{5,6},{9,10},{11,12},{13,14},{3,0},{7,4},{2,1},{4,3},{6,5},{... | collective-permute-start | bytes 2359304 | tf_op jit(solution)/shard_map/ppermute | solution.py:270
  21.4 39.5 %collective-permute-start.4 = (bf16[3,2,16,32,128]{4,3,2,1,0:T(8,128)(2,1)S(1)}, bf16[3,2,16,32,128]{4,3,2,1,0:T(8,128)(2,1)S(1)}, u32[]{:S(2)}, u32[]{:S(2)}) collective-permute-start(bf16[3,2,16,32,128]{4,3,2,1,0:T(8,128)(2,1)S(1)} %get-tuple-element.9), channel_id=1, source_target_pairs={{1,2},{5,6},{7,8},{9,10},{11,12},{13,14},{3,0},{2,1},{4,3},{6,5},{... | collective-permute-start | bytes 2359304 | tf_op jit(solution)/shard_map/ppermute | solution.py:270
  52.2 10.4 %collective-permute-start.3 = (bf16[6,2,16,32,128]{4,3,2,1,0:T(8,128)(2,1)S(1)}, bf16[6,2,16,32,128]{4,3,2,1,0:T(8,128)(2,1)}, u32[]{:S(2)}, u32[]{:S(2)}) collective-permute-start(bf16[6,2,16,32,128]{4,3,2,1,0:T(8,128)(2,1)S(1)} %constant_dynamic-update-slice_fusion), channel_id=1, source_target_pairs={{0,4},{4,8},{8,12},{7,3},{11,7},{15,11},{16,20},{20,24},{24,28},{2... | collective-permute-start | bytes 4718600 | tf_op jit(solution)/shard_map/ppermute | solution.py:280
  57.2 62.6 %collective-permute-start.6 = (bf16[7,2,16,32,128]{4,3,2,1,0:T(8,128)(2,1)}, bf16[7,2,16,32,128]{4,3,2,1,0:T(8,128)(2,1)}, u32[]{:S(2)}, u32[]{:S(2)}) collective-permute-start(bf16[7,2,16,32,128]{4,3,2,1,0:T(8,128)(2,1)} %slice.24), channel_id=1, source_target_pairs={{1,2},{3,4},{5,6},{7,8},{9,10},{11,12},{13,14},{2,1},{4,3},{6,5},{... | collective-permute-start | bytes 5505032 | tf_op jit(solution)/shard_map/ppermute | solution.py:270
  60.9 1.6 %collective-permute-start.5 = (bf16[3,2,16,32,128]{4,3,2,1,0:T(8,128)(2,1)S(1)}, bf16[3,2,16,32,128]{4,3,2,1,0:T(8,128)(2,1)}, u32[]{:S(2)}, u32[]{:S(2)}) collective-permute-start(bf16[3,2,16,32,128]{4,3,2,1,0:T(8,128)(2,1)S(1)} %collective-permute-done.4), channel_id=1, source_target_pairs={{0,4},{4,8},{8,12},{7,3},{11,7},{15,11},{16,20},{20,24},{24,28},{2... | collective-permute-start | bytes 2359304 | tf_op jit(solution)/shard_map/ppermute | solution.py:280
  65.4 30.0 %copy-start.2 = (bf16[6,2,16,32,128]{4,3,2,1,0:T(8,128)(2,1)S(1)}, bf16[6,2,16,32,128]{4,3,2,1,0:T(8,128)(2,1)}, u32[]{:S(2)}) copy-start(bf16[6,2,16,32,128]{4,3,2,1,0:T(8,128)(2,1)} %broadcast_select_fusion.refs_2_.refs_3_) | copy-start | bytes 4718596
  70.1 49.8 %collective-permute-start.7 = (f32[2,32,128]{2,1,0:T(8,128)}, f32[2,32,128]{2,1,0:T(8,128)S(1)}, u32[]{:S(2)}, u32[]{:S(2)}) collective-permute-start(f32[2,32,128]{2,1,0:T(8,128)} %get-tuple-element.7), channel_id=1, source_target_pairs={{0,1},{2,3},{4,5},{6,7},{8,9},{10,11},{12,13},{14,15},{1,0},{3,2},... | collective-permute-start | bytes 98312 | tf_op jit(solution)/shard_map/ppermute | solution.py:313
  91.0 28.8 %collective-permute-start.8 = (f32[2,32,128]{2,1,0:T(8,128)}, f32[2,32,128]{2,1,0:T(8,128)S(1)}, u32[]{:S(2)}, u32[]{:S(2)}) collective-permute-start(f32[2,32,128]{2,1,0:T(8,128)} %get-tuple-element.8), channel_id=1, source_target_pairs={{1,2},{3,4},{5,6},{7,8},{9,10},{11,12},{13,14},{2,1},{4,3},{6,5},{... | collective-permute-start | bytes 98312 | tf_op jit(solution)/shard_map/ppermute | solution.py:314
  95.4 2.2 %copy-start = (bf16[16,2,16,32,128]{4,3,2,1,0:T(8,128)(2,1)S(1)}, bf16[16,2,16,32,128]{4,3,2,1,0:T(8,128)(2,1)}, u32[]{:S(2)}) copy-start(bf16[16,2,16,32,128]{4,3,2,1,0:T(8,128)(2,1)} %pack.1.refs_0_.refs_1_) | copy-start | bytes 12582916
  97.6 7.6 %copy-start.1 = (bf16[16,2,16,32,128]{4,3,2,1,0:T(8,128)(2,1)S(1)}, bf16[16,2,16,32,128]{4,3,2,1,0:T(8,128)(2,1)}, u32[]{:S(2)}) copy-start(bf16[16,2,16,32,128]{4,3,2,1,0:T(8,128)(2,1)} %pack.1.refs_0_.refs_1_) | copy-start | bytes 12582916
  111.5 2.3 %copy-start.3 = (f32[6,3,18,32,128]{4,3,2,1,0:T(8,128)}, f32[6,3,18,32,128]{4,3,2,1,0:T(8,128)S(1)}, u32[]{:S(2)}) copy-start(f32[6,3,18,32,128]{4,3,2,1,0:T(8,128)S(1)} %partial.1.refs_6_) | copy-start | bytes 15925252
  119.9 2.5 %copy-start.4 = (f32[6,3,18,32,128]{4,3,2,1,0:T(8,128)S(1)}, f32[6,3,18,32,128]{4,3,2,1,0:T(8,128)}, u32[]{:S(2)}) copy-start(f32[6,3,18,32,128]{4,3,2,1,0:T(8,128)} %copy-done.3) | copy-start | bytes 15925252

commit v5 on v4

--- a/solution.py
+++ b/solution.py
@@ -18,8 +18,10 @@
 
 CHUNKS = ((16, 2, 1), (5, 4, 3), (8, 7, 6), (15, 14, 13, 12, 11, 10, 9))
 BUNDLES = ((0, 1), (2,))
-NEAR = ((1, (5, 4, 6)), (2, (3, 7)))
+NEAR = (5, 4, 6, 3, 7)
 FAR = (2, 8, 1, 9, 0, 10)
+ALL = NEAR + FAR
+SCOPED = 14 * 2**20
 
 VMEM = pl.BlockSpec(memory_space=pltpu.VMEM)
 ANY = pl.BlockSpec(memory_space=pl.ANY)
@@ -28,44 +30,86 @@
 SMEM = pl.BlockSpec(memory_space=pltpu.SMEM)
 
 
-def pack_kernel(core_ref, s_ref, r_ref, out_ref, flip):
+def pack_kernel(rows, order_ref, s_ref, r_ref, out_ref, flip):
     _, parts, freqs, width = s_ref.shape
-    for field, src in enumerate((s_ref, r_ref)):
-        for p in range(parts):
-            for g in range(width // (SUB * LANES)):
-                slot = flip.at[(field * parts + p) * 2 + g % 2]
-                for t in range(SUB):
-                    c = (g * SUB + t) * LANES
-                    slot[pl.ds(t, freqs, SUB), :] = src[0, p, :, c : c + LANES].astype(jnp.float32)
-                for f in range(freqs):
-                    out_ref[0, field, p * freqs + f, g * SUB : (g + 1) * SUB] = slot[
-                        f * SUB : (f + 1) * SUB
-                    ].astype(jnp.bfloat16)
-
-
-def pack(core, forward_field, adjoint_field):
-    cells, parts, freqs, width = forward_field.shape
-    spec = pl.BlockSpec(
-        (1, parts, freqs, width),
-        lambda i, core: (jnp.where(core[0] == 1, i, cells - 1 - i), 0, 0, 0),
-    )
+    for row in range(rows):
+        src_row = jnp.where(order_ref[0] == 1, row, rows - 1 - row)
+        for field, src in enumerate((s_ref, r_ref)):
+            for p in range(parts):
+                for g in range(width // (SUB * LANES)):
+                    slot = flip.at[(field * parts + p) * 2 + g % 2]
+                    for t in range(SUB):
+                        c = (g * SUB + t) * LANES
+                        slot[pl.ds(t, freqs, SUB), :] = src[src_row, p, :, c : c + LANES].astype(
+                            jnp.float32
+                        )
+                    for f in range(freqs):
+                        out_ref[row, field, p * freqs + f, g * SUB : (g + 1) * SUB] = slot[
+                            f * SUB : (f + 1) * SUB
+                        ].astype(jnp.bfloat16)
+
+
+def pack(straight, rows, steps, source, receiver, places, weight, name):
+    _, parts, freqs, width = source.shape
     tiles = width // LANES
+
+    def spec(base):
+        return pl.BlockSpec(
+            (rows, parts, freqs, width),
+            lambda i, order: (base + places[2] * jnp.where(order[0] == 1, i, steps - 1 - i), 0, 0, 0),
+        )
+
     return pl.pallas_call(
-        pack_kernel,
+        functools.partial(pack_kernel, rows),
         grid_spec=pltpu.PrefetchScalarGridSpec(
             num_scalar_prefetch=1,
-            grid=(cells,),
-            in_specs=[spec, spec],
+            grid=(steps,),
+            in_specs=[spec(places[0]), spec(places[1])],
             out_specs=pl.BlockSpec(
-                (1, 2, parts * freqs, tiles, LANES), lambda i, core: (i, 0, 0, 0, 0)
+                (rows, 2, parts * freqs, tiles, LANES), lambda i, order: (i, 0, 0, 0, 0)
             ),
             scratch_shapes=[pltpu.VMEM((4 * parts, SUB * freqs, LANES), jnp.float32)],
         ),
-        out_shape=jax.ShapeDtypeStruct((cells, 2, parts * freqs, tiles, LANES), jnp.bfloat16),
+        out_shape=jax.ShapeDtypeStruct(
+            (rows * steps, 2, parts * freqs, tiles, LANES), jnp.bfloat16
+        ),
         cost_estimate=pl.CostEstimate(
-            flops=0, bytes_accessed=8 * cells * parts * freqs * width, transcendentals=0
+            flops=weight * 8 * rows * steps * parts * freqs * width,
+            bytes_accessed=8 * rows * steps * parts * freqs * width,
+            transcendentals=0,
         ),
-        name="pack",
+        name=name,
+    )(straight, source, receiver)
+
+
+def first_kernel(core_ref, s_ref, r_ref, out_ref):
+    out_ref[0, 0] = s_ref[0]
+    out_ref[0, 1] = r_ref[0]
+
+
+def first_rows(core, forward_field, adjoint_field):
+    cells, parts, freqs, width = forward_field.shape
+    rows = [cells - i for i in CHUNKS[0]]
+
+    def at(i, core):
+        row = jnp.int32(rows[0])
+        for k in range(1, len(rows)):
+            row = jnp.where(i == k, rows[k], row)
+        return (jnp.where(core[0] == 1, row, cells - 1 - row), 0, 0, 0)
+
+    spec = pl.BlockSpec((1, parts, freqs, width), at)
+    return pl.pallas_call(
+        first_kernel,
+        grid_spec=pltpu.PrefetchScalarGridSpec(
+            num_scalar_prefetch=1,
+            grid=(len(rows),),
+            in_specs=[spec, spec],
+            out_specs=pl.BlockSpec(
+                (1, 2, parts, freqs, width), lambda i, core: (i, 0, 0, 0, 0)
+            ),
+        ),
+        out_shape=jax.ShapeDtypeStruct((len(rows), 2, parts, freqs, width), jnp.bfloat16),
+        name="first",
     )(core, forward_field, adjoint_field)
 
 
@@ -128,16 +172,19 @@
     return spans
 
 
-def part_kernel(cells, blocks, where, *refs):
+def part_kernel(cells, blocks, where, done, *refs):
     ins, out_ref = refs[:-1], refs[-1]
     terms, tiles = ins[0].shape[2], ins[0].shape[3]
     zero = jnp.zeros((SUB, LANES), jnp.float32)
+
+    def keep(a, b):
+        return a in where and b in where and not (a in done and b in done)
 
     def tile(g, _):
         at = pl.ds(pl.multiple_of(g * SUB, SUB), SUB)
         for n, blk in enumerate(blocks):
             lags = [blk * BLOCK + t - HALF for t in range(BLOCK)]
-            for pairs in blocks_of(cells, lags, lambda a, b: a in where and b in where):
+            for pairs in blocks_of(cells, lags, keep):
                 for (t, x), acc in sum_pairs(
                     ins, where, lags, pairs, terms, at, lambda t, x: zero
                 ):
@@ -147,13 +194,12 @@
     lax.fori_loop(0, tiles // SUB, tile, 0)
 
 
-def lag_kernel(cells, blocks, where, early, aliased, *refs):
+def lag_kernel(cells, blocks, where, stages, rim, aliased, *refs):
     refs = list(refs)
     core = refs.pop(0)[0]
     ins = [refs.pop(0) for _ in range(1 + max(w[0] for w in where.values()))]
-    if early is not None:
-        partial = refs.pop(0)
-        rims = [refs.pop(0) for _ in range(2)]
+    partials = [refs.pop(0) for _ in stages]
+    rims = [refs.pop(0) for _ in range(2)] if rim else None
     if aliased:
         refs.pop(0)
     out_ref, sums, flip, ready, sems = refs
@@ -172,28 +218,25 @@
         )
 
     def keep(a, b):
-        return early is None or a not in early or b not in early
+        return not any(a in rows and b in rows for rows, _ in stages)
 
     def tile(g, _):
         at = pl.ds(pl.multiple_of(g * SUB, SUB), SUB)
         for n, blk in enumerate(blocks):
             lags = [blk * BLOCK + t - HALF for t in range(BLOCK)]
-            new = set()
-
-            def init(t, x):
-                return zero
-
             for pairs in blocks_of(cells, lags, keep):
-                new |= set(pairs)
-                for (t, x), acc in sum_pairs(ins, where, lags, pairs, terms, at, init):
+                for (t, x), acc in sum_pairs(
+                    ins, where, lags, pairs, terms, at, lambda t, x: zero
+                ):
                     sums[t, x + 1] = acc
 
             def value(t, x):
                 if abs(lags[t]) == HALF and not 0 <= x < cells:
                     return rims[int(x > 0)][int(lags[t] > 0), at]
-                if (t, x) in new:
-                    return sums[t, x + 1]
-                return partial[n, t, x + 1, at]
+                for ref, (rows, order) in zip(partials, stages):
+                    if x - lags[t] in rows and x + lags[t] in rows:
+                        return ref[order.index(blk), t, x + 1, at]
+                return sums[t, x + 1]
 
             for t in range(BLOCK):
                 for x in range(cells):
@@ -256,23 +299,86 @@
     links = sum(exchange(peers), [])
     row_bytes = 2 * terms * width * 2
 
-    own = pack(core, forward_field, adjoint_field)
-    arrived = []
-    for g, chunk in enumerate(CHUNKS):
+    def spans_of(rows):
         spans = []
-        for i in chunk:
-            r = cells - i
+        for r in rows:
             if spans and spans[-1][1] == r:
                 spans[-1][1] = r + 1
             else:
                 spans.append([r, r + 1])
-        sent = jnp.concatenate([lax.slice_in_dim(own, a, b, axis=0) for a, b in spans], axis=0)
+        return spans
+
+    def cut(field, rows):
+        return [lax.slice_in_dim(field, a, b, axis=0) for a, b in spans_of(rows)]
+
+    n = len(CHUNKS[0])
+    raw = first_rows(core, forward_field, adjoint_field)
+    raw, forward_field, adjoint_field = lax.optimization_barrier(
+        (raw, forward_field, adjoint_field)
+    )
+    raw = lax.ppermute(raw, "gx", routes(peers, 0)[0]).reshape(2 * n, parts, freqs, width)
+    own = pack(core, 2, cells // 2, forward_field, adjoint_field, (0, 0, 1), RATE, "pack")
+    arrived = [None]
+    for g, chunk in enumerate(CHUNKS[1:], 1):
+        sent = jnp.concatenate(cut(own, [cells - i for i in chunk]), axis=0)
+        if g == 2:
+            sent, raw, swap = lax.optimization_barrier((sent, raw, own))
         arrived.append(lax.ppermute(sent, "gx", routes(peers, g)[0]))
-    beside = lax.ppermute(own, "gx", cores)
+    arrived[0] = pack(jnp.ones_like(core), 1, n, raw, raw, (0, 1, 2), RATE, "pack_first")
+    beside = lax.ppermute(swap, "gx", cores)
 
     pieces = []
+
+    def layout(count):
+        operands = [own, beside]
+        where = {a: (0, a) for a in range(cells)}
+        where.update({-1 - a: (1, a) for a in range(cells)})
+        for bundle, got in pieces[:count]:
+            order = [i for g in bundle for i in CHUNKS[g]]
+            where.update({cells - 1 + i: (len(operands), k) for k, i in enumerate(order)})
+            operands.append(got)
+        return operands, where
+
+    def count(blocks, keep):
+        total = 0
+        for blk in blocks:
+            lags = [blk * BLOCK + t - HALF for t in range(BLOCK)]
+            total += sum(len(pairs) for pairs in blocks_of(cells, lags, keep))
+        return total
+
+    def cost(pairs, lags):
+        return pl.CostEstimate(
+            flops=RATE * (2 * pairs * terms * width + 20 * lags * cells * width),
+            bytes_accessed=lags * cells * width * 4,
+            transcendentals=0,
+        )
+
+    groups = tiles // SUB
+
+    def partial(name, pieces_in, blocks, done):
+        operands, where = layout(pieces_in)
+        pairs = count(
+            blocks, lambda a, b: a in where and b in where and not (a in done and b in done)
+        )
+        out = pl.pallas_call(
+            functools.partial(part_kernel, cells, blocks, where, done),
+            in_specs=[VMEM] * len(operands),
+            out_specs=VMEM,
+            out_shape=jax.ShapeDtypeStruct(
+                (len(blocks), BLOCK, cells + 2, tiles, LANES), jnp.float32
+            ),
+            compiler_params=pltpu.CompilerParams(vmem_limit_bytes=SCOPED),
+            cost_estimate=cost(pairs, 0),
+            name=name,
+        )(*operands)
+        return out, (set(where), blocks)
+
+    inner, inner_stage = partial("inner", 0, ALL, ())
+
     for bundle in BUNDLES:
         got = jnp.concatenate([arrived[g] for g in bundle], axis=0) if len(bundle) > 1 else arrived[bundle[0]]
+        if bundle[0] == 0:
+            got, inner = lax.optimization_barrier((got, inner))
         if peers == 16:
             steps = peers // 4
             hop = [(4 * z, 4 * z + 4) for z in range(steps - 1)]
@@ -289,16 +395,6 @@
     for g in range(1 + BUNDLES[-1][-1], len(CHUNKS)):
         pieces.append(((g,), arrived[g]))
 
-    def layout(count):
-        operands = [own, beside]
-        where = {a: (0, a) for a in range(cells)}
-        where.update({-1 - a: (1, a) for a in range(cells)})
-        for bundle, got in pieces[:count]:
-            order = [i for g in bundle for i in CHUNKS[g]]
-            where.update({cells - 1 + i: (len(operands), k) for k, i in enumerate(order)})
-            operands.append(got)
-        return operands, where
-
     operands, where = layout(1)
     lo, hi = pl.pallas_call(
         functools.partial(rim_kernel, cells, where),
@@ -313,27 +409,23 @@
     rim_lo = lax.ppermute(lo, "gx", cores)
     rim_hi = lax.ppermute(hi, "gx", links)
 
-    def cost(operands, nblk, share):
-        return pl.CostEstimate(
-            flops=int(share * RATE * 2 * 3 * nblk * (cells + 2) * terms * width),
-            bytes_accessed=3 * nblk * cells * width * 4
-            + sum(o.shape[0] for o in operands) * row_bytes,
-            transcendentals=0,
-        )
-
-    groups = tiles // SUB
-
-    def lags(name, image, blocks, operands, where, early, extra):
-        specs = [SMEM] + [VMEM] * (len(operands) + len(extra))
-        operands = [core] + operands + extra
+    def lags(name, image, pieces_in, blocks, partials, stages, rims):
+        operands, where = layout(pieces_in)
+        operands = [core] + operands + partials + rims
+        specs = [SMEM] + [VMEM] * (len(operands) - 1)
         aliases = {}
         if image is not None:
             aliases = {len(operands): 0}
             operands.append(image)
             specs.append(ANY)
         nblk = len(blocks)
+        pairs = count(
+            blocks, lambda a, b: not any(a in rows and b in rows for rows, _ in stages)
+        )
         return pl.pallas_call(
-            functools.partial(lag_kernel, cells, blocks, where, early, image is not None),
+            functools.partial(
+                lag_kernel, cells, blocks, where, stages, bool(rims), image is not None
+            ),
             in_specs=specs,
             out_specs=ANY,
             out_shape=jax.ShapeDtypeStruct((LAGS, cells, width), jnp.float32),
@@ -344,27 +436,22 @@
                 pltpu.SemaphoreType.DMA((nblk, groups)),
             ],
             input_output_aliases=aliases,
-            compiler_params=pltpu.CompilerParams(vmem_limit_bytes=36 * 2**20),
-            cost_estimate=cost(operands[1 : 1 + max(w[0] for w in where.values())], nblk, 1.0 if early is None else 0.5),
+            compiler_params=pltpu.CompilerParams(vmem_limit_bytes=SCOPED),
+            cost_estimate=cost(pairs, BLOCK * nblk),
             name=name,
         )(*operands)
 
-    image = None
-    for stage, (count, blocks) in enumerate(NEAR):
-        operands, where = layout(count)
-        image = lags("lags_%d" % stage, image, blocks, operands, where, None, [])
-    operands, early = layout(len(pieces) - 1)
-    partial = pl.pallas_call(
-        functools.partial(part_kernel, cells, FAR, early),
-        in_specs=[VMEM] * len(operands),
-        out_specs=VMEM,
-        out_shape=jax.ShapeDtypeStruct((len(FAR), BLOCK, cells + 2, tiles, LANES), jnp.float32),
-        compiler_params=pltpu.CompilerParams(vmem_limit_bytes=36 * 2**20),
-        cost_estimate=cost(operands, len(FAR), 0.7),
-        name="partial",
-    )(*operands)
-    operands, where = layout(len(pieces))
-    return lags("lags_far", image, FAR, operands, where, set(early), [partial, rim_lo, rim_hi])
+    image = lags("near", None, len(pieces) - 1, NEAR, [inner], [inner_stage], [])
+    middle, middle_stage = partial("middle", len(pieces) - 1, FAR, inner_stage[0])
+    return lags(
+        "far",
+        image,
+        len(pieces),
+        FAR,
+        [inner, middle],
+        [inner_stage, middle_stage],
+        [rim_lo, rim_hi],
+    )
 
 
 def solution(mesh):

time: 131 us -> 131 us (level)
  waiting for transfers between devices: 28.2 us -> 22.2 us
  starting transfers between devices: 41 us -> 42.7 us
  other arithmetic: 2.94 us -> 4.38 us
    ppermute x4 -> x3, waiting for transfers between devices: 28.2 us -> 13.1 us  [on_device(): arrived.append(lax.ppermute(sent, 'gx', routes(peers, g)[0]))]
    ppermute x1 -> x2, waiting for transfers between devices: 0.01 us -> 9.14 us  [the longest x1 9.13 us: on_device(): lax.ppermute(raw, 'gx', routes(peers, 0)[0])]
    unnamed x11 -> x20, local copies, waits for them, and re-layouts: 7.08 us -> 11.9 us
    slice x4 -> x2, local copies, waits for them, and re-layouts: 6.88 us -> 3.39 us  [cut(): return [lax.slice_in_dim(field, a, b, axis=0) for a, b in spans_of(rows)]]
    ppermute x1 -> x2, starting transfers between devices: 0.68 us -> 4.09 us  [the longest x1 3.7 us: on_device(): lax.ppermute(raw, 'gx', routes(peers, 0)[0])]
    ppermute x4 -> x3, starting transfers between devices: 11.7 us -> 8.31 us  [on_device(): arrived.append(lax.ppermute(sent, 'gx', routes(peers, g)[0]))]
    ppermute x1, starting transfers between devices: 20.9 us -> 22.6 us  [on_device(): rim_lo = lax.ppermute(lo, 'gx', cores)]
    concatenate x1, other arithmetic: 0.07 us -> 1.51 us  [on_device(): jnp.concatenate([arrived[g] for g in bundle], axis=0)]
  transfers between devices with their start and end apart: 9 -> 9, of which waited for: 3 -> 2; matrix products, arithmetic and copies ran while one was open for 8% -> 6% of each run, Pallas kernels for 19% -> 26%
where the time goes in v5:
time: 131 us; the launch traced here: 130 us
  Pallas kernels  45 us (34%)
  starting transfers between devices  42.7 us (33%)
  waiting for transfers between devices  22.2 us (17%)
  local copies, waits for them, and re-layouts  15.3 us (12%)
  other arithmetic  4.38 us (3%)
    ppermute x1, starting transfers between devices, on_device(): rim_lo = lax.ppermute(lo, 'gx', cores)  22.6 us
    pallas_call x2, Pallas kernels, lags(): pl.pallas_call(functools.partial(lag_kernel, cells, blocks, where, stages...  14.6 us
    ppermute x3, waiting for transfers between devices, on_device(): arrived.append(lax.ppermute(sent, 'gx', routes(peers, g)[0]))  13.1 us
    pallas_call x2, Pallas kernels, partial(): pl.pallas_call(functools.partial(part_kernel, cells, blocks, where, done)...  12.1 us
    unnamed x20, local copies, waits for them, and re-layouts  11.9 us
    pallas_call x2, Pallas kernels, pack(): pl.pallas_call(functools.partial(pack_kernel, rows), grid_spec=pltpu.Pref...  10.7 us
    ppermute x1, waiting for transfers between devices, on_device(): lax.ppermute(raw, 'gx', routes(peers, 0)[0])  9.13 us
    ppermute x3, starting transfers between devices, on_device(): arrived.append(lax.ppermute(sent, 'gx', routes(peers, g)[0]))  8.31 us
  transfers between devices with their start and end apart: 9, of which 2 were waited for; matrix products, arithmetic and copies ran while one was open for 6% of the time, Pallas kernels for 26%

profile of v5, /device:TPU:17, one launch (start us, length us, event | category | flops | bytes accessed | tf_op | source)
XLA Modules:
  0.0 129.9 jit_solution(15040325769438025301)
XLA Ops:
  0.0 2.9 %first.1 = bf16[3,2,2,8,4096]{4,3,2,1,0:T(8,128)(2,1)} custom-call(s32[1]{0:T(128)} %bitcast.core_ref.order_ref.refs_0_, bf16[16,2,8,4096]{3,2,1,0:T(8,128)(2,1)} %s_ref.2, bf16[16,2,8,4096]{3,2,1,0:T(8,128)(2,1)} %r_ref.2), custom_call_target="tpu_custom_call" | custom-call | tf_op jit(solution)/shard_map/first/pallas_call | solution.py:101
  2.9 3.7 %collective-permute-start = (bf16[3,2,2,8,4096]{4,3,2,1,0:T(8,128)(2,1)}, bf16[3,2,2,8,4096]{4,3,2,1,0:T(8,128)(2,1)S(1)}, u32[]{:S(2)}, u32[]{:S(2)}) collective-permute-start(bf16[3,2,2,8,4096]{4,3,2,1,0:T(8,128)(2,1)} %first.1), channel_id=1, source_target_pairs={{1,2},{5,6},{9,10},{13,14},{3,0},{7,4},{11,8},{2,1},{6,5},{10,9},{... | collective-permute-start | bytes 2359304 | tf_op jit(solution)/shard_map/ppermute | solution.py:319
  6.6 7.6 %pack.1.refs_0_.refs_1_ = bf16[16,2,16,32,128]{4,3,2,1,0:T(8,128)(2,1)} custom-call(s32[1]{0:T(128)} %bitcast.core_ref.order_ref.refs_0_, bf16[16,2,8,4096]{3,2,1,0:T(8,128)(2,1)} %s_ref.2, bf16[16,2,8,4096]{3,2,1,0:T(8,128)(2,1)} %r_ref.2), custom_call_target="tpu_custom_call" | custom-call | flops 419430400 | bytes 8388608 | tf_op jit(solution)/shard_map/pack/pallas_call | solution.py:62
  14.2 1.7 %fusion = (bf16[3,2,16,32,128]{4,3,2,1,0:T(8,128)(2,1)S(1)}, bf16[3,2,16,32,128]{4,3,2,1,0:T(8,128)(2,1)S(1)}) fusion(bf16[16,2,16,32,128]{4,3,2,1,0:T(8,128)(2,1)} %pack.1.refs_0_.refs_1_), kind=kLoop, calls=%fused_computation.3 | loop fusion | bytes 3145728 | tf_op jit(solution)/shard_map/slice | solution.py:312
  15.9 9.1 %collective-permute-done = bf16[3,2,2,8,4096]{4,3,2,1,0:T(8,128)(2,1)S(1)} collective-permute-done((bf16[3,2,2,8,4096]{4,3,2,1,0:T(8,128)(2,1)}, bf16[3,2,2,8,4096]{4,3,2,1,0:T(8,128)(2,1)S(1)}, u32[]{:S(2)}, u32[]{:S(2)}) %collective-permute-start) | collective-permute-done | bytes 786464 | tf_op jit(solution)/shard_map/ppermute | solution.py:319
  25.0 0.0 copy-start.6
  25.0 0.4 collective-permute-start.1
  25.4 3.2 %collective-permute-start.2 = (bf16[3,2,16,32,128]{4,3,2,1,0:T(8,128)(2,1)S(1)}, bf16[3,2,16,32,128]{4,3,2,1,0:T(8,128)(2,1)}, u32[]{:S(2)}, u32[]{:S(2)}) collective-permute-start(bf16[3,2,16,32,128]{4,3,2,1,0:T(8,128)(2,1)S(1)} %get-tuple-element.25), channel_id=1, source_target_pairs={{1,2},{5,6},{9,10},{11,12},{13,14},{3,0},{7,4},{2,1},{4,3},{6,5},{... | collective-permute-start | bytes 2359304 | tf_op jit(solution)/shard_map/ppermute | solution.py:326
  28.7 2.3 %collective-permute-start.4 = (bf16[3,2,16,32,128]{4,3,2,1,0:T(8,128)(2,1)S(1)}, bf16[3,2,16,32,128]{4,3,2,1,0:T(8,128)(2,1)S(1)}, u32[]{:S(2)}, u32[]{:S(2)}) collective-permute-start(bf16[3,2,16,32,128]{4,3,2,1,0:T(8,128)(2,1)S(1)} %get-tuple-element.21), channel_id=1, source_target_pairs={{1,2},{5,6},{7,8},{9,10},{11,12},{13,14},{3,0},{2,1},{4,3},{6,5},{... | collective-permute-start | bytes 2359304 | tf_op jit(solution)/shard_map/ppermute | solution.py:326
  31.0 0.0 copy-done.6
  31.0 3.2 %pack_first.1 = bf16[3,2,16,32,128]{4,3,2,1,0:T(8,128)(2,1)} custom-call(s32[1]{0:T(128)} %constant.33.clone.1.order_ref, bf16[6,2,8,4096]{3,2,1,0:T(8,128)(2,1)} %bitcast.4, bf16[6,2,8,4096]{3,2,1,0:T(8,128)(2,1)} %bitcast.5), custom_call_target="tpu_custom_call" | custom-call | flops 78643200 | bytes 1572864 | tf_op jit(solution)/shard_map/pack_first/pallas_call | solution.py:62
  34.2 13.1 %collective-permute-done.2 = bf16[3,2,16,32,128]{4,3,2,1,0:T(8,128)(2,1)} collective-permute-done((bf16[3,2,16,32,128]{4,3,2,1,0:T(8,128)(2,1)S(1)}, bf16[3,2,16,32,128]{4,3,2,1,0:T(8,128)(2,1)}, u32[]{:S(2)}, u32[]{:S(2)}) %collective-permute-start.2) | collective-permute-done | bytes 786464 | tf_op jit(solution)/shard_map/ppermute | solution.py:326
  47.3 1.5 %pad_maximum_fusion = bf16[6,2,16,32,128]{4,3,2,1,0:T(8,128)(2,1)S(1)} fusion(bf16[3,2,16,32,128]{4,3,2,1,0:T(8,128)(2,1)} %collective-permute-done.2, bf16[3,2,16,32,128]{4,3,2,1,0:T(8,128)(2,1)} %pack_first.1), kind=kLoop, calls=%fused_computation | loop fusion | flops 786432 | bytes 3145728 | tf_op jit(solution)/shard_map/concatenate | solution.py:379
  48.8 0.0 collective-permute-done.1.refs_1_.refs_2_
  48.8 0.0 copy-start
  48.8 2.2 %copy-done = bf16[16,2,16,32,128]{4,3,2,1,0:T(8,128)(2,1)S(1)} copy-done((bf16[16,2,16,32,128]{4,3,2,1,0:T(8,128)(2,1)S(1)}, bf16[16,2,16,32,128]{4,3,2,1,0:T(8,128)(2,1)}, u32[]{:S(2)}) %copy-start) | copy-done | bytes 4194328
  51.0 7.5 %inner.1.refs_5_.refs_6_ = f32[11,3,18,32,128]{4,3,2,1,0:T(8,128)S(1)} custom-call(bf16[16,2,16,32,128]{4,3,2,1,0:T(8,128)(2,1)S(1)} %copy-done, bf16[16,2,16,32,128]{4,3,2,1,0:T(8,128)(2,1)} %collective-permute-done.1.refs_1_.refs_2_), custom_call_target="tpu_custom_call" | custom-call | flops 1880883200 | tf_op jit(solution)/shard_map/inner/pallas_call | solution.py:363
  58.5 0.0 copy-start.3
  58.5 3.7 %copy-done.3 = f32[11,3,18,32,128]{4,3,2,1,0:T(8,128)} copy-done((f32[11,3,18,32,128]{4,3,2,1,0:T(8,128)}, f32[11,3,18,32,128]{4,3,2,1,0:T(8,128)S(1)}, u32[]{:S(2)}) %copy-start.3) | copy-done | bytes 9732120
  62.2 1.9 %collective-permute-start.3 = (bf16[6,2,16,32,128]{4,3,2,1,0:T(8,128)(2,1)S(1)}, bf16[6,2,16,32,128]{4,3,2,1,0:T(8,128)(2,1)}, u32[]{:S(2)}, u32[]{:S(2)}) collective-permute-start(bf16[6,2,16,32,128]{4,3,2,1,0:T(8,128)(2,1)S(1)} %pad_maximum_fusion), channel_id=1, source_target_pairs={{0,4},{4,8},{8,12},{7,3},{11,7},{15,11},{16,20},{20,24},{24,28},{2... | collective-permute-start | bytes 4718600 | tf_op jit(solution)/shard_map/ppermute | solution.py:386
  64.1 1.7 %slice.14 = bf16[7,2,16,32,128]{4,3,2,1,0:T(8,128)(2,1)} slice(bf16[16,2,16,32,128]{4,3,2,1,0:T(8,128)(2,1)S(1)} %copy-done), slice={[1:8], [0:2], [0:16], [0:32], [0:128]} | slice | bytes 3670016 | tf_op jit(solution)/shard_map/slice | solution.py:312
  65.8 2.8 %collective-permute-start.6 = (bf16[7,2,16,32,128]{4,3,2,1,0:T(8,128)(2,1)}, bf16[7,2,16,32,128]{4,3,2,1,0:T(8,128)(2,1)}, u32[]{:S(2)}, u32[]{:S(2)}) collective-permute-start(bf16[7,2,16,32,128]{4,3,2,1,0:T(8,128)(2,1)} %slice.14), channel_id=1, source_target_pairs={{1,2},{3,4},{5,6},{7,8},{9,10},{11,12},{13,14},{2,1},{4,3},{6,5},{... | collective-permute-start | bytes 5505032 | tf_op jit(solution)/shard_map/ppermute | solution.py:326
  68.5 0.0 collective-permute-done.4
  68.5 1.6 %collective-permute-start.5 = (bf16[3,2,16,32,128]{4,3,2,1,0:T(8,128)(2,1)S(1)}, bf16[3,2,16,32,128]{4,3,2,1,0:T(8,128)(2,1)}, u32[]{:S(2)}, u32[]{:S(2)}) collective-permute-start(bf16[3,2,16,32,128]{4,3,2,1,0:T(8,128)(2,1)S(1)} %collective-permute-done.4), channel_id=1, source_target_pairs={{0,4},{4,8},{8,12},{7,3},{11,7},{15,11},{16,20},{20,24},{24,28},{2... | collective-permute-start | bytes 2359304 | tf_op jit(solution)/shard_map/ppermute | solution.py:386
  70.1 0.0 collective-permute-done.5
  70.1 0.1 broadcast_select_fusion.1.refs_3_.refs_4_
  70.2 0.0 collective-permute-done.3
  70.2 2.8 %broadcast_select_fusion.refs_2_.refs_3_ = bf16[6,2,16,32,128]{4,3,2,1,0:T(8,128)(2,1)} fusion(bf16[6,2,16,32,128]{4,3,2,1,0:T(8,128)(2,1)} %collective-permute-done.3, bf16[6,2,16,32,128]{4,3,2,1,0:T(8,128)(2,1)S(1)} %pad_maximum_fusion, pred[6]{0:T(512)(128)(4,1)S(1)} %concatenate.6), kind=kLoop, calls=%fused_computation.1 | loop fusion | flops 786432 | bytes 4718598 | tf_op jit(solution)/shard_map/jit(_where)/select_n | solution.py:393
  73.0 0.0 copy-start.5
  73.0 4.7 %rim.1 = (f32[2,32,128]{2,1,0:T(8,128)}, f32[2,32,128]{2,1,0:T(8,128)}) custom-call(bf16[16,2,16,32,128]{4,3,2,1,0:T(8,128)(2,1)} %pack.1.refs_0_.refs_1_, bf16[16,2,16,32,128]{4,3,2,1,0:T(8,128)(2,1)} %collective-permute-done.1.refs_1_.refs_2_, bf16[6,2,16,32,128]{4,3,2,1,0:T(8,128)(2,1)} %broadcast_select_fusion.refs_2_.refs_3_), custom_call_target="tpu_custom_call" | custom-call | flops 26214400 | bytes 1572864 | tf_op jit(solution)/shard_map/rim/pallas_call | solution.py:399
  77.7 22.6 %collective-permute-start.7 = (f32[2,32,128]{2,1,0:T(8,128)}, f32[2,32,128]{2,1,0:T(8,128)S(1)}, u32[]{:S(2)}, u32[]{:S(2)}) collective-permute-start(f32[2,32,128]{2,1,0:T(8,128)} %get-tuple-element.23), channel_id=1, source_target_pairs={{0,1},{2,3},{4,5},{6,7},{8,9},{10,11},{12,13},{14,15},{1,0},{3,2},... | collective-permute-start | bytes 98312 | tf_op jit(solution)/shard_map/ppermute | solution.py:409
  100.2 4.4 %collective-permute-start.8 = (f32[2,32,128]{2,1,0:T(8,128)}, f32[2,32,128]{2,1,0:T(8,128)S(1)}, u32[]{:S(2)}, u32[]{:S(2)}) collective-permute-start(f32[2,32,128]{2,1,0:T(8,128)} %get-tuple-element.24), channel_id=1, source_target_pairs={{1,2},{3,4},{5,6},{7,8},{9,10},{11,12},{13,14},{2,1},{4,3},{6,5},{... | collective-permute-start | bytes 98312 | tf_op jit(solution)/shard_map/ppermute | solution.py:410
  104.6 0.0 copy-done.5
  104.6 0.0 copy-start.1
  104.6 2.2 %copy-done.1 = bf16[16,2,16,32,128]{4,3,2,1,0:T(8,128)(2,1)S(1)} copy-done((bf16[16,2,16,32,128]{4,3,2,1,0:T(8,128)(2,1)S(1)}, bf16[16,2,16,32,128]{4,3,2,1,0:T(8,128)(2,1)}, u32[]{:S(2)}) %copy-start.1) | copy-done | bytes 4194328
  106.8 0.0 copy-start.4
  106.8 3.8 %copy-done.4 = f32[11,3,18,32,128]{4,3,2,1,0:T(8,128)S(1)} copy-done((f32[11,3,18,32,128]{4,3,2,1,0:T(8,128)S(1)}, f32[11,3,18,32,128]{4,3,2,1,0:T(8,128)}, u32[]{:S(2)}) %copy-start.4) | copy-done | bytes 9732120
  110.6 0.0 copy-start.2
  110.6 0.0 slice-start
  110.6 0.0 slice-start.1
  110.6 6.8 %near.1.refs_10_ = f32[33,16,4096]{2,1,0:T(8,128)} custom-call(s32[1]{0:T(128)} %bitcast.core_ref.order_ref.refs_0_, bf16[16,2,16,32,128]{4,3,2,1,0:T(8,128)(2,1)S(1)} %copy-done.1, bf16[16,2,16,32,128]{4,3,2,1,0:T(8,128)(2,1)} %collective-permute-done.1.refs_1_.refs_2_, bf16[6,2,16,32,128]{4,3,2,1,0:T(8,128)(2,1)S(1)} %copy-done.5, ...), custom_call_target="tpu_custom_call" | custom-call | flops 1448345600 | bytes 3932160 | tf_op jit(solution)/shard_map/near/pallas_call | solution.py:425
  117.4 0.0 copy-done.2
  117.4 0.0 slice-start.2
  117.4 4.6 %middle.1.refs_7_ = f32[6,3,18,32,128]{4,3,2,1,0:T(8,128)S(1)} custom-call(bf16[16,2,16,32,128]{4,3,2,1,0:T(8,128)(2,1)S(1)} %copy-done.2, bf16[16,2,16,32,128]{4,3,2,1,0:T(8,128)(2,1)} %collective-permute-done.1.refs_1_.refs_2_, bf16[6,2,16,32,128]{4,3,2,1,0:T(8,128)(2,1)S(1)} %copy-done.5, ...), custom_call_target="tpu_custom_call" | custom-call | flops 969932800 | tf_op jit(solution)/shard_map/middle/pallas_call | solution.py:363
  122.0 0.0 collective-permute-done.6.refs_5_
  122.0 0.0 collective-permute-done.7.refs_8_
  122.0 0.0 collective-permute-done.8.refs_9_
  122.0 0.0 slice-done
  122.0 0.0 slice-done.1
  122.1 0.0 slice-done.2
  122.1 7.8 %far.1 = f32[33,16,4096]{2,1,0:T(8,128)} custom-call(s32[1]{0:T(128)} %bitcast.core_ref.order_ref.refs_0_, bf16[16,2,16,32,128]{4,3,2,1,0:T(8,128)(2,1)S(1)} %copy-done.2, bf16[16,2,16,32,128]{4,3,2,1,0:T(8,128)(2,1)} %collective-permute-done.1.refs_1_.refs_2_, bf16[6,2,16,32,128]{4,3,2,1,0:T(8,128)(2,1)S(1)} %copy-done.5, ...), custom_call_target="tpu_custom_call", output_to_operand_aliasing={{}: (10, {})} | custom-call | flops 1730150400 | bytes 4718592 | tf_op jit(solution)/shard_map/far/pallas_call | solution.py:425
  (3 shorter events, 0.0 us)
Async XLA Ops:
  2.9 22.1 %collective-permute-start = (bf16[3,2,2,8,4096]{4,3,2,1,0:T(8,128)(2,1)}, bf16[3,2,2,8,4096]{4,3,2,1,0:T(8,128)(2,1)S(1)}, u32[]{:S(2)}, u32[]{:S(2)}) collective-permute-start(bf16[3,2,2,8,4096]{4,3,2,1,0:T(8,128)(2,1)} %first.1), channel_id=1, source_target_pairs={{1,2},{5,6},{9,10},{13,14},{3,0},{7,4},{11,8},{2,1},{6,5},{10,9},{... | collective-permute-start | bytes 2359304 | tf_op jit(solution)/shard_map/ppermute | solution.py:319
  25.0 6.0 %copy-start.6 = (bf16[3,2,2,8,4096]{4,3,2,1,0:T(8,128)(2,1)}, bf16[3,2,2,8,4096]{4,3,2,1,0:T(8,128)(2,1)S(1)}, u32[]{:S(2)}) copy-start(bf16[3,2,2,8,4096]{4,3,2,1,0:T(8,128)(2,1)S(1)} %collective-permute-done) | copy-start | bytes 2359300
  25.0 23.7 %collective-permute-start.1 = (bf16[16,2,16,32,128]{4,3,2,1,0:T(8,128)(2,1)}, bf16[16,2,16,32,128]{4,3,2,1,0:T(8,128)(2,1)}, u32[]{:S(2)}, u32[]{:S(2)}) collective-permute-start(bf16[16,2,16,32,128]{4,3,2,1,0:T(8,128)(2,1)} %pack.1.refs_0_.refs_1_), channel_id=1, source_target_pairs={{0,1},{2,3},{4,5},{6,7},{8,9},{10,11},{12,13},{14,15},{1,0},{3,2},... | collective-permute-start | bytes 12582920 | tf_op jit(solution)/shard_map/ppermute | solution.py:328
  25.4 21.8 %collective-permute-start.2 = (bf16[3,2,16,32,128]{4,3,2,1,0:T(8,128)(2,1)S(1)}, bf16[3,2,16,32,128]{4,3,2,1,0:T(8,128)(2,1)}, u32[]{:S(2)}, u32[]{:S(2)}) collective-permute-start(bf16[3,2,16,32,128]{4,3,2,1,0:T(8,128)(2,1)S(1)} %get-tuple-element.25), channel_id=1, source_target_pairs={{1,2},{5,6},{9,10},{11,12},{13,14},{3,0},{7,4},{2,1},{4,3},{6,5},{... | collective-permute-start | bytes 2359304 | tf_op jit(solution)/shard_map/ppermute | solution.py:326
  28.7 39.8 %collective-permute-start.4 = (bf16[3,2,16,32,128]{4,3,2,1,0:T(8,128)(2,1)S(1)}, bf16[3,2,16,32,128]{4,3,2,1,0:T(8,128)(2,1)S(1)}, u32[]{:S(2)}, u32[]{:S(2)}) collective-permute-start(bf16[3,2,16,32,128]{4,3,2,1,0:T(8,128)(2,1)S(1)} %get-tuple-element.21), channel_id=1, source_target_pairs={{1,2},{5,6},{7,8},{9,10},{11,12},{13,14},{3,0},{2,1},{4,3},{6,5},{... | collective-permute-start | bytes 2359304 | tf_op jit(solution)/shard_map/ppermute | solution.py:326
  48.8 2.2 %copy-start = (bf16[16,2,16,32,128]{4,3,2,1,0:T(8,128)(2,1)S(1)}, bf16[16,2,16,32,128]{4,3,2,1,0:T(8,128)(2,1)}, u32[]{:S(2)}) copy-start(bf16[16,2,16,32,128]{4,3,2,1,0:T(8,128)(2,1)} %pack.1.refs_0_.refs_1_) | copy-start | bytes 12582916
  58.5 3.7 %copy-start.3 = (f32[11,3,18,32,128]{4,3,2,1,0:T(8,128)}, f32[11,3,18,32,128]{4,3,2,1,0:T(8,128)S(1)}, u32[]{:S(2)}) copy-start(f32[11,3,18,32,128]{4,3,2,1,0:T(8,128)S(1)} %inner.1.refs_5_.refs_6_) | copy-start | bytes 29196292
  62.2 8.0 %collective-permute-start.3 = (bf16[6,2,16,32,128]{4,3,2,1,0:T(8,128)(2,1)S(1)}, bf16[6,2,16,32,128]{4,3,2,1,0:T(8,128)(2,1)}, u32[]{:S(2)}, u32[]{:S(2)}) collective-permute-start(bf16[6,2,16,32,128]{4,3,2,1,0:T(8,128)(2,1)S(1)} %pad_maximum_fusion), channel_id=1, source_target_pairs={{0,4},{4,8},{8,12},{7,3},{11,7},{15,11},{16,20},{20,24},{24,28},{2... | collective-permute-start | bytes 4718600 | tf_op jit(solution)/shard_map/ppermute | solution.py:386
  65.8 56.3 %collective-permute-start.6 = (bf16[7,2,16,32,128]{4,3,2,1,0:T(8,128)(2,1)}, bf16[7,2,16,32,128]{4,3,2,1,0:T(8,128)(2,1)}, u32[]{:S(2)}, u32[]{:S(2)}) collective-permute-start(bf16[7,2,16,32,128]{4,3,2,1,0:T(8,128)(2,1)} %slice.14), channel_id=1, source_target_pairs={{1,2},{3,4},{5,6},{7,8},{9,10},{11,12},{13,14},{2,1},{4,3},{6,5},{... | collective-permute-start | bytes 5505032 | tf_op jit(solution)/shard_map/ppermute | solution.py:326
  68.5 1.6 %collective-permute-start.5 = (bf16[3,2,16,32,128]{4,3,2,1,0:T(8,128)(2,1)S(1)}, bf16[3,2,16,32,128]{4,3,2,1,0:T(8,128)(2,1)}, u32[]{:S(2)}, u32[]{:S(2)}) collective-permute-start(bf16[3,2,16,32,128]{4,3,2,1,0:T(8,128)(2,1)S(1)} %collective-permute-done.4), channel_id=1, source_target_pairs={{0,4},{4,8},{8,12},{7,3},{11,7},{15,11},{16,20},{20,24},{24,28},{2... | collective-permute-start | bytes 2359304 | tf_op jit(solution)/shard_map/ppermute | solution.py:386
  73.0 31.6 %copy-start.5 = (bf16[6,2,16,32,128]{4,3,2,1,0:T(8,128)(2,1)S(1)}, bf16[6,2,16,32,128]{4,3,2,1,0:T(8,128)(2,1)}, u32[]{:S(2)}) copy-start(bf16[6,2,16,32,128]{4,3,2,1,0:T(8,128)(2,1)} %broadcast_select_fusion.refs_2_.refs_3_) | copy-start | bytes 4718596
  77.7 44.3 %collective-permute-start.7 = (f32[2,32,128]{2,1,0:T(8,128)}, f32[2,32,128]{2,1,0:T(8,128)S(1)}, u32[]{:S(2)}, u32[]{:S(2)}) collective-permute-start(f32[2,32,128]{2,1,0:T(8,128)} %get-tuple-element.23), channel_id=1, source_target_pairs={{0,1},{2,3},{4,5},{6,7},{8,9},{10,11},{12,13},{14,15},{1,0},{3,2},... | collective-permute-start | bytes 98312 | tf_op jit(solution)/shard_map/ppermute | solution.py:409
  100.2 21.8 %collective-permute-start.8 = (f32[2,32,128]{2,1,0:T(8,128)}, f32[2,32,128]{2,1,0:T(8,128)S(1)}, u32[]{:S(2)}, u32[]{:S(2)}) collective-permute-start(f32[2,32,128]{2,1,0:T(8,128)} %get-tuple-element.24), channel_id=1, source_target_pairs={{1,2},{3,4},{5,6},{7,8},{9,10},{11,12},{13,14},{2,1},{4,3},{6,5},{... | collective-permute-start | bytes 98312 | tf_op jit(solution)/shard_map/ppermute | solution.py:410
  104.6 2.2 %copy-start.1 = (bf16[16,2,16,32,128]{4,3,2,1,0:T(8,128)(2,1)S(1)}, bf16[16,2,16,32,128]{4,3,2,1,0:T(8,128)(2,1)}, u32[]{:S(2)}) copy-start(bf16[16,2,16,32,128]{4,3,2,1,0:T(8,128)(2,1)} %pack.1.refs_0_.refs_1_) | copy-start | bytes 12582916
  106.8 3.8 %copy-start.4 = (f32[11,3,18,32,128]{4,3,2,1,0:T(8,128)S(1)}, f32[11,3,18,32,128]{4,3,2,1,0:T(8,128)}, u32[]{:S(2)}) copy-start(f32[11,3,18,32,128]{4,3,2,1,0:T(8,128)} %copy-done.3) | copy-start | bytes 29196292
  110.6 6.8 %copy-start.2 = (bf16[16,2,16,32,128]{4,3,2,1,0:T(8,128)(2,1)S(1)}, bf16[16,2,16,32,128]{4,3,2,1,0:T(8,128)(2,1)}, u32[]{:S(2)}) copy-start(bf16[16,2,16,32,128]{4,3,2,1,0:T(8,128)(2,1)} %pack.1.refs_0_.refs_1_) | copy-start | bytes 12582916
  110.6 11.5 %slice-start = ((s8[9732096]{0:T(1024)(128)(4,1)}), s8[4194304]{0:T(1024)(128)(4,1)S(1)}, s32[]{:S(2)}) async-start(s8[9732096]{0:T(1024)(128)(4,1)} %bitcast.2), calls=%async_computation | async-start | bytes 8388608
  110.6 11.5 %slice-start.1 = ((s8[9732096]{0:T(1024)(128)(4,1)}), s8[4194304]{0:T(1024)(128)(4,1)S(1)}, s32[]{:S(2)}) async-start(s8[9732096]{0:T(1024)(128)(4,1)} %bitcast.2), calls=%async_computation.1 | async-start | bytes 8388608
  117.4 4.7 %slice-start.2 = ((s8[9732096]{0:T(1024)(128)(4,1)}), s8[1343488]{0:T(1024)(128)(4,1)S(1)}, s32[]{:S(2)}) async-start(s8[9732096]{0:T(1024)(128)(4,1)} %bitcast.2), calls=%async_computation.2 | async-start | bytes 2686976

commit v6 on v5

--- a/solution.py
+++ b/solution.py
@@ -16,11 +16,9 @@
 SPAN = 3
 RATE = 50
 
-CHUNKS = ((16, 2, 1), (5, 4, 3), (8, 7, 6), (15, 14, 13, 12, 11, 10, 9))
-BUNDLES = ((0, 1), (2,))
-NEAR = (5, 4, 6, 3, 7)
-FAR = (2, 8, 1, 9, 0, 10)
-ALL = NEAR + FAR
+CHUNKS = ((16, 4, 3, 2, 1), (11, 10, 9, 8, 7, 6, 5), (15, 14, 13, 12))
+NEAR = (5, 4, 6, 3, 7, 2, 8)
+FAR = (1, 9, 0, 10)
 SCOPED = 14 * 2**20
 
 VMEM = pl.BlockSpec(memory_space=pltpu.VMEM)
@@ -266,29 +264,6 @@
     return up, [(j, i) for i, j in up]
 
 
-def routes(peers, chunk):
-    up, down = exchange(peers)
-    if peers != 16 or chunk > 2:
-        return up + down, ()
-    steps = peers // 4
-    far_up = range(0, steps - 1 - chunk)
-    far_down = range(chunk, steps - 1)
-    up = [p for p in up if p not in [(4 * z + 3, 4 * z + 4) for z in far_up]]
-    up += [(4 * z + 3, 4 * z) for z in far_up]
-    down = [p for p in down if p not in [(4 * z + 4, 4 * z + 3) for z in far_down]]
-    down += [(4 * z + 4, 4 * z + 7) for z in far_down]
-    swap = {4 * z for z in far_up} | {4 * z + 4 for z in far_up}
-    swap |= {4 * z + 7 for z in far_down} | {4 * z + 3 for z in far_down}
-    return up + down, sorted(swap)
-
-
-def is_one_of(me, devices):
-    found = jnp.bool_(False)
-    for d in devices:
-        found |= me == d
-    return found
-
-
 def on_device(forward_field, adjoint_field):
     cells, parts, freqs, width = forward_field.shape
     terms, tiles = parts * freqs, width // LANES
@@ -316,26 +291,22 @@
     raw, forward_field, adjoint_field = lax.optimization_barrier(
         (raw, forward_field, adjoint_field)
     )
-    raw = lax.ppermute(raw, "gx", routes(peers, 0)[0]).reshape(2 * n, parts, freqs, width)
+    raw = lax.ppermute(raw, "gx", links).reshape(2 * n, parts, freqs, width)
     own = pack(core, 2, cells // 2, forward_field, adjoint_field, (0, 0, 1), RATE, "pack")
     arrived = [None]
     for g, chunk in enumerate(CHUNKS[1:], 1):
         sent = jnp.concatenate(cut(own, [cells - i for i in chunk]), axis=0)
-        if g == 2:
-            sent, raw, swap = lax.optimization_barrier((sent, raw, own))
-        arrived.append(lax.ppermute(sent, "gx", routes(peers, g)[0]))
+        arrived.append(lax.ppermute(sent, "gx", links))
+    swap, raw = lax.optimization_barrier((own, raw))
     arrived[0] = pack(jnp.ones_like(core), 1, n, raw, raw, (0, 1, 2), RATE, "pack_first")
     beside = lax.ppermute(swap, "gx", cores)
-
-    pieces = []
 
     def layout(count):
         operands = [own, beside]
         where = {a: (0, a) for a in range(cells)}
         where.update({-1 - a: (1, a) for a in range(cells)})
-        for bundle, got in pieces[:count]:
-            order = [i for g in bundle for i in CHUNKS[g]]
-            where.update({cells - 1 + i: (len(operands), k) for k, i in enumerate(order)})
+        for chunk, got in zip(CHUNKS[:count], arrived):
+            where.update({cells - 1 + i: (len(operands), k) for k, i in enumerate(chunk)})
             operands.append(got)
         return operands, where
 
@@ -372,28 +343,6 @@
             name=name,
         )(*operands)
         return out, (set(where), blocks)
-
-    inner, inner_stage = partial("inner", 0, ALL, ())
-
-    for bundle in BUNDLES:
-        got = jnp.concatenate([arrived[g] for g in bundle], axis=0) if len(bundle) > 1 else arrived[bundle[0]]
-        if bundle[0] == 0:
-            got, inner = lax.optimization_barrier((got, inner))
-        if peers == 16:
-            steps = peers // 4
-            hop = [(4 * z, 4 * z + 4) for z in range(steps - 1)]
-            hop += [(4 * z + 7, 4 * z + 3) for z in range(steps - 1)]
-            relayed = lax.ppermute(got, "gx", hop)
-            swapped = jnp.concatenate(
-                [
-                    jnp.broadcast_to(is_one_of(me, routes(peers, g)[1]), (len(CHUNKS[g]),))
-                    for g in bundle
-                ]
-            )
-            got = jnp.where(swapped[:, None, None, None, None], relayed, got)
-        pieces.append((bundle, got))
-    for g in range(1 + BUNDLES[-1][-1], len(CHUNKS)):
-        pieces.append(((g,), arrived[g]))
 
     operands, where = layout(1)
     lo, hi = pl.pallas_call(
@@ -441,17 +390,10 @@
             name=name,
         )(*operands)
 
-    image = lags("near", None, len(pieces) - 1, NEAR, [inner], [inner_stage], [])
-    middle, middle_stage = partial("middle", len(pieces) - 1, FAR, inner_stage[0])
-    return lags(
-        "far",
-        image,
-        len(pieces),
-        FAR,
-        [inner, middle],
-        [inner_stage, middle_stage],
-        [rim_lo, rim_hi],
-    )
+    last = len(CHUNKS) - 1
+    image = lags("near", None, last, NEAR, [], [], [])
+    sums, stage = partial("partial", last, FAR, ())
+    return lags("far", image, last + 1, FAR, [sums], [stage], [rim_lo, rim_hi])
 
 
 def solution(mesh):

time: 131 us -> 124 us (0.947)
  waiting for transfers between devices: 22.2 us -> 56.5 us
  starting transfers between devices: 42.7 us -> 13.8 us
  local copies, waits for them, and re-layouts: 15.3 us -> 8.08 us
  other arithmetic: 4.38 us -> 0 us
    ppermute x6 -> x3, waiting for transfers between devices: 22.2 us -> 56.5 us  [the longest x2 34.5 us: on_device(): arrived.append(lax.ppermute(sent, 'gx', links))]
    ppermute x1, starting transfers between devices: 22.6 us -> 0.93 us  [on_device(): rim_lo = lax.ppermute(lo, 'gx', cores)]
    unnamed x20 -> x6, local copies, waits for them, and re-layouts: 11.9 us -> 2.2 us
    pallas_call x2 -> x1, Pallas kernels: 12.1 us -> 5.28 us  [partial(): pl.pallas_call(functools.partial(part_kernel, cells, blocks, where, done)...]
    ppermute x6 -> x3, starting transfers between devices: 15.4 us -> 9.24 us  [the longest x2 5.54 us: on_device(): arrived.append(lax.ppermute(sent, 'gx', links))]
    pallas_call x2, Pallas kernels: 14.6 us -> 19.2 us  [lags(): pl.pallas_call(functools.partial(lag_kernel, cells, blocks, where, stages...]
    select_n x2 -> x0, other arithmetic: 2.87 us -> none  [on_device(): got = jnp.where(swapped[:, None, None, None, None], relayed, got)]
    slice x2, local copies, waits for them, and re-layouts: 3.39 us -> 5.88 us  [cut(): return [lax.slice_in_dim(field, a, b, axis=0) for a, b in spans_of(rows)]]
  transfers between devices with their start and end apart: 9 -> 6, of which waited for: 2 -> 2; matrix products, arithmetic and copies ran while one was open for 6% -> 5% of each run, Pallas kernels for 26% -> 29%
where the time goes in v6:
time: 124 us
  waiting for transfers between devices  56.5 us (46%)
  Pallas kernels  45.1 us (36%)
  starting transfers between devices  13.8 us (11%)
  local copies, waits for them, and re-layouts  8.08 us (7%)
    ppermute x2, waiting for transfers between devices, on_device(): arrived.append(lax.ppermute(sent, 'gx', links))  34.5 us
    ppermute x1, waiting for transfers between devices, on_device(): raw = lax.ppermute(raw, 'gx', links).reshape(2 * n, parts, freqs, width)  22 us
    pallas_call x2, Pallas kernels, lags(): pl.pallas_call(functools.partial(lag_kernel, cells, blocks, where, stages...  19.2 us
    pallas_call x2, Pallas kernels, pack(): pl.pallas_call(functools.partial(pack_kernel, rows), grid_spec=pltpu.Pref...  12 us
    slice x2, local copies, waits for them, and re-layouts, cut(): return [lax.slice_in_dim(field, a, b, axis=0) for a, b in spans_of(rows)]  5.88 us
    ppermute x2, starting transfers between devices, on_device(): arrived.append(lax.ppermute(sent, 'gx', links))  5.54 us
    pallas_call x1, Pallas kernels, partial(): pl.pallas_call(functools.partial(part_kernel, cells, blocks, where, done)...  5.28 us
    pallas_call x1, Pallas kernels, on_device(): pl.pallas_call(functools.partial(rim_kernel, cells, where), in_specs=[VME...  4.57 us
  transfers between devices with their start and end apart: 6, of which 2 were waited for; matrix products, arithmetic and copies ran while one was open for 5% of the time, Pallas kernels for 29%

profile of v6, /device:TPU:17, one launch (start us, length us, event | category | flops | bytes accessed | tf_op | source)
XLA Modules:
  0.0 123.5 jit_solution(1390584198486434167)
XLA Ops:
  0.0 4.0 %first.1 = bf16[5,2,2,8,4096]{4,3,2,1,0:T(8,128)(2,1)} custom-call(s32[1]{0:T(128)} %bitcast.core_ref.order_ref.refs_0_, bf16[16,2,8,4096]{3,2,1,0:T(8,128)(2,1)} %s_ref.2, bf16[16,2,8,4096]{3,2,1,0:T(8,128)(2,1)} %r_ref.2), custom_call_target="tpu_custom_call" | custom-call | tf_op jit(solution)/shard_map/first/pallas_call | solution.py:99
  4.0 3.7 %collective-permute-start = (bf16[5,2,2,8,4096]{4,3,2,1,0:T(8,128)(2,1)}, bf16[5,2,2,8,4096]{4,3,2,1,0:T(8,128)(2,1)S(1)}, u32[]{:S(2)}, u32[]{:S(2)}) collective-permute-start(bf16[5,2,2,8,4096]{4,3,2,1,0:T(8,128)(2,1)} %first.1), channel_id=1, source_target_pairs={{1,2},{3,4},{5,6},{7,8},{9,10},{11,12},{13,14},{2,1},{4,3},{6,5},{... | collective-permute-start | bytes 3932168 | tf_op jit(solution)/shard_map/ppermute | solution.py:294
  7.7 7.5 %pack.1.refs_0_.refs_1_ = bf16[16,2,16,32,128]{4,3,2,1,0:T(8,128)(2,1)} custom-call(s32[1]{0:T(128)} %bitcast.core_ref.order_ref.refs_0_, bf16[16,2,8,4096]{3,2,1,0:T(8,128)(2,1)} %s_ref.2, bf16[16,2,8,4096]{3,2,1,0:T(8,128)(2,1)} %r_ref.2), custom_call_target="tpu_custom_call" | custom-call | flops 419430400 | bytes 8388608 | tf_op jit(solution)/shard_map/pack/pallas_call | solution.py:60
  15.3 22.0 %collective-permute-done = bf16[5,2,2,8,4096]{4,3,2,1,0:T(8,128)(2,1)S(1)} collective-permute-done((bf16[5,2,2,8,4096]{4,3,2,1,0:T(8,128)(2,1)}, bf16[5,2,2,8,4096]{4,3,2,1,0:T(8,128)(2,1)S(1)}, u32[]{:S(2)}, u32[]{:S(2)}) %collective-permute-start) | collective-permute-done | bytes 1310752 | tf_op jit(solution)/shard_map/ppermute | solution.py:294
  37.3 0.0 copy-start.2
  37.3 0.0 collective-permute-start.1
  37.3 3.6 %slice.8 = bf16[7,2,16,32,128]{4,3,2,1,0:T(8,128)(2,1)} slice(bf16[16,2,16,32,128]{4,3,2,1,0:T(8,128)(2,1)} %pack.1.refs_0_.refs_1_), slice={[5:12], [0:2], [0:16], [0:32], [0:128]} | slice | bytes 3670016 | tf_op jit(solution)/shard_map/slice | solution.py:287
  40.9 3.6 %collective-permute-start.2 = (bf16[7,2,16,32,128]{4,3,2,1,0:T(8,128)(2,1)}, bf16[7,2,16,32,128]{4,3,2,1,0:T(8,128)(2,1)S(1)}, u32[]{:S(2)}, u32[]{:S(2)}) collective-permute-start(bf16[7,2,16,32,128]{4,3,2,1,0:T(8,128)(2,1)} %slice.8), channel_id=1, source_target_pairs={{1,2},{3,4},{5,6},{7,8},{9,10},{11,12},{13,14},{2,1},{4,3},{6,5},{... | collective-permute-start | bytes 5505032 | tf_op jit(solution)/shard_map/ppermute | solution.py:299
  44.5 2.3 %slice.9 = bf16[4,2,16,32,128]{4,3,2,1,0:T(8,128)(2,1)} slice(bf16[16,2,16,32,128]{4,3,2,1,0:T(8,128)(2,1)} %pack.1.refs_0_.refs_1_), slice={[1:5], [0:2], [0:16], [0:32], [0:128]} | slice | bytes 2097152 | tf_op jit(solution)/shard_map/slice | solution.py:287
  46.8 0.0 copy-done.2
  46.8 1.9 %collective-permute-start.3 = (bf16[4,2,16,32,128]{4,3,2,1,0:T(8,128)(2,1)}, bf16[4,2,16,32,128]{4,3,2,1,0:T(8,128)(2,1)}, u32[]{:S(2)}, u32[]{:S(2)}) collective-permute-start(bf16[4,2,16,32,128]{4,3,2,1,0:T(8,128)(2,1)} %slice.9), channel_id=1, source_target_pairs={{1,2},{3,4},{5,6},{7,8},{9,10},{11,12},{13,14},{2,1},{4,3},{6,5},{... | collective-permute-start | bytes 3145736 | tf_op jit(solution)/shard_map/ppermute | solution.py:299
  48.7 4.5 %pack_first.1.refs_2_.refs_3_ = bf16[5,2,16,32,128]{4,3,2,1,0:T(8,128)(2,1)} custom-call(s32[1]{0:T(128)} %constant.18.clone.1.order_ref, bf16[10,2,8,4096]{3,2,1,0:T(8,128)(2,1)} %bitcast.2, bf16[10,2,8,4096]{3,2,1,0:T(8,128)(2,1)} %bitcast.3), custom_call_target="tpu_custom_call" | custom-call | flops 131072000 | bytes 2621440 | tf_op jit(solution)/shard_map/pack_first/pallas_call | solution.py:60
  53.2 0.0 copy-start.1
  53.2 0.0 collective-permute-done.1.refs_1_.refs_2_
  53.2 4.6 %rim.1 = (f32[2,32,128]{2,1,0:T(8,128)}, f32[2,32,128]{2,1,0:T(8,128)}) custom-call(bf16[16,2,16,32,128]{4,3,2,1,0:T(8,128)(2,1)} %pack.1.refs_0_.refs_1_, bf16[16,2,16,32,128]{4,3,2,1,0:T(8,128)(2,1)} %collective-permute-done.1.refs_1_.refs_2_, bf16[5,2,16,32,128]{4,3,2,1,0:T(8,128)(2,1)} %pack_first.1.refs_2_.refs_3_), custom_call_target="tpu_custom_call" | custom-call | flops 26214400 | bytes 1572864 | tf_op jit(solution)/shard_map/rim/pallas_call | solution.py:348
  57.8 0.9 collective-permute-start.4
  58.7 3.6 %collective-permute-start.5 = (f32[2,32,128]{2,1,0:T(8,128)}, f32[2,32,128]{2,1,0:T(8,128)S(1)}, u32[]{:S(2)}, u32[]{:S(2)}) collective-permute-start(f32[2,32,128]{2,1,0:T(8,128)} %get-tuple-element.18), channel_id=1, source_target_pairs={{1,2},{3,4},{5,6},{7,8},{9,10},{11,12},{13,14},{2,1},{4,3},{6,5},{... | collective-permute-start | bytes 98312 | tf_op jit(solution)/shard_map/ppermute | solution.py:359
  62.4 34.5 %collective-permute-done.2.refs_3_.refs_4_ = bf16[7,2,16,32,128]{4,3,2,1,0:T(8,128)(2,1)S(1)} collective-permute-done((bf16[7,2,16,32,128]{4,3,2,1,0:T(8,128)(2,1)}, bf16[7,2,16,32,128]{4,3,2,1,0:T(8,128)(2,1)S(1)}, u32[]{:S(2)}, u32[]{:S(2)}) %collective-permute-start.2) | collective-permute-done | bytes 1835040 | tf_op jit(solution)/shard_map/ppermute | solution.py:299
  96.9 0.0 copy-done.1
  96.9 0.0 copy-start
  96.9 2.2 %copy-done = bf16[16,2,16,32,128]{4,3,2,1,0:T(8,128)(2,1)S(1)} copy-done((bf16[16,2,16,32,128]{4,3,2,1,0:T(8,128)(2,1)S(1)}, bf16[16,2,16,32,128]{4,3,2,1,0:T(8,128)(2,1)}, u32[]{:S(2)}) %copy-start) | copy-done | bytes 4194328
  99.1 13.5 %near.1.refs_9_ = f32[33,16,4096]{2,1,0:T(8,128)} custom-call(s32[1]{0:T(128)} %bitcast.core_ref.order_ref.refs_0_, bf16[16,2,16,32,128]{4,3,2,1,0:T(8,128)(2,1)S(1)} %copy-done, bf16[16,2,16,32,128]{4,3,2,1,0:T(8,128)(2,1)} %collective-permute-done.1.refs_1_.refs_2_, bf16[5,2,16,32,128]{4,3,2,1,0:T(8,128)(2,1)S(1)} %copy-done.1, ...), custom_call_target="tpu_custom_call" | custom-call | flops 3853516800 | bytes 5505024 | tf_op jit(solution)/shard_map/near/pallas_call | solution.py:374
  112.5 5.3 %partial.1.refs_6_ = f32[4,3,18,32,128]{4,3,2,1,0:T(8,128)S(1)} custom-call(bf16[16,2,16,32,128]{4,3,2,1,0:T(8,128)(2,1)S(1)} %copy-done, bf16[16,2,16,32,128]{4,3,2,1,0:T(8,128)(2,1)} %collective-permute-done.1.refs_1_.refs_2_, bf16[5,2,16,32,128]{4,3,2,1,0:T(8,128)(2,1)S(1)} %copy-done.1, ...), custom_call_target="tpu_custom_call" | custom-call | flops 1153433600 | tf_op jit(solution)/shard_map/partial/pallas_call | solution.py:334
  117.8 0.0 collective-permute-done.3.refs_5_
  117.8 0.0 collective-permute-done.4.refs_7_
  117.8 0.0 collective-permute-done.5.refs_8_
  117.8 5.7 %far.1 = f32[33,16,4096]{2,1,0:T(8,128)} custom-call(s32[1]{0:T(128)} %bitcast.core_ref.order_ref.refs_0_, bf16[16,2,16,32,128]{4,3,2,1,0:T(8,128)(2,1)S(1)} %copy-done, bf16[16,2,16,32,128]{4,3,2,1,0:T(8,128)(2,1)} %collective-permute-done.1.refs_1_.refs_2_, bf16[5,2,16,32,128]{4,3,2,1,0:T(8,128)(2,1)S(1)} %copy-done.1, ...), custom_call_target="tpu_custom_call", output_to_operand_aliasing={{}: (9, {})} | custom-call | flops 1022361600 | bytes 3145728 | tf_op jit(solution)/shard_map/far/pallas_call | solution.py:374
Async XLA Ops:
  4.0 33.2 %collective-permute-start = (bf16[5,2,2,8,4096]{4,3,2,1,0:T(8,128)(2,1)}, bf16[5,2,2,8,4096]{4,3,2,1,0:T(8,128)(2,1)S(1)}, u32[]{:S(2)}, u32[]{:S(2)}) collective-permute-start(bf16[5,2,2,8,4096]{4,3,2,1,0:T(8,128)(2,1)} %first.1), channel_id=1, source_target_pairs={{1,2},{3,4},{5,6},{7,8},{9,10},{11,12},{13,14},{2,1},{4,3},{6,5},{... | collective-permute-start | bytes 3932168 | tf_op jit(solution)/shard_map/ppermute | solution.py:294
  37.3 9.5 %copy-start.2 = (bf16[5,2,2,8,4096]{4,3,2,1,0:T(8,128)(2,1)}, bf16[5,2,2,8,4096]{4,3,2,1,0:T(8,128)(2,1)S(1)}, u32[]{:S(2)}) copy-start(bf16[5,2,2,8,4096]{4,3,2,1,0:T(8,128)(2,1)S(1)} %collective-permute-done) | copy-start | bytes 3932164
  37.3 15.9 %collective-permute-start.1 = (bf16[16,2,16,32,128]{4,3,2,1,0:T(8,128)(2,1)}, bf16[16,2,16,32,128]{4,3,2,1,0:T(8,128)(2,1)}, u32[]{:S(2)}, u32[]{:S(2)}) collective-permute-start(bf16[16,2,16,32,128]{4,3,2,1,0:T(8,128)(2,1)} %pack.1.refs_0_.refs_1_), channel_id=1, source_target_pairs={{0,1},{2,3},{4,5},{6,7},{8,9},{10,11},{12,13},{14,15},{1,0},{3,2},... | collective-permute-start | bytes 12582920 | tf_op jit(solution)/shard_map/ppermute | solution.py:302
  40.9 56.0 %collective-permute-start.2 = (bf16[7,2,16,32,128]{4,3,2,1,0:T(8,128)(2,1)}, bf16[7,2,16,32,128]{4,3,2,1,0:T(8,128)(2,1)S(1)}, u32[]{:S(2)}, u32[]{:S(2)}) collective-permute-start(bf16[7,2,16,32,128]{4,3,2,1,0:T(8,128)(2,1)} %slice.8), channel_id=1, source_target_pairs={{1,2},{3,4},{5,6},{7,8},{9,10},{11,12},{13,14},{2,1},{4,3},{6,5},{... | collective-permute-start | bytes 5505032 | tf_op jit(solution)/shard_map/ppermute | solution.py:299
  46.8 71.0 %collective-permute-start.3 = (bf16[4,2,16,32,128]{4,3,2,1,0:T(8,128)(2,1)}, bf16[4,2,16,32,128]{4,3,2,1,0:T(8,128)(2,1)}, u32[]{:S(2)}, u32[]{:S(2)}) collective-permute-start(bf16[4,2,16,32,128]{4,3,2,1,0:T(8,128)(2,1)} %slice.9), channel_id=1, source_target_pairs={{1,2},{3,4},{5,6},{7,8},{9,10},{11,12},{13,14},{2,1},{4,3},{6,5},{... | collective-permute-start | bytes 3145736 | tf_op jit(solution)/shard_map/ppermute | solution.py:299
  53.2 43.7 %copy-start.1 = (bf16[5,2,16,32,128]{4,3,2,1,0:T(8,128)(2,1)S(1)}, bf16[5,2,16,32,128]{4,3,2,1,0:T(8,128)(2,1)}, u32[]{:S(2)}) copy-start(bf16[5,2,16,32,128]{4,3,2,1,0:T(8,128)(2,1)} %pack_first.1.refs_2_.refs_3_) | copy-start | bytes 3932164
  57.8 60.0 %collective-permute-start.4 = (f32[2,32,128]{2,1,0:T(8,128)}, f32[2,32,128]{2,1,0:T(8,128)S(1)}, u32[]{:S(2)}, u32[]{:S(2)}) collective-permute-start(f32[2,32,128]{2,1,0:T(8,128)} %get-tuple-element.17), channel_id=1, source_target_pairs={{0,1},{2,3},{4,5},{6,7},{8,9},{10,11},{12,13},{14,15},{1,0},{3,2},... | collective-permute-start | bytes 98312 | tf_op jit(solution)/shard_map/ppermute | solution.py:358
  58.7 59.1 %collective-permute-start.5 = (f32[2,32,128]{2,1,0:T(8,128)}, f32[2,32,128]{2,1,0:T(8,128)S(1)}, u32[]{:S(2)}, u32[]{:S(2)}) collective-permute-start(f32[2,32,128]{2,1,0:T(8,128)} %get-tuple-element.18), channel_id=1, source_target_pairs={{1,2},{3,4},{5,6},{7,8},{9,10},{11,12},{13,14},{2,1},{4,3},{6,5},{... | collective-permute-start | bytes 98312 | tf_op jit(solution)/shard_map/ppermute | solution.py:359
  96.9 2.2 %copy-start = (bf16[16,2,16,32,128]{4,3,2,1,0:T(8,128)(2,1)S(1)}, bf16[16,2,16,32,128]{4,3,2,1,0:T(8,128)(2,1)}, u32[]{:S(2)}) copy-start(bf16[16,2,16,32,128]{4,3,2,1,0:T(8,128)(2,1)} %pack.1.refs_0_.refs_1_) | copy-start | bytes 12582916

commit v7 on v6

--- a/solution.py
+++ b/solution.py
@@ -15,10 +15,12 @@
 SUB = 16
 SPAN = 3
 RATE = 50
+PACK = 8000
 
 CHUNKS = ((16, 4, 3, 2, 1), (11, 10, 9, 8, 7, 6, 5), (15, 14, 13, 12))
 NEAR = (5, 4, 6, 3, 7, 2, 8)
 FAR = (1, 9, 0, 10)
+ALL = NEAR + FAR
 SCOPED = 14 * 2**20
 
 VMEM = pl.BlockSpec(memory_space=pltpu.VMEM)
@@ -28,87 +30,79 @@
 SMEM = pl.BlockSpec(memory_space=pltpu.SMEM)
 
 
-def pack_kernel(rows, order_ref, s_ref, r_ref, out_ref, flip):
+def pack_kernel(core_ref, s_ref, r_ref, *refs):
+    out_ref, flip = refs[-2:]
     _, parts, freqs, width = s_ref.shape
-    for row in range(rows):
-        src_row = jnp.where(order_ref[0] == 1, row, rows - 1 - row)
-        for field, src in enumerate((s_ref, r_ref)):
-            for p in range(parts):
-                for g in range(width // (SUB * LANES)):
-                    slot = flip.at[(field * parts + p) * 2 + g % 2]
-                    for t in range(SUB):
-                        c = (g * SUB + t) * LANES
-                        slot[pl.ds(t, freqs, SUB), :] = src[src_row, p, :, c : c + LANES].astype(
-                            jnp.float32
-                        )
-                    for f in range(freqs):
-                        out_ref[row, field, p * freqs + f, g * SUB : (g + 1) * SUB] = slot[
-                            f * SUB : (f + 1) * SUB
-                        ].astype(jnp.bfloat16)
-
-
-def pack(straight, rows, steps, source, receiver, places, weight, name):
-    _, parts, freqs, width = source.shape
+    for field, src in enumerate((s_ref, r_ref)):
+        for p in range(parts):
+            for g in range(width // (SUB * LANES)):
+                slot = flip.at[(field * parts + p) * 2 + g % 2]
+                for t in range(SUB):
+                    c = (g * SUB + t) * LANES
+                    slot[pl.ds(t, freqs, SUB), :] = src[0, p, :, c : c + LANES].astype(jnp.float32)
+                for f in range(freqs):
+                    out_ref[0, field, p * freqs + f, g * SUB : (g + 1) * SUB] = slot[
+                        f * SUB : (f + 1) * SUB
+                    ].astype(jnp.bfloat16)
+
+
+def pack(core, source, receiver, chunk, earlier, name):
+    cells, parts, freqs, width = source.shape
     tiles = width // LANES
 
-    def spec(base):
-        return pl.BlockSpec(
-            (rows, parts, freqs, width),
-            lambda i, order: (base + places[2] * jnp.where(order[0] == 1, i, steps - 1 - i), 0, 0, 0),
-        )
-
+    def at(i, core):
+        row = jnp.int32(cells - chunk[0])
+        for k in range(1, len(chunk)):
+            row = jnp.where(i == k, cells - chunk[k], row)
+        return (jnp.where(core[0] == 1, row, cells - 1 - row), 0, 0, 0)
+
+    spec = pl.BlockSpec((1, parts, freqs, width), at)
     return pl.pallas_call(
-        functools.partial(pack_kernel, rows),
+        pack_kernel,
         grid_spec=pltpu.PrefetchScalarGridSpec(
             num_scalar_prefetch=1,
-            grid=(steps,),
-            in_specs=[spec(places[0]), spec(places[1])],
+            grid=(len(chunk),),
+            in_specs=[spec, spec] + [VMEM] * len(earlier),
             out_specs=pl.BlockSpec(
-                (rows, 2, parts * freqs, tiles, LANES), lambda i, order: (i, 0, 0, 0, 0)
+                (1, 2, parts * freqs, tiles, LANES), lambda i, core: (i, 0, 0, 0, 0)
             ),
             scratch_shapes=[pltpu.VMEM((4 * parts, SUB * freqs, LANES), jnp.float32)],
         ),
         out_shape=jax.ShapeDtypeStruct(
-            (rows * steps, 2, parts * freqs, tiles, LANES), jnp.bfloat16
+            (len(chunk), 2, parts * freqs, tiles, LANES), jnp.bfloat16
         ),
         cost_estimate=pl.CostEstimate(
-            flops=weight * 8 * rows * steps * parts * freqs * width,
-            bytes_accessed=8 * rows * steps * parts * freqs * width,
+            flops=0 if earlier else PACK * len(chunk) * parts * freqs * width,
+            bytes_accessed=8 * len(chunk) * parts * freqs * width,
             transcendentals=0,
         ),
         name=name,
-    )(straight, source, receiver)
-
-
-def first_kernel(core_ref, s_ref, r_ref, out_ref):
-    out_ref[0, 0] = s_ref[0]
-    out_ref[0, 1] = r_ref[0]
-
-
-def first_rows(core, forward_field, adjoint_field):
-    cells, parts, freqs, width = forward_field.shape
-    rows = [cells - i for i in CHUNKS[0]]
-
-    def at(i, core):
-        row = jnp.int32(rows[0])
-        for k in range(1, len(rows)):
-            row = jnp.where(i == k, rows[k], row)
-        return (jnp.where(core[0] == 1, row, cells - 1 - row), 0, 0, 0)
-
-    spec = pl.BlockSpec((1, parts, freqs, width), at)
+    )(core, source, receiver, *earlier)
+
+
+def join_kernel(earlier_ref, *refs):
+    ins, (out_ref, sems) = refs[:-2], refs[-2:]
+    copies, at = [], 0
+    for k, ref in enumerate(ins):
+        n = ref.shape[0]
+        copies.append(pltpu.make_async_copy(ref, out_ref.at[pl.ds(at, n)], sems.at[k]))
+        at += n
+    for copy in copies:
+        copy.start()
+    for copy in copies:
+        copy.wait()
+
+
+def join(pieces, earlier):
+    rows = sum(p.shape[0] for p in pieces)
     return pl.pallas_call(
-        first_kernel,
-        grid_spec=pltpu.PrefetchScalarGridSpec(
-            num_scalar_prefetch=1,
-            grid=(len(rows),),
-            in_specs=[spec, spec],
-            out_specs=pl.BlockSpec(
-                (1, 2, parts, freqs, width), lambda i, core: (i, 0, 0, 0, 0)
-            ),
-        ),
-        out_shape=jax.ShapeDtypeStruct((len(rows), 2, parts, freqs, width), jnp.bfloat16),
-        name="first",
-    )(core, forward_field, adjoint_field)
+        join_kernel,
+        in_specs=[VMEM] + [ANY] * len(pieces),
+        out_specs=ANY,
+        out_shape=jax.ShapeDtypeStruct((rows, *pieces[0].shape[1:]), pieces[0].dtype),
+        scratch_shapes=[pltpu.SemaphoreType.DMA((len(pieces),))],
+        name="join",
+    )(earlier, *pieces)
 
 
 def rim_kernel(cells, where, *refs):
@@ -274,37 +268,20 @@
     links = sum(exchange(peers), [])
     row_bytes = 2 * terms * width * 2
 
-    def spans_of(rows):
-        spans = []
-        for r in rows:
-            if spans and spans[-1][1] == r:
-                spans[-1][1] = r + 1
-            else:
-                spans.append([r, r + 1])
-        return spans
-
-    def cut(field, rows):
-        return [lax.slice_in_dim(field, a, b, axis=0) for a, b in spans_of(rows)]
-
-    n = len(CHUNKS[0])
-    raw = first_rows(core, forward_field, adjoint_field)
-    raw, forward_field, adjoint_field = lax.optimization_barrier(
-        (raw, forward_field, adjoint_field)
-    )
-    raw = lax.ppermute(raw, "gx", links).reshape(2 * n, parts, freqs, width)
-    own = pack(core, 2, cells // 2, forward_field, adjoint_field, (0, 0, 1), RATE, "pack")
-    arrived = [None]
-    for g, chunk in enumerate(CHUNKS[1:], 1):
-        sent = jnp.concatenate(cut(own, [cells - i for i in chunk]), axis=0)
-        arrived.append(lax.ppermute(sent, "gx", links))
-    swap, raw = lax.optimization_barrier((own, raw))
-    arrived[0] = pack(jnp.ones_like(core), 1, n, raw, raw, (0, 1, 2), RATE, "pack_first")
-    beside = lax.ppermute(swap, "gx", cores)
+    own = []
+    arrived = []
+    for g, chunk in enumerate(CHUNKS):
+        own.append(pack(core, forward_field, adjoint_field, chunk, [], "pack_%d" % g))
+        arrived.append(lax.ppermute(own[g], "gx", links))
+    beside = lax.ppermute(join(own, arrived[0][0, 0, 0]), "gx", cores)
 
     def layout(count):
-        operands = [own, beside]
-        where = {a: (0, a) for a in range(cells)}
-        where.update({-1 - a: (1, a) for a in range(cells)})
+        operands = own + [beside]
+        where = {}
+        order = [i for chunk in CHUNKS for i in chunk]
+        for g, chunk in enumerate(CHUNKS):
+            where.update({cells - i: (g, k) for k, i in enumerate(chunk)})
+        where.update({i - cells - 1: (len(own), k) for k, i in enumerate(order)})
         for chunk, got in zip(CHUNKS[:count], arrived):
             where.update({cells - 1 + i: (len(operands), k) for k, i in enumerate(chunk)})
             operands.append(got)
@@ -339,7 +316,7 @@
                 (len(blocks), BLOCK, cells + 2, tiles, LANES), jnp.float32
             ),
             compiler_params=pltpu.CompilerParams(vmem_limit_bytes=SCOPED),
-            cost_estimate=cost(pairs, 0),
+            cost_estimate=cost(pairs if done else 0, 0),
             name=name,
         )(*operands)
         return out, (set(where), blocks)
@@ -351,7 +328,7 @@
         out_specs=[VMEM, VMEM],
         out_shape=[jax.ShapeDtypeStruct((2, tiles, LANES), jnp.float32)] * 2,
         cost_estimate=pl.CostEstimate(
-            flops=RATE * 8 * terms * width, bytes_accessed=6 * row_bytes, transcendentals=0
+            flops=0, bytes_accessed=0, transcendentals=0
         ),
         name="rim",
     )(*operands)
@@ -390,10 +367,10 @@
             name=name,
         )(*operands)
 
-    last = len(CHUNKS) - 1
-    image = lags("near", None, last, NEAR, [], [], [])
-    sums, stage = partial("partial", last, FAR, ())
-    return lags("far", image, last + 1, FAR, [sums], [stage], [rim_lo, rim_hi])
+    inner, first = partial("inner", 1, ALL, ())
+    image = lags("near", None, 2, NEAR, [inner], [first], [])
+    middle, second = partial("middle", 2, FAR, first[0])
+    return lags("far", image, 3, FAR, [inner, middle], [first, second], [rim_lo, rim_hi])
 
 
 def solution(mesh):

time: 124 us -> 245 us (1.98)
  Pallas kernels: 45.1 us -> 177 us
  waiting for transfers between devices: 56.5 us -> 50.8 us
  local copies, waits for them, and re-layouts: 8.08 us -> 2.38 us
    pallas_call x3 -> x4, Pallas kernels: 16.1 us -> 143 us  [the longest x1 129 us: join(): pl.pallas_call(join_kernel, in_specs=[VMEM] + [ANY] * len(pieces), out_sp...]
    pallas_call x1 -> x2, Pallas kernels: 5.28 us -> 15 us  [partial(): pl.pallas_call(functools.partial(part_kernel, cells, blocks, where, done)...]
    slice x2 -> x0, local copies, waits for them, and re-layouts: 5.88 us -> none  [cut(): return [lax.slice_in_dim(field, a, b, axis=0) for a, b in spans_of(rows)]]
    ppermute x4, waiting for transfers between devices: 56.5 us -> 50.8 us  [the longest x3 49 us: on_device(): arrived.append(lax.ppermute(own[g], 'gx', links))]
    pallas_call x2, Pallas kernels: 19.2 us -> 15.3 us  [lags(): pl.pallas_call(functools.partial(lag_kernel, cells, blocks, where, stages...]
  transfers between devices with their start and end apart: 6 -> 6, of which waited for: 2 -> 3; matrix products, arithmetic and copies ran while one was open for 5% -> 0% of each run, Pallas kernels for 29% -> 15%
where the time goes in v7:
time: 245 us; the launch traced here: 244 us
  Pallas kernels  177 us (72%)
  waiting for transfers between devices  50.8 us (21%)
  starting transfers between devices  13.2 us (5%)
    pallas_call x1, Pallas kernels, join(): pl.pallas_call(join_kernel, in_specs=[VMEM] + [ANY] * len(pieces), out_sp...  129 us
    ppermute x3, waiting for transfers between devices, on_device(): arrived.append(lax.ppermute(own[g], 'gx', links))  49 us
    pallas_call x2, Pallas kernels, lags(): pl.pallas_call(functools.partial(lag_kernel, cells, blocks, where, stages...  15.3 us
    pallas_call x2, Pallas kernels, partial(): pl.pallas_call(functools.partial(part_kernel, cells, blocks, where, done)...  15 us
    pallas_call x3, Pallas kernels, pack(): pl.pallas_call(pack_kernel, grid_spec=pltpu.PrefetchScalarGridSpec(num_sc...  13.9 us
    ppermute x3, starting transfers between devices, on_device(): arrived.append(lax.ppermute(own[g], 'gx', links))  9.39 us
  transfers between devices with their start and end apart: 6, of which 3 were waited for; matrix products, arithmetic and copies ran while one was open for 0% of the time, Pallas kernels for 15%

profile of v7, /device:TPU:17, one launch (start us, length us, event | category | flops | bytes accessed | tf_op | source)
XLA Modules:
  0.0 244.1 jit_solution(17127781110845963687)
XLA Ops:
  0.0 4.4 %pack_0.1.refs_0_.refs_1_ = bf16[5,2,16,32,128]{4,3,2,1,0:T(8,128)(2,1)} custom-call(s32[1]{0:T(128)} %bitcast.core_ref.refs_0_, bf16[16,2,8,4096]{3,2,1,0:T(8,128)(2,1)} %s_ref.5, bf16[16,2,8,4096]{3,2,1,0:T(8,128)(2,1)} %r_ref.5), custom_call_target="tpu_custom_call" | custom-call | flops 2621440000 | bytes 2621440 | tf_op jit(solution)/shard_map/pack_0/pallas_call | solution.py:60
  4.4 3.7 %collective-permute-start = (bf16[5,2,16,32,128]{4,3,2,1,0:T(8,128)(2,1)}, bf16[5,2,16,32,128]{4,3,2,1,0:T(8,128)(2,1)S(1)}, u32[]{:S(2)}, u32[]{:S(2)}) collective-permute-start(bf16[5,2,16,32,128]{4,3,2,1,0:T(8,128)(2,1)} %pack_0.1.refs_0_.refs_1_), channel_id=1, source_target_pairs={{1,2},{3,4},{5,6},{7,8},{9,10},{11,12},{13,14},{2,1},{4,3},{6,5},{... | collective-permute-start | bytes 3932168 | tf_op jit(solution)/shard_map/ppermute | solution.py:275
  8.1 3.7 %pack_2.1.refs_2_.refs_3_ = bf16[4,2,16,32,128]{4,3,2,1,0:T(8,128)(2,1)} custom-call(s32[1]{0:T(128)} %bitcast.core_ref.refs_0_, bf16[16,2,8,4096]{3,2,1,0:T(8,128)(2,1)} %s_ref.5, bf16[16,2,8,4096]{3,2,1,0:T(8,128)(2,1)} %r_ref.5), custom_call_target="tpu_custom_call" | custom-call | flops 2097152000 | bytes 2097152 | tf_op jit(solution)/shard_map/pack_2/pallas_call | solution.py:60
  11.9 5.7 %pack_1.1.refs_1_.refs_2_ = bf16[7,2,16,32,128]{4,3,2,1,0:T(8,128)(2,1)} custom-call(s32[1]{0:T(128)} %bitcast.core_ref.refs_0_, bf16[16,2,8,4096]{3,2,1,0:T(8,128)(2,1)} %s_ref.5, bf16[16,2,8,4096]{3,2,1,0:T(8,128)(2,1)} %r_ref.5), custom_call_target="tpu_custom_call" | custom-call | flops 3670016000 | bytes 3670016 | tf_op jit(solution)/shard_map/pack_1/pallas_call | solution.py:60
  17.6 20.1 %collective-permute-done.refs_4_.refs_5_ = bf16[5,2,16,32,128]{4,3,2,1,0:T(8,128)(2,1)S(1)} collective-permute-done((bf16[5,2,16,32,128]{4,3,2,1,0:T(8,128)(2,1)}, bf16[5,2,16,32,128]{4,3,2,1,0:T(8,128)(2,1)S(1)}, u32[]{:S(2)}, u32[]{:S(2)}) %collective-permute-start) | collective-permute-done | bytes 1310752 | tf_op jit(solution)/shard_map/ppermute | solution.py:275
  37.7 0.0 copy-start.3
  37.7 0.6 slice_bitcast_fusion.earlier_ref
  38.3 0.4 copy-done.3
  38.7 0.0 copy-start.1
  38.7 129.0 %join.1 = bf16[16,2,16,32,128]{4,3,2,1,0:T(8,128)(2,1)} custom-call(bf16[32,128]{1,0:T(8,128)(2,1)} %slice_bitcast_fusion.earlier_ref, bf16[5,2,16,32,128]{4,3,2,1,0:T(8,128)(2,1)} %pack_0.1.refs_0_.refs_1_, bf16[7,2,16,32,128]{4,3,2,1,0:T(8,128)(2,1)} %pack_1.1.refs_1_.refs_2_, bf16[4,2,16,32,128]{4,3,2,1,0:T(8,128)(2,1)} %pack_2.1.refs_2_.refs_3_), custom_call_target="tpu_custom_call" | custom-call | tf_op jit(solution)/shard_map/join/pallas_call | solution.py:98
  167.7 0.0 copy-start
  167.7 0.0 copy-start.2
  167.7 0.1 collective-permute-start.1
  167.8 3.8 %collective-permute-start.2 = (bf16[7,2,16,32,128]{4,3,2,1,0:T(8,128)(2,1)}, bf16[7,2,16,32,128]{4,3,2,1,0:T(8,128)(2,1)}, u32[]{:S(2)}, u32[]{:S(2)}) collective-permute-start(bf16[7,2,16,32,128]{4,3,2,1,0:T(8,128)(2,1)} %pack_1.1.refs_1_.refs_2_), channel_id=1, source_target_pairs={{1,2},{3,4},{5,6},{7,8},{9,10},{11,12},{13,14},{2,1},{4,3},{6,5},{... | collective-permute-start | bytes 5505032 | tf_op jit(solution)/shard_map/ppermute | solution.py:275
  171.6 0.0 copy-done.1
  171.6 1.9 collective-permute-start.3
  173.5 1.8 collective-permute-done.1.refs_3_.refs_4_
  175.3 4.5 %rim.1 = (f32[2,32,128]{2,1,0:T(8,128)}, f32[2,32,128]{2,1,0:T(8,128)}) custom-call(bf16[5,2,16,32,128]{4,3,2,1,0:T(8,128)(2,1)} %pack_0.1.refs_0_.refs_1_, bf16[7,2,16,32,128]{4,3,2,1,0:T(8,128)(2,1)} %pack_1.1.refs_1_.refs_2_, bf16[4,2,16,32,128]{4,3,2,1,0:T(8,128)(2,1)} %pack_2.1.refs_2_.refs_3_, ...), custom_call_target="tpu_custom_call" | custom-call | tf_op jit(solution)/shard_map/rim/pallas_call | solution.py:325
  179.8 0.1 collective-permute-start.4
  179.9 3.6 %collective-permute-start.5 = (f32[2,32,128]{2,1,0:T(8,128)}, f32[2,32,128]{2,1,0:T(8,128)S(1)}, u32[]{:S(2)}, u32[]{:S(2)}) collective-permute-start(f32[2,32,128]{2,1,0:T(8,128)} %get-tuple-element.8), channel_id=1, source_target_pairs={{1,2},{3,4},{5,6},{7,8},{9,10},{11,12},{13,14},{2,1},{4,3},{6,5},{... | collective-permute-start | bytes 98312 | tf_op jit(solution)/shard_map/ppermute | solution.py:336
  183.5 0.0 copy-done
  183.5 0.0 copy-done.2
  183.6 0.0 copy-start.4
  183.6 1.3 copy-done.4
  184.9 0.0 copy-start.5
  184.9 10.2 %inner.1.refs_7_.refs_8_ = f32[11,3,18,32,128]{4,3,2,1,0:T(8,128)S(1)} custom-call(bf16[5,2,16,32,128]{4,3,2,1,0:T(8,128)(2,1)S(1)} %copy-done, bf16[7,2,16,32,128]{4,3,2,1,0:T(8,128)(2,1)} %pack_1.1.refs_1_.refs_2_, bf16[4,2,16,32,128]{4,3,2,1,0:T(8,128)(2,1)S(1)} %copy-done.2, bf16[16,2,16,32,128]{4,3,2,1,0:T(8,128)(2,1)} %collective-permute-done.1.refs_3_.refs_4_, ...), custom_call_target="tpu_custom_call" | custom-call | tf_op jit(solution)/shard_map/inner/pallas_call | solution.py:311
  195.1 28.9 %collective-permute-done.2.refs_5_.refs_6_ = bf16[7,2,16,32,128]{4,3,2,1,0:T(8,128)(2,1)} collective-permute-done((bf16[7,2,16,32,128]{4,3,2,1,0:T(8,128)(2,1)}, bf16[7,2,16,32,128]{4,3,2,1,0:T(8,128)(2,1)}, u32[]{:S(2)}, u32[]{:S(2)}) %collective-permute-start.2) | collective-permute-done | bytes 1835040 | tf_op jit(solution)/shard_map/ppermute | solution.py:275
  224.1 0.0 copy-done.5
  224.1 8.5 %near.1.refs_12_ = f32[33,16,4096]{2,1,0:T(8,128)} custom-call(s32[1]{0:T(128)} %bitcast.core_ref.refs_0_, bf16[5,2,16,32,128]{4,3,2,1,0:T(8,128)(2,1)S(1)} %copy-done, bf16[7,2,16,32,128]{4,3,2,1,0:T(8,128)(2,1)} %pack_1.1.refs_1_.refs_2_, bf16[4,2,16,32,128]{4,3,2,1,0:T(8,128)(2,1)S(1)} %copy-done.2, ...), custom_call_target="tpu_custom_call" | custom-call | flops 1743257600 | bytes 5505024 | tf_op jit(solution)/shard_map/near/pallas_call | solution.py:351
  232.6 4.7 %middle.1.refs_9_ = f32[4,3,18,32,128]{4,3,2,1,0:T(8,128)S(1)} custom-call(bf16[5,2,16,32,128]{4,3,2,1,0:T(8,128)(2,1)S(1)} %copy-done, bf16[7,2,16,32,128]{4,3,2,1,0:T(8,128)(2,1)} %pack_1.1.refs_1_.refs_2_, bf16[4,2,16,32,128]{4,3,2,1,0:T(8,128)(2,1)S(1)} %copy-done.2, bf16[16,2,16,32,128]{4,3,2,1,0:T(8,128)(2,1)} %collective-permute-done.1.refs_3_.refs_4_, ...), custom_call_target="tpu_custom_call" | custom-call | flops 550502400 | tf_op jit(solution)/shard_map/middle/pallas_call | solution.py:311
  237.3 0.0 collective-permute-done.3.refs_7_
  237.3 0.0 collective-permute-done.4.refs_10_
  237.3 0.0 collective-permute-done.5.refs_11_
  237.3 6.8 %far.1 = f32[33,16,4096]{2,1,0:T(8,128)} custom-call(s32[1]{0:T(128)} %bitcast.core_ref.refs_0_, bf16[5,2,16,32,128]{4,3,2,1,0:T(8,128)(2,1)S(1)} %copy-done, bf16[7,2,16,32,128]{4,3,2,1,0:T(8,128)(2,1)} %pack_1.1.refs_1_.refs_2_, bf16[4,2,16,32,128]{4,3,2,1,0:T(8,128)(2,1)S(1)} %copy-done.2, ...), custom_call_target="tpu_custom_call", output_to_operand_aliasing={{}: (12, {})} | custom-call | flops 1022361600 | bytes 3145728 | tf_op jit(solution)/shard_map/far/pallas_call | solution.py:351
Async XLA Ops:
  4.4 33.2 %collective-permute-start = (bf16[5,2,16,32,128]{4,3,2,1,0:T(8,128)(2,1)}, bf16[5,2,16,32,128]{4,3,2,1,0:T(8,128)(2,1)S(1)}, u32[]{:S(2)}, u32[]{:S(2)}) collective-permute-start(bf16[5,2,16,32,128]{4,3,2,1,0:T(8,128)(2,1)} %pack_0.1.refs_0_.refs_1_), channel_id=1, source_target_pairs={{1,2},{3,4},{5,6},{7,8},{9,10},{11,12},{13,14},{2,1},{4,3},{6,5},{... | collective-permute-start | bytes 3932168 | tf_op jit(solution)/shard_map/ppermute | solution.py:275
  37.7 1.1 copy-start.3
  38.7 132.9 %copy-start.1 = (bf16[4,2,16,32,128]{4,3,2,1,0:T(8,128)(2,1)S(1)}, bf16[4,2,16,32,128]{4,3,2,1,0:T(8,128)(2,1)}, u32[]{:S(2)}) copy-start(bf16[4,2,16,32,128]{4,3,2,1,0:T(8,128)(2,1)} %pack_2.1.refs_2_.refs_3_) | copy-start | bytes 3145732
  167.7 15.8 %copy-start = (bf16[5,2,16,32,128]{4,3,2,1,0:T(8,128)(2,1)S(1)}, bf16[5,2,16,32,128]{4,3,2,1,0:T(8,128)(2,1)}, u32[]{:S(2)}) copy-start(bf16[5,2,16,32,128]{4,3,2,1,0:T(8,128)(2,1)} %pack_0.1.refs_0_.refs_1_) | copy-start | bytes 3932164
  167.7 15.8 %copy-start.2 = (bf16[4,2,16,32,128]{4,3,2,1,0:T(8,128)(2,1)S(1)}, bf16[4,2,16,32,128]{4,3,2,1,0:T(8,128)(2,1)}, u32[]{:S(2)}) copy-start(bf16[4,2,16,32,128]{4,3,2,1,0:T(8,128)(2,1)} %pack_2.1.refs_2_.refs_3_) | copy-start | bytes 3145732
  167.7 7.6 %collective-permute-start.1 = (bf16[16,2,16,32,128]{4,3,2,1,0:T(8,128)(2,1)}, bf16[16,2,16,32,128]{4,3,2,1,0:T(8,128)(2,1)}, u32[]{:S(2)}, u32[]{:S(2)}) collective-permute-start(bf16[16,2,16,32,128]{4,3,2,1,0:T(8,128)(2,1)} %join.1), channel_id=1, source_target_pairs={{0,1},{2,3},{4,5},{6,7},{8,9},{10,11},{12,13},{14,15},{1,0},{3,2},... | collective-permute-start | bytes 12582920 | tf_op jit(solution)/shard_map/ppermute | solution.py:276
  167.8 56.2 %collective-permute-start.2 = (bf16[7,2,16,32,128]{4,3,2,1,0:T(8,128)(2,1)}, bf16[7,2,16,32,128]{4,3,2,1,0:T(8,128)(2,1)}, u32[]{:S(2)}, u32[]{:S(2)}) collective-permute-start(bf16[7,2,16,32,128]{4,3,2,1,0:T(8,128)(2,1)} %pack_1.1.refs_1_.refs_2_), channel_id=1, source_target_pairs={{1,2},{3,4},{5,6},{7,8},{9,10},{11,12},{13,14},{2,1},{4,3},{6,5},{... | collective-permute-start | bytes 5505032 | tf_op jit(solution)/shard_map/ppermute | solution.py:275
  171.6 65.7 %collective-permute-start.3 = (bf16[4,2,16,32,128]{4,3,2,1,0:T(8,128)(2,1)S(1)}, bf16[4,2,16,32,128]{4,3,2,1,0:T(8,128)(2,1)}, u32[]{:S(2)}, u32[]{:S(2)}) collective-permute-start(bf16[4,2,16,32,128]{4,3,2,1,0:T(8,128)(2,1)S(1)} %copy-done.1), channel_id=1, source_target_pairs={{1,2},{3,4},{5,6},{7,8},{9,10},{11,12},{13,14},{2,1},{4,3},{6,5},{... | collective-permute-start | bytes 3145736 | tf_op jit(solution)/shard_map/ppermute | solution.py:275
  179.8 57.5 %collective-permute-start.4 = (f32[2,32,128]{2,1,0:T(8,128)}, f32[2,32,128]{2,1,0:T(8,128)S(1)}, u32[]{:S(2)}, u32[]{:S(2)}) collective-permute-start(f32[2,32,128]{2,1,0:T(8,128)} %get-tuple-element.7), channel_id=1, source_target_pairs={{0,1},{2,3},{4,5},{6,7},{8,9},{10,11},{12,13},{14,15},{1,0},{3,2},... | collective-permute-start | bytes 98312 | tf_op jit(solution)/shard_map/ppermute | solution.py:335
  179.9 57.4 %collective-permute-start.5 = (f32[2,32,128]{2,1,0:T(8,128)}, f32[2,32,128]{2,1,0:T(8,128)S(1)}, u32[]{:S(2)}, u32[]{:S(2)}) collective-permute-start(f32[2,32,128]{2,1,0:T(8,128)} %get-tuple-element.8), channel_id=1, source_target_pairs={{1,2},{3,4},{5,6},{7,8},{9,10},{11,12},{13,14},{2,1},{4,3},{6,5},{... | collective-permute-start | bytes 98312 | tf_op jit(solution)/shard_map/ppermute | solution.py:336
  183.6 1.3 copy-start.4
  184.9 39.2 %copy-start.5 = (bf16[5,2,16,32,128]{4,3,2,1,0:T(8,128)(2,1)S(1)}, bf16[5,2,16,32,128]{4,3,2,1,0:T(8,128)(2,1)}, u32[]{:S(2)}) copy-start(bf16[5,2,16,32,128]{4,3,2,1,0:T(8,128)(2,1)} %copy-done.3) | copy-start | bytes 3932164

commit v8 on v7

--- a/solution.py
+++ b/solution.py
@@ -17,11 +17,12 @@
 RATE = 50
 PACK = 8000
 
-CHUNKS = ((16, 4, 3, 2, 1), (11, 10, 9, 8, 7, 6, 5), (15, 14, 13, 12))
+CHUNKS = ((16, 15, 4, 3, 2, 1), (12, 11, 10, 9, 8, 7, 6, 5), (14, 13))
 NEAR = (5, 4, 6, 3, 7, 2, 8)
 FAR = (1, 9, 0, 10)
 ALL = NEAR + FAR
-SCOPED = 14 * 2**20
+SCOPED = 12 * 2**20
+SMALL = 6 * 2**20
 
 VMEM = pl.BlockSpec(memory_space=pltpu.VMEM)
 ANY = pl.BlockSpec(memory_space=pl.ANY)
@@ -30,41 +31,45 @@
 SMEM = pl.BlockSpec(memory_space=pltpu.SMEM)
 
 
-def pack_kernel(core_ref, s_ref, r_ref, *refs):
-    out_ref, flip = refs[-2:]
-    _, parts, freqs, width = s_ref.shape
-    for field, src in enumerate((s_ref, r_ref)):
-        for p in range(parts):
-            for g in range(width // (SUB * LANES)):
-                slot = flip.at[(field * parts + p) * 2 + g % 2]
-                for t in range(SUB):
-                    c = (g * SUB + t) * LANES
-                    slot[pl.ds(t, freqs, SUB), :] = src[0, p, :, c : c + LANES].astype(jnp.float32)
-                for f in range(freqs):
-                    out_ref[0, field, p * freqs + f, g * SUB : (g + 1) * SUB] = slot[
-                        f * SUB : (f + 1) * SUB
-                    ].astype(jnp.bfloat16)
-
-
-def pack(core, source, receiver, chunk, earlier, name):
+def pack_kernel(core_ref, s_ref, r_ref, out_ref, flip):
+    rows, parts, freqs, width = s_ref.shape
+    for row in range(rows):
+        src_row = jnp.where(core_ref[0] == 1, row, rows - 1 - row)
+        for field, src in enumerate((s_ref, r_ref)):
+            for p in range(parts):
+                for g in range(width // (SUB * LANES)):
+                    slot = flip.at[(field * parts + p) * 2 + g % 2]
+                    for t in range(SUB):
+                        c = (g * SUB + t) * LANES
+                        slot[pl.ds(t, freqs, SUB), :] = src[src_row, p, :, c : c + LANES].astype(
+                            jnp.float32
+                        )
+                    for f in range(freqs):
+                        out_ref[row, field, p * freqs + f, g * SUB : (g + 1) * SUB] = slot[
+                            f * SUB : (f + 1) * SUB
+                        ].astype(jnp.bfloat16)
+
+
+def pack(core, source, receiver, chunk, name):
     cells, parts, freqs, width = source.shape
     tiles = width // LANES
+    pairs = [(cells - i) // 2 for i in chunk[::2]]
 
     def at(i, core):
-        row = jnp.int32(cells - chunk[0])
-        for k in range(1, len(chunk)):
-            row = jnp.where(i == k, cells - chunk[k], row)
-        return (jnp.where(core[0] == 1, row, cells - 1 - row), 0, 0, 0)
-
-    spec = pl.BlockSpec((1, parts, freqs, width), at)
+        pair = jnp.int32(pairs[0])
+        for k in range(1, len(pairs)):
+            pair = jnp.where(i == k, pairs[k], pair)
+        return (jnp.where(core[0] == 1, pair, cells // 2 - 1 - pair), 0, 0, 0)
+
+    spec = pl.BlockSpec((2, parts, freqs, width), at)
     return pl.pallas_call(
         pack_kernel,
         grid_spec=pltpu.PrefetchScalarGridSpec(
             num_scalar_prefetch=1,
-            grid=(len(chunk),),
-            in_specs=[spec, spec] + [VMEM] * len(earlier),
+            grid=(len(pairs),),
+            in_specs=[spec, spec],
             out_specs=pl.BlockSpec(
-                (1, 2, parts * freqs, tiles, LANES), lambda i, core: (i, 0, 0, 0, 0)
+                (2, 2, parts * freqs, tiles, LANES), lambda i, core: (i, 0, 0, 0, 0)
             ),
             scratch_shapes=[pltpu.VMEM((4 * parts, SUB * freqs, LANES), jnp.float32)],
         ),
@@ -72,37 +77,32 @@
             (len(chunk), 2, parts * freqs, tiles, LANES), jnp.bfloat16
         ),
         cost_estimate=pl.CostEstimate(
-            flops=0 if earlier else PACK * len(chunk) * parts * freqs * width,
+            flops=PACK * len(chunk) * parts * freqs * width,
             bytes_accessed=8 * len(chunk) * parts * freqs * width,
             transcendentals=0,
         ),
+        compiler_params=pltpu.CompilerParams(vmem_limit_bytes=SMALL),
         name=name,
-    )(core, source, receiver, *earlier)
-
-
-def join_kernel(earlier_ref, *refs):
-    ins, (out_ref, sems) = refs[:-2], refs[-2:]
-    copies, at = [], 0
-    for k, ref in enumerate(ins):
-        n = ref.shape[0]
-        copies.append(pltpu.make_async_copy(ref, out_ref.at[pl.ds(at, n)], sems.at[k]))
-        at += n
-    for copy in copies:
-        copy.start()
-    for copy in copies:
-        copy.wait()
-
-
-def join(pieces, earlier):
-    rows = sum(p.shape[0] for p in pieces)
+    )(core, source, receiver)
+
+
+def held_kernel(earlier_ref, in_ref, out_ref):
+    def row(k, _):
+        out_ref[k] = in_ref[k]
+        return 0
+
+    lax.fori_loop(0, in_ref.shape[0], row, 0)
+
+
+def held(value, earlier):
     return pl.pallas_call(
-        join_kernel,
-        in_specs=[VMEM] + [ANY] * len(pieces),
-        out_specs=ANY,
-        out_shape=jax.ShapeDtypeStruct((rows, *pieces[0].shape[1:]), pieces[0].dtype),
-        scratch_shapes=[pltpu.SemaphoreType.DMA((len(pieces),))],
-        name="join",
-    )(earlier, *pieces)
+        held_kernel,
+        in_specs=[VMEM, VMEM],
+        out_specs=VMEM,
+        out_shape=jax.ShapeDtypeStruct(value.shape, value.dtype),
+        compiler_params=pltpu.CompilerParams(vmem_limit_bytes=SMALL),
+        name="held",
+    )(earlier, value)
 
 
 def rim_kernel(cells, where, *refs):
@@ -271,9 +271,12 @@
     own = []
     arrived = []
     for g, chunk in enumerate(CHUNKS):
-        own.append(pack(core, forward_field, adjoint_field, chunk, [], "pack_%d" % g))
-        arrived.append(lax.ppermute(own[g], "gx", links))
-    beside = lax.ppermute(join(own, arrived[0][0, 0, 0]), "gx", cores)
+        own.append(pack(core, forward_field, adjoint_field, chunk, "pack_%d" % g))
+        sent = own[g]
+        if g == 2:
+            sent = held(sent, arrived[0][0, 0, 0])
+        arrived.append(lax.ppermute(sent, "gx", links))
+    beside = lax.ppermute(jnp.concatenate(own, axis=0), "gx", cores)
 
     def layout(count):
         operands = own + [beside]
@@ -330,6 +333,7 @@
         cost_estimate=pl.CostEstimate(
             flops=0, bytes_accessed=0, transcendentals=0
         ),
+        compiler_params=pltpu.CompilerParams(vmem_limit_bytes=SMALL),
         name="rim",
     )(*operands)
     rim_lo = lax.ppermute(lo, "gx", cores)

time: 245 us -> 107 us (0.44)
  Pallas kernels: 177 us -> 20.3 us
  waiting for transfers between devices: 50.8 us -> 70.6 us
    pallas_call x1, Pallas kernels: 129 us -> 0.04 us  [held(): pl.pallas_call(held_kernel, in_specs=[VMEM, VMEM], out_specs=VMEM, out_sh...]
    ppermute x4, waiting for transfers between devices: 50.8 us -> 70.6 us  [the longest x3 70.6 us: on_device(): arrived.append(lax.ppermute(sent, 'gx', links))]
    pallas_call x3, Pallas kernels: 13.9 us -> 2.82 us  [pack(): pl.pallas_call(pack_kernel, grid_spec=pltpu.PrefetchScalarGridSpec(num_sc...]
    pallas_call x2, Pallas kernels: 15.3 us -> 8.24 us  [lags(): pl.pallas_call(functools.partial(lag_kernel, cells, blocks, where, stages...]
    pallas_call x2, Pallas kernels: 15 us -> 9.13 us  [partial(): pl.pallas_call(functools.partial(part_kernel, cells, blocks, where, done)...]
    pallas_call x1, Pallas kernels: 4.46 us -> 0.09 us  [on_device(): pl.pallas_call(functools.partial(rim_kernel, cells, where), in_specs=[VME...]
  transfers between devices with their start and end apart: 6 -> 6, of which waited for: 3 -> 2; matrix products, arithmetic and copies ran while one was open for 0% -> 0% of each run, Pallas kernels for 15% -> 14%
where the time goes in v8:
time: 107 us
  waiting for transfers between devices  70.6 us (66%)
  Pallas kernels  20.3 us (19%)
  starting transfers between devices  11.9 us (11%)
  local copies, waits for them, and re-layouts  3.18 us (3%)
    ppermute x3, waiting for transfers between devices, on_device(): arrived.append(lax.ppermute(sent, 'gx', links))  70.6 us
    pallas_call x2, Pallas kernels, partial(): pl.pallas_call(functools.partial(part_kernel, cells, blocks, where, done)...  9.13 us
    ppermute x3, starting transfers between devices, on_device(): arrived.append(lax.ppermute(sent, 'gx', links))  8.61 us
    pallas_call x2, Pallas kernels, lags(): pl.pallas_call(functools.partial(lag_kernel, cells, blocks, where, stages...  8.24 us
    unnamed x4, local copies, waits for them, and re-layouts  3.18 us
    pallas_call x3, Pallas kernels, pack(): pl.pallas_call(pack_kernel, grid_spec=pltpu.PrefetchScalarGridSpec(num_sc...  2.82 us
    ppermute x1, starting transfers between devices, on_device(): rim_hi = lax.ppermute(hi, 'gx', links)  2.5 us
  transfers between devices with their start and end apart: 6, of which 2 were waited for; matrix products, arithmetic and copies ran while one was open for 0% of the time, Pallas kernels for 14%

profile of v8, /device:TPU:17, one launch (start us, length us, event | category | flops | bytes accessed | tf_op | source)
XLA Modules:
  0.0 106.8 jit_solution(11730266383484064596)
XLA Ops:
  0.0 0.0 copy-start
  0.0 1.6 %copy-done = bf16[16,2,8,4096]{3,2,1,0:T(8,128)(2,1)S(1)} copy-done((bf16[16,2,8,4096]{3,2,1,0:T(8,128)(2,1)S(1)}, bf16[16,2,8,4096]{3,2,1,0:T(8,128)(2,1)}, u32[]{:S(2)}) %copy-start) | copy-done | bytes 2097176
  1.6 0.0 copy-start.1
  1.6 1.6 %copy-done.1 = bf16[16,2,8,4096]{3,2,1,0:T(8,128)(2,1)S(1)} copy-done((bf16[16,2,8,4096]{3,2,1,0:T(8,128)(2,1)S(1)}, bf16[16,2,8,4096]{3,2,1,0:T(8,128)(2,1)}, u32[]{:S(2)}) %copy-start.1) | copy-done | bytes 2097176
  3.2 0.3 pack_2.1.in_ref.refs_2_.refs_3_
  3.5 1.1 pack_0.1.refs_0_.refs_1_
  4.6 1.4 %pack_1.1.refs_1_.refs_2_ = bf16[8,2,16,32,128]{4,3,2,1,0:T(8,128)(2,1)S(1)} custom-call(s32[1]{0:T(128)} %bitcast.core_ref.refs_0_, bf16[16,2,8,4096]{3,2,1,0:T(8,128)(2,1)S(1)} %copy-done, bf16[16,2,8,4096]{3,2,1,0:T(8,128)(2,1)S(1)} %copy-done.1), custom_call_target="tpu_custom_call" | custom-call | flops 4194304000 | bytes 4194304 | tf_op jit(solution)/shard_map/pack_1/pallas_call | solution.py:65
  6.0 0.6 pad_maximum_fusion
  6.6 0.7 collective-permute-start
  7.3 3.0 %collective-permute-start.1 = (bf16[6,2,16,32,128]{4,3,2,1,0:T(8,128)(2,1)S(1)}, bf16[6,2,16,32,128]{4,3,2,1,0:T(8,128)(2,1)S(1)}, u32[]{:S(2)}, u32[]{:S(2)}) collective-permute-start(bf16[6,2,16,32,128]{4,3,2,1,0:T(8,128)(2,1)S(1)} %pack_0.1.refs_0_.refs_1_), channel_id=1, source_target_pairs={{1,2},{3,4},{5,6},{7,8},{9,10},{11,12},{13,14},{2,1},{4,3},{6,5},{... | collective-permute-start | bytes 4718600 | tf_op jit(solution)/shard_map/ppermute | solution.py:278
  10.4 2.5 %collective-permute-start.2 = (bf16[8,2,16,32,128]{4,3,2,1,0:T(8,128)(2,1)S(1)}, bf16[8,2,16,32,128]{4,3,2,1,0:T(8,128)(2,1)S(1)}, u32[]{:S(2)}, u32[]{:S(2)}) collective-permute-start(bf16[8,2,16,32,128]{4,3,2,1,0:T(8,128)(2,1)S(1)} %pack_1.1.refs_1_.refs_2_), channel_id=1, source_target_pairs={{1,2},{3,4},{5,6},{7,8},{9,10},{11,12},{13,14},{2,1},{4,3},{6,5},{... | collective-permute-start | bytes 6291464 | tf_op jit(solution)/shard_map/ppermute | solution.py:278
  12.9 61.1 %collective-permute-done.1.refs_4_.refs_5_ = bf16[6,2,16,32,128]{4,3,2,1,0:T(8,128)(2,1)S(1)} collective-permute-done((bf16[6,2,16,32,128]{4,3,2,1,0:T(8,128)(2,1)S(1)}, bf16[6,2,16,32,128]{4,3,2,1,0:T(8,128)(2,1)S(1)}, u32[]{:S(2)}, u32[]{:S(2)}) %collective-permute-start.1) | collective-permute-done | bytes 1572896 | tf_op jit(solution)/shard_map/ppermute | solution.py:278
  74.0 3.1 %collective-permute-start.3 = (bf16[2,2,16,32,128]{4,3,2,1,0:T(8,128)(2,1)S(1)}, bf16[2,2,16,32,128]{4,3,2,1,0:T(8,128)(2,1)S(1)}, u32[]{:S(2)}, u32[]{:S(2)}) collective-permute-start(bf16[2,2,16,32,128]{4,3,2,1,0:T(8,128)(2,1)S(1)} %held.1), channel_id=1, source_target_pairs={{1,2},{3,4},{5,6},{7,8},{9,10},{11,12},{13,14},{2,1},{4,3},{6,5},{... | collective-permute-start | bytes 1572872 | tf_op jit(solution)/shard_map/ppermute | solution.py:278
  77.1 0.0 collective-permute-done.refs_3_.refs_4_
  77.1 0.1 rim.1
  77.2 0.1 collective-permute-start.4
  77.3 2.5 %collective-permute-start.5 = (f32[2,32,128]{2,1,0:T(8,128)S(1)}, f32[2,32,128]{2,1,0:T(8,128)S(1)}, u32[]{:S(2)}, u32[]{:S(2)}) collective-permute-start(f32[2,32,128]{2,1,0:T(8,128)S(1)} %get-tuple-element.8), channel_id=1, source_target_pairs={{1,2},{3,4},{5,6},{7,8},{9,10},{11,12},{13,14},{2,1},{4,3},{6,5},{... | collective-permute-start | bytes 98312 | tf_op jit(solution)/shard_map/ppermute | solution.py:340
  79.8 7.5 %inner.1.refs_7_.refs_8_ = f32[11,3,18,32,128]{4,3,2,1,0:T(8,128)S(1)} custom-call(bf16[6,2,16,32,128]{4,3,2,1,0:T(8,128)(2,1)S(1)} %pack_0.1.refs_0_.refs_1_, bf16[8,2,16,32,128]{4,3,2,1,0:T(8,128)(2,1)S(1)} %pack_1.1.refs_1_.refs_2_, bf16[2,2,16,32,128]{4,3,2,1,0:T(8,128)(2,1)S(1)} %pack_2.1.in_ref.refs_2_.refs_3_, ...), custom_call_target="tpu_custom_call" | custom-call | tf_op jit(solution)/shard_map/inner/pallas_call | solution.py:314
  87.3 9.5 %collective-permute-done.2.refs_5_.refs_6_ = bf16[8,2,16,32,128]{4,3,2,1,0:T(8,128)(2,1)S(1)} collective-permute-done((bf16[8,2,16,32,128]{4,3,2,1,0:T(8,128)(2,1)S(1)}, bf16[8,2,16,32,128]{4,3,2,1,0:T(8,128)(2,1)S(1)}, u32[]{:S(2)}, u32[]{:S(2)}) %collective-permute-start.2) | collective-permute-done | bytes 2097184 | tf_op jit(solution)/shard_map/ppermute | solution.py:278
  96.8 5.3 %near.1.refs_12_ = f32[33,16,4096]{2,1,0:T(8,128)} custom-call(s32[1]{0:T(128)} %bitcast.core_ref.refs_0_, bf16[6,2,16,32,128]{4,3,2,1,0:T(8,128)(2,1)S(1)} %pack_0.1.refs_0_.refs_1_, bf16[8,2,16,32,128]{4,3,2,1,0:T(8,128)(2,1)S(1)} %pack_1.1.refs_1_.refs_2_, bf16[2,2,16,32,128]{4,3,2,1,0:T(8,128)(2,1)S(1)} %pack_2.1.in_ref.refs_2_.refs_3_, ...), custom_call_target="tpu_custom_call" | custom-call | flops 1743257600 | bytes 5505024 | tf_op jit(solution)/shard_map/near/pallas_call | solution.py:355
  102.1 1.7 %middle.1.refs_9_ = f32[4,3,18,32,128]{4,3,2,1,0:T(8,128)S(1)} custom-call(bf16[6,2,16,32,128]{4,3,2,1,0:T(8,128)(2,1)S(1)} %pack_0.1.refs_0_.refs_1_, bf16[8,2,16,32,128]{4,3,2,1,0:T(8,128)(2,1)S(1)} %pack_1.1.refs_1_.refs_2_, bf16[2,2,16,32,128]{4,3,2,1,0:T(8,128)(2,1)S(1)} %pack_2.1.in_ref.refs_2_.refs_3_, ...), custom_call_target="tpu_custom_call" | custom-call | flops 629145600 | tf_op jit(solution)/shard_map/middle/pallas_call | solution.py:314
  103.8 0.0 collective-permute-done.3.refs_7_
  103.8 0.0 collective-permute-done.4.refs_10_
  103.8 0.0 collective-permute-done.5.refs_11_
  103.8 3.0 %far.1 = f32[33,16,4096]{2,1,0:T(8,128)} custom-call(s32[1]{0:T(128)} %bitcast.core_ref.refs_0_, bf16[6,2,16,32,128]{4,3,2,1,0:T(8,128)(2,1)S(1)} %pack_0.1.refs_0_.refs_1_, bf16[8,2,16,32,128]{4,3,2,1,0:T(8,128)(2,1)S(1)} %pack_1.1.refs_1_.refs_2_, bf16[2,2,16,32,128]{4,3,2,1,0:T(8,128)(2,1)S(1)} %pack_2.1.in_ref.refs_2_.refs_3_, ...), custom_call_target="tpu_custom_call", output_to_operand_aliasing={{}: (12, {})} | custom-call | flops 904396800 | bytes 3145728 | tf_op jit(solution)/shard_map/far/pallas_call | solution.py:355
  (2 shorter events, 0.0 us)
Async XLA Ops:
  0.0 1.6 %copy-start = (bf16[16,2,8,4096]{3,2,1,0:T(8,128)(2,1)S(1)}, bf16[16,2,8,4096]{3,2,1,0:T(8,128)(2,1)}, u32[]{:S(2)}) copy-start(bf16[16,2,8,4096]{3,2,1,0:T(8,128)(2,1)} %s_ref.5) | copy-start | bytes 6291460
  1.6 1.6 %copy-start.1 = (bf16[16,2,8,4096]{3,2,1,0:T(8,128)(2,1)S(1)}, bf16[16,2,8,4096]{3,2,1,0:T(8,128)(2,1)}, u32[]{:S(2)}) copy-start(bf16[16,2,8,4096]{3,2,1,0:T(8,128)(2,1)} %r_ref.5) | copy-start | bytes 6291460
  6.6 70.5 %collective-permute-start = (bf16[16,2,16,32,128]{4,3,2,1,0:T(8,128)(2,1)S(1)}, bf16[16,2,16,32,128]{4,3,2,1,0:T(8,128)(2,1)S(1)}, u32[]{:S(2)}, u32[]{:S(2)}) collective-permute-start(bf16[16,2,16,32,128]{4,3,2,1,0:T(8,128)(2,1)S(1)} %pad_maximum_fusion), channel_id=1, source_target_pairs={{0,1},{2,3},{4,5},{6,7},{8,9},{10,11},{12,13},{14,15},{1,0},{3,2},... | collective-permute-start | bytes 12582920 | tf_op jit(solution)/shard_map/ppermute | solution.py:279
  7.3 66.7 %collective-permute-start.1 = (bf16[6,2,16,32,128]{4,3,2,1,0:T(8,128)(2,1)S(1)}, bf16[6,2,16,32,128]{4,3,2,1,0:T(8,128)(2,1)S(1)}, u32[]{:S(2)}, u32[]{:S(2)}) collective-permute-start(bf16[6,2,16,32,128]{4,3,2,1,0:T(8,128)(2,1)S(1)} %pack_0.1.refs_0_.refs_1_), channel_id=1, source_target_pairs={{1,2},{3,4},{5,6},{7,8},{9,10},{11,12},{13,14},{2,1},{4,3},{6,5},{... | collective-permute-start | bytes 4718600 | tf_op jit(solution)/shard_map/ppermute | solution.py:278
  10.4 86.4 %collective-permute-start.2 = (bf16[8,2,16,32,128]{4,3,2,1,0:T(8,128)(2,1)S(1)}, bf16[8,2,16,32,128]{4,3,2,1,0:T(8,128)(2,1)S(1)}, u32[]{:S(2)}, u32[]{:S(2)}) collective-permute-start(bf16[8,2,16,32,128]{4,3,2,1,0:T(8,128)(2,1)S(1)} %pack_1.1.refs_1_.refs_2_), channel_id=1, source_target_pairs={{1,2},{3,4},{5,6},{7,8},{9,10},{11,12},{13,14},{2,1},{4,3},{6,5},{... | collective-permute-start | bytes 6291464 | tf_op jit(solution)/shard_map/ppermute | solution.py:278
  74.0 29.7 %collective-permute-start.3 = (bf16[2,2,16,32,128]{4,3,2,1,0:T(8,128)(2,1)S(1)}, bf16[2,2,16,32,128]{4,3,2,1,0:T(8,128)(2,1)S(1)}, u32[]{:S(2)}, u32[]{:S(2)}) collective-permute-start(bf16[2,2,16,32,128]{4,3,2,1,0:T(8,128)(2,1)S(1)} %held.1), channel_id=1, source_target_pairs={{1,2},{3,4},{5,6},{7,8},{9,10},{11,12},{13,14},{2,1},{4,3},{6,5},{... | collective-permute-start | bytes 1572872 | tf_op jit(solution)/shard_map/ppermute | solution.py:278
  77.2 26.6 %collective-permute-start.4 = (f32[2,32,128]{2,1,0:T(8,128)S(1)}, f32[2,32,128]{2,1,0:T(8,128)S(1)}, u32[]{:S(2)}, u32[]{:S(2)}) collective-permute-start(f32[2,32,128]{2,1,0:T(8,128)S(1)} %get-tuple-element.7), channel_id=1, source_target_pairs={{0,1},{2,3},{4,5},{6,7},{8,9},{10,11},{12,13},{14,15},{1,0},{3,2},... | collective-permute-start | bytes 98312 | tf_op jit(solution)/shard_map/ppermute | solution.py:339
  77.3 26.5 %collective-permute-start.5 = (f32[2,32,128]{2,1,0:T(8,128)S(1)}, f32[2,32,128]{2,1,0:T(8,128)S(1)}, u32[]{:S(2)}, u32[]{:S(2)}) collective-permute-start(f32[2,32,128]{2,1,0:T(8,128)S(1)} %get-tuple-element.8), channel_id=1, source_target_pairs={{1,2},{3,4},{5,6},{7,8},{9,10},{11,12},{13,14},{2,1},{4,3},{6,5},{... | collective-permute-start | bytes 98312 | tf_op jit(solution)/shard_map/ppermute | solution.py:340

commit v9 on v8

--- a/solution.py
+++ b/solution.py
@@ -17,12 +17,13 @@
 RATE = 50
 PACK = 8000
 
-CHUNKS = ((16, 15, 4, 3, 2, 1), (12, 11, 10, 9, 8, 7, 6, 5), (14, 13))
+CHUNKS = ((16, 4, 3, 2, 1), (11, 10, 9, 8, 7, 6, 5), (15, 14, 13, 12))
 NEAR = (5, 4, 6, 3, 7, 2, 8)
 FAR = (1, 9, 0, 10)
 ALL = NEAR + FAR
 SCOPED = 12 * 2**20
 SMALL = 6 * 2**20
+LARGE = 48 * 2**20
 
 VMEM = pl.BlockSpec(memory_space=pltpu.VMEM)
 ANY = pl.BlockSpec(memory_space=pl.ANY)
@@ -31,58 +32,68 @@
 SMEM = pl.BlockSpec(memory_space=pltpu.SMEM)
 
 
-def pack_kernel(core_ref, s_ref, r_ref, out_ref, flip):
-    rows, parts, freqs, width = s_ref.shape
-    for row in range(rows):
-        src_row = jnp.where(core_ref[0] == 1, row, rows - 1 - row)
-        for field, src in enumerate((s_ref, r_ref)):
-            for p in range(parts):
-                for g in range(width // (SUB * LANES)):
-                    slot = flip.at[(field * parts + p) * 2 + g % 2]
-                    for t in range(SUB):
-                        c = (g * SUB + t) * LANES
-                        slot[pl.ds(t, freqs, SUB), :] = src[src_row, p, :, c : c + LANES].astype(
-                            jnp.float32
-                        )
-                    for f in range(freqs):
-                        out_ref[row, field, p * freqs + f, g * SUB : (g + 1) * SUB] = slot[
-                            f * SUB : (f + 1) * SUB
-                        ].astype(jnp.bfloat16)
-
-
-def pack(core, source, receiver, chunk, name):
+def pack_kernel(core_ref, s_ref, r_ref, *refs):
+    outs, (whole_ref, inbox, flip, sems) = refs[:-4], refs[-4:]
+    cells, parts, freqs, width = s_ref.shape
+    order = [cells - i for chunk in CHUNKS for i in chunk]
+
+    def copy(k, field, row):
+        src = (s_ref, r_ref)[field]
+        return pltpu.make_async_copy(src.at[row], inbox.at[k, field], sems.at[k, field])
+
+    for k, row in enumerate(order):
+        for field in (0, 1):
+            copy(k, field, jnp.where(core_ref[0] == 1, row, cells - 1 - row)).start()
+    base = 0
+    for out_ref in outs:
+
+        def one(n, _):
+            k = base + n
+            for field in (0, 1):
+                copy(k, field, 0).wait()
+                for p in range(parts):
+                    for g in range(width // (SUB * LANES)):
+                        slot = flip.at[(field * parts + p) * 2 + g % 2]
+                        for t in range(SUB):
+                            c = (g * SUB + t) * LANES
+                            slot[pl.ds(t, freqs, SUB), :] = inbox[
+                                k, field, p, :, c : c + LANES
+                            ].astype(jnp.float32)
+                        for f in range(freqs):
+                            lines = slot[f * SUB : (f + 1) * SUB].astype(jnp.bfloat16)
+                            at = (field, p * freqs + f, slice(g * SUB, (g + 1) * SUB))
+                            out_ref[(n, *at)] = lines
+                            whole_ref[(k, *at)] = lines
+            return 0
+
+        lax.fori_loop(0, out_ref.shape[0], one, 0)
+        base += out_ref.shape[0]
+
+
+def pack(core, source, receiver):
     cells, parts, freqs, width = source.shape
-    tiles = width // LANES
-    pairs = [(cells - i) // 2 for i in chunk[::2]]
-
-    def at(i, core):
-        pair = jnp.int32(pairs[0])
-        for k in range(1, len(pairs)):
-            pair = jnp.where(i == k, pairs[k], pair)
-        return (jnp.where(core[0] == 1, pair, cells // 2 - 1 - pair), 0, 0, 0)
-
-    spec = pl.BlockSpec((2, parts, freqs, width), at)
+    terms, tiles = parts * freqs, width // LANES
+    counts = [len(chunk) for chunk in CHUNKS] + [cells]
+    hbm = pl.BlockSpec(memory_space=pltpu.HBM)
     return pl.pallas_call(
         pack_kernel,
-        grid_spec=pltpu.PrefetchScalarGridSpec(
-            num_scalar_prefetch=1,
-            grid=(len(pairs),),
-            in_specs=[spec, spec],
-            out_specs=pl.BlockSpec(
-                (2, 2, parts * freqs, tiles, LANES), lambda i, core: (i, 0, 0, 0, 0)
-            ),
-            scratch_shapes=[pltpu.VMEM((4 * parts, SUB * freqs, LANES), jnp.float32)],
-        ),
-        out_shape=jax.ShapeDtypeStruct(
-            (len(chunk), 2, parts * freqs, tiles, LANES), jnp.bfloat16
-        ),
+        in_specs=[SMEM, hbm, hbm],
+        out_specs=[VMEM] * len(counts),
+        out_shape=[
+            jax.ShapeDtypeStruct((n, 2, terms, tiles, LANES), jnp.bfloat16) for n in counts
+        ],
+        scratch_shapes=[
+            pltpu.VMEM((cells, 2, parts, freqs, width), jnp.bfloat16),
+            pltpu.VMEM((4 * parts, SUB * freqs, LANES), jnp.float32),
+            pltpu.SemaphoreType.DMA((cells, 2)),
+        ],
         cost_estimate=pl.CostEstimate(
-            flops=PACK * len(chunk) * parts * freqs * width,
-            bytes_accessed=8 * len(chunk) * parts * freqs * width,
+            flops=PACK * cells * terms * width,
+            bytes_accessed=8 * cells * terms * width,
             transcendentals=0,
         ),
-        compiler_params=pltpu.CompilerParams(vmem_limit_bytes=SMALL),
-        name=name,
+        compiler_params=pltpu.CompilerParams(vmem_limit_bytes=LARGE),
+        name="pack",
     )(core, source, receiver)
 
 
@@ -268,15 +279,13 @@
     links = sum(exchange(peers), [])
     row_bytes = 2 * terms * width * 2
 
-    own = []
+    *own, whole = pack(core, forward_field, adjoint_field)
     arrived = []
-    for g, chunk in enumerate(CHUNKS):
-        own.append(pack(core, forward_field, adjoint_field, chunk, "pack_%d" % g))
-        sent = own[g]
+    for g, sent in enumerate(own):
         if g == 2:
             sent = held(sent, arrived[0][0, 0, 0])
         arrived.append(lax.ppermute(sent, "gx", links))
-    beside = lax.ppermute(jnp.concatenate(own, axis=0), "gx", cores)
+    beside = lax.ppermute(whole, "gx", cores)
 
     def layout(count):
         operands = own + [beside]

time: 107 us -> 106 us (level)
  Pallas kernels: 20.3 us -> 23.6 us
  local copies, waits for them, and re-layouts: 3.18 us -> 0.01 us
    pallas_call x3 -> x1, Pallas kernels: 2.82 us -> 6.14 us  [pack(): pl.pallas_call(pack_kernel, in_specs=[SMEM, hbm, hbm], out_specs=[VMEM] *...]
    unnamed x4 -> x0, local copies, waits for them, and re-layouts: 3.18 us -> none
  transfers between devices with their start and end apart: 6 -> 6, of which waited for: 2 -> 4; matrix products, arithmetic and copies ran while one was open for 0% -> 0% of each run, Pallas kernels for 14% -> 13%
where the time goes in v9:
time: 106 us
  waiting for transfers between devices  70 us (66%)
  Pallas kernels  23.6 us (22%)
  starting transfers between devices  11.9 us (11%)
    ppermute x3, waiting for transfers between devices, on_device(): arrived.append(lax.ppermute(sent, 'gx', links))  69.6 us
    pallas_call x2, Pallas kernels, partial(): pl.pallas_call(functools.partial(part_kernel, cells, blocks, where, done)...  8.81 us
    ppermute x3, starting transfers between devices, on_device(): arrived.append(lax.ppermute(sent, 'gx', links))  8.61 us
    pallas_call x2, Pallas kernels, lags(): pl.pallas_call(functools.partial(lag_kernel, cells, blocks, where, stages...  8.5 us
    pallas_call x1, Pallas kernels, pack(): pl.pallas_call(pack_kernel, in_specs=[SMEM, hbm, hbm], out_specs=[VMEM] *...  6.14 us
    ppermute x1, starting transfers between devices, on_device(): rim_hi = lax.ppermute(hi, 'gx', links)  2.5 us
  transfers between devices with their start and end apart: 6, of which 4 were waited for; matrix products, arithmetic and copies ran while one was open for 0% of the time, Pallas kernels for 13%

profile of v9, /device:TPU:17, one launch (start us, length us, event | category | flops | bytes accessed | tf_op | source)
XLA Modules:
  0.0 105.6 jit_solution(9033274920134063492)
XLA Ops:
  0.0 6.1 %pack.1 = (bf16[5,2,16,32,128]{4,3,2,1,0:T(8,128)(2,1)S(1)}, bf16[7,2,16,32,128]{4,3,2,1,0:T(8,128)(2,1)S(1)}, bf16[4,2,16,32,128]{4,3,2,1,0:T(8,128)(2,1)S(1)}, bf16[16,2,16,32,128]{4,3,2,1,0:T(8,128)(2,1)}) custom-call(s32[1]{0:T(128)} %bitcast.core_ref.refs_0_, bf16[16,2,8,4096]{3,2,1,0:T(8,128)(2,1)} %s_ref.1, bf16[16,2,8,4096]{3,2,1,0:T(8,128)(2,1)} %r_ref.1), custom_call_target="tpu_custom_call" | custom-call | flops 8388608000 | bytes 8388608 | tf_op jit(solution)/shard_map/pack/pallas_call | solution.py:78
  6.1 0.7 collective-permute-start
  6.9 3.0 %collective-permute-start.1 = (bf16[5,2,16,32,128]{4,3,2,1,0:T(8,128)(2,1)S(1)}, bf16[5,2,16,32,128]{4,3,2,1,0:T(8,128)(2,1)S(1)}, u32[]{:S(2)}, u32[]{:S(2)}) collective-permute-start(bf16[5,2,16,32,128]{4,3,2,1,0:T(8,128)(2,1)S(1)} %get-tuple-element.11.refs_0_.refs_1_), channel_id=1, source_target_pairs={{1,2},{3,4},{5,6},{7,8},{9,10},{11,12},{13,14},{2,1},{4,3},{6,5},{... | collective-permute-start | bytes 3932168 | tf_op jit(solution)/shard_map/ppermute | solution.py:287
  9.9 2.5 %collective-permute-start.2 = (bf16[7,2,16,32,128]{4,3,2,1,0:T(8,128)(2,1)S(1)}, bf16[7,2,16,32,128]{4,3,2,1,0:T(8,128)(2,1)S(1)}, u32[]{:S(2)}, u32[]{:S(2)}) collective-permute-start(bf16[7,2,16,32,128]{4,3,2,1,0:T(8,128)(2,1)S(1)} %get-tuple-element.12.refs_1_.refs_2_), channel_id=1, source_target_pairs={{1,2},{3,4},{5,6},{7,8},{9,10},{11,12},{13,14},{2,1},{4,3},{6,5},{... | collective-permute-start | bytes 5505032 | tf_op jit(solution)/shard_map/ppermute | solution.py:287
  12.5 58.3 %collective-permute-done.1.refs_4_.refs_5_ = bf16[5,2,16,32,128]{4,3,2,1,0:T(8,128)(2,1)S(1)} collective-permute-done((bf16[5,2,16,32,128]{4,3,2,1,0:T(8,128)(2,1)S(1)}, bf16[5,2,16,32,128]{4,3,2,1,0:T(8,128)(2,1)S(1)}, u32[]{:S(2)}, u32[]{:S(2)}) %collective-permute-start.1) | collective-permute-done | bytes 1310752 | tf_op jit(solution)/shard_map/ppermute | solution.py:287
  70.7 0.1 held.1
  70.8 3.1 %collective-permute-start.3 = (bf16[4,2,16,32,128]{4,3,2,1,0:T(8,128)(2,1)S(1)}, bf16[4,2,16,32,128]{4,3,2,1,0:T(8,128)(2,1)S(1)}, u32[]{:S(2)}, u32[]{:S(2)}) collective-permute-start(bf16[4,2,16,32,128]{4,3,2,1,0:T(8,128)(2,1)S(1)} %held.1), channel_id=1, source_target_pairs={{1,2},{3,4},{5,6},{7,8},{9,10},{11,12},{13,14},{2,1},{4,3},{6,5},{... | collective-permute-start | bytes 3145736 | tf_op jit(solution)/shard_map/ppermute | solution.py:287
  73.9 0.0 collective-permute-done.refs_3_.refs_4_
  73.9 0.1 rim.1
  74.0 0.1 collective-permute-start.4
  74.1 2.5 %collective-permute-start.5 = (f32[2,32,128]{2,1,0:T(8,128)S(1)}, f32[2,32,128]{2,1,0:T(8,128)S(1)}, u32[]{:S(2)}, u32[]{:S(2)}) collective-permute-start(f32[2,32,128]{2,1,0:T(8,128)S(1)} %get-tuple-element.16), channel_id=1, source_target_pairs={{1,2},{3,4},{5,6},{7,8},{9,10},{11,12},{13,14},{2,1},{4,3},{6,5},{... | collective-permute-start | bytes 98312 | tf_op jit(solution)/shard_map/ppermute | solution.py:349
  76.6 7.4 %inner.1.refs_7_.refs_8_ = f32[11,3,18,32,128]{4,3,2,1,0:T(8,128)S(1)} custom-call(bf16[5,2,16,32,128]{4,3,2,1,0:T(8,128)(2,1)S(1)} %get-tuple-element.11.refs_0_.refs_1_, bf16[7,2,16,32,128]{4,3,2,1,0:T(8,128)(2,1)S(1)} %get-tuple-element.12.refs_1_.refs_2_, bf16[4,2,16,32,128]{4,3,2,1,0:T(8,128)(2,1)S(1)} %get-tuple-element.13.in_ref.refs_2_.refs_3_, ...), custom_call_target="tpu_custom_call" | custom-call | tf_op jit(solution)/shard_map/inner/pallas_call | solution.py:323
  84.0 6.8 %collective-permute-done.2.refs_5_.refs_6_ = bf16[7,2,16,32,128]{4,3,2,1,0:T(8,128)(2,1)S(1)} collective-permute-done((bf16[7,2,16,32,128]{4,3,2,1,0:T(8,128)(2,1)S(1)}, bf16[7,2,16,32,128]{4,3,2,1,0:T(8,128)(2,1)S(1)}, u32[]{:S(2)}, u32[]{:S(2)}) %collective-permute-start.2) | collective-permute-done | bytes 1835040 | tf_op jit(solution)/shard_map/ppermute | solution.py:287
  90.8 5.3 %near.1.refs_12_ = f32[33,16,4096]{2,1,0:T(8,128)} custom-call(s32[1]{0:T(128)} %bitcast.core_ref.refs_0_, bf16[5,2,16,32,128]{4,3,2,1,0:T(8,128)(2,1)S(1)} %get-tuple-element.11.refs_0_.refs_1_, bf16[7,2,16,32,128]{4,3,2,1,0:T(8,128)(2,1)S(1)} %get-tuple-element.12.refs_1_.refs_2_, ...), custom_call_target="tpu_custom_call" | custom-call | flops 1743257600 | bytes 5505024 | tf_op jit(solution)/shard_map/near/pallas_call | solution.py:364
  96.0 1.4 %middle.1.refs_9_ = f32[4,3,18,32,128]{4,3,2,1,0:T(8,128)S(1)} custom-call(bf16[5,2,16,32,128]{4,3,2,1,0:T(8,128)(2,1)S(1)} %get-tuple-element.11.refs_0_.refs_1_, bf16[7,2,16,32,128]{4,3,2,1,0:T(8,128)(2,1)S(1)} %get-tuple-element.12.refs_1_.refs_2_, bf16[4,2,16,32,128]{4,3,2,1,0:T(8,128)(2,1)S(1)} %get-tuple-element.13.in_ref.refs_2_.refs_3_, ...), custom_call_target="tpu_custom_call" | custom-call | flops 550502400 | tf_op jit(solution)/shard_map/middle/pallas_call | solution.py:323
  97.4 4.6 %collective-permute-done.3.refs_7_ = bf16[4,2,16,32,128]{4,3,2,1,0:T(8,128)(2,1)S(1)} collective-permute-done((bf16[4,2,16,32,128]{4,3,2,1,0:T(8,128)(2,1)S(1)}, bf16[4,2,16,32,128]{4,3,2,1,0:T(8,128)(2,1)S(1)}, u32[]{:S(2)}, u32[]{:S(2)}) %collective-permute-start.3) | collective-permute-done | bytes 1048608 | tf_op jit(solution)/shard_map/ppermute | solution.py:287
  102.0 0.0 collective-permute-done.4.refs_10_
  102.0 0.3 collective-permute-done.5.refs_11_
  102.3 3.2 %far.1 = f32[33,16,4096]{2,1,0:T(8,128)} custom-call(s32[1]{0:T(128)} %bitcast.core_ref.refs_0_, bf16[5,2,16,32,128]{4,3,2,1,0:T(8,128)(2,1)S(1)} %get-tuple-element.11.refs_0_.refs_1_, bf16[7,2,16,32,128]{4,3,2,1,0:T(8,128)(2,1)S(1)} %get-tuple-element.12.refs_1_.refs_2_, ...), custom_call_target="tpu_custom_call", output_to_operand_aliasing={{}: (12, {})} | custom-call | flops 1022361600 | bytes 3145728 | tf_op jit(solution)/shard_map/far/pallas_call | solution.py:364
  (1 shorter events, 0.0 us)
Async XLA Ops:
  6.1 67.7 %collective-permute-start = (bf16[16,2,16,32,128]{4,3,2,1,0:T(8,128)(2,1)}, bf16[16,2,16,32,128]{4,3,2,1,0:T(8,128)(2,1)S(1)}, u32[]{:S(2)}, u32[]{:S(2)}) collective-permute-start(bf16[16,2,16,32,128]{4,3,2,1,0:T(8,128)(2,1)} %get-tuple-element.14), channel_id=1, source_target_pairs={{0,1},{2,3},{4,5},{6,7},{8,9},{10,11},{12,13},{14,15},{1,0},{3,2},... | collective-permute-start | bytes 12582920 | tf_op jit(solution)/shard_map/ppermute | solution.py:288
  6.9 63.9 %collective-permute-start.1 = (bf16[5,2,16,32,128]{4,3,2,1,0:T(8,128)(2,1)S(1)}, bf16[5,2,16,32,128]{4,3,2,1,0:T(8,128)(2,1)S(1)}, u32[]{:S(2)}, u32[]{:S(2)}) collective-permute-start(bf16[5,2,16,32,128]{4,3,2,1,0:T(8,128)(2,1)S(1)} %get-tuple-element.11.refs_0_.refs_1_), channel_id=1, source_target_pairs={{1,2},{3,4},{5,6},{7,8},{9,10},{11,12},{13,14},{2,1},{4,3},{6,5},{... | collective-permute-start | bytes 3932168 | tf_op jit(solution)/shard_map/ppermute | solution.py:287
  9.9 80.8 %collective-permute-start.2 = (bf16[7,2,16,32,128]{4,3,2,1,0:T(8,128)(2,1)S(1)}, bf16[7,2,16,32,128]{4,3,2,1,0:T(8,128)(2,1)S(1)}, u32[]{:S(2)}, u32[]{:S(2)}) collective-permute-start(bf16[7,2,16,32,128]{4,3,2,1,0:T(8,128)(2,1)S(1)} %get-tuple-element.12.refs_1_.refs_2_), channel_id=1, source_target_pairs={{1,2},{3,4},{5,6},{7,8},{9,10},{11,12},{13,14},{2,1},{4,3},{6,5},{... | collective-permute-start | bytes 5505032 | tf_op jit(solution)/shard_map/ppermute | solution.py:287
  70.8 31.2 %collective-permute-start.3 = (bf16[4,2,16,32,128]{4,3,2,1,0:T(8,128)(2,1)S(1)}, bf16[4,2,16,32,128]{4,3,2,1,0:T(8,128)(2,1)S(1)}, u32[]{:S(2)}, u32[]{:S(2)}) collective-permute-start(bf16[4,2,16,32,128]{4,3,2,1,0:T(8,128)(2,1)S(1)} %held.1), channel_id=1, source_target_pairs={{1,2},{3,4},{5,6},{7,8},{9,10},{11,12},{13,14},{2,1},{4,3},{6,5},{... | collective-permute-start | bytes 3145736 | tf_op jit(solution)/shard_map/ppermute | solution.py:287
  74.0 28.0 %collective-permute-start.4 = (f32[2,32,128]{2,1,0:T(8,128)S(1)}, f32[2,32,128]{2,1,0:T(8,128)S(1)}, u32[]{:S(2)}, u32[]{:S(2)}) collective-permute-start(f32[2,32,128]{2,1,0:T(8,128)S(1)} %get-tuple-element.15), channel_id=1, source_target_pairs={{0,1},{2,3},{4,5},{6,7},{8,9},{10,11},{12,13},{14,15},{1,0},{3,2},... | collective-permute-start | bytes 98312 | tf_op jit(solution)/shard_map/ppermute | solution.py:348
  74.1 28.3 %collective-permute-start.5 = (f32[2,32,128]{2,1,0:T(8,128)S(1)}, f32[2,32,128]{2,1,0:T(8,128)S(1)}, u32[]{:S(2)}, u32[]{:S(2)}) collective-permute-start(f32[2,32,128]{2,1,0:T(8,128)S(1)} %get-tuple-element.16), channel_id=1, source_target_pairs={{1,2},{3,4},{5,6},{7,8},{9,10},{11,12},{13,14},{2,1},{4,3},{6,5},{... | collective-permute-start | bytes 98312 | tf_op jit(solution)/shard_map/ppermute | solution.py:349

commit v10 on v9

--- a/solution.py
+++ b/solution.py
@@ -17,7 +17,9 @@
 RATE = 50
 PACK = 8000
 
-CHUNKS = ((16, 4, 3, 2, 1), (11, 10, 9, 8, 7, 6, 5), (15, 14, 13, 12))
+CHUNKS = ((16, 1), (3, 2), (5, 4), (12, 11, 10, 9, 8, 7, 6), (15, 14, 13))
+HOLD = 2
+BUNDLES = ((0, 1), (2,))
 NEAR = (5, 4, 6, 3, 7, 2, 8)
 FAR = (1, 9, 0, 10)
 ALL = NEAR + FAR
@@ -33,7 +35,7 @@
 
 
 def pack_kernel(core_ref, s_ref, r_ref, *refs):
-    outs, (whole_ref, inbox, flip, sems) = refs[:-4], refs[-4:]
+    outs, (inbox, flip, sems) = refs[:-3], refs[-3:]
     cells, parts, freqs, width = s_ref.shape
     order = [cells - i for chunk in CHUNKS for i in chunk]
 
@@ -60,10 +62,9 @@
                                 k, field, p, :, c : c + LANES
                             ].astype(jnp.float32)
                         for f in range(freqs):
-                            lines = slot[f * SUB : (f + 1) * SUB].astype(jnp.bfloat16)
-                            at = (field, p * freqs + f, slice(g * SUB, (g + 1) * SUB))
-                            out_ref[(n, *at)] = lines
-                            whole_ref[(k, *at)] = lines
+                            out_ref[n, field, p * freqs + f, g * SUB : (g + 1) * SUB] = slot[
+                                f * SUB : (f + 1) * SUB
+                            ].astype(jnp.bfloat16)
             return 0
 
         lax.fori_loop(0, out_ref.shape[0], one, 0)
@@ -73,7 +74,7 @@
 def pack(core, source, receiver):
     cells, parts, freqs, width = source.shape
     terms, tiles = parts * freqs, width // LANES
-    counts = [len(chunk) for chunk in CHUNKS] + [cells]
+    counts = [len(chunk) for chunk in CHUNKS]
     hbm = pl.BlockSpec(memory_space=pltpu.HBM)
     return pl.pallas_call(
         pack_kernel,
@@ -269,6 +270,29 @@
     return up, [(j, i) for i, j in up]
 
 
+def routes(peers, chunk):
+    up, down = exchange(peers)
+    if peers != 16 or chunk > 2:
+        return up + down, ()
+    steps = peers // 4
+    far_up = range(0, steps - 1 - chunk)
+    far_down = range(chunk, steps - 1)
+    up = [p for p in up if p not in [(4 * z + 3, 4 * z + 4) for z in far_up]]
+    up += [(4 * z + 3, 4 * z) for z in far_up]
+    down = [p for p in down if p not in [(4 * z + 4, 4 * z + 3) for z in far_down]]
+    down += [(4 * z + 4, 4 * z + 7) for z in far_down]
+    swap = {4 * z for z in far_up} | {4 * z + 4 for z in far_up}
+    swap |= {4 * z + 7 for z in far_down} | {4 * z + 3 for z in far_down}
+    return up + down, sorted(swap)
+
+
+def is_one_of(me, devices):
+    found = jnp.bool_(False)
+    for d in devices:
+        found |= me == d
+    return found
+
+
 def on_device(forward_field, adjoint_field):
     cells, parts, freqs, width = forward_field.shape
     terms, tiles = parts * freqs, width // LANES
@@ -279,13 +303,32 @@
     links = sum(exchange(peers), [])
     row_bytes = 2 * terms * width * 2
 
-    *own, whole = pack(core, forward_field, adjoint_field)
+    own = list(pack(core, forward_field, adjoint_field))
     arrived = []
     for g, sent in enumerate(own):
-        if g == 2:
-            sent = held(sent, arrived[0][0, 0, 0])
-        arrived.append(lax.ppermute(sent, "gx", links))
-    beside = lax.ppermute(whole, "gx", cores)
+        if g == len(CHUNKS) - 1:
+            sent = held(sent, arrived[HOLD][0, 0, 0])
+        arrived.append(lax.ppermute(sent, "gx", routes(peers, g)[0]))
+    beside = lax.ppermute(jnp.concatenate(own, axis=0), "gx", cores)
+
+    pieces = []
+    for bundle in BUNDLES:
+        got = jnp.concatenate([arrived[g] for g in bundle], axis=0)
+        if peers == 16:
+            steps = peers // 4
+            hop = [(4 * z, 4 * z + 4) for z in range(steps - 1)]
+            hop += [(4 * z + 7, 4 * z + 3) for z in range(steps - 1)]
+            relayed = lax.ppermute(got, "gx", hop)
+            swapped = jnp.concatenate(
+                [
+                    jnp.broadcast_to(is_one_of(me, routes(peers, g)[1]), (len(CHUNKS[g]),))
+                    for g in bundle
+                ]
+            )
+            got = jnp.where(swapped[:, None, None, None, None], relayed, got)
+        pieces.append((sum((CHUNKS[g] for g in bundle), ()), got))
+    for g in range(1 + BUNDLES[-1][-1], len(CHUNKS)):
+        pieces.append((CHUNKS[g], arrived[g]))
 
     def layout(count):
         operands = own + [beside]
@@ -294,7 +337,7 @@
         for g, chunk in enumerate(CHUNKS):
             where.update({cells - i: (g, k) for k, i in enumerate(chunk)})
         where.update({i - cells - 1: (len(own), k) for k, i in enumerate(order)})
-        for chunk, got in zip(CHUNKS[:count], arrived):
+        for chunk, got in pieces[:count]:
             where.update({cells - 1 + i: (len(operands), k) for k, i in enumerate(chunk)})
             operands.append(got)
         return operands, where
@@ -380,10 +423,10 @@
             name=name,
         )(*operands)
 
-    inner, first = partial("inner", 1, ALL, ())
-    image = lags("near", None, 2, NEAR, [inner], [first], [])
-    middle, second = partial("middle", 2, FAR, first[0])
-    return lags("far", image, 3, FAR, [inner, middle], [first, second], [rim_lo, rim_hi])
+    inner, first = partial("inner", 2, ALL, ())
+    image = lags("near", None, 3, NEAR, [inner], [first], [])
+    middle, second = partial("middle", 3, FAR, first[0])
+    return lags("far", image, 4, FAR, [inner, middle], [first, second], [rim_lo, rim_hi])
 
 
 def solution(mesh):

time: 106 us -> 134 us (1.26); the launches traced: 106 us -> 132 us
  Pallas kernels: 23.6 us -> 35.1 us
  starting transfers between devices: 11.9 us -> 20.6 us
  local copies, waits for them, and re-layouts: 0.01 us -> 7.53 us
  waiting for transfers between devices: 70 us -> 65.6 us
  other arithmetic: 0 us -> 2.9 us
    ppermute x4 -> x8, starting transfers between devices: 9.35 us -> 18.6 us  [the longest x5 14.8 us: on_device(): arrived.append(lax.ppermute(sent, 'gx', routes(peers, g)[0]))]
    pallas_call x2, Pallas kernels: 8.81 us -> 14.2 us  [partial(): pl.pallas_call(functools.partial(part_kernel, cells, blocks, where, done)...]
    pallas_call x2, Pallas kernels: 8.5 us -> 13.8 us  [lags(): pl.pallas_call(functools.partial(lag_kernel, cells, blocks, where, stages...]
    unnamed x0 -> x13, local copies, waits for them, and re-layouts: none -> 5.04 us
    ppermute x4 -> x8, waiting for transfers between devices: 69.6 us -> 65.6 us  [the longest x5 65.6 us: on_device(): arrived.append(lax.ppermute(sent, 'gx', routes(peers, g)[0]))]
    select_n x0 -> x2, other arithmetic: none -> 2.9 us  [on_device(): got = jnp.where(swapped[:, None, None, None, None], relayed, got)]
    pallas_call x1, Pallas kernels: 6.14 us -> 3.92 us  [pack(): pl.pallas_call(pack_kernel, in_specs=[SMEM, hbm, hbm], out_specs=[VMEM] *...]
    pallas_call x1, Pallas kernels: 0.09 us -> 2.27 us  [on_device(): pl.pallas_call(functools.partial(rim_kernel, cells, where), in_specs=[VME...]
  transfers between devices with their start and end apart: 6 -> 10, of which waited for: 4 -> 3; matrix products, arithmetic and copies ran while one was open for 0% -> 4% of each run, Pallas kernels for 13% -> 19%
where the time goes in v10:
time: 134 us; the launch traced here: 132 us
  waiting for transfers between devices  65.6 us (49%)
  Pallas kernels  35.1 us (26%)
  starting transfers between devices  20.6 us (15%)
  local copies, waits for them, and re-layouts  7.53 us (6%)
  other arithmetic  2.9 us (2%)
    ppermute x5, waiting for transfers between devices, on_device(): arrived.append(lax.ppermute(sent, 'gx', routes(peers, g)[0]))  65.6 us
    ppermute x5, starting transfers between devices, on_device(): arrived.append(lax.ppermute(sent, 'gx', routes(peers, g)[0]))  14.8 us
    pallas_call x2, Pallas kernels, partial(): pl.pallas_call(functools.partial(part_kernel, cells, blocks, where, done)...  14.2 us
    pallas_call x2, Pallas kernels, lags(): pl.pallas_call(functools.partial(lag_kernel, cells, blocks, where, stages...  13.8 us
    unnamed x13, local copies, waits for them, and re-layouts  5.04 us
    pallas_call x1, Pallas kernels, pack(): pl.pallas_call(pack_kernel, in_specs=[SMEM, hbm, hbm], out_specs=[VMEM] *...  3.92 us
    ppermute x2, starting transfers between devices, on_device(): relayed = lax.ppermute(got, 'gx', hop)  3.11 us
    select_n x2, other arithmetic, on_device(): got = jnp.where(swapped[:, None, None, None, None], relayed, got)  2.9 us
  transfers between devices with their start and end apart: 10, of which 3 were waited for; matrix products, arithmetic and copies ran while one was open for 4% of the time, Pallas kernels for 19%

profile of v10, /device:TPU:17, one launch (start us, length us, event | category | flops | bytes accessed | tf_op | source)
XLA Modules:
  0.0 132.1 jit_solution(2862905192131247050)
XLA Ops:
  0.0 3.9 %pack.1 = (bf16[2,2,16,32,128]{4,3,2,1,0:T(8,128)(2,1)S(1)}, bf16[2,2,16,32,128]{4,3,2,1,0:T(8,128)(2,1)S(1)}, bf16[2,2,16,32,128]{4,3,2,1,0:T(8,128)(2,1)S(1)},...) custom-call(s32[1]{0:T(128)} %bitcast.core_ref.refs_0_, bf16[16,2,8,4096]{3,2,1,0:T(8,128)(2,1)} %s_ref.1, ...), custom_call_target="tpu_custom_call" | custom-call | flops 8388608000 | bytes 8388608 | tf_op jit(solution)/shard_map/pack/pallas_call | solution.py:79
  3.9 0.0 copy-start
  3.9 0.0 copy-start.2
  4.0 0.9 constant_dynamic-update-slice_fusion.4
  4.9 0.8 constant_dynamic-update-slice_fusion.3
  5.7 0.8 constant_dynamic-update-slice_fusion.2
  6.5 1.6 %constant_dynamic-update-slice_fusion.1 = bf16[16,2,16,32,128]{4,3,2,1,0:T(8,128)(2,1)} fusion(bf16[16,2,16,32,128]{4,3,2,1,0:T(8,128)(2,1)} %constant_dynamic-update-slice_fusion.2, bf16[7,2,16,32,128]{4,3,2,1,0:T(8,128)(2,1)S(1)} %get-tuple-element.15.refs_3_.refs_4_), kind=kLoop, calls=%fused_computation.3 | loop fusion | bytes 3670016
  8.1 0.9 constant_dynamic-update-slice_fusion
  9.1 0.7 collective-permute-start
  9.8 3.0 %collective-permute-start.1 = (bf16[2,2,16,32,128]{4,3,2,1,0:T(8,128)(2,1)S(1)}, bf16[2,2,16,32,128]{4,3,2,1,0:T(8,128)(2,1)S(1)}, u32[]{:S(2)}, u32[]{:S(2)}) collective-permute-start(bf16[2,2,16,32,128]{4,3,2,1,0:T(8,128)(2,1)S(1)} %get-tuple-element.12.refs_0_.refs_1_), channel_id=1, source_target_pairs={{1,2},{5,6},{9,10},{13,14},{3,0},{7,4},{11,8},{2,1},{6,5},{10,9},{... | collective-permute-start | bytes 1572872 | tf_op jit(solution)/shard_map/ppermute | solution.py:311
  12.8 0.0 copy-done
  12.8 2.5 %collective-permute-start.2 = (bf16[2,2,16,32,128]{4,3,2,1,0:T(8,128)(2,1)S(1)}, bf16[2,2,16,32,128]{4,3,2,1,0:T(8,128)(2,1)S(1)}, u32[]{:S(2)}, u32[]{:S(2)}) collective-permute-start(bf16[2,2,16,32,128]{4,3,2,1,0:T(8,128)(2,1)S(1)} %get-tuple-element.13.refs_1_.refs_2_), channel_id=1, source_target_pairs={{1,2},{5,6},{9,10},{11,12},{13,14},{3,0},{7,4},{2,1},{4,3},{6,5},{... | collective-permute-start | bytes 1572872 | tf_op jit(solution)/shard_map/ppermute | solution.py:311
  15.3 3.0 %collective-permute-start.6 = (bf16[7,2,16,32,128]{4,3,2,1,0:T(8,128)(2,1)S(1)}, bf16[7,2,16,32,128]{4,3,2,1,0:T(8,128)(2,1)}, u32[]{:S(2)}, u32[]{:S(2)}) collective-permute-start(bf16[7,2,16,32,128]{4,3,2,1,0:T(8,128)(2,1)S(1)} %get-tuple-element.15.refs_3_.refs_4_), channel_id=1, source_target_pairs={{1,2},{3,4},{5,6},{7,8},{9,10},{11,12},{13,14},{2,1},{4,3},{6,5},{... | collective-permute-start | bytes 5505032 | tf_op jit(solution)/shard_map/ppermute | solution.py:311
  18.4 0.0 copy-done.2
  18.4 2.5 %collective-permute-start.4 = (bf16[2,2,16,32,128]{4,3,2,1,0:T(8,128)(2,1)S(1)}, bf16[2,2,16,32,128]{4,3,2,1,0:T(8,128)(2,1)}, u32[]{:S(2)}, u32[]{:S(2)}) collective-permute-start(bf16[2,2,16,32,128]{4,3,2,1,0:T(8,128)(2,1)S(1)} %get-tuple-element.14.refs_2_.refs_3_), channel_id=1, source_target_pairs={{1,2},{5,6},{7,8},{9,10},{11,12},{13,14},{3,0},{2,1},{4,3},{6,5},{... | collective-permute-start | bytes 1572872 | tf_op jit(solution)/shard_map/ppermute | solution.py:311
  20.9 29.5 %collective-permute-done.1 = bf16[2,2,16,32,128]{4,3,2,1,0:T(8,128)(2,1)S(1)} collective-permute-done((bf16[2,2,16,32,128]{4,3,2,1,0:T(8,128)(2,1)S(1)}, bf16[2,2,16,32,128]{4,3,2,1,0:T(8,128)(2,1)S(1)}, u32[]{:S(2)}, u32[]{:S(2)}) %collective-permute-start.1) | collective-permute-done | bytes 524320 | tf_op jit(solution)/shard_map/ppermute | solution.py:311
  50.5 0.8 constant_dynamic-update-slice_fusion.6
  51.3 4.8 %collective-permute-done.2 = bf16[2,2,16,32,128]{4,3,2,1,0:T(8,128)(2,1)S(1)} collective-permute-done((bf16[2,2,16,32,128]{4,3,2,1,0:T(8,128)(2,1)S(1)}, bf16[2,2,16,32,128]{4,3,2,1,0:T(8,128)(2,1)S(1)}, u32[]{:S(2)}, u32[]{:S(2)}) %collective-permute-start.2) | collective-permute-done | bytes 524320 | tf_op jit(solution)/shard_map/ppermute | solution.py:311
  56.1 0.9 constant_dynamic-update-slice_fusion.5
  56.9 1.7 %collective-permute-start.3 = (bf16[4,2,16,32,128]{4,3,2,1,0:T(8,128)(2,1)}, bf16[4,2,16,32,128]{4,3,2,1,0:T(8,128)(2,1)}, u32[]{:S(2)}, u32[]{:S(2)}) collective-permute-start(bf16[4,2,16,32,128]{4,3,2,1,0:T(8,128)(2,1)} %constant_dynamic-update-slice_fusion.5), channel_id=1, source_target_pairs={{0,4},{4,8},{8,12},{7,3},{11,7},{15,11},{16,20},{20,24},{24,28},{2... | collective-permute-start | bytes 3145736 | tf_op jit(solution)/shard_map/ppermute | solution.py:321
  58.6 31.3 %collective-permute-done.4 = bf16[2,2,16,32,128]{4,3,2,1,0:T(8,128)(2,1)} collective-permute-done((bf16[2,2,16,32,128]{4,3,2,1,0:T(8,128)(2,1)S(1)}, bf16[2,2,16,32,128]{4,3,2,1,0:T(8,128)(2,1)}, u32[]{:S(2)}, u32[]{:S(2)}) %collective-permute-start.4) | collective-permute-done | bytes 524320 | tf_op jit(solution)/shard_map/ppermute | solution.py:311
  89.9 1.5 %collective-permute-start.5 = (bf16[2,2,16,32,128]{4,3,2,1,0:T(8,128)(2,1)}, bf16[2,2,16,32,128]{4,3,2,1,0:T(8,128)(2,1)}, u32[]{:S(2)}, u32[]{:S(2)}) collective-permute-start(bf16[2,2,16,32,128]{4,3,2,1,0:T(8,128)(2,1)} %collective-permute-done.4), channel_id=1, source_target_pairs={{0,4},{4,8},{8,12},{7,3},{11,7},{15,11},{16,20},{20,24},{24,28},{2... | collective-permute-start | bytes 1572872 | tf_op jit(solution)/shard_map/ppermute | solution.py:321
  91.3 0.7 slice_bitcast_fusion.earlier_ref
  92.0 0.9 held.1
  93.0 3.7 %collective-permute-start.7 = (bf16[3,2,16,32,128]{4,3,2,1,0:T(8,128)(2,1)}, bf16[3,2,16,32,128]{4,3,2,1,0:T(8,128)(2,1)}, u32[]{:S(2)}, u32[]{:S(2)}) collective-permute-start(bf16[3,2,16,32,128]{4,3,2,1,0:T(8,128)(2,1)} %held.1), channel_id=1, source_target_pairs={{1,2},{3,4},{5,6},{7,8},{9,10},{11,12},{13,14},{2,1},{4,3},{6,5},{... | collective-permute-start | bytes 2359304 | tf_op jit(solution)/shard_map/ppermute | solution.py:311
  96.7 0.0 copy-start.1
  96.7 0.0 copy-start.3
  96.8 0.0 collective-permute-done.5
  96.8 1.2 broadcast_select_fusion.1.refs_7_.refs_8_
  98.0 0.0 collective-permute-done.3
  98.0 1.7 %broadcast_select_fusion.refs_6_.refs_7_ = bf16[4,2,16,32,128]{4,3,2,1,0:T(8,128)(2,1)S(1)} fusion(bf16[4,2,16,32,128]{4,3,2,1,0:T(8,128)(2,1)} %collective-permute-done.3, bf16[4,2,16,32,128]{4,3,2,1,0:T(8,128)(2,1)} %constant_dynamic-update-slice_fusion.5, pred[4]{0:T(512)(128)(4,1)S(1)} %concatenate.10), kind=kLoop, calls=%fused_computation | loop fusion | flops 524288 | bytes 3145732 | tf_op jit(solution)/shard_map/jit(_where)/select_n | solution.py:328
  99.7 0.0 collective-permute-done.refs_5_.refs_6_
  99.7 0.0 copy-done.1
  99.7 0.0 copy-done.3
  99.7 2.3 %rim.1 = (f32[2,32,128]{2,1,0:T(8,128)S(1)}, f32[2,32,128]{2,1,0:T(8,128)S(1)}) custom-call(bf16[2,2,16,32,128]{4,3,2,1,0:T(8,128)(2,1)S(1)} %get-tuple-element.12.refs_0_.refs_1_, bf16[2,2,16,32,128]{4,3,2,1,0:T(8,128)(2,1)S(1)} %copy-done.1, bf16[2,2,16,32,128]{4,3,2,1,0:T(8,128)(2,1)S(1)} %copy-done.3, ...), custom_call_target="tpu_custom_call" | custom-call | tf_op jit(solution)/shard_map/rim/pallas_call | solution.py:380
  102.0 0.1 collective-permute-start.8
  102.1 1.9 %collective-permute-start.9 = (f32[2,32,128]{2,1,0:T(8,128)S(1)}, f32[2,32,128]{2,1,0:T(8,128)S(1)}, u32[]{:S(2)}, u32[]{:S(2)}) collective-permute-start(f32[2,32,128]{2,1,0:T(8,128)S(1)} %get-tuple-element.18), channel_id=1, source_target_pairs={{1,2},{3,4},{5,6},{7,8},{9,10},{11,12},{13,14},{2,1},{4,3},{6,5},{... | collective-permute-start | bytes 98312 | tf_op jit(solution)/shard_map/ppermute | solution.py:392
  104.0 10.1 %inner.1.refs_10_.refs_11_ = f32[11,3,18,32,128]{4,3,2,1,0:T(8,128)S(1)} custom-call(bf16[2,2,16,32,128]{4,3,2,1,0:T(8,128)(2,1)S(1)} %get-tuple-element.12.refs_0_.refs_1_, bf16[2,2,16,32,128]{4,3,2,1,0:T(8,128)(2,1)S(1)} %copy-done.1, bf16[2,2,16,32,128]{4,3,2,1,0:T(8,128)(2,1)S(1)} %copy-done.3, ...), custom_call_target="tpu_custom_call" | custom-call | tf_op jit(solution)/shard_map/inner/pallas_call | solution.py:366
  114.1 0.0 collective-permute-done.6.refs_8_.refs_9_
  114.1 7.7 %near.1.refs_15_ = f32[33,16,4096]{2,1,0:T(8,128)} custom-call(s32[1]{0:T(128)} %bitcast.core_ref.refs_0_, bf16[2,2,16,32,128]{4,3,2,1,0:T(8,128)(2,1)S(1)} %get-tuple-element.12.refs_0_.refs_1_, bf16[2,2,16,32,128]{4,3,2,1,0:T(8,128)(2,1)S(1)} %copy-done.1, bf16[2,2,16,32,128]{4,3,2,1,0:T(8,128)(2,1)S(1)} %copy-done.3, ...), custom_call_target="tpu_custom_call" | custom-call | flops 1651507200 | bytes 5505024 | tf_op jit(solution)/shard_map/near/pallas_call | solution.py:407
  121.8 4.1 %middle.1.refs_12_ = f32[4,3,18,32,128]{4,3,2,1,0:T(8,128)S(1)} custom-call(bf16[2,2,16,32,128]{4,3,2,1,0:T(8,128)(2,1)S(1)} %get-tuple-element.12.refs_0_.refs_1_, bf16[2,2,16,32,128]{4,3,2,1,0:T(8,128)(2,1)S(1)} %copy-done.1, bf16[2,2,16,32,128]{4,3,2,1,0:T(8,128)(2,1)S(1)} %copy-done.3, ...), custom_call_target="tpu_custom_call" | custom-call | flops 550502400 | tf_op jit(solution)/shard_map/middle/pallas_call | solution.py:366
  125.9 0.0 collective-permute-done.7.refs_10_
  125.9 0.0 collective-permute-done.8.refs_13_
  126.0 0.0 collective-permute-done.9.refs_14_
  126.0 6.1 %far.1 = f32[33,16,4096]{2,1,0:T(8,128)} custom-call(s32[1]{0:T(128)} %bitcast.core_ref.refs_0_, bf16[2,2,16,32,128]{4,3,2,1,0:T(8,128)(2,1)S(1)} %get-tuple-element.12.refs_0_.refs_1_, bf16[2,2,16,32,128]{4,3,2,1,0:T(8,128)(2,1)S(1)} %copy-done.1, bf16[2,2,16,32,128]{4,3,2,1,0:T(8,128)(2,1)S(1)} %copy-done.3, ...), custom_call_target="tpu_custom_call", output_to_operand_aliasing={{}: (15, {})} | custom-call | flops 943718400 | bytes 3145728 | tf_op jit(solution)/shard_map/far/pallas_call | solution.py:407
  (2 shorter events, 0.0 us)
Async XLA Ops:
  3.9 8.9 %copy-start = (bf16[2,2,16,32,128]{4,3,2,1,0:T(8,128)(2,1)}, bf16[2,2,16,32,128]{4,3,2,1,0:T(8,128)(2,1)S(1)}, u32[]{:S(2)}) copy-start(bf16[2,2,16,32,128]{4,3,2,1,0:T(8,128)(2,1)S(1)} %get-tuple-element.13.refs_1_.refs_2_) | copy-start | bytes 1572868
  3.9 14.4 %copy-start.2 = (bf16[2,2,16,32,128]{4,3,2,1,0:T(8,128)(2,1)}, bf16[2,2,16,32,128]{4,3,2,1,0:T(8,128)(2,1)S(1)}, u32[]{:S(2)}) copy-start(bf16[2,2,16,32,128]{4,3,2,1,0:T(8,128)(2,1)S(1)} %get-tuple-element.14.refs_2_.refs_3_) | copy-start | bytes 1572868
  9.1 90.6 %collective-permute-start = (bf16[16,2,16,32,128]{4,3,2,1,0:T(8,128)(2,1)}, bf16[16,2,16,32,128]{4,3,2,1,0:T(8,128)(2,1)}, u32[]{:S(2)}, u32[]{:S(2)}) collective-permute-start(bf16[16,2,16,32,128]{4,3,2,1,0:T(8,128)(2,1)} %constant_dynamic-update-slice_fusion), channel_id=1, source_target_pairs={{0,1},{2,3},{4,5},{6,7},{8,9},{10,11},{12,13},{14,15},{1,0},{3,2},... | collective-permute-start | bytes 12582920 | tf_op jit(solution)/shard_map/ppermute | solution.py:312
  9.8 40.7 %collective-permute-start.1 = (bf16[2,2,16,32,128]{4,3,2,1,0:T(8,128)(2,1)S(1)}, bf16[2,2,16,32,128]{4,3,2,1,0:T(8,128)(2,1)S(1)}, u32[]{:S(2)}, u32[]{:S(2)}) collective-permute-start(bf16[2,2,16,32,128]{4,3,2,1,0:T(8,128)(2,1)S(1)} %get-tuple-element.12.refs_0_.refs_1_), channel_id=1, source_target_pairs={{1,2},{5,6},{9,10},{13,14},{3,0},{7,4},{11,8},{2,1},{6,5},{10,9},{... | collective-permute-start | bytes 1572872 | tf_op jit(solution)/shard_map/ppermute | solution.py:311
  12.8 43.3 %collective-permute-start.2 = (bf16[2,2,16,32,128]{4,3,2,1,0:T(8,128)(2,1)S(1)}, bf16[2,2,16,32,128]{4,3,2,1,0:T(8,128)(2,1)S(1)}, u32[]{:S(2)}, u32[]{:S(2)}) collective-permute-start(bf16[2,2,16,32,128]{4,3,2,1,0:T(8,128)(2,1)S(1)} %get-tuple-element.13.refs_1_.refs_2_), channel_id=1, source_target_pairs={{1,2},{5,6},{9,10},{11,12},{13,14},{3,0},{7,4},{2,1},{4,3},{6,5},{... | collective-permute-start | bytes 1572872 | tf_op jit(solution)/shard_map/ppermute | solution.py:311
  15.3 98.8 %collective-permute-start.6 = (bf16[7,2,16,32,128]{4,3,2,1,0:T(8,128)(2,1)S(1)}, bf16[7,2,16,32,128]{4,3,2,1,0:T(8,128)(2,1)}, u32[]{:S(2)}, u32[]{:S(2)}) collective-permute-start(bf16[7,2,16,32,128]{4,3,2,1,0:T(8,128)(2,1)S(1)} %get-tuple-element.15.refs_3_.refs_4_), channel_id=1, source_target_pairs={{1,2},{3,4},{5,6},{7,8},{9,10},{11,12},{13,14},{2,1},{4,3},{6,5},{... | collective-permute-start | bytes 5505032 | tf_op jit(solution)/shard_map/ppermute | solution.py:311
  18.4 71.5 %collective-permute-start.4 = (bf16[2,2,16,32,128]{4,3,2,1,0:T(8,128)(2,1)S(1)}, bf16[2,2,16,32,128]{4,3,2,1,0:T(8,128)(2,1)}, u32[]{:S(2)}, u32[]{:S(2)}) collective-permute-start(bf16[2,2,16,32,128]{4,3,2,1,0:T(8,128)(2,1)S(1)} %get-tuple-element.14.refs_2_.refs_3_), channel_id=1, source_target_pairs={{1,2},{5,6},{7,8},{9,10},{11,12},{13,14},{3,0},{2,1},{4,3},{6,5},{... | collective-permute-start | bytes 1572872 | tf_op jit(solution)/shard_map/ppermute | solution.py:311
  56.9 41.1 %collective-permute-start.3 = (bf16[4,2,16,32,128]{4,3,2,1,0:T(8,128)(2,1)}, bf16[4,2,16,32,128]{4,3,2,1,0:T(8,128)(2,1)}, u32[]{:S(2)}, u32[]{:S(2)}) collective-permute-start(bf16[4,2,16,32,128]{4,3,2,1,0:T(8,128)(2,1)} %constant_dynamic-update-slice_fusion.5), channel_id=1, source_target_pairs={{0,4},{4,8},{8,12},{7,3},{11,7},{15,11},{16,20},{20,24},{24,28},{2... | collective-permute-start | bytes 3145736 | tf_op jit(solution)/shard_map/ppermute | solution.py:321
  89.9 6.9 %collective-permute-start.5 = (bf16[2,2,16,32,128]{4,3,2,1,0:T(8,128)(2,1)}, bf16[2,2,16,32,128]{4,3,2,1,0:T(8,128)(2,1)}, u32[]{:S(2)}, u32[]{:S(2)}) collective-permute-start(bf16[2,2,16,32,128]{4,3,2,1,0:T(8,128)(2,1)} %collective-permute-done.4), channel_id=1, source_target_pairs={{0,4},{4,8},{8,12},{7,3},{11,7},{15,11},{16,20},{20,24},{24,28},{2... | collective-permute-start | bytes 1572872 | tf_op jit(solution)/shard_map/ppermute | solution.py:321
  93.0 33.0 %collective-permute-start.7 = (bf16[3,2,16,32,128]{4,3,2,1,0:T(8,128)(2,1)}, bf16[3,2,16,32,128]{4,3,2,1,0:T(8,128)(2,1)}, u32[]{:S(2)}, u32[]{:S(2)}) collective-permute-start(bf16[3,2,16,32,128]{4,3,2,1,0:T(8,128)(2,1)} %held.1), channel_id=1, source_target_pairs={{1,2},{3,4},{5,6},{7,8},{9,10},{11,12},{13,14},{2,1},{4,3},{6,5},{... | collective-permute-start | bytes 2359304 | tf_op jit(solution)/shard_map/ppermute | solution.py:311
  96.7 3.0 %copy-start.1 = (bf16[2,2,16,32,128]{4,3,2,1,0:T(8,128)(2,1)S(1)}, bf16[2,2,16,32,128]{4,3,2,1,0:T(8,128)(2,1)}, u32[]{:S(2)}) copy-start(bf16[2,2,16,32,128]{4,3,2,1,0:T(8,128)(2,1)} %copy-done) | copy-start | bytes 1572868
  96.7 3.0 %copy-start.3 = (bf16[2,2,16,32,128]{4,3,2,1,0:T(8,128)(2,1)S(1)}, bf16[2,2,16,32,128]{4,3,2,1,0:T(8,128)(2,1)}, u32[]{:S(2)}) copy-start(bf16[2,2,16,32,128]{4,3,2,1,0:T(8,128)(2,1)} %copy-done.2) | copy-start | bytes 1572868
  102.0 23.9 %collective-permute-start.8 = (f32[2,32,128]{2,1,0:T(8,128)S(1)}, f32[2,32,128]{2,1,0:T(8,128)S(1)}, u32[]{:S(2)}, u32[]{:S(2)}) collective-permute-start(f32[2,32,128]{2,1,0:T(8,128)S(1)} %get-tuple-element.17), channel_id=1, source_target_pairs={{0,1},{2,3},{4,5},{6,7},{8,9},{10,11},{12,13},{14,15},{1,0},{3,2},... | collective-permute-start | bytes 98312 | tf_op jit(solution)/shard_map/ppermute | solution.py:391
  102.1 23.9 %collective-permute-start.9 = (f32[2,32,128]{2,1,0:T(8,128)S(1)}, f32[2,32,128]{2,1,0:T(8,128)S(1)}, u32[]{:S(2)}, u32[]{:S(2)}) collective-permute-start(f32[2,32,128]{2,1,0:T(8,128)S(1)} %get-tuple-element.18), channel_id=1, source_target_pairs={{1,2},{3,4},{5,6},{7,8},{9,10},{11,12},{13,14},{2,1},{4,3},{6,5},{... | collective-permute-start | bytes 98312 | tf_op jit(solution)/shard_map/ppermute | solution.py:392

commit v11 on v9

--- a/solution.py
+++ b/solution.py
@@ -33,7 +33,7 @@
 
 
 def pack_kernel(core_ref, s_ref, r_ref, *refs):
-    outs, (whole_ref, inbox, flip, sems) = refs[:-4], refs[-4:]
+    outs, (whole_ref, inbox, flip, sems, sent) = refs[:-5], refs[-5:]
     cells, parts, freqs, width = s_ref.shape
     order = [cells - i for chunk in CHUNKS for i in chunk]
 
@@ -45,6 +45,7 @@
         for field in (0, 1):
             copy(k, field, jnp.where(core_ref[0] == 1, row, cells - 1 - row)).start()
     base = 0
+    kept = []
     for out_ref in outs:
 
         def one(n, _):
@@ -60,14 +61,20 @@
                                 k, field, p, :, c : c + LANES
                             ].astype(jnp.float32)
                         for f in range(freqs):
-                            lines = slot[f * SUB : (f + 1) * SUB].astype(jnp.bfloat16)
-                            at = (field, p * freqs + f, slice(g * SUB, (g + 1) * SUB))
-                            out_ref[(n, *at)] = lines
-                            whole_ref[(k, *at)] = lines
+                            out_ref[n, field, p * freqs + f, g * SUB : (g + 1) * SUB] = slot[
+                                f * SUB : (f + 1) * SUB
+                            ].astype(jnp.bfloat16)
             return 0
 
-        lax.fori_loop(0, out_ref.shape[0], one, 0)
-        base += out_ref.shape[0]
+        count = out_ref.shape[0]
+        lax.fori_loop(0, count, one, 0)
+        kept.append(
+            pltpu.make_async_copy(out_ref, whole_ref.at[pl.ds(base, count)], sent.at[len(kept)])
+        )
+        kept[-1].start()
+        base += count
+    for copied in kept:
+        copied.wait()
 
 
 def pack(core, source, receiver):
@@ -78,7 +85,7 @@
     return pl.pallas_call(
         pack_kernel,
         in_specs=[SMEM, hbm, hbm],
-        out_specs=[VMEM] * len(counts),
+        out_specs=[VMEM] * len(CHUNKS) + [hbm],
         out_shape=[
             jax.ShapeDtypeStruct((n, 2, terms, tiles, LANES), jnp.bfloat16) for n in counts
         ],
@@ -86,6 +93,7 @@
             pltpu.VMEM((cells, 2, parts, freqs, width), jnp.bfloat16),
             pltpu.VMEM((4 * parts, SUB * freqs, LANES), jnp.float32),
             pltpu.SemaphoreType.DMA((cells, 2)),
+            pltpu.SemaphoreType.DMA((len(CHUNKS),)),
         ],
         cost_estimate=pl.CostEstimate(
             flops=PACK * cells * terms * width,

time: 106 us -> 105 us (level)
  Pallas kernels: 23.6 us -> 22.4 us
    pallas_call x1, Pallas kernels: 6.14 us -> 4.92 us  [pack(): pl.pallas_call(pack_kernel, in_specs=[SMEM, hbm, hbm], out_specs=[VMEM] *...]
  transfers between devices with their start and end apart: 6 -> 6, of which waited for: 4 -> 4; matrix products, arithmetic and copies ran while one was open for 0% -> 0% of each run, Pallas kernels for 13% -> 14%
where the time goes in v11:
time: 105 us; the launch traced here: 104 us
  waiting for transfers between devices  70 us (67%)
  Pallas kernels  22.4 us (21%)
  starting transfers between devices  11.9 us (11%)
    ppermute x3, waiting for transfers between devices, on_device(): arrived.append(lax.ppermute(sent, 'gx', links))  69.6 us
    pallas_call x2, Pallas kernels, partial(): pl.pallas_call(functools.partial(part_kernel, cells, blocks, where, done)...  8.81 us
    ppermute x3, starting transfers between devices, on_device(): arrived.append(lax.ppermute(sent, 'gx', links))  8.61 us
    pallas_call x2, Pallas kernels, lags(): pl.pallas_call(functools.partial(lag_kernel, cells, blocks, where, stages...  8.5 us
    pallas_call x1, Pallas kernels, pack(): pl.pallas_call(pack_kernel, in_specs=[SMEM, hbm, hbm], out_specs=[VMEM] *...  4.92 us
    ppermute x1, starting transfers between devices, on_device(): rim_hi = lax.ppermute(hi, 'gx', links)  2.5 us
  transfers between devices with their start and end apart: 6, of which 4 were waited for; matrix products, arithmetic and copies ran while one was open for 0% of the time, Pallas kernels for 14%

profile of v11, /device:TPU:17, one launch (start us, length us, event | category | flops | bytes accessed | tf_op | source)
XLA Modules:
  0.0 104.4 jit_solution(16929043117764558544)
XLA Ops:
  0.0 4.9 %pack.1 = (bf16[5,2,16,32,128]{4,3,2,1,0:T(8,128)(2,1)S(1)}, bf16[7,2,16,32,128]{4,3,2,1,0:T(8,128)(2,1)S(1)}, bf16[4,2,16,32,128]{4,3,2,1,0:T(8,128)(2,1)S(1)}, bf16[16,2,16,32,128]{4,3,2,1,0:T(8,128)(2,1)}) custom-call(s32[1]{0:T(128)} %bitcast.core_ref.refs_0_, bf16[16,2,8,4096]{3,2,1,0:T(8,128)(2,1)} %s_ref.1, bf16[16,2,8,4096]{3,2,1,0:T(8,128)(2,1)} %r_ref.1), custom_call_target="tpu_custom_call" | custom-call | flops 8388608000 | bytes 8388608 | tf_op jit(solution)/shard_map/pack/pallas_call | solution.py:85
  4.9 0.7 collective-permute-start
  5.7 3.0 %collective-permute-start.1 = (bf16[5,2,16,32,128]{4,3,2,1,0:T(8,128)(2,1)S(1)}, bf16[5,2,16,32,128]{4,3,2,1,0:T(8,128)(2,1)S(1)}, u32[]{:S(2)}, u32[]{:S(2)}) collective-permute-start(bf16[5,2,16,32,128]{4,3,2,1,0:T(8,128)(2,1)S(1)} %get-tuple-element.11.refs_0_.refs_1_), channel_id=1, source_target_pairs={{1,2},{3,4},{5,6},{7,8},{9,10},{11,12},{13,14},{2,1},{4,3},{6,5},{... | collective-permute-start | bytes 3932168 | tf_op jit(solution)/shard_map/ppermute | solution.py:295
  8.7 2.5 %collective-permute-start.2 = (bf16[7,2,16,32,128]{4,3,2,1,0:T(8,128)(2,1)S(1)}, bf16[7,2,16,32,128]{4,3,2,1,0:T(8,128)(2,1)S(1)}, u32[]{:S(2)}, u32[]{:S(2)}) collective-permute-start(bf16[7,2,16,32,128]{4,3,2,1,0:T(8,128)(2,1)S(1)} %get-tuple-element.12.refs_1_.refs_2_), channel_id=1, source_target_pairs={{1,2},{3,4},{5,6},{7,8},{9,10},{11,12},{13,14},{2,1},{4,3},{6,5},{... | collective-permute-start | bytes 5505032 | tf_op jit(solution)/shard_map/ppermute | solution.py:295
  11.2 58.3 %collective-permute-done.1.refs_4_.refs_5_ = bf16[5,2,16,32,128]{4,3,2,1,0:T(8,128)(2,1)S(1)} collective-permute-done((bf16[5,2,16,32,128]{4,3,2,1,0:T(8,128)(2,1)S(1)}, bf16[5,2,16,32,128]{4,3,2,1,0:T(8,128)(2,1)S(1)}, u32[]{:S(2)}, u32[]{:S(2)}) %collective-permute-start.1) | collective-permute-done | bytes 1310752 | tf_op jit(solution)/shard_map/ppermute | solution.py:295
  69.5 0.1 held.1
  69.6 3.1 %collective-permute-start.3 = (bf16[4,2,16,32,128]{4,3,2,1,0:T(8,128)(2,1)S(1)}, bf16[4,2,16,32,128]{4,3,2,1,0:T(8,128)(2,1)S(1)}, u32[]{:S(2)}, u32[]{:S(2)}) collective-permute-start(bf16[4,2,16,32,128]{4,3,2,1,0:T(8,128)(2,1)S(1)} %held.1), channel_id=1, source_target_pairs={{1,2},{3,4},{5,6},{7,8},{9,10},{11,12},{13,14},{2,1},{4,3},{6,5},{... | collective-permute-start | bytes 3145736 | tf_op jit(solution)/shard_map/ppermute | solution.py:295
  72.7 0.0 collective-permute-done.refs_3_.refs_4_
  72.7 0.1 rim.1
  72.8 0.1 collective-permute-start.4
  72.9 2.5 %collective-permute-start.5 = (f32[2,32,128]{2,1,0:T(8,128)S(1)}, f32[2,32,128]{2,1,0:T(8,128)S(1)}, u32[]{:S(2)}, u32[]{:S(2)}) collective-permute-start(f32[2,32,128]{2,1,0:T(8,128)S(1)} %get-tuple-element.16), channel_id=1, source_target_pairs={{1,2},{3,4},{5,6},{7,8},{9,10},{11,12},{13,14},{2,1},{4,3},{6,5},{... | collective-permute-start | bytes 98312 | tf_op jit(solution)/shard_map/ppermute | solution.py:357
  75.4 7.4 %inner.1.refs_7_.refs_8_ = f32[11,3,18,32,128]{4,3,2,1,0:T(8,128)S(1)} custom-call(bf16[5,2,16,32,128]{4,3,2,1,0:T(8,128)(2,1)S(1)} %get-tuple-element.11.refs_0_.refs_1_, bf16[7,2,16,32,128]{4,3,2,1,0:T(8,128)(2,1)S(1)} %get-tuple-element.12.refs_1_.refs_2_, bf16[4,2,16,32,128]{4,3,2,1,0:T(8,128)(2,1)S(1)} %get-tuple-element.13.in_ref.refs_2_.refs_3_, ...), custom_call_target="tpu_custom_call" | custom-call | tf_op jit(solution)/shard_map/inner/pallas_call | solution.py:331
  82.8 6.8 %collective-permute-done.2.refs_5_.refs_6_ = bf16[7,2,16,32,128]{4,3,2,1,0:T(8,128)(2,1)S(1)} collective-permute-done((bf16[7,2,16,32,128]{4,3,2,1,0:T(8,128)(2,1)S(1)}, bf16[7,2,16,32,128]{4,3,2,1,0:T(8,128)(2,1)S(1)}, u32[]{:S(2)}, u32[]{:S(2)}) %collective-permute-start.2) | collective-permute-done | bytes 1835040 | tf_op jit(solution)/shard_map/ppermute | solution.py:295
  89.5 5.3 %near.1.refs_12_ = f32[33,16,4096]{2,1,0:T(8,128)} custom-call(s32[1]{0:T(128)} %bitcast.core_ref.refs_0_, bf16[5,2,16,32,128]{4,3,2,1,0:T(8,128)(2,1)S(1)} %get-tuple-element.11.refs_0_.refs_1_, bf16[7,2,16,32,128]{4,3,2,1,0:T(8,128)(2,1)S(1)} %get-tuple-element.12.refs_1_.refs_2_, ...), custom_call_target="tpu_custom_call" | custom-call | flops 1743257600 | bytes 5505024 | tf_op jit(solution)/shard_map/near/pallas_call | solution.py:372
  94.8 1.4 %middle.1.refs_9_ = f32[4,3,18,32,128]{4,3,2,1,0:T(8,128)S(1)} custom-call(bf16[5,2,16,32,128]{4,3,2,1,0:T(8,128)(2,1)S(1)} %get-tuple-element.11.refs_0_.refs_1_, bf16[7,2,16,32,128]{4,3,2,1,0:T(8,128)(2,1)S(1)} %get-tuple-element.12.refs_1_.refs_2_, bf16[4,2,16,32,128]{4,3,2,1,0:T(8,128)(2,1)S(1)} %get-tuple-element.13.in_ref.refs_2_.refs_3_, ...), custom_call_target="tpu_custom_call" | custom-call | flops 550502400 | tf_op jit(solution)/shard_map/middle/pallas_call | solution.py:331
  96.2 4.6 %collective-permute-done.3.refs_7_ = bf16[4,2,16,32,128]{4,3,2,1,0:T(8,128)(2,1)S(1)} collective-permute-done((bf16[4,2,16,32,128]{4,3,2,1,0:T(8,128)(2,1)S(1)}, bf16[4,2,16,32,128]{4,3,2,1,0:T(8,128)(2,1)S(1)}, u32[]{:S(2)}, u32[]{:S(2)}) %collective-permute-start.3) | collective-permute-done | bytes 1048608 | tf_op jit(solution)/shard_map/ppermute | solution.py:295
  100.8 0.0 collective-permute-done.4.refs_10_
  100.8 0.3 collective-permute-done.5.refs_11_
  101.1 3.2 %far.1 = f32[33,16,4096]{2,1,0:T(8,128)} custom-call(s32[1]{0:T(128)} %bitcast.core_ref.refs_0_, bf16[5,2,16,32,128]{4,3,2,1,0:T(8,128)(2,1)S(1)} %get-tuple-element.11.refs_0_.refs_1_, bf16[7,2,16,32,128]{4,3,2,1,0:T(8,128)(2,1)S(1)} %get-tuple-element.12.refs_1_.refs_2_, ...), custom_call_target="tpu_custom_call", output_to_operand_aliasing={{}: (12, {})} | custom-call | flops 1022361600 | bytes 3145728 | tf_op jit(solution)/shard_map/far/pallas_call | solution.py:372
  (1 shorter events, 0.0 us)
Async XLA Ops:
  4.9 67.7 %collective-permute-start = (bf16[16,2,16,32,128]{4,3,2,1,0:T(8,128)(2,1)}, bf16[16,2,16,32,128]{4,3,2,1,0:T(8,128)(2,1)S(1)}, u32[]{:S(2)}, u32[]{:S(2)}) collective-permute-start(bf16[16,2,16,32,128]{4,3,2,1,0:T(8,128)(2,1)} %get-tuple-element.14), channel_id=1, source_target_pairs={{0,1},{2,3},{4,5},{6,7},{8,9},{10,11},{12,13},{14,15},{1,0},{3,2},... | collective-permute-start | bytes 12582920 | tf_op jit(solution)/shard_map/ppermute | solution.py:296
  5.7 63.9 %collective-permute-start.1 = (bf16[5,2,16,32,128]{4,3,2,1,0:T(8,128)(2,1)S(1)}, bf16[5,2,16,32,128]{4,3,2,1,0:T(8,128)(2,1)S(1)}, u32[]{:S(2)}, u32[]{:S(2)}) collective-permute-start(bf16[5,2,16,32,128]{4,3,2,1,0:T(8,128)(2,1)S(1)} %get-tuple-element.11.refs_0_.refs_1_), channel_id=1, source_target_pairs={{1,2},{3,4},{5,6},{7,8},{9,10},{11,12},{13,14},{2,1},{4,3},{6,5},{... | collective-permute-start | bytes 3932168 | tf_op jit(solution)/shard_map/ppermute | solution.py:295
  8.7 80.8 %collective-permute-start.2 = (bf16[7,2,16,32,128]{4,3,2,1,0:T(8,128)(2,1)S(1)}, bf16[7,2,16,32,128]{4,3,2,1,0:T(8,128)(2,1)S(1)}, u32[]{:S(2)}, u32[]{:S(2)}) collective-permute-start(bf16[7,2,16,32,128]{4,3,2,1,0:T(8,128)(2,1)S(1)} %get-tuple-element.12.refs_1_.refs_2_), channel_id=1, source_target_pairs={{1,2},{3,4},{5,6},{7,8},{9,10},{11,12},{13,14},{2,1},{4,3},{6,5},{... | collective-permute-start | bytes 5505032 | tf_op jit(solution)/shard_map/ppermute | solution.py:295
  69.6 31.2 %collective-permute-start.3 = (bf16[4,2,16,32,128]{4,3,2,1,0:T(8,128)(2,1)S(1)}, bf16[4,2,16,32,128]{4,3,2,1,0:T(8,128)(2,1)S(1)}, u32[]{:S(2)}, u32[]{:S(2)}) collective-permute-start(bf16[4,2,16,32,128]{4,3,2,1,0:T(8,128)(2,1)S(1)} %held.1), channel_id=1, source_target_pairs={{1,2},{3,4},{5,6},{7,8},{9,10},{11,12},{13,14},{2,1},{4,3},{6,5},{... | collective-permute-start | bytes 3145736 | tf_op jit(solution)/shard_map/ppermute | solution.py:295
  72.8 28.0 %collective-permute-start.4 = (f32[2,32,128]{2,1,0:T(8,128)S(1)}, f32[2,32,128]{2,1,0:T(8,128)S(1)}, u32[]{:S(2)}, u32[]{:S(2)}) collective-permute-start(f32[2,32,128]{2,1,0:T(8,128)S(1)} %get-tuple-element.15), channel_id=1, source_target_pairs={{0,1},{2,3},{4,5},{6,7},{8,9},{10,11},{12,13},{14,15},{1,0},{3,2},... | collective-permute-start | bytes 98312 | tf_op jit(solution)/shard_map/ppermute | solution.py:356
  72.9 28.3 %collective-permute-start.5 = (f32[2,32,128]{2,1,0:T(8,128)S(1)}, f32[2,32,128]{2,1,0:T(8,128)S(1)}, u32[]{:S(2)}, u32[]{:S(2)}) collective-permute-start(f32[2,32,128]{2,1,0:T(8,128)S(1)} %get-tuple-element.16), channel_id=1, source_target_pairs={{1,2},{3,4},{5,6},{7,8},{9,10},{11,12},{13,14},{2,1},{4,3},{6,5},{... | collective-permute-start | bytes 98312 | tf_op jit(solution)/shard_map/ppermute | solution.py:357

commit v12 on v11

--- a/solution.py
+++ b/solution.py
@@ -67,7 +67,7 @@
             return 0
 
         count = out_ref.shape[0]
-        lax.fori_loop(0, count, one, 0)
+        lax.fori_loop(0, count, one, 0, unroll=count)
         kept.append(
             pltpu.make_async_copy(out_ref, whole_ref.at[pl.ds(base, count)], sent.at[len(kept)])
         )

time: 105 us -> 105 us (level)
  no operation moved by 1% of the time
where the time goes in v12:
time: 105 us
  waiting for transfers between devices  69.8 us (66%)
  Pallas kernels  22.4 us (21%)
  starting transfers between devices  12.1 us (12%)
    ppermute x3, waiting for transfers between devices, on_device(): arrived.append(lax.ppermute(sent, 'gx', links))  69.4 us
    pallas_call x2, Pallas kernels, partial(): pl.pallas_call(functools.partial(part_kernel, cells, blocks, where, done)...  8.81 us
    ppermute x3, starting transfers between devices, on_device(): arrived.append(lax.ppermute(sent, 'gx', links))  8.61 us
    pallas_call x2, Pallas kernels, lags(): pl.pallas_call(functools.partial(lag_kernel, cells, blocks, where, stages...  8.5 us
    pallas_call x1, Pallas kernels, pack(): pl.pallas_call(pack_kernel, in_specs=[SMEM, hbm, hbm], out_specs=[VMEM] *...  4.91 us
    ppermute x1, starting transfers between devices, on_device(): rim_hi = lax.ppermute(hi, 'gx', links)  2.69 us
  transfers between devices with their start and end apart: 6, of which 4 were waited for; matrix products, arithmetic and copies ran while one was open for 0% of the time, Pallas kernels for 14%

profile of v12, /device:TPU:17, one launch (start us, length us, event | category | flops | bytes accessed | tf_op | source)
XLA Modules:
  0.0 104.5 jit_solution(12102237960470106806)
XLA Ops:
  0.0 4.9 %pack.1 = (bf16[5,2,16,32,128]{4,3,2,1,0:T(8,128)(2,1)S(1)}, bf16[7,2,16,32,128]{4,3,2,1,0:T(8,128)(2,1)S(1)}, bf16[4,2,16,32,128]{4,3,2,1,0:T(8,128)(2,1)S(1)}, bf16[16,2,16,32,128]{4,3,2,1,0:T(8,128)(2,1)}) custom-call(s32[1]{0:T(128)} %bitcast.core_ref.refs_0_, bf16[16,2,8,4096]{3,2,1,0:T(8,128)(2,1)} %s_ref.1, bf16[16,2,8,4096]{3,2,1,0:T(8,128)(2,1)} %r_ref.1), custom_call_target="tpu_custom_call" | custom-call | flops 8388608000 | bytes 8388608 | tf_op jit(solution)/shard_map/pack/pallas_call | solution.py:85
  4.9 0.7 collective-permute-start
  5.7 3.0 %collective-permute-start.1 = (bf16[5,2,16,32,128]{4,3,2,1,0:T(8,128)(2,1)S(1)}, bf16[5,2,16,32,128]{4,3,2,1,0:T(8,128)(2,1)S(1)}, u32[]{:S(2)}, u32[]{:S(2)}) collective-permute-start(bf16[5,2,16,32,128]{4,3,2,1,0:T(8,128)(2,1)S(1)} %get-tuple-element.11.refs_0_.refs_1_), channel_id=1, source_target_pairs={{1,2},{3,4},{5,6},{7,8},{9,10},{11,12},{13,14},{2,1},{4,3},{6,5},{... | collective-permute-start | bytes 3932168 | tf_op jit(solution)/shard_map/ppermute | solution.py:295
  8.7 2.5 %collective-permute-start.2 = (bf16[7,2,16,32,128]{4,3,2,1,0:T(8,128)(2,1)S(1)}, bf16[7,2,16,32,128]{4,3,2,1,0:T(8,128)(2,1)S(1)}, u32[]{:S(2)}, u32[]{:S(2)}) collective-permute-start(bf16[7,2,16,32,128]{4,3,2,1,0:T(8,128)(2,1)S(1)} %get-tuple-element.12.refs_1_.refs_2_), channel_id=1, source_target_pairs={{1,2},{3,4},{5,6},{7,8},{9,10},{11,12},{13,14},{2,1},{4,3},{6,5},{... | collective-permute-start | bytes 5505032 | tf_op jit(solution)/shard_map/ppermute | solution.py:295
  11.2 58.3 %collective-permute-done.1.refs_4_.refs_5_ = bf16[5,2,16,32,128]{4,3,2,1,0:T(8,128)(2,1)S(1)} collective-permute-done((bf16[5,2,16,32,128]{4,3,2,1,0:T(8,128)(2,1)S(1)}, bf16[5,2,16,32,128]{4,3,2,1,0:T(8,128)(2,1)S(1)}, u32[]{:S(2)}, u32[]{:S(2)}) %collective-permute-start.1) | collective-permute-done | bytes 1310752 | tf_op jit(solution)/shard_map/ppermute | solution.py:295
  69.5 0.1 held.1
  69.6 3.1 %collective-permute-start.3 = (bf16[4,2,16,32,128]{4,3,2,1,0:T(8,128)(2,1)S(1)}, bf16[4,2,16,32,128]{4,3,2,1,0:T(8,128)(2,1)S(1)}, u32[]{:S(2)}, u32[]{:S(2)}) collective-permute-start(bf16[4,2,16,32,128]{4,3,2,1,0:T(8,128)(2,1)S(1)} %held.1), channel_id=1, source_target_pairs={{1,2},{3,4},{5,6},{7,8},{9,10},{11,12},{13,14},{2,1},{4,3},{6,5},{... | collective-permute-start | bytes 3145736 | tf_op jit(solution)/shard_map/ppermute | solution.py:295
  72.7 0.0 collective-permute-done.refs_3_.refs_4_
  72.7 0.1 rim.1
  72.8 0.1 collective-permute-start.4
  72.8 2.7 %collective-permute-start.5 = (f32[2,32,128]{2,1,0:T(8,128)S(1)}, f32[2,32,128]{2,1,0:T(8,128)S(1)}, u32[]{:S(2)}, u32[]{:S(2)}) collective-permute-start(f32[2,32,128]{2,1,0:T(8,128)S(1)} %get-tuple-element.16), channel_id=1, source_target_pairs={{1,2},{3,4},{5,6},{7,8},{9,10},{11,12},{13,14},{2,1},{4,3},{6,5},{... | collective-permute-start | bytes 98312 | tf_op jit(solution)/shard_map/ppermute | solution.py:357
  75.5 7.4 %inner.1.refs_7_.refs_8_ = f32[11,3,18,32,128]{4,3,2,1,0:T(8,128)S(1)} custom-call(bf16[5,2,16,32,128]{4,3,2,1,0:T(8,128)(2,1)S(1)} %get-tuple-element.11.refs_0_.refs_1_, bf16[7,2,16,32,128]{4,3,2,1,0:T(8,128)(2,1)S(1)} %get-tuple-element.12.refs_1_.refs_2_, bf16[4,2,16,32,128]{4,3,2,1,0:T(8,128)(2,1)S(1)} %get-tuple-element.13.in_ref.refs_2_.refs_3_, ...), custom_call_target="tpu_custom_call" | custom-call | tf_op jit(solution)/shard_map/inner/pallas_call | solution.py:331
  82.9 6.6 %collective-permute-done.2.refs_5_.refs_6_ = bf16[7,2,16,32,128]{4,3,2,1,0:T(8,128)(2,1)S(1)} collective-permute-done((bf16[7,2,16,32,128]{4,3,2,1,0:T(8,128)(2,1)S(1)}, bf16[7,2,16,32,128]{4,3,2,1,0:T(8,128)(2,1)S(1)}, u32[]{:S(2)}, u32[]{:S(2)}) %collective-permute-start.2) | collective-permute-done | bytes 1835040 | tf_op jit(solution)/shard_map/ppermute | solution.py:295
  89.5 5.3 %near.1.refs_12_ = f32[33,16,4096]{2,1,0:T(8,128)} custom-call(s32[1]{0:T(128)} %bitcast.core_ref.refs_0_, bf16[5,2,16,32,128]{4,3,2,1,0:T(8,128)(2,1)S(1)} %get-tuple-element.11.refs_0_.refs_1_, bf16[7,2,16,32,128]{4,3,2,1,0:T(8,128)(2,1)S(1)} %get-tuple-element.12.refs_1_.refs_2_, ...), custom_call_target="tpu_custom_call" | custom-call | flops 1743257600 | bytes 5505024 | tf_op jit(solution)/shard_map/near/pallas_call | solution.py:372
  94.8 1.4 %middle.1.refs_9_ = f32[4,3,18,32,128]{4,3,2,1,0:T(8,128)S(1)} custom-call(bf16[5,2,16,32,128]{4,3,2,1,0:T(8,128)(2,1)S(1)} %get-tuple-element.11.refs_0_.refs_1_, bf16[7,2,16,32,128]{4,3,2,1,0:T(8,128)(2,1)S(1)} %get-tuple-element.12.refs_1_.refs_2_, bf16[4,2,16,32,128]{4,3,2,1,0:T(8,128)(2,1)S(1)} %get-tuple-element.13.in_ref.refs_2_.refs_3_, ...), custom_call_target="tpu_custom_call" | custom-call | flops 550502400 | tf_op jit(solution)/shard_map/middle/pallas_call | solution.py:331
  96.2 4.6 %collective-permute-done.3.refs_7_ = bf16[4,2,16,32,128]{4,3,2,1,0:T(8,128)(2,1)S(1)} collective-permute-done((bf16[4,2,16,32,128]{4,3,2,1,0:T(8,128)(2,1)S(1)}, bf16[4,2,16,32,128]{4,3,2,1,0:T(8,128)(2,1)S(1)}, u32[]{:S(2)}, u32[]{:S(2)}) %collective-permute-start.3) | collective-permute-done | bytes 1048608 | tf_op jit(solution)/shard_map/ppermute | solution.py:295
  100.8 0.0 collective-permute-done.4.refs_10_
  100.8 0.3 collective-permute-done.5.refs_11_
  101.1 3.2 %far.1 = f32[33,16,4096]{2,1,0:T(8,128)} custom-call(s32[1]{0:T(128)} %bitcast.core_ref.refs_0_, bf16[5,2,16,32,128]{4,3,2,1,0:T(8,128)(2,1)S(1)} %get-tuple-element.11.refs_0_.refs_1_, bf16[7,2,16,32,128]{4,3,2,1,0:T(8,128)(2,1)S(1)} %get-tuple-element.12.refs_1_.refs_2_, ...), custom_call_target="tpu_custom_call", output_to_operand_aliasing={{}: (12, {})} | custom-call | flops 1022361600 | bytes 3145728 | tf_op jit(solution)/shard_map/far/pallas_call | solution.py:372
  (1 shorter events, 0.0 us)
Async XLA Ops:
  4.9 67.7 %collective-permute-start = (bf16[16,2,16,32,128]{4,3,2,1,0:T(8,128)(2,1)}, bf16[16,2,16,32,128]{4,3,2,1,0:T(8,128)(2,1)S(1)}, u32[]{:S(2)}, u32[]{:S(2)}) collective-permute-start(bf16[16,2,16,32,128]{4,3,2,1,0:T(8,128)(2,1)} %get-tuple-element.14), channel_id=1, source_target_pairs={{0,1},{2,3},{4,5},{6,7},{8,9},{10,11},{12,13},{14,15},{1,0},{3,2},... | collective-permute-start | bytes 12582920 | tf_op jit(solution)/shard_map/ppermute | solution.py:296
  5.7 63.9 %collective-permute-start.1 = (bf16[5,2,16,32,128]{4,3,2,1,0:T(8,128)(2,1)S(1)}, bf16[5,2,16,32,128]{4,3,2,1,0:T(8,128)(2,1)S(1)}, u32[]{:S(2)}, u32[]{:S(2)}) collective-permute-start(bf16[5,2,16,32,128]{4,3,2,1,0:T(8,128)(2,1)S(1)} %get-tuple-element.11.refs_0_.refs_1_), channel_id=1, source_target_pairs={{1,2},{3,4},{5,6},{7,8},{9,10},{11,12},{13,14},{2,1},{4,3},{6,5},{... | collective-permute-start | bytes 3932168 | tf_op jit(solution)/shard_map/ppermute | solution.py:295
  8.7 80.8 %collective-permute-start.2 = (bf16[7,2,16,32,128]{4,3,2,1,0:T(8,128)(2,1)S(1)}, bf16[7,2,16,32,128]{4,3,2,1,0:T(8,128)(2,1)S(1)}, u32[]{:S(2)}, u32[]{:S(2)}) collective-permute-start(bf16[7,2,16,32,128]{4,3,2,1,0:T(8,128)(2,1)S(1)} %get-tuple-element.12.refs_1_.refs_2_), channel_id=1, source_target_pairs={{1,2},{3,4},{5,6},{7,8},{9,10},{11,12},{13,14},{2,1},{4,3},{6,5},{... | collective-permute-start | bytes 5505032 | tf_op jit(solution)/shard_map/ppermute | solution.py:295
  69.6 31.2 %collective-permute-start.3 = (bf16[4,2,16,32,128]{4,3,2,1,0:T(8,128)(2,1)S(1)}, bf16[4,2,16,32,128]{4,3,2,1,0:T(8,128)(2,1)S(1)}, u32[]{:S(2)}, u32[]{:S(2)}) collective-permute-start(bf16[4,2,16,32,128]{4,3,2,1,0:T(8,128)(2,1)S(1)} %held.1), channel_id=1, source_target_pairs={{1,2},{3,4},{5,6},{7,8},{9,10},{11,12},{13,14},{2,1},{4,3},{6,5},{... | collective-permute-start | bytes 3145736 | tf_op jit(solution)/shard_map/ppermute | solution.py:295
  72.8 28.0 %collective-permute-start.4 = (f32[2,32,128]{2,1,0:T(8,128)S(1)}, f32[2,32,128]{2,1,0:T(8,128)S(1)}, u32[]{:S(2)}, u32[]{:S(2)}) collective-permute-start(f32[2,32,128]{2,1,0:T(8,128)S(1)} %get-tuple-element.15), channel_id=1, source_target_pairs={{0,1},{2,3},{4,5},{6,7},{8,9},{10,11},{12,13},{14,15},{1,0},{3,2},... | collective-permute-start | bytes 98312 | tf_op jit(solution)/shard_map/ppermute | solution.py:356
  72.8 28.3 %collective-permute-start.5 = (f32[2,32,128]{2,1,0:T(8,128)S(1)}, f32[2,32,128]{2,1,0:T(8,128)S(1)}, u32[]{:S(2)}, u32[]{:S(2)}) collective-permute-start(f32[2,32,128]{2,1,0:T(8,128)S(1)} %get-tuple-element.16), channel_id=1, source_target_pairs={{1,2},{3,4},{5,6},{7,8},{9,10},{11,12},{13,14},{2,1},{4,3},{6,5},{... | collective-permute-start | bytes 98312 | tf_op jit(solution)/shard_map/ppermute | solution.py:357
